TPU v7x, 32 devices: a whole 2x2x4 slice. The times are simulated.
32 devices in a mesh: ctx: 8 (over z, x), head: 4 (over y, core).
Axes of the slice: x: 2, y: 2, z: 4, core: 2. Of those that a mesh axis runs over, the one named last changes fastest.
Arguments:
- tokens: float32 [4096, 2048], P('ctx', 'head'), may hold values from -6 to 6
- w_proj: float32 [2048, 2048], P(None, 'head'), may hold values from -0.125 to 0.125
- w_mix: float32 [2048, 36], P(None, 'head'), may hold values from -0.125 to 0.125
- conv_w: float32 [4, 1536], P(None, 'head'), may hold values from -3 to 3
- rates: float32 [4], P('head'), may hold values from 0.0001 to 0.05
- doc_start: int32 [4096], P('ctx'), may hold values 0 or 1
- norm_gain: float32 [512], P('head'), may hold values from 0.5 to 1.5
- w_out: float32 [512, 2048], P(None, 'head'), may hold values from -0.25 to 0.25
Outputs:
- output: float32 [4096, 2048], P('ctx', 'head')
All inputs are finite; a program needn't handle non-finite values. No bound on the sum of `doc_start` on one device may be relied on, other than what follows from the above.
Results may differ from a plain program's by a relative error of at most 0.00021.
Values sent between devices are 32-bit elements; how exact they have to be, the bound alone decides.
No kernel may reach another device: no remote copies, remote signals or barrier semaphores. Data moves between devices by JAX's collectives and lax.ppermute only.
A program may use at most 64 MiB of HBM per device.

v0:
```python
import jax
import jax.numpy as jnp
from jax import lax
from jax.sharding import PartitionSpec as P


def shifted(value, axis, steps):
    count = lax.axis_size(axis)
    initial, last = (max(0, -steps), min(count, count - steps))
    return lax.ppermute(value, axis, [(source, source + steps) for source in range(initial, last)])


def partner(value, axis, bit):
    mask = 2**bit
    pairs = [(source, source ^ mask) for source in range(lax.axis_size(axis))]
    return lax.ppermute(value, axis, pairs)


def shards(tokens, w_proj, w_mix, conv_w, rates, doc_start, norm_gain, w_out):
    highest = lax.Precision.HIGHEST
    tok_rows = tokens.shape[0]
    width = w_proj.shape[1] // 4
    kernel = conv_w.shape[0]
    rim_rows = kernel - 1
    portion = lax.all_gather(tokens, "head", axis=1, tiled=True)
    projected = jnp.dot(portion, w_proj, precision=highest, preferred_element_type=jnp.float32)
    mixing = jnp.dot(portion, w_mix, precision=highest, preferred_element_type=jnp.float32)
    raw_qkv = projected[:, : 3 * width]
    prior_qkv = shifted(raw_qkv[tok_rows - rim_rows :], "ctx", 1)
    padded = jnp.concatenate([prior_qkv, raw_qkv], axis=0)
    gate_raw = projected[:, 3 * width :]
    convolved = jnp.zeros((tok_rows, 3 * width), jnp.float32)
    for step in range(kernel):
        convolved = convolved + conv_w[step][None, :] * padded[step : step + tok_rows]
    convolved = jax.nn.silu(convolved)
    query = convolved[:, :width]
    keys = convolved[:, width : 2 * width]
    values = convolved[:, 2 * width :]
    query = query / jnp.sqrt(jnp.sum(query * query, axis=1, keepdims=True) + 1e-06)
    keys = keys / jnp.sqrt(jnp.sum(keys * keys, axis=1, keepdims=True) + 1e-06)
    beta = jax.nn.sigmoid(mixing[:, 0])
    log_decay = -rates[0] * jax.nn.softplus(mixing[:, 1]) - 20.0 * doc_start.astype(jnp.float32)
    weights = jax.nn.softplus(mixing[:, 2:])
    cumlog = jnp.cumsum(log_decay)
    row_ids = jnp.arange(tok_rows)[:, None]
    col_ids = jnp.arange(tok_rows)[None, :]
    lower_incl = row_ids >= col_ids
    strict_lower = row_ids > col_ids
    decay_grid = jnp.exp(jnp.where(lower_incl, cumlog[:, None] - cumlog[None, :], -jnp.inf))
    key_gram = jnp.dot(keys, keys.T, precision=highest, preferred_element_type=jnp.float32)
    identity_t = jnp.eye(tok_rows, dtype=jnp.float32)
    identity_d = jnp.eye(width, dtype=jnp.float32)
    lhs_plain = identity_t + beta[:, None] * jnp.where(strict_lower, key_gram, 0.0)
    factor_x = jax.scipy.linalg.solve_triangular(
        lhs_plain, beta[:, None] * keys, lower=True, unit_diagonal=True
    )
    lhs_decay = identity_t + beta[:, None] * jnp.where(strict_lower, decay_grid * key_gram, 0.0)
    factor_y = jax.scipy.linalg.solve_triangular(
        lhs_decay, beta[:, None] * values, lower=True, unit_diagonal=True
    )
    gamma = jnp.exp(cumlog)
    block_a = gamma[-1] * (
        identity_d
        - jnp.dot(factor_x.T, keys, precision=highest, preferred_element_type=jnp.float32)
    )
    tail = jnp.exp(cumlog[-1] - cumlog)
    block_b = jnp.dot(
        (factor_y * tail[:, None]).T, keys, precision=highest, preferred_element_type=jnp.float32
    )
    qk_grid = jnp.dot(query, keys.T, precision=highest, preferred_element_type=jnp.float32)
    carried = gamma[:, None] * (
        query
        - jnp.dot(
            jnp.where(lower_incl, qk_grid, 0.0),
            factor_x,
            precision=highest,
            preferred_element_type=jnp.float32,
        )
    )
    local = jnp.dot(
        decay_grid * qk_grid, factor_y, precision=highest, preferred_element_type=jnp.float32
    )
    my_index = lax.axis_index("ctx")
    nbits = lax.axis_size("ctx").bit_length() - 1
    group_a, group_b = (block_a, block_b)
    carry_m = identity_d
    level_states = []
    for level in range(nbits):
        other_a, other_b = partner((group_a, group_b), "ctx", level)
        upper = my_index >> level & 1 == 1
        seg_a = jnp.where(upper, other_a, identity_d)
        seg_b = jnp.where(upper, other_b, 0.0)
        first_a = jnp.where(upper, other_a, group_a)
        first_b = jnp.where(upper, other_b, group_b)
        second_a = jnp.where(upper, group_a, other_a)
        second_b = jnp.where(upper, group_b, other_b)
        group_a = jnp.dot(first_a, second_a, precision=highest, preferred_element_type=jnp.float32)
        group_b = (
            jnp.dot(first_b, second_a, precision=highest, preferred_element_type=jnp.float32)
            + second_b
        )
        level_states.append(
            jnp.dot(seg_b, carry_m, precision=highest, preferred_element_type=jnp.float32)
        )
        carry_m = jnp.dot(seg_a, carry_m, precision=highest, preferred_element_type=jnp.float32)
    mixed = weights[:, 0:1] * local
    for level in range(nbits):
        mixed = mixed + weights[:, level + 1 : level + 2] * jnp.dot(
            carried, level_states[level].T, precision=highest, preferred_element_type=jnp.float32
        )
    scale = jnp.sqrt(jnp.mean(mixed * mixed, axis=1, keepdims=True) + 1e-05)
    normed = mixed / scale * norm_gain[None, :] * jax.nn.silu(gate_raw)
    own_rows = lax.all_to_all(w_out, "head", split_axis=0, concat_axis=1, tiled=True)
    partial_out = jnp.dot(normed, own_rows, precision=highest, preferred_element_type=jnp.float32)
    result = lax.psum_scatter(partial_out, "head", scatter_dimension=1, tiled=True)
    return result


def solution(mesh):
    placed = (
        P("ctx", "head"),
        P(None, "head"),
        P(None, "head"),
        P(None, "head"),
        P("head"),
        P("ctx"),
        P("head"),
        P(None, "head"),
    )
    return jax.shard_map(
        shards, mesh=mesh, in_specs=placed, out_specs=P("ctx", "head"), check_vma=False
    )
```

profile of v0, /device:TPU:0, one launch (start us, length us, event | category | flops | bytes accessed | tf_op | source)
XLA Modules:
  0.0 283.4 jit_solution(1933743480194011348)
XLA Ops:
  7.3 4.2 %all-to-all-start = ((f32[4,128,512]{2,1,0:T(8,128)}), f32[4,128,512]{2,1,0:T(8,128)S(1)}, u32[]{:S(2)}, u32[]{:S(2)}) async-start(f32[4,128,512]{2,1,0:T(8,128)} %bitcast.85), calls=%async_computation | async-start | bytes 2097152 | tf_op jit(solution)/shard_map/all_to_all | solution.py:113
  14.2 16.3 %all-to-all-done = f32[4,128,512]{2,1,0:T(8,128)S(1)} async-done(((f32[4,128,512]{2,1,0:T(8,128)}), f32[4,128,512]{2,1,0:T(8,128)S(1)}, u32[]{:S(2)}, u32[]{:S(2)}) %all-to-all-start) | async-done | bytes 1048608 | tf_op jit(solution)/shard_map/all_to_all | solution.py:113
  30.8 19.3 %all-gather.2.cloned.1.call-done = f32[512,2048]{1,0:T(8,128)} async-done(((f32[512,512]{1,0:T(8,128)}), f32[512,2048]{1,0:T(8,128)}) %all-gather.2.cloned.1.call-update) | async-done | bytes 4194320 | tf_op jit(solution)/shard_map/all_gather | solution.py:25
  50.1 5.9 %fusion.118 = f32[512,9]{0,1:T(8,128)S(1)} fusion(f32[512,2048]{1,0:T(8,128)} %all-gather.2.cloned.1.call-done, f32[2048,9]{0,1:T(8,128)S(1)} %copy-done), kind=kOutput, calls=%fused_computation.186 | convolution fusion | flops 113246208 | bytes 4286464 | tf_op jit(solution)/shard_map/dot_general | solution.py:27
  56.0 9.0 %fusion.119 = f32[512,512]{1,0:T(8,128)S(1)} fusion(f32[512,2048]{1,0:T(8,128)S(1)} %copy-done.1, f32[2048,512]{1,0:T(8,128)} %param.11), kind=kOutput, calls=%fused_computation.187 | convolution fusion | flops 6442450944 | bytes 9437184 | tf_op jit(solution)/shard_map/dot_general | solution.py:26
  65.1 4.3 %collective-permute-start = (f32[3,384]{1,0:T(4,128)S(1)}, f32[3,384]{1,0:T(4,128)S(1)}, u32[]{:S(2)}, u32[]{:S(2)}) collective-permute-start(f32[3,384]{1,0:T(4,128)S(1)} %slice.136), channel_id=1, source_target_pairs={{0,4},{4,8},{8,12},{12,16},{16,20},{20,24},{24,28},{1,5},{5,9},{9,... | collective-permute-start | bytes 13832 | tf_op jit(solution)/shard_map/ppermute | solution.py:10
  71.2 1.2 subtract_exponential_fusion
  74.1 3.3 %convert_add_fusion = (f32[512,512]{1,0:T(8,128)}, f32[512,512]{1,0:T(8,128)}) fusion(s32[512]{0:T(512)} %iota_add_fusion, f32[512]{0:T(512)S(1)} %bitcast.87, f32[512]{0:T(512)S(1)} %get-tuple-element.45, f32[512,384]{1,0:T(8,128)S(1)} %divide_multiply_fusion, f32[512]{0:T(512)S(1)} %add_sqrt_fusion.1), kind=kOutput, calls=%fused_computation.4 | convolution fusion | flops 407961600 | bytes 2369536 | tf_op jit(solution)/shard_map/dot_general | solution.py:50
  78.2 13.7 %while.5 = (s32[]{:T(128)}, f32[512,512]{1,0:T(8,128)}, s32[4,2]{0,1:T(2,128)S(1)}, f32[4,128,128]{2,1,0:T(8,128)}, s32[]{:T(128)}) while((s32[]{:T(128)}, f32[512,512]{1,0:T(8,128)}, s32[4,2]{0,1:T(2,128)S(1)}, f32[4,128,128]{2,1,0:T(8,128)}, s32[]{:T(128)}) %tuple.50), condition=%wide.while_cond.clone, body=%wide.while_body.clone.sunk | while | flops 2 | bytes 132705 | solution.py:54
  78.8 2.8 %bitcast_dynamic-update-slice_fusion.5 = f32[4,128,128]{2,1,0:T(8,128)} fusion(f32[4,128,128]{2,1,0:T(8,128)} %get-tuple-element.143, s32[]{:T(128)} %get-tuple-element.140, f32[512,512]{1,0:T(8,128)} %get-tuple-element.146, s32[]{:T(128)} %bitcast.81, s32[]{:T(128)} %bitcast.82), kind=kLoop, calls=%fused_computation.2.clone.1 | loop fusion | bytes 132608 | tf_op jit(solution)/shard_map/jit(_solve_triangular) | solution.py:54
  82.3 2.8 bitcast_dynamic-update-slice_fusion.5
  85.7 2.8 bitcast_dynamic-update-slice_fusion.5
  89.1 2.8 bitcast_dynamic-update-slice_fusion.5
  91.9 40.7 %custom-call.5 = f32[4,128,128]{1,2,0:T(8,128)} custom-call(f32[4,128,128]{2,1,0:T(8,128)} %get-tuple-element.21), custom_call_target="InvertDiagBlocksLowerTriangular" | custom-call | tf_op jit(solution)/shard_map/jit(_solve_triangular)/triangular_solve | solution.py:54
  138.4 1.3 convolution_subtract_fusion.6
  141.4 1.4 fusion.4
  142.8 1.6 collective-permute-start.2
  145.1 13.7 %while.4 = (s32[]{:T(128)}, f32[512,512]{1,0:T(8,128)}, s32[4,2]{0,1:T(2,128)S(1)}, f32[4,128,128]{2,1,0:T(8,128)}, s32[]{:T(128)}) while((s32[]{:T(128)}, f32[512,512]{1,0:T(8,128)}, s32[4,2]{0,1:T(2,128)S(1)}, f32[4,128,128]{2,1,0:T(8,128)}, s32[]{:T(128)}) %tuple.57), condition=%wide.while_cond, body=%wide.while_body.sunk | while | flops 2 | bytes 132705 | solution.py:58
  145.8 2.8 bitcast_dynamic-update-slice_fusion.4
  149.2 2.8 bitcast_dynamic-update-slice_fusion.4
  152.7 2.8 bitcast_dynamic-update-slice_fusion.4
  156.1 2.8 bitcast_dynamic-update-slice_fusion.4
  158.9 40.7 %custom-call.4 = f32[4,128,128]{1,2,0:T(8,128)} custom-call(f32[4,128,128]{2,1,0:T(8,128)} %get-tuple-element.20), custom_call_target="InvertDiagBlocksLowerTriangular" | custom-call | tf_op jit(solution)/shard_map/jit(_solve_triangular)/triangular_solve | solution.py:58
  207.7 1.4 fusion.31
  210.8 1.7 fusion.3
  212.5 1.8 convolution_multiply_fusion.3
  214.6 1.6 collective-permute-start.4
  217.7 1.9 collective-permute-done.4
  220.9 2.9 %collective-permute-start.5 = (f32[128,128]{1,0:T(8,128)S(1)}, f32[128,128]{1,0:T(8,128)S(1)}, u32[]{:S(2)}, u32[]{:S(2)}) collective-permute-start(f32[128,128]{1,0:T(8,128)S(1)} %convolution_add_fusion), channel_id=1, source_target_pairs={{0,16},{4,20},{8,24},{12,28},{16,0},{20,4},{24,8},{28,12},{1,17},{... | collective-permute-start | bytes 196616 | tf_op jit(solution)/shard_map/ppermute | solution.py:16
  224.7 2.1 collective-permute-done.5
  227.5 5.2 %fusion.21 = f32[512,2048]{1,0:T(8,128)} fusion(f32[128,2048]{0,1:T(8,128)S(1)} %bitcast.84, f32[512,512]{1,0:T(8,128)S(1)} %fusion.119, f32[512,128]{1,0:T(8,128)S(1)} %get-tuple-element.61, f32[128]{0:T(128)S(1)} %copy-done.15, f32[512]{0:T(512)S(1)} %add_sqrt_fusion), kind=kOutput, calls=%fused_computation.56 | convolution fusion | flops 1611071488 | bytes 5769728 | tf_op jit(solution)/shard_map/dot_general | solution.py:114
  232.7 43.9 %reduce-scatter.2.cloned.1.call-done = f32[512,512]{1,0:T(8,128)} async-done(((f32[512,2048]{1,0:T(8,128)}), f32[512,512]{1,0:T(8,128)}) %reduce-scatter.2.cloned.1.call-update) | async-done | bytes 1048592 | tf_op jit(solution)/shard_map/reduce_scatter | solution.py:115
  (111 shorter events, 34.5 us)
Async XLA Ops:
  6.5 43.5 %copy-start = (f32[2048,9]{0,1:T(8,128)S(1)}, f32[2048,9]{0,1:T(8,128)}, u32[]{:S(2)}) copy-start(f32[2048,9]{0,1:T(8,128)} %param.12) | copy-start | bytes 221188
  6.5 43.5 %all-gather.2.cloned.1.call-start = ((), (), s32[]{:S(2)}) async-start(), calls=%async_computation.2 | async-start | bytes 5242880 | tf_op jit(solution)/shard_map/all_gather | solution.py:25
  7.3 23.2 %all-to-all-start = ((f32[4,128,512]{2,1,0:T(8,128)}), f32[4,128,512]{2,1,0:T(8,128)S(1)}, u32[]{:S(2)}, u32[]{:S(2)}) async-start(f32[4,128,512]{2,1,0:T(8,128)} %bitcast.85), calls=%async_computation | async-start | bytes 2097152 | tf_op jit(solution)/shard_map/all_to_all | solution.py:113
  11.5 265.0 %reduce-scatter.2.cloned.1.call-start = ((), (), s32[]{:S(2)}) async-start(), calls=%async_computation.3 | async-start | bytes 5242880 | tf_op jit(solution)/shard_map/reduce_scatter | solution.py:115
  50.1 6.0 %copy-start.1 = (f32[512,2048]{1,0:T(8,128)S(1)}, f32[512,2048]{1,0:T(8,128)}, u32[]{:S(2)}) copy-start(f32[512,2048]{1,0:T(8,128)} %all-gather.2.cloned.1.call-done) | copy-start | bytes 12582916
  56.0 13.3 %copy-start.13 = (s32[512]{0:T(512)S(1)}, s32[512]{0:T(512)}, u32[]{:S(2)}) copy-start(s32[512]{0:T(512)} %param.15) | copy-start | bytes 6148
  65.1 8.1 %collective-permute-start = (f32[3,384]{1,0:T(4,128)S(1)}, f32[3,384]{1,0:T(4,128)S(1)}, u32[]{:S(2)}, u32[]{:S(2)}) collective-permute-start(f32[3,384]{1,0:T(4,128)S(1)} %slice.136), channel_id=1, source_target_pairs={{0,4},{4,8},{8,12},{12,16},{16,20},{20,24},{24,28},{1,5},{5,9},{9,... | collective-permute-start | bytes 13832 | tf_op jit(solution)/shard_map/ppermute | solution.py:10
  70.0 3.9 %copy-start.14 = (f32[512]{0:T(512)}, f32[512]{0:T(512)S(1)}, u32[]{:S(2)}) copy-start(f32[512]{0:T(512)S(1)} %get-tuple-element.44) | copy-start | bytes 6148
  70.0 7.4 %copy-start.12 = (f32[512]{0:T(512)}, f32[512]{0:T(512)S(1)}, u32[]{:S(2)}) copy-start(f32[512]{0:T(512)S(1)} %get-tuple-element.45) | copy-start | bytes 6148
  73.7 3.8 %copy-start.16 = (s32[4]{0:T(128)S(1)}, s32[4]{0:T(128)}, u32[]{:S(2)}) copy-start(s32[4]{0:T(128)} %iota_multiply_fusion) | copy-start | bytes 52
  133.8 7.0 %copy-start.2 = (f32[128,128]{1,0:T(8,128)}, f32[128,128]{1,0:T(8,128)S(1)}, u32[]{:S(2)}) copy-start(f32[128,128]{1,0:T(8,128)S(1)} %fusion.63) | copy-start | bytes 196612
  136.0 6.8 %copy-start.4 = (f32[128,128]{1,0:T(8,128)}, f32[128,128]{1,0:T(8,128)S(1)}, u32[]{:S(2)}) copy-start(f32[128,128]{1,0:T(8,128)S(1)} %fusion.62) | copy-start | bytes 196612
  138.3 6.1 %copy-start.6 = (f32[128,128]{1,0:T(8,128)}, f32[128,128]{1,0:T(8,128)S(1)}, u32[]{:S(2)}) copy-start(f32[128,128]{1,0:T(8,128)S(1)} %fusion.60) | copy-start | bytes 196612
  140.8 0.6 copy-start.8
  142.8 68.0 %copy-start.3 = (f32[128,128]{1,0:T(8,128)S(1)}, f32[128,128]{1,0:T(8,128)}, u32[]{:S(2)}) copy-start(f32[128,128]{1,0:T(8,128)} %copy-done.2) | copy-start | bytes 196612
  142.8 71.6 %collective-permute-start.2 = (f32[128,128]{1,0:T(8,128)S(1)}, f32[128,128]{1,0:T(8,128)S(1)}, u32[]{:S(2)}, u32[]{:S(2)}) collective-permute-start(f32[128,128]{1,0:T(8,128)S(1)} %fusion.4), channel_id=1, source_target_pairs={{0,4},{4,0},{8,12},{12,8},{16,20},{20,16},{24,28},{28,24},{1,5},{5... | collective-permute-start | bytes 196616 | tf_op jit(solution)/shard_map/ppermute | solution.py:16
  144.4 66.4 %copy-start.5 = (f32[128,128]{1,0:T(8,128)S(1)}, f32[128,128]{1,0:T(8,128)}, u32[]{:S(2)}) copy-start(f32[128,128]{1,0:T(8,128)} %copy-done.4) | copy-start | bytes 196612
  199.6 11.2 %copy-start.7 = (f32[128,128]{1,0:T(8,128)S(1)}, f32[128,128]{1,0:T(8,128)}, u32[]{:S(2)}) copy-start(f32[128,128]{1,0:T(8,128)} %copy-done.6) | copy-start | bytes 196612
  199.6 11.2 %copy-start.9 = (f32[128,128]{1,0:T(8,128)S(1)}, f32[128,128]{1,0:T(8,128)}, u32[]{:S(2)}) copy-start(f32[128,128]{1,0:T(8,128)} %copy-done.8) | copy-start | bytes 196612
  207.7 9.5 %copy-start.11 = (f32[512,1]{0,1:T(1,128)S(1)}, f32[512,1]{0,1:T(1,128)}, u32[]{:S(2)}) copy-start(f32[512,1]{0,1:T(1,128)} %get-tuple-element.58) | copy-start | bytes 6148
  209.1 7.1 %collective-permute-start.1 = (f32[128,128]{1,0:T(8,128)S(1)}, f32[128,128]{1,0:T(8,128)S(1)}, u32[]{:S(2)}, u32[]{:S(2)}) collective-permute-start(f32[128,128]{1,0:T(8,128)S(1)} %fusion.31), channel_id=1, source_target_pairs={{0,4},{4,0},{8,12},{12,8},{16,20},{20,16},{24,28},{28,24},{1,5},{5... | collective-permute-start | bytes 196616 | tf_op jit(solution)/shard_map/ppermute | solution.py:16
  209.7 14.4 %copy-start.10 = (f32[512,1]{0,1:T(1,128)S(1)}, f32[512,1]{0,1:T(1,128)}, u32[]{:S(2)}) copy-start(f32[512,1]{0,1:T(1,128)} %get-tuple-element.57) | copy-start | bytes 6148
  210.8 16.7 %copy-start.15 = (f32[128]{0:T(128)S(1)}, f32[128]{0:T(128)}, u32[]{:S(2)}) copy-start(f32[128]{0:T(128)} %param.16) | copy-start | bytes 1540
  214.6 5.0 %collective-permute-start.4 = (f32[128,128]{1,0:T(8,128)S(1)}, f32[128,128]{1,0:T(8,128)S(1)}, u32[]{:S(2)}, u32[]{:S(2)}) collective-permute-start(f32[128,128]{1,0:T(8,128)S(1)} %fusion.74), channel_id=1, source_target_pairs={{0,8},{4,12},{8,0},{12,4},{16,24},{20,28},{24,16},{28,20},{1,9},{5... | collective-permute-start | bytes 196616 | tf_op jit(solution)/shard_map/ppermute | solution.py:16
  216.4 4.3 %collective-permute-start.3 = (f32[128,128]{1,0:T(8,128)S(1)}, f32[128,128]{1,0:T(8,128)S(1)}, u32[]{:S(2)}, u32[]{:S(2)}) collective-permute-start(f32[128,128]{1,0:T(8,128)S(1)} %convolution_add_fusion.1), channel_id=1, source_target_pairs={{0,8},{4,12},{8,0},{12,4},{16,24},{20,28},{24,16},{28,20},{1,9},{5... | collective-permute-start | bytes 196616 | tf_op jit(solution)/shard_map/ppermute | solution.py:16
  220.9 5.8 %collective-permute-start.5 = (f32[128,128]{1,0:T(8,128)S(1)}, f32[128,128]{1,0:T(8,128)S(1)}, u32[]{:S(2)}, u32[]{:S(2)}) collective-permute-start(f32[128,128]{1,0:T(8,128)S(1)} %convolution_add_fusion), channel_id=1, source_target_pairs={{0,16},{4,20},{8,24},{12,28},{16,0},{20,4},{24,8},{28,12},{1,17},{... | collective-permute-start | bytes 196616 | tf_op jit(solution)/shard_map/ppermute | solution.py:16
Sparse Core Ops, SparseCore 0:
  8.9 41.0 all-gather.1
  232.8 43.6 reduce-scatter.1
where the time goes:
time: 285 us; the launch traced here: 283 us
  waiting for transfers between devices  85.3 us (30%)
  other arithmetic  85.3 us (30%)
  matrix products  49.6 us (17%)
  local copies, waits for them, and re-layouts  32.9 us (12%)
  starting transfers between devices  15.7 us (6%)
  between operations  14.5 us (5%)
    reduce_scatter x1, waiting for transfers between devices, shards(): lax.psum_scatter(partial_out, 'head', scatter_dimension=1, tiled=True)  43.9 us
    another operation x3, other arithmetic, shards(): jax.scipy.linalg.solve_triangular(lhs_decay, beta[:, None] * values, lowe...  41.9 us
    another operation x1, other arithmetic, shards(): jax.scipy.linalg.solve_triangular(lhs_plain, beta[:, None] * keys, lower=...  40.7 us
    all_gather x1, waiting for transfers between devices, shards(): portion = lax.all_gather(tokens, 'head', axis=1, tiled=True)  19.3 us
    all_to_all x1, waiting for transfers between devices, shards(): lax.all_to_all(w_out, 'head', split_axis=0, concat_axis=1, tiled=True)  16.3 us
    another operation x15, local copies, waits for them, and re-layouts, shards(): jax.scipy.linalg.solve_triangular(lhs_decay, beta[:, None] * values, lowe...  15.2 us
    another operation x12, local copies, waits for them, and re-layouts, shards(): jax.scipy.linalg.solve_triangular(lhs_plain, beta[:, None] * keys, lower=...  13.7 us
    dot_general x1, matrix products, shards(): jnp.dot(portion, w_proj, precision=highest, preferred_element_type=jnp.fl...  9.03 us
  transfers between devices with their start and end apart: 9, of which 6 were waited for; matrix products, arithmetic and copies ran while one was open for 27% of the time, Pallas kernels for 0%

commit v1 on v0

v1 whole, which is shorter than its diff:
```python
import functools

import jax
import jax.numpy as jnp
from jax import lax
from jax.experimental import pallas as pl
from jax.experimental.pallas import tpu as pltpu
from jax.sharding import PartitionSpec as P

CHUNK = 128
F32 = jnp.float32
BF16 = jnp.bfloat16


def halves(value):
    high = value.astype(BF16)
    return high, (value - high.astype(F32)).astype(BF16)


def left_parts(value):
    return jnp.concatenate(halves(value), axis=1)


def right_parts(value):
    row = jnp.concatenate(halves(value), axis=1)
    return jnp.concatenate([row, row], axis=0)


def parts_dot(left, right):
    both = jnp.dot(left, right, preferred_element_type=F32)
    half = both.shape[1] // 2
    return both[:, :half] + both[:, half:]


def product(left, right):
    return parts_dot(left_parts(left), right_parts(right))


def softplus(value):
    return jnp.maximum(value, 0.0) + jnp.log1p(jnp.exp(-jnp.abs(value)))


def sigmoid(value):
    return 1.0 / (1.0 + jnp.exp(-value))


def unit_lower_inverse(lowers, row, col):
    size = lowers[0].shape[0]
    eye = jnp.where(row == col, 1.0, 0.0).astype(F32)
    inverses = [eye - jnp.where((row >> 1) == (col >> 1), lower, 0.0) for lower in lowers]
    lower_parts = [halves(lower) for lower in lowers]
    step = 1
    while 2 << (step - 1) < size:
        off = ((row >> (step + 1)) == (col >> (step + 1))) & ((row >> step) > (col >> step))
        lefts = [left_parts(inverse) for inverse in inverses]
        offs = [
            jnp.concatenate([jnp.where(off, part, jnp.zeros_like(part)) for part in parts], axis=1)
            for parts in lower_parts
        ]
        inner = [
            parts_dot(offdiag, right_parts(inverse)) for offdiag, inverse in zip(offs, inverses)
        ]
        inverses = [
            inverse - parts_dot(left, right_parts(value))
            for inverse, left, value in zip(inverses, lefts, inner)
        ]
        step += 1
    return inverses


def local_kernel(
    raw_ref, rim_ref, mix_ref, conv_ref, rate_ref, doc_ref,
    carried_ref, local_ref, weight_ref, pair_ref, padded,
):
    tok_rows = raw_ref.shape[0]
    width = raw_ref.shape[1] // 3
    taps = conv_ref.shape[0]
    rim = rim_ref.shape[0]
    chunks = tok_rows // CHUNK
    padded[0:rim, :] = rim_ref[...]
    padded[rim:, :] = raw_ref[...]
    row = lax.broadcasted_iota(jnp.int32, (CHUNK, CHUNK), 0)
    col = lax.broadcasted_iota(jnp.int32, (CHUNK, CHUNK), 1)
    lower = row >= col
    tri = jnp.where(lower, 1.0, 0.0).astype(F32)
    rate = rate_ref[0, 0]
    queries, keys, values, betas, grids, gammas, tails = [], [], [], [], [], [], []
    for part in range(chunks):
        base = part * CHUNK
        conv = conv_ref[0:1, :] * padded[base + rim - taps + 1 : base + rim - taps + 1 + CHUNK, :]
        for tap in range(1, taps):
            start = base + rim - taps + 1 + tap
            conv = conv + conv_ref[tap : tap + 1, :] * padded[start : start + CHUNK, :]
        conv = conv * sigmoid(conv)
        query = conv[:, :width]
        key = conv[:, width : 2 * width]
        query = query * lax.rsqrt(jnp.sum(query * query, axis=1, keepdims=True) + 1e-06)
        key = key * lax.rsqrt(jnp.sum(key * key, axis=1, keepdims=True) + 1e-06)
        queries.append(query)
        keys.append(key)
        values.append(conv[:, 2 * width :])
        mixing = mix_ref[base : base + CHUNK, :]
        plus = softplus(mixing)
        weight_ref[base : base + CHUNK, :] = plus
        betas.append(sigmoid(mixing[:, 0:1]))
        docs = jnp.transpose(jnp.broadcast_to(doc_ref[part : part + 1, :], (CHUNK, CHUNK)))
        steps = jnp.where(col == 1, -rate * plus, jnp.where(col == 0, docs, 0.0))
        sums = jnp.dot(tri, steps, precision=lax.Precision.HIGHEST, preferred_element_type=F32)
        across = jnp.transpose(sums)
        smooth, count = sums[:, 1:2], sums[:, 0:1]
        span = (smooth - across[1:2, :]) - 20.0 * (count - across[0:1, :])
        grids.append(jnp.exp(jnp.where(lower, span, -1e30)))
        gammas.append(jnp.exp(smooth - 20.0 * count))
        last = sums[CHUNK - 1 : CHUNK, :]
        tails.append(jnp.exp((last[:, 1:2] - smooth) - 20.0 * (last[:, 0:1] - count)))
    across_keys = [jnp.transpose(key) for key in keys]
    grams = [
        parts_dot(left_parts(jnp.concatenate([key, query], axis=0)), right_parts(across))
        for key, query, across in zip(keys, queries, across_keys)
    ]
    lowers = [
        jnp.where(row > col, beta * gram[:CHUNK], 0.0) for beta, gram in zip(betas, grams)
    ]
    inverses = unit_lower_inverse(lowers, row, col)
    states = None
    eye = jnp.where(row == col, 1.0, 0.0).astype(F32)
    for part in range(chunks):
        base = part * CHUNK
        inverse, beta, grid = inverses[part], betas[part], grids[part]
        factor_x = product(inverse, beta * keys[part])
        factor_y = product(grid * inverse, beta * values[part])
        left_keys = left_parts(across_keys[part])
        gamma, tail = gammas[part], tails[part]
        trans = gamma[CHUNK - 1 : CHUNK, :] * (eye - parts_dot(left_keys, right_parts(factor_x)))
        memory = parts_dot(left_keys, right_parts(tail * factor_y))
        overlap = grams[part][CHUNK:]
        carried = gamma * (
            queries[part] - product(jnp.where(lower, overlap, 0.0), factor_x)
        )
        local = product(grid * overlap, factor_y)
        if states is None:
            states = (memory, trans)
        else:
            left = left_parts(jnp.concatenate([carried, trans], axis=0))
            onto_s = parts_dot(left, right_parts(states[0]))
            onto_a = parts_dot(left, right_parts(states[1]))
            local = local + onto_s[:CHUNK]
            carried = onto_a[:CHUNK]
            states = (onto_s[CHUNK:] + memory, onto_a[CHUNK:])
        carried_ref[base : base + CHUNK, :] = carried
        local_ref[base : base + CHUNK, :] = local
    pair_ref[0] = states[1]
    pair_ref[1] = states[0]


def mix_kernel(carried_ref, local_ref, weight_ref, level_ref, gate_ref, gain_ref, normed_ref):
    levels = level_ref.shape[0]
    carried = left_parts(carried_ref[...])
    weights = weight_ref[...]
    mixed = weights[:, 2:3] * local_ref[...]
    for level in range(levels):
        mixed = mixed + weights[:, level + 3 : level + 4] * parts_dot(
            carried, right_parts(level_ref[level])
        )
    scale = lax.rsqrt(jnp.mean(mixed * mixed, axis=1, keepdims=True) + 1e-05)
    gate = gate_ref[...]
    normed_ref[...] = mixed * scale * gain_ref[...] * (gate * sigmoid(gate))


def vmem_call(kernel, outs, scratch, *args):
    spec = pl.BlockSpec(memory_space=pltpu.VMEM)
    return pl.pallas_call(
        kernel,
        out_shape=outs,
        in_specs=[spec] * len(args),
        out_specs=jax.tree.map(lambda unused: spec, outs),
        scratch_shapes=scratch,
        compiler_params=pltpu.CompilerParams(vmem_limit_bytes=40 << 20),
    )(*args)


def gather_head(value):
    count = lax.axis_size("head")
    me = lax.axis_index("head")
    siblings = [(source, source ^ 1) for source in range(count)]
    gathered = [(me, value)]
    for step in range(1, count // 2):
        pairs = [(source, (source + 2 * step) % count) for source in range(count)]
        gathered.append(((me + count - 2 * step) % count, lax.ppermute(value, "head", pairs)))
    for index, held in list(gathered):
        gathered.append((index ^ 1, lax.ppermute(held, "head", siblings)))
    return gathered


def gathered_dot(pieces, weight):
    total = 0.0
    for index, piece in pieces:
        depth = piece.shape[1]
        rows = lax.dynamic_slice_in_dim(weight, index * depth, depth, 0)
        total = total + jnp.dot(
            piece, rows, precision=lax.Precision.HIGH, preferred_element_type=F32
        )
    return total


def partner(value, axis, bit):
    pairs = [(source, source ^ (1 << bit)) for source in range(lax.axis_size(axis))]
    return lax.ppermute(value, axis, pairs)


def shards(tokens, w_proj, w_mix, conv_w, rates, doc_start, norm_gain, w_out):
    tok_rows = tokens.shape[0]
    width = w_proj.shape[1] // 4
    mixes = w_mix.shape[1]
    rim_rows = conv_w.shape[0] - 1
    weight = jnp.concatenate([w_proj, jnp.pad(w_mix, ((0, 0), (0, CHUNK - mixes)))], axis=1)
    raw = gathered_dot(gather_head(tokens), weight)
    raw_qkv = raw[:, : 3 * width]
    gate_raw = raw[:, 3 * width : 4 * width]
    mixing = raw[:, 4 * width :]
    blocks = lax.axis_size("ctx")
    rim = lax.ppermute(
        raw_qkv[tok_rows - 8 :], "ctx", [(source, source + 1) for source in range(blocks - 1)]
    )
    shape = jax.ShapeDtypeStruct((tok_rows, width), F32)
    carried, local, weights, pair = vmem_call(
        local_kernel,
        [shape, shape, jax.ShapeDtypeStruct((tok_rows, CHUNK), F32),
         jax.ShapeDtypeStruct((2, width, width), F32)],
        [pltpu.VMEM((tok_rows + 8, 3 * width), F32)],
        raw_qkv, rim, mixing, conv_w, rates[:, None],
        doc_start.astype(F32).reshape(tok_rows // CHUNK, CHUNK),
    )
    my_index = lax.axis_index("ctx")
    high = functools.partial(
        jnp.dot, precision=lax.Precision.HIGHEST, preferred_element_type=F32
    )
    group_a, group_s = pair[0], pair[1]
    identity = jnp.eye(width, dtype=F32)
    carry = identity
    level_states = []
    for level in range(blocks.bit_length() - 1):
        other_a, other_s = partner((group_a, group_s), "ctx", level)
        upper = my_index >> level & 1 == 1
        seg_a = jnp.where(upper, other_a, identity)
        seg_s = jnp.where(upper, other_s, 0.0)
        first_a = jnp.where(upper, other_a, group_a)
        first_s = jnp.where(upper, other_s, group_s)
        second_a = jnp.where(upper, group_a, other_a)
        second_s = jnp.where(upper, group_s, other_s)
        group_a = high(second_a, first_a)
        group_s = high(second_a, first_s) + second_s
        level_states.append(high(carry, seg_s))
        carry = high(carry, seg_a)
    normed = vmem_call(
        mix_kernel, shape, [],
        carried, local, weights, jnp.stack(level_states), gate_raw, norm_gain[None, :],
    )
    return gathered_dot(gather_head(normed), w_out)


def solution(mesh):
    placed = (
        P("ctx", "head"),
        P(None, "head"),
        P(None, "head"),
        P(None, "head"),
        P("head"),
        P("ctx"),
        P("head"),
        P(None, "head"),
    )
    return jax.shard_map(
        shards, mesh=mesh, in_specs=placed, out_specs=P("ctx", "head"), check_vma=False
    )
```

time: 285 us -> 72.7 us (0.26)
  other arithmetic: 85.3 us -> 2.79 us
  waiting for transfers between devices: 85.3 us -> 33.5 us
  matrix products: 49.6 us -> 12.1 us
  local copies, waits for them, and re-layouts: 32.9 us -> 1.38 us
  between operations: 14.5 us -> 0.95 us
  Pallas kernels: 0 us -> 5.28 us
    another operation x7 -> x1, other arithmetic: 83 us -> 0.02 us  [shards(): jnp.stack(level_states)]
    reduce_scatter x1 -> x0, waiting for transfers between devices: 43.9 us -> none  [shards(): lax.psum_scatter(partial_out, 'head', scatter_dimension=1, tiled=True)]
    another operation x29 -> x0, local copies, waits for them, and re-layouts: 29.1 us -> none  [the longest x15 15.2 us: shards(): jax.scipy.linalg.solve_triangular(lhs_decay, beta[:, None] * values, lowe...]
    ppermute x1 -> x7, waiting for transfers between devices: 0.01 us -> 24.6 us  [the longest x2 23.5 us: gather_head(): lax.ppermute(value, 'head', pairs)]
    dot_general x20 -> x16, matrix products: 33.6 us -> 12.1 us  [the longest x8 10.5 us: gathered_dot(): jnp.dot(piece, rows, precision=lax.Precision.HIGH, preferred_element_type...]
    all_gather x1 -> x0, waiting for transfers between devices: 19.3 us -> none  [shards(): portion = lax.all_gather(tokens, 'head', axis=1, tiled=True)]
    all_to_all x1 -> x0, waiting for transfers between devices: 16.3 us -> none  [shards(): lax.all_to_all(w_out, 'head', split_axis=0, concat_axis=1, tiled=True)]
    another operation x14 -> x0, matrix products: 16 us -> none  [the longest x7 8.03 us: shards(): jax.scipy.linalg.solve_triangular(lhs_plain, beta[:, None] * keys, lower=...]
  transfers between devices with their start and end apart: 9 -> 12, of which waited for: 6 -> 7; matrix products, arithmetic and copies ran while one was open for 27% -> 18% of each run, Pallas kernels for 0% -> 0%
where the time goes in v1:
time: 72.7 us; the launch traced here: 72.4 us
  waiting for transfers between devices  33.5 us (46%)
  starting transfers between devices  16.5 us (23%)
  matrix products  12.1 us (17%)
  Pallas kernels  5.28 us (7%)
  other arithmetic  2.79 us (4%)
  local copies, waits for them, and re-layouts  1.38 us (2%)
  between operations  0.95 us (1%)
    ppermute x2, waiting for transfers between devices, gather_head(): lax.ppermute(value, 'head', pairs)  23.5 us
    dot_general x8, matrix products, gathered_dot(): jnp.dot(piece, rows, precision=lax.Precision.HIGH, preferred_element_type...  10.5 us
    ppermute x5, waiting for transfers between devices, partner(): return lax.ppermute(value, axis, pairs)  8.86 us
    ppermute x5, starting transfers between devices, partner(): return lax.ppermute(value, axis, pairs)  8.12 us
    pallas_call x2, Pallas kernels, vmem_call(): pl.pallas_call(kernel, out_shape=outs, in_specs=[spec] * len(args), out_s...  5.28 us
    ppermute x2, starting transfers between devices, gather_head(): lax.ppermute(value, 'head', pairs)  4.55 us
    ppermute x1, starting transfers between devices, shards(): lax.ppermute(raw_qkv[tok_rows - 8:], 'ctx', [(source, source + 1) for sou...  3.8 us
    concatenate x1, other arithmetic, shards(): jnp.concatenate([w_proj, jnp.pad(w_mix, ((0, 0), (0, CHUNK - mixes)))], a...  2.77 us
  transfers between devices with their start and end apart: 12, of which 7 were waited for; matrix products, arithmetic and copies ran while one was open for 18% of the time, Pallas kernels for 0%

profile of v1, /device:TPU:0, one launch (start us, length us, event | category | flops | bytes accessed | tf_op | source)
XLA Modules:
  0.0 72.4 jit_solution(15093956703913254198)
XLA Ops:
  0.0 3.0 %collective-permute-start = (f32[512,512]{1,0:T(8,128)}, f32[512,512]{1,0:T(8,128)S(1)}, u32[]{:S(2)}, u32[]{:S(2)}) collective-permute-start(f32[512,512]{1,0:T(8,128)} %param.8), channel_id=1, source_target_pairs={{0,2},{1,3},{2,0},{3,1},{4,6},{5,7},{6,4},{7,5},{8,10},{9,11},{10,... | collective-permute-start | bytes 3145736 | tf_op jit(solution)/shard_map/ppermute | solution.py:189
  3.0 1.3 %copy.10 = f32[2048,9]{1,0:T(8,128)S(1)} copy(f32[2048,9]{0,1:T(8,128)} %param.10) | data formatting | bytes 147456
  4.9 2.8 %select_maximum_fusion = f32[2048,640]{1,0:T(8,128)S(1)} fusion(f32[2048,9]{1,0:T(8,128)S(1)} %copy.10, f32[2048,512]{1,0:T(8,128)} %param.9), kind=kLoop, calls=%fused_computation | loop fusion | flops 3932160 | bytes 9510912 | tf_op jit(solution)/shard_map/concatenate | solution.py:216
  7.7 18.6 %collective-permute-done = f32[512,512]{1,0:T(8,128)S(1)} collective-permute-done((f32[512,512]{1,0:T(8,128)}, f32[512,512]{1,0:T(8,128)S(1)}, u32[]{:S(2)}, u32[]{:S(2)}) %collective-permute-start) | collective-permute-done | bytes 1048608 | tf_op jit(solution)/shard_map/ppermute | solution.py:189
  26.4 1.5 %fusion.5 = f32[640,512]{0,1:T(8,128)S(1)} fusion(f32[512,512]{1,0:T(8,128)S(1)} %copy-done.3, f32[2048,640]{1,0:T(8,128)S(1)} %select_maximum_fusion, s32[]{:T(128)S(6)} %select_n.91), kind=kOutput, calls=%fused_computation.12 | convolution fusion | flops 1006632960 | bytes 3670020 | tf_op jit(solution)/shard_map/dot_general | solution.py:200
  27.9 1.5 %convolution_add_fusion.2 = f32[640,512]{0,1:T(8,128)S(1)} fusion(f32[640,512]{0,1:T(8,128)S(1)} %fusion.5, f32[512,512]{1,0:T(8,128)S(1)} %collective-permute-done, f32[2048,640]{1,0:T(8,128)S(1)} %select_maximum_fusion, s32[]{:T(128)S(6)} %select_n.93), kind=kOutput, calls=%fused_computation.5 | convolution fusion | flops 1006960640 | bytes 4980740 | tf_op jit(solution)/shard_map/dot_general | solution.py:200
  29.4 2.7 %convolution_add_fusion.1 = f32[640,512]{0,1:T(8,128)S(1)} fusion(f32[640,512]{0,1:T(8,128)S(1)} %convolution_add_fusion.2, f32[512,512]{1,0:T(8,128)} %collective-permute-done.1, f32[2048,640]{1,0:T(8,128)S(1)} %select_maximum_fusion, s32[]{:T(128)S(6)} %select_n.94), kind=kOutput, calls=%fused_computation.4 | convolution fusion | flops 1006960640 | bytes 4980740 | tf_op jit(solution)/shard_map/dot_general | solution.py:200
  32.1 1.5 %fusion = f32[512,640]{1,0:T(8,128)S(1)} fusion(f32[640,512]{0,1:T(8,128)S(1)} %convolution_add_fusion.1, f32[512,512]{1,0:T(8,128)S(1)} %collective-permute-done.2, f32[2048,640]{1,0:T(8,128)S(1)} %select_maximum_fusion, s32[]{:T(128)S(6)} %select_n.95), kind=kOutput, calls=%fused_computation.3 | convolution fusion | flops 1006960640 | bytes 4980740 | tf_op jit(solution)/shard_map/dot_general | solution.py:200
  33.6 3.8 %collective-permute-start.3 = (f32[8,384]{1,0:T(8,128)S(1)}, f32[8,384]{1,0:T(8,128)S(1)}, u32[]{:S(2)}, u32[]{:S(2)}) collective-permute-start(f32[8,384]{1,0:T(8,128)S(1)} %slice.26), channel_id=1, source_target_pairs={{0,4},{4,8},{8,12},{12,16},{16,20},{20,24},{24,28},{1,5},{5,9},{9,... | collective-permute-start | bytes 36872 | tf_op jit(solution)/shard_map/ppermute | solution.py:222
  37.6 1.1 %collective-permute-done.3.rim_ref = f32[8,384]{1,0:T(8,128)S(1)} collective-permute-done((f32[8,384]{1,0:T(8,128)S(1)}, f32[8,384]{1,0:T(8,128)S(1)}, u32[]{:S(2)}, u32[]{:S(2)}) %collective-permute-start.3) | collective-permute-done | bytes 12320 | tf_op jit(solution)/shard_map/ppermute | solution.py:222
  38.7 4.8 %shard_map.82 = (f32[512,128]{1,0:T(8,128)S(1)}, f32[512,128]{1,0:T(8,128)S(1)}, f32[512,128]{1,0:T(8,128)S(1)}, f32[2,128,128]{2,1,0:T(8,128)S(1)}) custom-call(f32[512,384]{1,0:T(8,128)S(1)} %slice.25.raw_ref, f32[8,384]{1,0:T(8,128)S(1)} %collective-permute-done.3.rim_ref, f32[512,128]{1,0:T(8,128)S(1)} %get-tuple-element.14.mix_ref, ...), custom_call_target="tpu_custom_call" | custom-call | tf_op jit(solution)/shard_map/pallas_call | solution.py:172
  43.5 2.4 %collective-permute-start.5 = (f32[128,128]{1,0:T(8,128)S(1)}, f32[128,128]{1,0:T(8,128)S(1)}, u32[]{:S(2)}, u32[]{:S(2)}) collective-permute-start(f32[128,128]{1,0:T(8,128)S(1)} %get-tuple-element.16), channel_id=1, source_target_pairs={{0,4},{4,0},{8,12},{12,8},{16,20},{20,16},{24,28},{28,24},{1,5},{5... | collective-permute-start | bytes 196616 | tf_op jit(solution)/shard_map/ppermute | solution.py:208
  45.9 2.7 %collective-permute-done.5 = f32[128,128]{1,0:T(8,128)S(1)} collective-permute-done((f32[128,128]{1,0:T(8,128)S(1)}, f32[128,128]{1,0:T(8,128)S(1)}, u32[]{:S(2)}, u32[]{:S(2)}) %collective-permute-start.5) | collective-permute-done | bytes 65568 | tf_op jit(solution)/shard_map/ppermute | solution.py:208
  48.7 0.2 fusion.18
  48.9 2.5 %collective-permute-start.7 = (f32[128,128]{1,0:T(8,128)S(1)}, f32[128,128]{1,0:T(8,128)S(1)}, u32[]{:S(2)}, u32[]{:S(2)}) collective-permute-start(f32[128,128]{1,0:T(8,128)S(1)} %fusion.18), channel_id=1, source_target_pairs={{0,8},{4,12},{8,0},{12,4},{16,24},{20,28},{24,16},{28,20},{1,9},{5... | collective-permute-start | bytes 196616 | tf_op jit(solution)/shard_map/ppermute | solution.py:208
  51.4 0.2 convolution_add_fusion.6
  51.6 0.5 collective-permute-start.6
  52.5 1.2 %collective-permute-done.7 = f32[128,128]{1,0:T(8,128)S(1)} collective-permute-done((f32[128,128]{1,0:T(8,128)S(1)}, f32[128,128]{1,0:T(8,128)S(1)}, u32[]{:S(2)}, u32[]{:S(2)}) %collective-permute-start.7) | collective-permute-done | bytes 65568 | tf_op jit(solution)/shard_map/ppermute | solution.py:208
  53.6 2.3 %collective-permute-done.6 = f32[128,128]{1,0:T(8,128)S(1)} collective-permute-done((f32[128,128]{1,0:T(8,128)S(1)}, f32[128,128]{1,0:T(8,128)S(1)}, u32[]{:S(2)}, u32[]{:S(2)}) %collective-permute-start.6) | collective-permute-done | bytes 65568 | tf_op jit(solution)/shard_map/ppermute | solution.py:208
  55.9 0.2 convolution_add_fusion.5
  56.1 2.7 %collective-permute-start.8 = (f32[128,128]{1,0:T(8,128)S(1)}, f32[128,128]{1,0:T(8,128)S(1)}, u32[]{:S(2)}, u32[]{:S(2)}) collective-permute-start(f32[128,128]{1,0:T(8,128)S(1)} %convolution_add_fusion.5), channel_id=1, source_target_pairs={{0,16},{4,20},{8,24},{12,28},{16,0},{20,4},{24,8},{28,12},{1,17},{... | collective-permute-start | bytes 196616 | tf_op jit(solution)/shard_map/ppermute | solution.py:208
  58.8 0.2 fusion.14
  59.1 0.2 convolution_bitcast_fusion.1
  59.3 2.7 %collective-permute-done.8 = f32[128,128]{1,0:T(8,128)S(1)} collective-permute-done((f32[128,128]{1,0:T(8,128)S(1)}, f32[128,128]{1,0:T(8,128)S(1)}, u32[]{:S(2)}, u32[]{:S(2)}) %collective-permute-start.8) | collective-permute-done | bytes 65568 | tf_op jit(solution)/shard_map/ppermute | solution.py:208
  61.9 0.2 convolution_bitcast_fusion
  62.2 0.5 shard_map.83
  62.7 1.6 %collective-permute-start.9 = (f32[512,128]{1,0:T(8,128)S(1)}, f32[512,128]{1,0:T(8,128)S(1)}, u32[]{:S(2)}, u32[]{:S(2)}) collective-permute-start(f32[512,128]{1,0:T(8,128)S(1)} %shard_map.83), channel_id=1, source_target_pairs={{0,2},{1,3},{2,0},{3,1},{4,6},{5,7},{6,4},{7,5},{8,10},{9,11},{10,... | collective-permute-start | bytes 786440 | tf_op jit(solution)/shard_map/ppermute | solution.py:189
  64.2 4.8 %collective-permute-done.9 = f32[512,128]{1,0:T(8,128)S(1)} collective-permute-done((f32[512,128]{1,0:T(8,128)S(1)}, f32[512,128]{1,0:T(8,128)S(1)}, u32[]{:S(2)}, u32[]{:S(2)}) %collective-permute-start.9) | collective-permute-done | bytes 262176 | tf_op jit(solution)/shard_map/ppermute | solution.py:189
  69.1 0.6 fusion.10
  69.7 0.6 fusion.8
  70.3 0.6 fusion.1
  70.9 1.5 %convolution_add_fusion.3 = f32[512,512]{1,0:T(8,128)} fusion(f32[512,512]{1,0:T(8,128)S(1)} %fusion.1, f32[512,128]{1,0:T(8,128)S(1)} %collective-permute-done.11, f32[512,512]{1,0:T(8,128)S(1)} %copy-done, s32[]{:T(128)S(6)} %select_n.114), kind=kOutput, calls=%fused_computation.6 | convolution fusion | flops 201588736 | bytes 2621444 | tf_op jit(solution)/shard_map/dot_general | solution.py:200
  (28 shorter events, 0.6 us)
Async XLA Ops:
  0.0 69.1 %copy-start = (f32[512,512]{1,0:T(8,128)S(1)}, f32[512,512]{1,0:T(8,128)}, u32[]{:S(2)}) copy-start(f32[512,512]{1,0:T(8,128)} %param.15) | copy-start | bytes 3145732
  0.0 26.3 %collective-permute-start = (f32[512,512]{1,0:T(8,128)}, f32[512,512]{1,0:T(8,128)S(1)}, u32[]{:S(2)}, u32[]{:S(2)}) collective-permute-start(f32[512,512]{1,0:T(8,128)} %param.8), channel_id=1, source_target_pairs={{0,2},{1,3},{2,0},{3,1},{4,6},{5,7},{6,4},{7,5},{8,10},{9,11},{10,... | collective-permute-start | bytes 3145736 | tf_op jit(solution)/shard_map/ppermute | solution.py:189
  3.0 26.4 %collective-permute-start.1 = (f32[512,512]{1,0:T(8,128)}, f32[512,512]{1,0:T(8,128)}, u32[]{:S(2)}, u32[]{:S(2)}) collective-permute-start(f32[512,512]{1,0:T(8,128)} %param.8), channel_id=1, source_target_pairs={{0,1},{1,0},{2,3},{3,2},{4,5},{5,4},{6,7},{7,6},{8,9},{9,8},{10,11... | collective-permute-start | bytes 3145736 | tf_op jit(solution)/shard_map/ppermute | solution.py:191
  4.9 21.4 %copy-start.4 = (s32[512]{0:T(512)S(1)}, s32[512]{0:T(512)}, u32[]{:S(2)}) copy-start(s32[512]{0:T(512)} %param.13) | copy-start | bytes 6148
  4.9 21.4 %copy-start.3 = (f32[512,512]{1,0:T(8,128)S(1)}, f32[512,512]{1,0:T(8,128)}, u32[]{:S(2)}) copy-start(f32[512,512]{1,0:T(8,128)} %param.8) | copy-start | bytes 3145732
  26.3 5.8 %collective-permute-start.2 = (f32[512,512]{1,0:T(8,128)S(1)}, f32[512,512]{1,0:T(8,128)S(1)}, u32[]{:S(2)}, u32[]{:S(2)}) collective-permute-start(f32[512,512]{1,0:T(8,128)S(1)} %collective-permute-done), channel_id=1, source_target_pairs={{0,1},{1,0},{2,3},{3,2},{4,5},{5,4},{6,7},{7,6},{8,9},{9,8},{10,11... | collective-permute-start | bytes 3145736 | tf_op jit(solution)/shard_map/ppermute | solution.py:191
  33.6 5.0 %copy-start.1 = (f32[4,384]{1,0:T(4,128)S(1)}, f32[4,384]{1,0:T(4,128)}, u32[]{:S(2)}) copy-start(f32[4,384]{1,0:T(4,128)} %conv_ref.1) | copy-start | bytes 18436
  33.6 5.0 %collective-permute-start.3 = (f32[8,384]{1,0:T(8,128)S(1)}, f32[8,384]{1,0:T(8,128)S(1)}, u32[]{:S(2)}, u32[]{:S(2)}) collective-permute-start(f32[8,384]{1,0:T(8,128)S(1)} %slice.26), channel_id=1, source_target_pairs={{0,4},{4,8},{8,12},{12,16},{16,20},{20,24},{24,28},{1,5},{5,9},{9,... | collective-permute-start | bytes 36872 | tf_op jit(solution)/shard_map/ppermute | solution.py:222
  43.5 18.7 %copy-start.2 = (f32[128]{0:T(128)S(1)}, f32[128]{0:T(128)}, u32[]{:S(2)}) copy-start(f32[128]{0:T(128)} %param.14) | copy-start | bytes 1540
  43.5 5.2 %collective-permute-start.5 = (f32[128,128]{1,0:T(8,128)S(1)}, f32[128,128]{1,0:T(8,128)S(1)}, u32[]{:S(2)}, u32[]{:S(2)}) collective-permute-start(f32[128,128]{1,0:T(8,128)S(1)} %get-tuple-element.16), channel_id=1, source_target_pairs={{0,4},{4,0},{8,12},{12,8},{16,20},{20,16},{24,28},{28,24},{1,5},{5... | collective-permute-start | bytes 196616 | tf_op jit(solution)/shard_map/ppermute | solution.py:208
  45.8 5.5 %collective-permute-start.4 = (f32[128,128]{1,0:T(8,128)S(1)}, f32[128,128]{1,0:T(8,128)S(1)}, u32[]{:S(2)}, u32[]{:S(2)}) collective-permute-start(f32[128,128]{1,0:T(8,128)S(1)} %get-tuple-element.15), channel_id=1, source_target_pairs={{0,4},{4,0},{8,12},{12,8},{16,20},{20,16},{24,28},{28,24},{1,5},{5... | collective-permute-start | bytes 196616 | tf_op jit(solution)/shard_map/ppermute | solution.py:208
  48.9 4.7 %collective-permute-start.7 = (f32[128,128]{1,0:T(8,128)S(1)}, f32[128,128]{1,0:T(8,128)S(1)}, u32[]{:S(2)}, u32[]{:S(2)}) collective-permute-start(f32[128,128]{1,0:T(8,128)S(1)} %fusion.18), channel_id=1, source_target_pairs={{0,8},{4,12},{8,0},{12,4},{16,24},{20,28},{24,16},{28,20},{1,9},{5... | collective-permute-start | bytes 196616 | tf_op jit(solution)/shard_map/ppermute | solution.py:208
  51.6 4.3 %collective-permute-start.6 = (f32[128,128]{1,0:T(8,128)S(1)}, f32[128,128]{1,0:T(8,128)S(1)}, u32[]{:S(2)}, u32[]{:S(2)}) collective-permute-start(f32[128,128]{1,0:T(8,128)S(1)} %convolution_add_fusion.6), channel_id=1, source_target_pairs={{0,8},{4,12},{8,0},{12,4},{16,24},{20,28},{24,16},{28,20},{1,9},{5... | collective-permute-start | bytes 196616 | tf_op jit(solution)/shard_map/ppermute | solution.py:208
  56.1 5.8 %collective-permute-start.8 = (f32[128,128]{1,0:T(8,128)S(1)}, f32[128,128]{1,0:T(8,128)S(1)}, u32[]{:S(2)}, u32[]{:S(2)}) collective-permute-start(f32[128,128]{1,0:T(8,128)S(1)} %convolution_add_fusion.5), channel_id=1, source_target_pairs={{0,16},{4,20},{8,24},{12,28},{16,0},{20,4},{24,8},{28,12},{1,17},{... | collective-permute-start | bytes 196616 | tf_op jit(solution)/shard_map/ppermute | solution.py:208
  62.7 6.4 %collective-permute-start.9 = (f32[512,128]{1,0:T(8,128)S(1)}, f32[512,128]{1,0:T(8,128)S(1)}, u32[]{:S(2)}, u32[]{:S(2)}) collective-permute-start(f32[512,128]{1,0:T(8,128)S(1)} %shard_map.83), channel_id=1, source_target_pairs={{0,2},{1,3},{2,0},{3,1},{4,6},{5,7},{6,4},{7,5},{8,10},{9,11},{10,... | collective-permute-start | bytes 786440 | tf_op jit(solution)/shard_map/ppermute | solution.py:189
  64.2 5.4 %collective-permute-start.10 = (f32[512,128]{1,0:T(8,128)S(1)}, f32[512,128]{1,0:T(8,128)S(1)}, u32[]{:S(2)}, u32[]{:S(2)}) collective-permute-start(f32[512,128]{1,0:T(8,128)S(1)} %shard_map.83), channel_id=1, source_target_pairs={{0,1},{1,0},{2,3},{3,2},{4,5},{5,4},{6,7},{7,6},{8,9},{9,8},{10,11... | collective-permute-start | bytes 786440 | tf_op jit(solution)/shard_map/ppermute | solution.py:191
  69.1 1.8 %collective-permute-start.11 = (f32[512,128]{1,0:T(8,128)S(1)}, f32[512,128]{1,0:T(8,128)S(1)}, u32[]{:S(2)}, u32[]{:S(2)}) collective-permute-start(f32[512,128]{1,0:T(8,128)S(1)} %collective-permute-done.9), channel_id=1, source_target_pairs={{0,1},{1,0},{2,3},{3,2},{4,5},{5,4},{6,7},{7,6},{8,9},{9,8},{10,11... | collective-permute-start | bytes 786440 | tf_op jit(solution)/shard_map/ppermute | solution.py:191

commit v2 on v1

v2 whole, which is shorter than its diff:
```python
import functools

import jax
import jax.numpy as jnp
from jax import lax
from jax.experimental import pallas as pl
from jax.experimental.pallas import tpu as pltpu
from jax.sharding import PartitionSpec as P

CHUNK = 128
RIM = 16
F32 = jnp.float32
BF16 = jnp.bfloat16


def halves(value):
    high = value.astype(BF16)
    return high, (value - high.astype(F32)).astype(BF16)


def left_parts(value):
    return jnp.concatenate(halves(value), axis=1)


def right_parts(value):
    row = jnp.concatenate(halves(value), axis=1)
    return jnp.concatenate([row, row], axis=0)


def parts_dot(left, right):
    both = jnp.dot(left, right, preferred_element_type=F32)
    half = both.shape[1] // 2
    return both[:, :half] + both[:, half:]


def product(left, right):
    return parts_dot(left_parts(left), right_parts(right))


def softplus(value):
    return jnp.maximum(value, 0.0) + jnp.log1p(jnp.exp(-jnp.abs(value)))


def sigmoid(value):
    return 1.0 / (1.0 + jnp.exp(-value))


def unit_lower_inverse(lowers, row, col):
    size = lowers[0].shape[0]
    eye = jnp.where(row == col, 1.0, 0.0).astype(F32)
    inverses = [eye - jnp.where((row >> 1) == (col >> 1), lower, 0.0) for lower in lowers]
    lower_parts = [halves(lower) for lower in lowers]
    step = 1
    while 2 << (step - 1) < size:
        off = ((row >> (step + 1)) == (col >> (step + 1))) & ((row >> step) > (col >> step))
        lefts = [left_parts(inverse) for inverse in inverses]
        offs = [
            jnp.concatenate([jnp.where(off, part, jnp.zeros_like(part)) for part in parts], axis=1)
            for parts in lower_parts
        ]
        inner = [
            parts_dot(offdiag, right_parts(inverse)) for offdiag, inverse in zip(offs, inverses)
        ]
        inverses = [
            inverse - parts_dot(left, right_parts(value))
            for inverse, left, value in zip(inverses, lefts, inner)
        ]
        step += 1
    return inverses


def chunk_pass(raw, conv_ref, rate, doc_ref, first_chunk, rim, width, state, outs):
    carried_ref, local_ref, weight_ref, gate_ref = outs
    taps = conv_ref.shape[0]
    chunks = carried_ref.shape[0] // CHUNK
    row = lax.broadcasted_iota(jnp.int32, (CHUNK, CHUNK), 0)
    col = lax.broadcasted_iota(jnp.int32, (CHUNK, CHUNK), 1)
    lower = row >= col
    tri = jnp.where(lower, 1.0, 0.0).astype(F32)
    eye = jnp.where(row == col, 1.0, 0.0).astype(F32)
    queries, keys, values, betas, grids, gammas, tails = [], [], [], [], [], [], []
    for part in range(chunks):
        base = part * CHUNK
        start = base + rim - taps + 1
        conv = conv_ref[0:1, :] * raw[start : start + CHUNK, : 3 * width]
        for tap in range(1, taps):
            conv = conv + conv_ref[tap : tap + 1, :] * raw[
                start + tap : start + tap + CHUNK, : 3 * width
            ]
        conv = conv * sigmoid(conv)
        query = conv[:, :width]
        key = conv[:, width : 2 * width]
        query = query * lax.rsqrt(jnp.sum(query * query, axis=1, keepdims=True) + 1e-06)
        key = key * lax.rsqrt(jnp.sum(key * key, axis=1, keepdims=True) + 1e-06)
        queries.append(query)
        keys.append(key)
        values.append(conv[:, 2 * width :])
        gate = raw[base + rim : base + rim + CHUNK, 3 * width : 4 * width]
        gate_ref[base : base + CHUNK, :] = gate * sigmoid(gate)
        mixing = raw[base + rim : base + rim + CHUNK, 4 * width :]
        plus = softplus(mixing)
        weight_ref[base : base + CHUNK, :] = plus
        betas.append(sigmoid(mixing[:, 0:1]))
        spot = first_chunk + part
        docs = jnp.transpose(jnp.broadcast_to(doc_ref[spot : spot + 1, :], (CHUNK, CHUNK)))
        steps = jnp.where(col == 1, -rate * plus, jnp.where(col == 0, docs, 0.0))
        sums = jnp.dot(tri, steps, precision=lax.Precision.HIGHEST, preferred_element_type=F32)
        across = jnp.transpose(sums)
        smooth, count = sums[:, 1:2], sums[:, 0:1]
        span = (smooth - across[1:2, :]) - 20.0 * (count - across[0:1, :])
        grids.append(jnp.exp(jnp.where(lower, span, -1e30)))
        gammas.append(jnp.exp(smooth - 20.0 * count))
        last = sums[CHUNK - 1 : CHUNK, :]
        tails.append(jnp.exp((last[:, 1:2] - smooth) - 20.0 * (last[:, 0:1] - count)))
    across_keys = [jnp.transpose(key) for key in keys]
    grams = [
        parts_dot(left_parts(jnp.concatenate([key, query], axis=0)), right_parts(across))
        for key, query, across in zip(keys, queries, across_keys)
    ]
    lowers = [
        jnp.where(row > col, beta * gram[:CHUNK], 0.0) for beta, gram in zip(betas, grams)
    ]
    inverses = unit_lower_inverse(lowers, row, col)
    for part in range(chunks):
        base = part * CHUNK
        inverse, beta, grid = inverses[part], betas[part], grids[part]
        factor_x = product(inverse, beta * keys[part])
        factor_y = product(grid * inverse, beta * values[part])
        left_keys = left_parts(across_keys[part])
        gamma, tail = gammas[part], tails[part]
        trans = gamma[CHUNK - 1 : CHUNK, :] * (eye - parts_dot(left_keys, right_parts(factor_x)))
        memory = parts_dot(left_keys, right_parts(tail * factor_y))
        overlap = grams[part][CHUNK:]
        carried = gamma * (
            queries[part] - product(jnp.where(lower, overlap, 0.0), factor_x)
        )
        local = product(grid * overlap, factor_y)
        if state is None:
            state = (trans, memory)
        else:
            left = left_parts(jnp.concatenate([trans, carried], axis=0))
            onto_a = parts_dot(left, right_parts(state[0]))
            onto_s = parts_dot(left, right_parts(state[1]))
            local = local + onto_s[CHUNK:]
            carried = onto_a[CHUNK:]
            state = (onto_a[:CHUNK], onto_s[:CHUNK] + memory)
        carried_ref[base : base + CHUNK, :] = carried
        local_ref[base : base + CHUNK, :] = local
    return state


def part_kernel(segments, width, first_chunk, *refs):
    sources = len(segments[0][2])
    arrays = 1 + max(spot for _, _, places in segments for spot, _ in places)
    index_ref, refs = refs[0], refs[1:]
    held, refs = refs[:arrays], refs[arrays:]
    weight_ref, conv_ref, rate_ref, doc_ref = refs[:4]
    refs = refs[4:]
    state = None
    if first_chunk:
        rim_ref, state_ref = refs[:2]
        refs = refs[2:]
    carried_ref, local_ref, plus_ref, gate_ref, pair_ref, last_ref, raw, high, low = refs
    depth = held[0].shape[1]
    columns = weight_ref.shape[1] // 2
    for start, rows, places in segments:
        for source in range(sources):
            spot, begin = places[source]
            piece = held[spot][begin : begin + rows, :]
            piece_high, piece_low = halves(piece)
            where = pl.ds(pl.multiple_of(index_ref[source] * depth, depth), depth)
            high[start : start + rows, where] = piece_high
            low[start : start + rows, where] = piece_low
    begin = segments[0][0]
    both = jnp.dot(high[begin:, :], weight_ref[...], preferred_element_type=F32)
    rest = jnp.dot(low[begin:, :], weight_ref[:, :columns], preferred_element_type=F32)
    raw[begin:, :] = (both[:, :columns] + both[:, columns:]) + rest
    if first_chunk:
        raw[:begin, : 3 * width] = rim_ref[...]
        state = (state_ref[0], state_ref[1])
    state = chunk_pass(
        raw, conv_ref, rate_ref[0, 0], doc_ref, first_chunk, RIM, width, state,
        (carried_ref, local_ref, plus_ref, gate_ref),
    )
    pair_ref[0] = state[0]
    pair_ref[1] = state[1]
    last_ref[...] = raw[raw.shape[0] - RIM :, : 3 * width]


def four_kernel(bits_ref, own_ref, one_ref, two_ref, three_ref, carry_ref, group_ref, level_ref, next_ref, pairs):
    low_bit, high_bit = bits_ref[0], bits_ref[1]
    place = 2 * high_bit + low_bit
    for mask, ref in enumerate((own_ref, one_ref, two_ref, three_ref)):
        pairs[place ^ mask] = ref[...]
    width = carry_ref.shape[0]
    joined = lambda spot: jnp.concatenate([pairs[spot, 0], pairs[spot, 1]], axis=1)
    onto_low = product(pairs[1, 0], joined(0))
    onto_high = product(pairs[3, 0], joined(2))
    low_a, low_s = onto_low[:, :width], onto_low[:, width:] + pairs[1, 1]
    high_a, high_s = onto_high[:, :width], onto_high[:, width:] + pairs[3, 1]
    onto = product(high_a, jnp.concatenate([low_a, low_s], axis=1))
    group_ref[0] = onto[:, :width]
    group_ref[1] = onto[:, width:] + high_s
    carry = carry_ref[...]
    first = product(carry, jnp.concatenate([one_ref[0], one_ref[1]], axis=1))
    set_low = jnp.broadcast_to(low_bit, (width, width)) == 1
    set_high = jnp.broadcast_to(high_bit, (width, width)) == 1
    level_ref[0] = jnp.where(set_low, first[:, width:], 0.0)
    carry = jnp.where(set_low, first[:, :width], carry)
    second = product(carry, jnp.concatenate([low_a, low_s], axis=1))
    level_ref[1] = jnp.where(set_high, second[:, width:], 0.0)
    next_ref[...] = jnp.where(set_high, second[:, :width], carry)


def mix_kernel(parts, stages, single, *refs):
    pieces = [refs[4 * part : 4 * part + 4] for part in range(parts)]
    refs = refs[4 * parts :]
    level_refs, refs = refs[:stages], refs[stages:]
    states = [ref[spot] for ref in level_refs for spot in range(ref.shape[0])]
    if single:
        carry_ref, seg_ref = refs[:2]
        refs = refs[2:]
        states.append(product(carry_ref[...], seg_ref[...]))
    gain_ref, normed_ref = refs
    states = [right_parts(state) for state in states]
    base = 0
    for carried_ref, local_ref, weight_ref, gate_ref in pieces:
        rows = carried_ref.shape[0]
        carried = left_parts(carried_ref[...])
        weights = weight_ref[...]
        mixed = weights[:, 2:3] * local_ref[...]
        for level, state in enumerate(states):
            mixed = mixed + weights[:, level + 3 : level + 4] * parts_dot(carried, state)
        scale = lax.rsqrt(jnp.mean(mixed * mixed, axis=1, keepdims=True) + 1e-05)
        normed_ref[base : base + rows, :] = mixed * scale * gain_ref[...] * gate_ref[...]
        base += rows


def out_kernel(pieces, added, index_ref, *refs):
    held, weight_ref, refs = refs[:pieces], refs[pieces], refs[pieces + 1 :]
    total = refs[0][...] if added else 0.0
    out_ref = refs[-1]
    columns = out_ref.shape[1]
    for source in range(pieces):
        depth = held[source].shape[1]
        rows = pl.ds(pl.multiple_of(index_ref[source] * depth, depth), depth)
        high, low = halves(held[source][...])
        both = jnp.dot(high, weight_ref[rows, :], preferred_element_type=F32)
        rest = jnp.dot(low, weight_ref[rows, :columns], preferred_element_type=F32)
        total = total + ((both[:, :columns] + both[:, columns:]) + rest)
    out_ref[...] = total


def vmem_call(kernel, outs, scratch, *args):
    spec = pl.BlockSpec(memory_space=pltpu.VMEM)
    small = pl.BlockSpec(memory_space=pltpu.SMEM)
    return pl.pallas_call(
        kernel,
        out_shape=outs,
        in_specs=[small if arg.dtype == jnp.int32 else spec for arg in args],
        out_specs=jax.tree.map(lambda unused: spec, outs),
        scratch_shapes=scratch,
        compiler_params=pltpu.CompilerParams(vmem_limit_bytes=44 << 20),
    )(*args)


def split_columns(weight):
    high = lax.reduce_precision(weight, 8, 7)
    return jnp.concatenate([high.astype(BF16), (weight - high).astype(BF16)], axis=1)


def to_sibling(value):
    count = lax.axis_size("head")
    return lax.ppermute(value, "head", [(source, source ^ 1) for source in range(count)])


def to_chips(value):
    count = lax.axis_size("head")
    return [
        lax.ppermute(
            value, "head", [(source, (source + 2 * step) % count) for source in range(count)]
        )
        for step in range(1, count // 2)
    ]


def after(value, earlier):
    return lax.optimization_barrier((value, earlier))


def shards(tokens, w_proj, w_mix, conv_w, rates, doc_start, norm_gain, w_out):
    tok_rows = tokens.shape[0]
    width = w_proj.shape[1] // 4
    features = w_proj.shape[0]
    heads, me = lax.axis_size("head"), lax.axis_index("head")
    blocks, my_index = lax.axis_size("ctx"), lax.axis_index("ctx")
    remote = [(me + heads - 2 * step) % heads for step in range(1, heads // 2)]
    order = [me, me ^ 1] + remote + [index ^ 1 for index in remote]
    index = jnp.stack(order).astype(jnp.int32)

    half = tok_rows // 2
    quarter = half // 2
    rim = lax.ppermute(
        tokens[tok_rows - RIM :], "ctx", [(source, source + 1) for source in range(blocks - 1)]
    )
    second = to_chips(tokens[quarter:half])
    extended = jnp.concatenate([rim, tokens], axis=0)
    beside = to_sibling(extended)
    first = to_chips(extended[: quarter + RIM])
    third_rows, second = after(tokens[half : half + quarter], second)
    third = to_chips(third_rows)
    second_on = [to_sibling(value) for value in second]
    fourth_rows, first = after(tokens[half + quarter :], first)
    fourth = to_chips(fourth_rows)
    first_on = [to_sibling(value) for value in first]
    third_on = [to_sibling(value) for value in third]
    fourth_on = [to_sibling(value) for value in fourth]

    weight = split_columns(
        jnp.concatenate([w_proj, jnp.pad(w_mix, ((0, 0), (0, CHUNK - w_mix.shape[1])))], axis=1)
    )
    docs = doc_start.astype(F32).reshape(tok_rows // CHUNK, CHUNK)

    def part(segments, arrays, rows, first_chunk, earlier):
        shape = jax.ShapeDtypeStruct((rows, width), F32)
        return vmem_call(
            functools.partial(part_kernel, segments, width, first_chunk),
            [shape, shape, jax.ShapeDtypeStruct((rows, CHUNK), F32), shape,
             jax.ShapeDtypeStruct((2, width, width), F32),
             jax.ShapeDtypeStruct((RIM, 3 * width), F32)],
            [pltpu.VMEM((RIM + rows, weight.shape[1] // 2), F32)]
            + [pltpu.VMEM((RIM + rows, features), BF16)] * 2,
            index, *arrays, weight, conv_w, rates[:, None], docs, *earlier,
        )

    count = heads - 2
    top = quarter + RIM
    arrays = [extended, beside, *first, *first_on, *second, *second_on]
    segments = [
        (0, top, [(0, 0), (1, 0)] + [(2 + spot, 0) for spot in range(count)]),
        (top, quarter, [(0, top), (1, top)] + [(2 + count + spot, 0) for spot in range(count)]),
    ]
    results = [part(segments, arrays, half, 0, ())]
    for turn, (moved, moved_on) in enumerate(((third, third_on), (fourth, fourth_on))):
        begin = RIM + half + turn * quarter
        segments = [(RIM, quarter, [(0, begin), (1, begin)] + [(2 + spot, 0) for spot in range(count)])]
        earlier = (results[-1][5], results[-1][4])
        arrays = [extended, beside, *moved, *moved_on]
        first_chunk = (half + turn * quarter) // CHUNK
        results.append(part(segments, arrays, quarter, first_chunk, earlier))

    pair = results[-1][4]
    carry = jnp.eye(width, dtype=F32)
    square = jax.ShapeDtypeStruct((width, width), F32)
    double = jax.ShapeDtypeStruct((2, width, width), F32)
    bits = blocks.bit_length() - 1
    levels = []
    for bit in range(0, bits - 1, 2):
        others = [
            lax.ppermute(
                pair, "ctx", [(source, source ^ (mask << bit)) for source in range(blocks)]
            )
            for mask in (1, 2, 3)
        ]
        flags = jnp.stack([my_index >> bit & 1, my_index >> (bit + 1) & 1]).astype(jnp.int32)
        pair, level, carry = vmem_call(
            four_kernel, [double, double, square], [pltpu.VMEM((4, 2, width, width), F32)],
            flags, pair, *others, carry,
        )
        levels.append(level)
    single = []
    if bits % 2:
        reach = blocks // 2
        single = [
            carry,
            lax.ppermute(pair[1], "ctx", [(source, source + reach) for source in range(reach)]),
        ]
    fields = [field for result in results for field in result[:4]]
    normed = vmem_call(
        functools.partial(mix_kernel, len(results), len(levels), bool(single)),
        jax.ShapeDtypeStruct((tok_rows, width), F32), [],
        *fields, *levels, *single, norm_gain[None, :],
    )
    own_weight = split_columns(w_out)
    out_shape = jax.ShapeDtypeStruct((tok_rows, w_out.shape[1]), F32)
    far = to_chips(normed)
    near = to_sibling(normed)
    far_on = [to_sibling(value) for value in far]
    total = vmem_call(
        functools.partial(out_kernel, 2, False), out_shape, [], index[:2], normed, near, own_weight
    )
    return vmem_call(
        functools.partial(out_kernel, 2 * len(far), True), out_shape, [],
        index[2:], *far, *far_on, own_weight, total,
    )


def solution(mesh):
    placed = (
        P("ctx", "head"),
        P(None, "head"),
        P(None, "head"),
        P(None, "head"),
        P("head"),
        P("ctx"),
        P("head"),
        P(None, "head"),
    )
    return jax.shard_map(
        shards, mesh=mesh, in_specs=placed, out_specs=P("ctx", "head"), check_vma=False
    )
```

time: 72.7 us -> 83.9 us (1.15)
  Pallas kernels: 5.28 us -> 23.2 us
  matrix products: 12.1 us -> 0 us
  waiting for transfers between devices: 33.5 us -> 22.8 us
  local copies, waits for them, and re-layouts: 1.38 us -> 7.84 us
  starting transfers between devices: 16.5 us -> 22.1 us
  other arithmetic: 2.79 us -> 6.35 us
    pallas_call x2 -> x7, Pallas kernels: 5.28 us -> 23.2 us  [vmem_call(): pl.pallas_call(kernel, out_shape=outs, in_specs=[small if arg.dtype == jn...]
    dot_general x16 -> x0, matrix products: 12.1 us -> none  [the longest x8 10.5 us: gathered_dot(): jnp.dot(piece, rows, precision=lax.Precision.HIGH, preferred_element_type...]
    ppermute x12 -> x17, waiting for transfers between devices: 33.5 us -> 22.8 us  [the longest x5 14.6 us: to_chips(): lax.ppermute(value, 'head', [(source, (source + 2 * step) % count) for so...]
    ppermute x12 -> x17, starting transfers between devices: 16.5 us -> 22.1 us  [the longest x5 8.55 us: to_chips(): lax.ppermute(value, 'head', [(source, (source + 2 * step) % count) for so...]
    convert_element_type x0 -> x3, other arithmetic: none -> 3.19 us  [the longest x2 3.18 us: split_columns(): high.astype(BF16)]
    slice x3, local copies, waits for them, and re-layouts: 0.09 us -> 2.78 us  [the longest x1 2 us: shards(): second = to_chips(tokens[quarter:half])]
    unnamed x11 -> x14, local copies, waits for them, and re-layouts: 1.28 us -> 3.76 us
    concatenate x0 -> x1, local copies, waits for them, and re-layouts: none -> 1.3 us  [shards(): extended = jnp.concatenate([rim, tokens], axis=0)]
  transfers between devices with their start and end apart: 12 -> 17, of which waited for: 7 -> 8; matrix products, arithmetic and copies ran while one was open for 18% -> 13% of each run, Pallas kernels for 0% -> 17%
where the time goes in v2:
time: 83.9 us; the launch traced here: 83.2 us
  Pallas kernels  23.2 us (28%)
  waiting for transfers between devices  22.8 us (27%)
  starting transfers between devices  22.1 us (26%)
  local copies, waits for them, and re-layouts  7.84 us (9%)
  other arithmetic  6.35 us (8%)
  between operations  0.92 us (1%)
    pallas_call x7, Pallas kernels, vmem_call(): pl.pallas_call(kernel, out_shape=outs, in_specs=[small if arg.dtype == jn...  23.2 us
    ppermute x5, waiting for transfers between devices, to_chips(): lax.ppermute(value, 'head', [(source, (source + 2 * step) % count) for so...  14.6 us
    ppermute x5, starting transfers between devices, to_chips(): lax.ppermute(value, 'head', [(source, (source + 2 * step) % count) for so...  8.55 us
    ppermute x3, waiting for transfers between devices, shards(): lax.ppermute(pair, 'ctx', [(source, source ^ mask << bit) for source in r...  6.32 us
    ppermute x1, starting transfers between devices, shards(): lax.ppermute(tokens[tok_rows - RIM:], 'ctx', [(source, source + 1) for so...  4.83 us
    ppermute x1, starting transfers between devices, shards(): lax.ppermute(pair[1], 'ctx', [(source, source + reach) for source in rang...  4.5 us
    unnamed x14, local copies, waits for them, and re-layouts  3.76 us
    ppermute x3, starting transfers between devices, shards(): lax.ppermute(pair, 'ctx', [(source, source ^ mask << bit) for source in r...  3.55 us
  transfers between devices with their start and end apart: 17, of which 8 were waited for; matrix products, arithmetic and copies ran while one was open for 13% of the time, Pallas kernels for 17%

profile of v2, /device:TPU:0, one launch (start us, length us, event | category | flops | bytes accessed | tf_op | source)
XLA Modules:
  0.0 83.2 jit_solution(15966445456473292428)
XLA Ops:
  0.0 0.8 slice.22
  0.8 4.8 %collective-permute-start = (f32[16,512]{1,0:T(8,128)S(1)}, f32[16,512]{1,0:T(8,128)S(1)}, u32[]{:S(2)}, u32[]{:S(2)}) collective-permute-start(f32[16,512]{1,0:T(8,128)S(1)} %slice.22), channel_id=1, source_target_pairs={{0,4},{4,8},{8,12},{12,16},{16,20},{20,24},{24,28},{1,5},{5,9},{9,... | collective-permute-start | bytes 98312 | tf_op jit(solution)/shard_map/ppermute | solution.py:303
  5.6 2.0 %fusion.3 = (f32[128,512]{1,0:T(8,128)}, f32[128,512]{1,0:T(8,128)}, f32[128,512]{1,0:T(8,128)}) fusion(f32[512,512]{1,0:T(8,128)} %param.8), kind=kLoop, calls=%fused_computation.20 | loop fusion | bytes 1572864 | tf_op jit(solution)/shard_map/slice | solution.py:306
  7.6 1.5 %collective-permute-start.4 = (f32[128,512]{1,0:T(8,128)}, f32[128,512]{1,0:T(8,128)}, u32[]{:S(2)}, u32[]{:S(2)}) collective-permute-start(f32[128,512]{1,0:T(8,128)} %get-tuple-element.57), channel_id=1, source_target_pairs={{0,2},{1,3},{2,0},{3,1},{4,6},{5,7},{6,4},{7,5},{8,10},{9,11},{10,... | collective-permute-start | bytes 786440 | tf_op jit(solution)/shard_map/ppermute | solution.py:280
  9.1 1.3 %copy.9 = f32[2048,9]{1,0:T(8,128)S(1)} copy(f32[2048,9]{0,1:T(8,128)} %param.10) | data formatting | bytes 147456 | tf_op args[2]
  10.4 1.3 %constant_dynamic-update-slice_fusion.refs_1_ = f32[528,512]{1,0:T(8,128)S(1)} fusion(f32[528,512]{1,0:T(8,128)S(1)} %constant_dynamic-update-slice_fusion.1, f32[512,512]{1,0:T(8,128)} %param.8), kind=kLoop, calls=%fused_computation.13 | loop fusion | bytes 2097152 | tf_op jit(solution)/shard_map/concatenate | solution.py:307
  11.8 0.6 collective-permute-start.2
  12.4 3.0 %reduce-precision_convert_fusion = (bf16[2048,640]{1,0:T(8,128)(2,1)S(1)}, bf16[2048,640]{1,0:T(8,128)(2,1)S(1)}) fusion(f32[2048,9]{1,0:T(8,128)S(1)} %copy.9, f32[2048,512]{1,0:T(8,128)} %param.9), kind=kLoop, calls=%fused_computation.1 | loop fusion | flops 9175040 | bytes 9510912 | tf_op jit(solution)/shard_map/convert_element_type | solution.py:269
  15.4 0.8 %collective-permute-done.4.refs_5_ = f32[128,512]{1,0:T(8,128)} collective-permute-done((f32[128,512]{1,0:T(8,128)}, f32[128,512]{1,0:T(8,128)}, u32[]{:S(2)}, u32[]{:S(2)}) %collective-permute-start.4) | collective-permute-done | bytes 262176 | tf_op jit(solution)/shard_map/ppermute | solution.py:280
  16.2 2.4 %collective-permute-start.6 = (f32[128,512]{1,0:T(8,128)}, f32[128,512]{1,0:T(8,128)S(1)}, u32[]{:S(2)}, u32[]{:S(2)}) collective-permute-start(f32[128,512]{1,0:T(8,128)} %get-tuple-element.35), channel_id=1, source_target_pairs={{0,2},{1,3},{2,0},{3,1},{4,6},{5,7},{6,4},{7,5},{8,10},{9,11},{10,... | collective-permute-start | bytes 786440 | tf_op jit(solution)/shard_map/ppermute | solution.py:280
  18.7 3.8 %collective-permute-done.2.refs_3_ = f32[144,512]{1,0:T(8,128)S(1)} collective-permute-done((f32[144,512]{1,0:T(8,128)S(1)}, f32[144,512]{1,0:T(8,128)S(1)}, u32[]{:S(2)}, u32[]{:S(2)}) %collective-permute-start.2) | collective-permute-done | bytes 294944 | tf_op jit(solution)/shard_map/ppermute | solution.py:280
  22.4 2.4 %collective-permute-start.8 = (f32[128,512]{1,0:T(8,128)}, f32[128,512]{1,0:T(8,128)S(1)}, u32[]{:S(2)}, u32[]{:S(2)}) collective-permute-start(f32[128,512]{1,0:T(8,128)} %get-tuple-element.42), channel_id=1, source_target_pairs={{0,2},{1,3},{2,0},{3,1},{4,6},{5,7},{6,4},{7,5},{8,10},{9,11},{10,... | collective-permute-start | bytes 786440 | tf_op jit(solution)/shard_map/ppermute | solution.py:280
  24.9 2.7 %pad_maximum_fusion.refs_7_.refs_5_ = bf16[2048,1280]{1,0:T(8,128)(2,1)} fusion(bf16[2048,640]{1,0:T(8,128)(2,1)S(1)} %get-tuple-element.54, bf16[2048,640]{1,0:T(8,128)(2,1)S(1)} %get-tuple-element.53), kind=kLoop, calls=%fused_computation.5 | loop fusion | flops 10485760 | bytes 10485760 | tf_op jit(solution)/shard_map/concatenate | solution.py:269
  27.6 0.5 collective-permute-start.3
  28.1 5.0 %collective-permute-done.8.refs_3_ = f32[128,512]{1,0:T(8,128)S(1)} collective-permute-done((f32[128,512]{1,0:T(8,128)}, f32[128,512]{1,0:T(8,128)S(1)}, u32[]{:S(2)}, u32[]{:S(2)}) %collective-permute-start.8) | collective-permute-done | bytes 262176 | tf_op jit(solution)/shard_map/ppermute | solution.py:280
  33.9 2.5 %copy-done = bf16[2048,1280]{1,0:T(8,128)(2,1)S(1)} copy-done((bf16[2048,1280]{1,0:T(8,128)(2,1)S(1)}, bf16[2048,1280]{1,0:T(8,128)(2,1)}, u32[]{:S(2)}) %copy-start) | copy-done | bytes 5242904
  36.4 7.4 %shard_map.82 = (f32[256,128]{1,0:T(8,128)S(1)}, f32[256,128]{1,0:T(8,128)S(1)}, f32[256,128]{1,0:T(8,128)S(1)}, f32[256,128]{1,0:T(8,128)S(1)}, f32[2,128,128]{2,1,0:T(8,128)S(1)}, /*index=5*/f32[16,384]{1,0:T(8,128)S(1)}) custom-call(s32[4]{0:T(128)S(1)} %pad_add_fusion.1.refs_0_, f32[528,512]{1,0:T(8,128)S(1)} %constant_dynamic-update-slice_fusion.refs_1_, ...), custom_call_target="tpu_custom_call" | custom-call | tf_op jit(solution)/shard_map/pallas_call | solution.py:257
  43.9 5.2 %shard_map.83 = (f32[128,128]{1,0:T(8,128)S(1)}, f32[128,128]{1,0:T(8,128)S(1)}, f32[128,128]{1,0:T(8,128)S(1)}, f32[128,128]{1,0:T(8,128)S(1)}, f32[2,128,128]{2,1,0:T(8,128)S(1)}, /*index=5*/f32[16,384]{1,0:T(8,128)S(1)}) custom-call(s32[4]{0:T(128)S(1)} %pad_add_fusion.1.refs_0_, f32[528,512]{1,0:T(8,128)S(1)} %constant_dynamic-update-slice_fusion.refs_1_, ...), custom_call_target="tpu_custom_call" | custom-call | tf_op jit(solution)/shard_map/pallas_call | solution.py:257
  49.2 4.9 %shard_map.84 = (f32[128,128]{1,0:T(8,128)S(1)}, f32[128,128]{1,0:T(8,128)S(1)}, f32[128,128]{1,0:T(8,128)S(1)}, f32[128,128]{1,0:T(8,128)S(1)}, f32[2,128,128]{2,1,0:T(8,128)S(1)}, /*index=5*/f32[16,384]{1,0:T(8,128)}) custom-call(s32[4]{0:T(128)S(1)} %pad_add_fusion.1.refs_0_, f32[528,512]{1,0:T(8,128)S(1)} %constant_dynamic-update-slice_fusion.refs_1_, ...), custom_call_target="tpu_custom_call" | custom-call | tf_op jit(solution)/shard_map/pallas_call | solution.py:257
  54.1 1.6 %collective-permute-start.10 = (f32[2,128,128]{2,1,0:T(8,128)S(1)}, f32[2,128,128]{2,1,0:T(8,128)S(1)}, u32[]{:S(2)}, u32[]{:S(2)}) collective-permute-start(f32[2,128,128]{2,1,0:T(8,128)S(1)} %get-tuple-element.49.own_ref), channel_id=1, source_target_pairs={{0,4},{4,0},{8,12},{12,8},{16,20},{20,16},{24,28},{28,24},{1,5},{5... | collective-permute-start | bytes 393224 | tf_op jit(solution)/shard_map/ppermute | solution.py:360
  55.7 1.6 %collective-permute-start.11 = (f32[2,128,128]{2,1,0:T(8,128)S(1)}, f32[2,128,128]{2,1,0:T(8,128)S(1)}, u32[]{:S(2)}, u32[]{:S(2)}) collective-permute-start(f32[2,128,128]{2,1,0:T(8,128)S(1)} %get-tuple-element.49.own_ref), channel_id=1, source_target_pairs={{0,8},{4,12},{8,0},{12,4},{16,24},{20,28},{24,16},{28,20},{1,9},{5... | collective-permute-start | bytes 393224 | tf_op jit(solution)/shard_map/ppermute | solution.py:360
  57.7 2.3 %collective-permute-done.10.one_ref = f32[2,128,128]{2,1,0:T(8,128)S(1)} collective-permute-done((f32[2,128,128]{2,1,0:T(8,128)S(1)}, f32[2,128,128]{2,1,0:T(8,128)S(1)}, u32[]{:S(2)}, u32[]{:S(2)}) %collective-permute-start.10) | collective-permute-done | bytes 131104 | tf_op jit(solution)/shard_map/ppermute | solution.py:360
  60.0 2.0 %collective-permute-done.11.two_ref = f32[2,128,128]{2,1,0:T(8,128)S(1)} collective-permute-done((f32[2,128,128]{2,1,0:T(8,128)S(1)}, f32[2,128,128]{2,1,0:T(8,128)S(1)}, u32[]{:S(2)}, u32[]{:S(2)}) %collective-permute-start.11) | collective-permute-done | bytes 131104 | tf_op jit(solution)/shard_map/ppermute | solution.py:360
  62.0 2.0 %collective-permute-done.12.three_ref = f32[2,128,128]{2,1,0:T(8,128)S(1)} collective-permute-done((f32[2,128,128]{2,1,0:T(8,128)S(1)}, f32[2,128,128]{2,1,0:T(8,128)S(1)}, u32[]{:S(2)}, u32[]{:S(2)}) %collective-permute-start.12) | collective-permute-done | bytes 131104 | tf_op jit(solution)/shard_map/ppermute | solution.py:360
  64.0 1.1 %shard_map.85 = (f32[2,128,128]{2,1,0:T(8,128)S(1)}, f32[2,128,128]{2,1,0:T(8,128)S(1)}, f32[128,128]{1,0:T(8,128)S(1)}) custom-call(s32[2]{0:T(128)S(1)} %pad_add_fusion.2.bits_ref, f32[2,128,128]{2,1,0:T(8,128)S(1)} %get-tuple-element.49.own_ref, f32[2,128,128]{2,1,0:T(8,128)S(1)} %collective-permute-done.10.one_ref, ...), custom_call_target="tpu_custom_call" | custom-call | tf_op jit(solution)/shard_map/pallas_call | solution.py:257
  65.1 4.5 %collective-permute-start.13 = (f32[128,128]{1,0:T(8,128)S(1)}, f32[128,128]{1,0:T(8,128)S(1)}, u32[]{:S(2)}, u32[]{:S(2)}) collective-permute-start(f32[128,128]{1,0:T(8,128)S(1)} %slice_bitcast_fusion), channel_id=1, source_target_pairs={{0,16},{4,20},{8,24},{12,28},{1,17},{5,21},{9,25},{13,29},{2,18},{... | collective-permute-start | bytes 196616 | tf_op jit(solution)/shard_map/ppermute | solution.py:376
  69.6 1.9 %collective-permute-done.13.refs_14_ = f32[128,128]{1,0:T(8,128)S(1)} collective-permute-done((f32[128,128]{1,0:T(8,128)S(1)}, f32[128,128]{1,0:T(8,128)S(1)}, u32[]{:S(2)}, u32[]{:S(2)}) %collective-permute-start.13) | collective-permute-done | bytes 65568 | tf_op jit(solution)/shard_map/ppermute | solution.py:376
  71.5 0.6 shard_map.86.refs_0_
  72.1 1.6 %collective-permute-start.14 = (f32[512,128]{1,0:T(8,128)S(1)}, f32[512,128]{1,0:T(8,128)S(1)}, u32[]{:S(2)}, u32[]{:S(2)}) collective-permute-start(f32[512,128]{1,0:T(8,128)S(1)} %shard_map.86.refs_0_), channel_id=1, source_target_pairs={{0,2},{1,3},{2,0},{3,1},{4,6},{5,7},{6,4},{7,5},{8,10},{9,11},{10,... | collective-permute-start | bytes 786440 | tf_op jit(solution)/shard_map/ppermute | solution.py:280
  74.0 5.0 %collective-permute-done.14.refs_0_ = f32[512,128]{1,0:T(8,128)S(1)} collective-permute-done((f32[512,128]{1,0:T(8,128)S(1)}, f32[512,128]{1,0:T(8,128)S(1)}, u32[]{:S(2)}, u32[]{:S(2)}) %collective-permute-start.14) | collective-permute-done | bytes 262176 | tf_op jit(solution)/shard_map/ppermute | solution.py:280
  79.2 1.5 %shard_map.87.refs_3_ = f32[512,512]{1,0:T(8,128)S(1)} custom-call(s32[2]{0:T(128)S(1)} %pad_add_fusion.3.index_ref, f32[512,128]{1,0:T(8,128)S(1)} %shard_map.86.refs_0_, f32[512,128]{1,0:T(8,128)S(1)} %collective-permute-done.16.refs_1_, bf16[512,1024]{1,0:T(8,128)(2,1)S(1)} %pad_maximum_fusion.1.refs_2_), custom_call_target="tpu_custom_call" | custom-call | tf_op jit(solution)/shard_map/pallas_call | solution.py:257
  80.8 2.5 %shard_map.88 = f32[512,512]{1,0:T(8,128)} custom-call(s32[2]{0:T(128)S(1)} %pad_add_fusion.index_ref, f32[512,128]{1,0:T(8,128)S(1)} %collective-permute-done.14.refs_0_, f32[512,128]{1,0:T(8,128)S(1)} %collective-permute-done.15.refs_1_, bf16[512,1024]{1,0:T(8,128)(2,1)S(1)} %pad_maximum_fusion.1.refs_2_, f32[512,512]{1,0:T(8,128)S(1)} %shard_map.87.refs_3_), custom_call_target="tpu_custom_call" | custom-call | tf_op jit(solution)/shard_map/pallas_call | solution.py:257
  (38 shorter events, 1.2 us)
Async XLA Ops:
  0.8 9.6 %collective-permute-start = (f32[16,512]{1,0:T(8,128)S(1)}, f32[16,512]{1,0:T(8,128)S(1)}, u32[]{:S(2)}, u32[]{:S(2)}) collective-permute-start(f32[16,512]{1,0:T(8,128)S(1)} %slice.22), channel_id=1, source_target_pairs={{0,4},{4,8},{8,12},{12,16},{16,20},{20,24},{24,28},{1,5},{5,9},{9,... | collective-permute-start | bytes 98312 | tf_op jit(solution)/shard_map/ppermute | solution.py:303
  7.6 8.6 %collective-permute-start.4 = (f32[128,512]{1,0:T(8,128)}, f32[128,512]{1,0:T(8,128)}, u32[]{:S(2)}, u32[]{:S(2)}) collective-permute-start(f32[128,512]{1,0:T(8,128)} %get-tuple-element.57), channel_id=1, source_target_pairs={{0,2},{1,3},{2,0},{3,1},{4,6},{5,7},{6,4},{7,5},{8,10},{9,11},{10,... | collective-permute-start | bytes 786440 | tf_op jit(solution)/shard_map/ppermute | solution.py:280
  11.7 22.2 %collective-permute-start.1 = (f32[528,512]{1,0:T(8,128)S(1)}, f32[528,512]{1,0:T(8,128)S(1)}, u32[]{:S(2)}, u32[]{:S(2)}) collective-permute-start(f32[528,512]{1,0:T(8,128)S(1)} %constant_dynamic-update-slice_fusion.refs_1_), channel_id=1, source_target_pairs={{0,1},{1,0},{2,3},{3,2},{4,5},{5,4},{6,7},{7,6},{8,9},{9,8},{10,11... | collective-permute-start | bytes 3244040 | tf_op jit(solution)/shard_map/ppermute | solution.py:274
  11.8 10.6 %collective-permute-start.2 = (f32[144,512]{1,0:T(8,128)S(1)}, f32[144,512]{1,0:T(8,128)S(1)}, u32[]{:S(2)}, u32[]{:S(2)}) collective-permute-start(f32[144,512]{1,0:T(8,128)S(1)} %slice.28), channel_id=1, source_target_pairs={{0,2},{1,3},{2,0},{3,1},{4,6},{5,7},{6,4},{7,5},{8,10},{9,11},{10,... | collective-permute-start | bytes 884744 | tf_op jit(solution)/shard_map/ppermute | solution.py:280
  16.2 11.9 %collective-permute-start.6 = (f32[128,512]{1,0:T(8,128)}, f32[128,512]{1,0:T(8,128)S(1)}, u32[]{:S(2)}, u32[]{:S(2)}) collective-permute-start(f32[128,512]{1,0:T(8,128)} %get-tuple-element.35), channel_id=1, source_target_pairs={{0,2},{1,3},{2,0},{3,1},{4,6},{5,7},{6,4},{7,5},{8,10},{9,11},{10,... | collective-permute-start | bytes 786440 | tf_op jit(solution)/shard_map/ppermute | solution.py:280
  22.4 10.7 %collective-permute-start.8 = (f32[128,512]{1,0:T(8,128)}, f32[128,512]{1,0:T(8,128)S(1)}, u32[]{:S(2)}, u32[]{:S(2)}) collective-permute-start(f32[128,512]{1,0:T(8,128)} %get-tuple-element.42), channel_id=1, source_target_pairs={{0,2},{1,3},{2,0},{3,1},{4,6},{5,7},{6,4},{7,5},{8,10},{9,11},{10,... | collective-permute-start | bytes 786440 | tf_op jit(solution)/shard_map/ppermute | solution.py:280
  24.9 9.0 %copy-start.5 = (s32[512]{0:T(512)S(1)}, s32[512]{0:T(512)}, u32[]{:S(2)}) copy-start(s32[512]{0:T(512)} %param.13) | copy-start | bytes 6148
  24.9 9.0 %copy-start.2 = (f32[4,384]{1,0:T(4,128)S(1)}, f32[4,384]{1,0:T(4,128)}, u32[]{:S(2)}) copy-start(f32[4,384]{1,0:T(4,128)} %refs_6_.3) | copy-start | bytes 18436
  27.6 6.3 %collective-permute-start.5 = (f32[128,512]{1,0:T(8,128)}, f32[128,512]{1,0:T(8,128)}, u32[]{:S(2)}, u32[]{:S(2)}) collective-permute-start(f32[128,512]{1,0:T(8,128)} %collective-permute-done.4.refs_5_), channel_id=1, source_target_pairs={{0,1},{1,0},{2,3},{3,2},{4,5},{5,4},{6,7},{7,6},{8,9},{9,8},{10,11... | collective-permute-start | bytes 786440 | tf_op jit(solution)/shard_map/ppermute | solution.py:274
  27.6 6.3 %collective-permute-start.3 = (f32[144,512]{1,0:T(8,128)S(1)}, f32[144,512]{1,0:T(8,128)S(1)}, u32[]{:S(2)}, u32[]{:S(2)}) collective-permute-start(f32[144,512]{1,0:T(8,128)S(1)} %collective-permute-done.2.refs_3_), channel_id=1, source_target_pairs={{0,1},{1,0},{2,3},{3,2},{4,5},{5,4},{6,7},{7,6},{8,9},{9,8},{10,11... | collective-permute-start | bytes 884744 | tf_op jit(solution)/shard_map/ppermute | solution.py:274
  28.1 15.8 %collective-permute-start.7 = (f32[128,512]{1,0:T(8,128)S(1)}, f32[128,512]{1,0:T(8,128)}, u32[]{:S(2)}, u32[]{:S(2)}) collective-permute-start(f32[128,512]{1,0:T(8,128)S(1)} %collective-permute-done.6.refs_3_), channel_id=1, source_target_pairs={{0,1},{1,0},{2,3},{3,2},{4,5},{5,4},{6,7},{7,6},{8,9},{9,8},{10,11... | collective-permute-start | bytes 786440 | tf_op jit(solution)/shard_map/ppermute | solution.py:274
  33.1 16.0 %collective-permute-start.9 = (f32[128,512]{1,0:T(8,128)S(1)}, f32[128,512]{1,0:T(8,128)S(1)}, u32[]{:S(2)}, u32[]{:S(2)}) collective-permute-start(f32[128,512]{1,0:T(8,128)S(1)} %collective-permute-done.8.refs_3_), channel_id=1, source_target_pairs={{0,1},{1,0},{2,3},{3,2},{4,5},{5,4},{6,7},{7,6},{8,9},{9,8},{10,11... | collective-permute-start | bytes 786440 | tf_op jit(solution)/shard_map/ppermute | solution.py:274
  33.9 2.5 %copy-start = (bf16[2048,1280]{1,0:T(8,128)(2,1)S(1)}, bf16[2048,1280]{1,0:T(8,128)(2,1)}, u32[]{:S(2)}) copy-start(bf16[2048,1280]{1,0:T(8,128)(2,1)} %pad_maximum_fusion.refs_7_.refs_5_) | copy-start | bytes 15728644
  36.4 7.5 %copy-start.1 = (bf16[2048,1280]{1,0:T(8,128)(2,1)S(1)}, bf16[2048,1280]{1,0:T(8,128)(2,1)}, u32[]{:S(2)}) copy-start(bf16[2048,1280]{1,0:T(8,128)(2,1)} %pad_maximum_fusion.refs_7_.refs_5_) | copy-start | bytes 15728644
  49.1 22.4 %copy-start.3 = (f32[128]{0:T(128)S(1)}, f32[128]{0:T(128)}, u32[]{:S(2)}) copy-start(f32[128]{0:T(128)} %param.14) | copy-start | bytes 1540
  49.1 24.6 %copy-start.4 = (f32[512,512]{1,0:T(8,128)S(1)}, f32[512,512]{1,0:T(8,128)}, u32[]{:S(2)}) copy-start(f32[512,512]{1,0:T(8,128)} %param.15) | copy-start | bytes 3145732
  54.1 6.0 %collective-permute-start.10 = (f32[2,128,128]{2,1,0:T(8,128)S(1)}, f32[2,128,128]{2,1,0:T(8,128)S(1)}, u32[]{:S(2)}, u32[]{:S(2)}) collective-permute-start(f32[2,128,128]{2,1,0:T(8,128)S(1)} %get-tuple-element.49.own_ref), channel_id=1, source_target_pairs={{0,4},{4,0},{8,12},{12,8},{16,20},{20,16},{24,28},{28,24},{1,5},{5... | collective-permute-start | bytes 393224 | tf_op jit(solution)/shard_map/ppermute | solution.py:360
  55.7 6.3 %collective-permute-start.11 = (f32[2,128,128]{2,1,0:T(8,128)S(1)}, f32[2,128,128]{2,1,0:T(8,128)S(1)}, u32[]{:S(2)}, u32[]{:S(2)}) collective-permute-start(f32[2,128,128]{2,1,0:T(8,128)S(1)} %get-tuple-element.49.own_ref), channel_id=1, source_target_pairs={{0,8},{4,12},{8,0},{12,4},{16,24},{20,28},{24,16},{28,20},{1,9},{5... | collective-permute-start | bytes 393224 | tf_op jit(solution)/shard_map/ppermute | solution.py:360
  57.3 6.8 %collective-permute-start.12 = (f32[2,128,128]{2,1,0:T(8,128)S(1)}, f32[2,128,128]{2,1,0:T(8,128)S(1)}, u32[]{:S(2)}, u32[]{:S(2)}) collective-permute-start(f32[2,128,128]{2,1,0:T(8,128)S(1)} %get-tuple-element.49.own_ref), channel_id=1, source_target_pairs={{0,12},{4,8},{8,4},{12,0},{16,28},{20,24},{24,20},{28,16},{1,13},{... | collective-permute-start | bytes 393224 | tf_op jit(solution)/shard_map/ppermute | solution.py:360
  65.1 6.4 %collective-permute-start.13 = (f32[128,128]{1,0:T(8,128)S(1)}, f32[128,128]{1,0:T(8,128)S(1)}, u32[]{:S(2)}, u32[]{:S(2)}) collective-permute-start(f32[128,128]{1,0:T(8,128)S(1)} %slice_bitcast_fusion), channel_id=1, source_target_pairs={{0,16},{4,20},{8,24},{12,28},{1,17},{5,21},{9,25},{13,29},{2,18},{... | collective-permute-start | bytes 196616 | tf_op jit(solution)/shard_map/ppermute | solution.py:376
  72.1 6.8 %collective-permute-start.14 = (f32[512,128]{1,0:T(8,128)S(1)}, f32[512,128]{1,0:T(8,128)S(1)}, u32[]{:S(2)}, u32[]{:S(2)}) collective-permute-start(f32[512,128]{1,0:T(8,128)S(1)} %shard_map.86.refs_0_), channel_id=1, source_target_pairs={{0,2},{1,3},{2,0},{3,1},{4,6},{5,7},{6,4},{7,5},{8,10},{9,11},{10,... | collective-permute-start | bytes 786440 | tf_op jit(solution)/shard_map/ppermute | solution.py:280
  73.9 5.4 %collective-permute-start.16 = (f32[512,128]{1,0:T(8,128)S(1)}, f32[512,128]{1,0:T(8,128)S(1)}, u32[]{:S(2)}, u32[]{:S(2)}) collective-permute-start(f32[512,128]{1,0:T(8,128)S(1)} %shard_map.86.refs_0_), channel_id=1, source_target_pairs={{0,1},{1,0},{2,3},{3,2},{4,5},{5,4},{6,7},{7,6},{8,9},{9,8},{10,11... | collective-permute-start | bytes 786440 | tf_op jit(solution)/shard_map/ppermute | solution.py:274
  78.9 1.8 %collective-permute-start.15 = (f32[512,128]{1,0:T(8,128)S(1)}, f32[512,128]{1,0:T(8,128)S(1)}, u32[]{:S(2)}, u32[]{:S(2)}) collective-permute-start(f32[512,128]{1,0:T(8,128)S(1)} %collective-permute-done.14.refs_0_), channel_id=1, source_target_pairs={{0,1},{1,0},{2,3},{3,2},{4,5},{5,4},{6,7},{7,6},{8,9},{9,8},{10,11... | collective-permute-start | bytes 786440 | tf_op jit(solution)/shard_map/ppermute | solution.py:274

commit v3 on v2

v3 whole, which is shorter than its diff:
```python
import functools

import jax
import jax.numpy as jnp
from jax import lax
from jax.experimental import pallas as pl
from jax.experimental.pallas import tpu as pltpu
from jax.sharding import PartitionSpec as P

CHUNK = 128
RIM = 16
F32 = jnp.float32
BF16 = jnp.bfloat16


def halves(value):
    high = value.astype(BF16)
    return high, (value - high.astype(F32)).astype(BF16)


def left_parts(value):
    return jnp.concatenate(halves(value), axis=1)


def right_parts(value):
    row = jnp.concatenate(halves(value), axis=1)
    return jnp.concatenate([row, row], axis=0)


def parts_dot(left, right):
    both = jnp.dot(left, right, preferred_element_type=F32)
    half = both.shape[1] // 2
    return both[:, :half] + both[:, half:]


def product(left, right):
    return parts_dot(left_parts(left), right_parts(right))


def softplus(value):
    return jnp.maximum(value, 0.0) + jnp.log1p(jnp.exp(-jnp.abs(value)))


def sigmoid(value):
    return 1.0 / (1.0 + jnp.exp(-value))


def unit_lower_inverse(lowers, row, col):
    size = lowers[0].shape[0]
    eye = jnp.where(row == col, 1.0, 0.0).astype(F32)
    inverses = [eye - jnp.where((row >> 1) == (col >> 1), lower, 0.0) for lower in lowers]
    lower_parts = [halves(lower) for lower in lowers]
    step = 1
    while 2 << (step - 1) < size:
        off = ((row >> (step + 1)) == (col >> (step + 1))) & ((row >> step) > (col >> step))
        lefts = [left_parts(inverse) for inverse in inverses]
        offs = [
            jnp.concatenate([jnp.where(off, part, jnp.zeros_like(part)) for part in parts], axis=1)
            for parts in lower_parts
        ]
        inner = [
            parts_dot(offdiag, right_parts(inverse)) for offdiag, inverse in zip(offs, inverses)
        ]
        inverses = [
            inverse - parts_dot(left, right_parts(value))
            for inverse, left, value in zip(inverses, lefts, inner)
        ]
        step += 1
    return inverses


def prepare_kernel(proj_ref, mix_ref, out_ref, weight_ref, own_ref):
    width = proj_ref.shape[1]
    columns = weight_ref.shape[1] // 2
    mixes = mix_ref.shape[0]
    for base in range(0, proj_ref.shape[0], CHUNK):
        rows = slice(base, base + CHUNK)
        high, low = halves(proj_ref[rows, :])
        weight_ref[rows, :width] = high
        weight_ref[rows, columns : columns + width] = low
        mixing = jnp.concatenate(
            [mix_ref[:, rows], jnp.zeros((CHUNK - mixes, CHUNK), F32)], axis=0
        )
        high, low = halves(jnp.transpose(mixing))
        weight_ref[rows, width:columns] = high
        weight_ref[rows, columns + width :] = low
    for base in range(0, out_ref.shape[0], CHUNK):
        rows = slice(base, base + CHUNK)
        own_ref[rows, :] = left_parts(out_ref[rows, :])


def add_products(total, pieces, index_ref, first, weight_ref):
    columns = weight_ref.shape[1] // 2
    for spot, piece in enumerate(pieces):
        depth = piece.shape[1]
        rows = pl.ds(pl.multiple_of(index_ref[first + spot] * depth, depth), depth)
        high, low = halves(piece)
        both = jnp.dot(high, weight_ref[rows, :], preferred_element_type=F32)
        rest = jnp.dot(low, weight_ref[rows, :columns], preferred_element_type=F32)
        part = (both[:, :columns] + both[:, columns:]) + rest
        total = part if total is None else total + part
    return total


def base_kernel(index_ref, own_ref, beside_ref, weight_ref, base_ref):
    half = own_ref.shape[0] // 2
    for rows in (slice(0, half), slice(half, 2 * half)):
        base_ref[rows, :] = add_products(
            None, [own_ref[rows, :], beside_ref[rows, :]], index_ref, 0, weight_ref
        )


def late_kernel(count, begin, index_ref, *refs):
    base_ref, weight_ref, raw_ref = refs[count:]
    raw_ref[...] = add_products(
        base_ref[begin:, :], [ref[...] for ref in refs[:count]], index_ref, 2, weight_ref
    )


def convolve(raw, start, conv_ref, columns):
    taps = conv_ref.shape[0]
    conv = 0.0
    for tap in range(taps):
        spot = start - taps + 1 + tap
        conv = conv + conv_ref[tap : tap + 1, columns] * raw[spot : spot + CHUNK, columns]
    return conv * sigmoid(conv)


def unit_rows(value):
    return value * lax.rsqrt(jnp.sum(value * value, axis=1, keepdims=True) + 1e-06)


def key_pass(raw, conv_ref, rate, doc_ref, first_chunk, outs, state):
    key_ref, x_ref, y_ref, grid_ref, gamma_ref, chunk_ref, pair_ref = outs
    width = key_ref.shape[1]
    chunks = key_ref.shape[0] // CHUNK
    row = lax.broadcasted_iota(jnp.int32, (CHUNK, CHUNK), 0)
    col = lax.broadcasted_iota(jnp.int32, (CHUNK, CHUNK), 1)
    lower = row >= col
    tri = jnp.where(lower, 1.0, 0.0).astype(F32)
    eye = jnp.where(row == col, 1.0, 0.0).astype(F32)
    keys, values, betas, grids, gammas, tails = [], [], [], [], [], []
    for part in range(chunks):
        start = RIM + part * CHUNK
        rows = slice(part * CHUNK, (part + 1) * CHUNK)
        keys.append(unit_rows(convolve(raw, start, conv_ref, slice(width, 2 * width))))
        values.append(convolve(raw, start, conv_ref, slice(2 * width, 3 * width)))
        mixing = raw[start : start + CHUNK, 4 * width :]
        betas.append(sigmoid(mixing[:, 0:1]))
        spot = first_chunk + part
        docs = jnp.transpose(jnp.broadcast_to(doc_ref[spot : spot + 1, :], (CHUNK, CHUNK)))
        steps = jnp.where(col == 1, -rate * softplus(mixing), jnp.where(col == 0, docs, 0.0))
        sums = jnp.dot(tri, steps, precision=lax.Precision.HIGHEST, preferred_element_type=F32)
        across = jnp.transpose(sums)
        smooth, count = sums[:, 1:2], sums[:, 0:1]
        span = (smooth - across[1:2, :]) - 20.0 * (count - across[0:1, :])
        grids.append(jnp.exp(jnp.where(lower, span, -1e30)))
        gammas.append(jnp.exp(smooth - 20.0 * count))
        last = sums[CHUNK - 1 : CHUNK, :]
        tails.append(jnp.exp((last[:, 1:2] - smooth) - 20.0 * (last[:, 0:1] - count)))
        key_ref[rows, :] = keys[part]
        grid_ref[rows, :] = grids[part]
        gamma_ref[rows, :] = jnp.broadcast_to(gammas[part], (CHUNK, width))
    across_keys = [jnp.transpose(key) for key in keys]
    grams = [
        parts_dot(left_parts(key), right_parts(across)) for key, across in zip(keys, across_keys)
    ]
    lowers = [jnp.where(row > col, beta * gram, 0.0) for beta, gram in zip(betas, grams)]
    inverses = unit_lower_inverse(lowers, row, col)
    states = []
    for part in range(chunks):
        rows = slice(part * CHUNK, (part + 1) * CHUNK)
        inverse, beta = inverses[part], betas[part]
        factor_x = product(inverse, beta * keys[part])
        factor_y = product(grids[part] * inverse, beta * values[part])
        x_ref[rows, :] = factor_x
        y_ref[rows, :] = factor_y
        onto = product(
            across_keys[part], jnp.concatenate([factor_x, tails[part] * factor_y], axis=1)
        )
        trans = gammas[part][CHUNK - 1 : CHUNK, :] * (eye - onto[:, :width])
        states.append((trans, onto[:, width:]))
        chunk_ref[part, 0] = trans
        chunk_ref[part, 1] = onto[:, width:]
    for part in range(1, chunks):
        states[0] = followed(states[0], states[part])
    total = states[0] if state is None else followed(states[0], state)
    pair_ref[0] = total[0]
    pair_ref[1] = total[1]


def followed(first, second):
    width = first[0].shape[0]
    onto = product(second[0], jnp.concatenate(first, axis=1))
    return onto[:, :width], onto[:, width:] + second[1]


def later_kernel(first_chunk, raw_ref, conv_ref, rate_ref, doc_ref, *outs):
    key_pass(raw_ref, conv_ref, rate_ref[0, 0], doc_ref, first_chunk, outs, None)


def earlier_kernel(count, index_ref, *refs):
    held, refs = refs[:count], refs[count:]
    base_ref, weight_ref, rim_ref, next_ref, state_ref, conv_ref, rate_ref, doc_ref, raw = refs[:9]
    rows = held[0].shape[0]
    raw[RIM : RIM + rows, :] = add_products(
        base_ref[:rows, :], [ref[...] for ref in held], index_ref, 2, weight_ref
    )
    raw[:RIM, : rim_ref.shape[1]] = rim_ref[...]
    raw[RIM + rows :, :] = next_ref[:RIM, :]
    key_pass(
        raw, conv_ref, rate_ref[0, 0], doc_ref, 0, refs[9:], (state_ref[0], state_ref[1])
    )


def query_kernel(pieces, *refs):
    fields = [refs[7 * piece : 7 * piece + 7] for piece in range(pieces)]
    conv_ref, carried_ref, local_ref, plus_ref, gate_ref = refs[7 * pieces :]
    width = carried_ref.shape[1]
    row = lax.broadcasted_iota(jnp.int32, (CHUNK, CHUNK), 0)
    col = lax.broadcasted_iota(jnp.int32, (CHUNK, CHUNK), 1)
    state = None
    base = 0
    for raw, key_ref, x_ref, y_ref, grid_ref, gamma_ref, chunk_ref in fields:
        for part in range(key_ref.shape[0] // CHUNK):
            start = RIM + part * CHUNK
            rows = slice(part * CHUNK, (part + 1) * CHUNK)
            out = slice(base, base + CHUNK)
            base += CHUNK
            query = unit_rows(convolve(raw, start, conv_ref, slice(0, width)))
            gate = raw[start : start + CHUNK, 3 * width : 4 * width]
            gate_ref[out, :] = gate * sigmoid(gate)
            plus_ref[out, :] = softplus(raw[start : start + CHUNK, 4 * width :])
            overlap = product(query, jnp.transpose(key_ref[rows, :]))
            carried = gamma_ref[rows, :] * (
                query - product(jnp.where(row >= col, overlap, 0.0), x_ref[rows, :])
            )
            local = product(grid_ref[rows, :] * overlap, y_ref[rows, :])
            trans, memory = chunk_ref[part, 0], chunk_ref[part, 1]
            if state is None:
                state = (trans, memory)
            else:
                onto = product(
                    jnp.concatenate([trans, carried], axis=0), jnp.concatenate(state, axis=1)
                )
                carried = onto[CHUNK:, :width]
                local = local + onto[CHUNK:, width:]
                state = (onto[:CHUNK, :width], onto[:CHUNK, width:] + memory)
            carried_ref[out, :] = carried
            local_ref[out, :] = local


def four_kernel(bits_ref, own_ref, one_ref, two_ref, three_ref, carry_ref, group_ref, level_ref, next_ref, pairs):
    low_bit, high_bit = bits_ref[0], bits_ref[1]
    place = 2 * high_bit + low_bit
    for mask, ref in enumerate((own_ref, one_ref, two_ref, three_ref)):
        pairs[place ^ mask] = ref[...]
    width = carry_ref.shape[0]
    joined = lambda spot: jnp.concatenate([pairs[spot, 0], pairs[spot, 1]], axis=1)
    onto_low = product(pairs[1, 0], joined(0))
    onto_high = product(pairs[3, 0], joined(2))
    low_a, low_s = onto_low[:, :width], onto_low[:, width:] + pairs[1, 1]
    high_a, high_s = onto_high[:, :width], onto_high[:, width:] + pairs[3, 1]
    onto = product(high_a, jnp.concatenate([low_a, low_s], axis=1))
    group_ref[0] = onto[:, :width]
    group_ref[1] = onto[:, width:] + high_s
    carry = carry_ref[...]
    first = product(carry, jnp.concatenate([one_ref[0], one_ref[1]], axis=1))
    set_low = jnp.broadcast_to(low_bit, (width, width)) == 1
    set_high = jnp.broadcast_to(high_bit, (width, width)) == 1
    level_ref[0] = jnp.where(set_low, first[:, width:], 0.0)
    carry = jnp.where(set_low, first[:, :width], carry)
    second = product(carry, jnp.concatenate([low_a, low_s], axis=1))
    level_ref[1] = jnp.where(set_high, second[:, width:], 0.0)
    next_ref[...] = jnp.where(set_high, second[:, :width], carry)


def mix_kernel(stages, single, carried_ref, local_ref, weight_ref, gate_ref, gain_ref, *refs):
    states = [ref[spot] for ref in refs[:stages] for spot in range(ref.shape[0])]
    if single:
        states.append(product(refs[stages][...], refs[stages + 1][...]))
    normed_ref = refs[-1]
    states = [right_parts(state) for state in states]
    carried = left_parts(carried_ref[...])
    weights = weight_ref[...]
    mixed = weights[:, 2:3] * local_ref[...]
    for level, state in enumerate(states):
        mixed = mixed + weights[:, level + 3 : level + 4] * parts_dot(carried, state)
    scale = lax.rsqrt(jnp.mean(mixed * mixed, axis=1, keepdims=True) + 1e-05)
    normed_ref[...] = mixed * scale * gain_ref[...] * gate_ref[...]


def out_kernel(pieces, first, index_ref, *refs):
    weight_ref = refs[pieces]
    total = refs[pieces + 1][...] if first else None
    refs[-1][...] = add_products(
        total, [ref[...] for ref in refs[:pieces]], index_ref, first, weight_ref
    )


def vmem_call(kernel, outs, scratch, cost, *args):
    spec = pl.BlockSpec(memory_space=pltpu.VMEM)
    small = pl.BlockSpec(memory_space=pltpu.SMEM)
    return pl.pallas_call(
        kernel,
        out_shape=outs,
        in_specs=[small if arg.dtype == jnp.int32 else spec for arg in args],
        out_specs=jax.tree.map(lambda unused: spec, outs),
        scratch_shapes=scratch,
        compiler_params=pltpu.CompilerParams(vmem_limit_bytes=40 << 20),
        cost_estimate=pl.CostEstimate(flops=int(cost * 1e9), bytes_accessed=1 << 20, transcendentals=0),
    )(*args)


def to_sibling(value):
    count = lax.axis_size("head")
    return lax.ppermute(value, "head", [(source, source ^ 1) for source in range(count)])


def to_chips(value):
    count = lax.axis_size("head")
    return [
        lax.ppermute(
            value, "head", [(source, (source + 2 * step) % count) for source in range(count)]
        )
        for step in range(1, count // 2)
    ]


def after(value, *earlier):
    return lax.optimization_barrier((value, *earlier))


def shards(tokens, w_proj, w_mix, conv_w, rates, doc_start, norm_gain, w_out):
    tok_rows, depth = tokens.shape
    width = w_proj.shape[1] // 4
    features = w_proj.shape[0]
    columns = 4 * width + CHUNK
    heads, me = lax.axis_size("head"), lax.axis_index("head")
    blocks, my_index = lax.axis_size("ctx"), lax.axis_index("ctx")
    remote = [(me + heads - 2 * step) % heads for step in range(1, heads // 2)]
    order = [me, me ^ 1] + remote + [index ^ 1 for index in remote]
    index = jnp.stack(order).astype(jnp.int32)
    count = heads - 2
    like = lambda *shape: jax.ShapeDtypeStruct(shape, F32)

    half = tok_rows // 2
    cut = half - RIM
    late = to_chips(tokens[cut:])
    beside = to_sibling(tokens)
    weight, own_weight = vmem_call(
        prepare_kernel,
        [jax.ShapeDtypeStruct((features, 2 * columns), BF16),
         jax.ShapeDtypeStruct((w_out.shape[0], 2 * w_out.shape[1]), BF16)],
        [], 3, w_proj, w_mix.T, w_out,
    )
    base = vmem_call(base_kernel, like(tok_rows, columns), [], 3, index, tokens, beside, weight)
    early_rows, base = after(tokens[:cut], base)
    early = to_chips(early_rows)
    late, base = after(late, base)
    late_on = [to_sibling(value) for value in late]
    raw_late = vmem_call(
        functools.partial(late_kernel, count, cut), like(tok_rows - cut, columns), [], 2,
        index, *late, *late_on, base, weight,
    )
    rim = lax.ppermute(
        raw_late[tok_rows - cut - RIM :, : 3 * width], "ctx",
        [(source, source + 1) for source in range(blocks - 1)],
    )
    docs = doc_start.astype(F32).reshape(tok_rows // CHUNK, CHUNK)
    rate = rates[:, None]
    outs = [like(half, width)] * 5 + [like(half // CHUNK, 2, width, width), like(2, width, width)]
    later = vmem_call(
        functools.partial(later_kernel, half // CHUNK), outs, [], 4, raw_late, conv_w, rate, docs
    )
    early, pair_late, rim = after(early, later[6], rim)
    early_on = [to_sibling(value) for value in early]
    raw_early, *earlier = vmem_call(
        functools.partial(earlier_kernel, count), [like(half + RIM, columns)] + outs, [], 5,
        index, *early, *early_on, base, weight, rim, raw_late, pair_late, conv_w, rate, docs,
    )

    pair = earlier[6]
    carry = jnp.eye(width, dtype=F32)
    bits = blocks.bit_length() - 1
    levels = []
    moved = None
    for bit in range(0, bits - 1, 2):
        others = [
            lax.ppermute(
                pair, "ctx", [(source, source ^ (mask << bit)) for source in range(blocks)]
            )
            for mask in (1, 2, 3)
        ]
        flags = jnp.stack([my_index >> bit & 1, my_index >> (bit + 1) & 1]).astype(jnp.int32)
        pair, level, carry = vmem_call(
            four_kernel, [like(2, width, width)] * 2 + [like(width, width)],
            [pltpu.VMEM((4, 2, width, width), F32)], 1,
            flags, pair, *others, carry,
        )
        levels.append(level)
    fields = vmem_call(
        functools.partial(query_kernel, 2), [like(tok_rows, width)] * 4, [], 5,
        raw_early, *earlier[:6], raw_late, *later[:6], conv_w,
    )
    single = []
    if bits % 2:
        reach = blocks // 2
        single = [
            carry,
            lax.ppermute(pair[1], "ctx", [(source, source + reach) for source in range(reach)]),
        ]
    normed = vmem_call(
        functools.partial(mix_kernel, len(levels), bool(single)), like(tok_rows, width), [], 1,
        *fields, norm_gain[None, :], *levels, *single,
    )
    far = to_chips(normed)
    near = to_sibling(normed)
    out_shape = like(tok_rows, w_out.shape[1])
    total = vmem_call(
        functools.partial(out_kernel, 2, 0), out_shape, [], 2, index, normed, near, own_weight
    )
    far, total = after(far, total)
    far_on = [to_sibling(value) for value in far]
    return vmem_call(
        functools.partial(out_kernel, count, 2), out_shape, [], 2,
        index, *far, *far_on, own_weight, total,
    )


def solution(mesh):
    placed = (
        P("ctx", "head"),
        P(None, "head"),
        P(None, "head"),
        P(None, "head"),
        P("head"),
        P("ctx"),
        P("head"),
        P(None, "head"),
    )
    return jax.shard_map(
        shards, mesh=mesh, in_specs=placed, out_specs=P("ctx", "head"), check_vma=False
    )
```

time: 83.9 us -> 73.8 us (0.88)
  local copies, waits for them, and re-layouts: 7.84 us -> 17.1 us
  other arithmetic: 6.35 us -> 0.16 us
  starting transfers between devices: 22.1 us -> 16 us
  waiting for transfers between devices: 22.8 us -> 17.3 us
  Pallas kernels: 23.2 us -> 21.8 us
    unnamed x14 -> x48, local copies, waits for them, and re-layouts: 3.76 us -> 14.1 us
    ppermute x5 -> x3, waiting for transfers between devices: 14.6 us -> 6.23 us  [to_chips(): lax.ppermute(value, 'head', [(source, (source + 2 * step) % count) for so...]
    ppermute x5 -> x3, starting transfers between devices: 8.55 us -> 3.56 us  [to_chips(): lax.ppermute(value, 'head', [(source, (source + 2 * step) % count) for so...]
    ppermute x7 -> x5, waiting for transfers between devices: 0.02 us -> 4.98 us  [to_sibling(): lax.ppermute(value, 'head', [(source, source ^ 1) for source in range(cou...]
    convert_element_type x2 -> x0, other arithmetic: 3.18 us -> none  [split_columns(): high.astype(BF16)]
    concatenate x2 -> x0, other arithmetic: 2.85 us -> none  [split_columns(): jnp.concatenate([high.astype(BF16), (weight - high).astype(BF16)], axis=1)]
    ppermute x1, waiting for transfers between devices: 1.88 us -> 0.16 us  [shards(): lax.ppermute(pair[1], 'ctx', [(source, source + reach) for source in rang...]
    ppermute x1, starting transfers between devices: 4.83 us -> 3.39 us  [shards(): lax.ppermute(raw_late[tok_rows - cut - RIM:, :3 * width], 'ctx', [(source...]
  transfers between devices with their start and end apart: 17 -> 13, of which waited for: 8 -> 10; matrix products, arithmetic and copies ran while one was open for 13% -> 4% of each run, Pallas kernels for 17% -> 17%
where the time goes in v3:
time: 73.8 us; the launch traced here: 73.2 us
  Pallas kernels  21.8 us (30%)
  waiting for transfers between devices  17.3 us (23%)
  local copies, waits for them, and re-layouts  17.1 us (23%)
  starting transfers between devices  16 us (22%)
  between operations  0.92 us (1%)
    pallas_call x10, Pallas kernels, vmem_call(): pl.pallas_call(kernel, out_shape=outs, in_specs=[small if arg.dtype == jn...  21.8 us
    unnamed x48, local copies, waits for them, and re-layouts  14.1 us
    ppermute x3, waiting for transfers between devices, to_chips(): lax.ppermute(value, 'head', [(source, (source + 2 * step) % count) for so...  6.23 us
    ppermute x3, waiting for transfers between devices, shards(): lax.ppermute(pair, 'ctx', [(source, source ^ mask << bit) for source in r...  5.95 us
    ppermute x5, waiting for transfers between devices, to_sibling(): lax.ppermute(value, 'head', [(source, source ^ 1) for source in range(cou...  4.98 us
    ppermute x1, starting transfers between devices, shards(): lax.ppermute(pair[1], 'ctx', [(source, source + reach) for source in rang...  4.67 us
    ppermute x3, starting transfers between devices, to_chips(): lax.ppermute(value, 'head', [(source, (source + 2 * step) % count) for so...  3.56 us
    ppermute x3, starting transfers between devices, shards(): lax.ppermute(pair, 'ctx', [(source, source ^ mask << bit) for source in r...  3.55 us
  transfers between devices with their start and end apart: 13, of which 10 were waited for; matrix products, arithmetic and copies ran while one was open for 4% of the time, Pallas kernels for 17%

profile of v3, /device:TPU:0, one launch (start us, length us, event | category | flops | bytes accessed | tf_op | source)
XLA Modules:
  0.0 73.2 jit_solution(3986726269897368415)
XLA Ops:
  0.5 1.1 %slice.13 = f32[272,512]{1,0:T(8,128)S(1)} slice(f32[512,512]{1,0:T(8,128)} %own_ref.1), slice={[240:512], [0:512]} | slice | bytes 1114112 | tf_op jit(solution)/shard_map/slice | solution.py:349
  1.5 2.6 %collective-permute-start.2 = (f32[272,512]{1,0:T(8,128)S(1)}, f32[272,512]{1,0:T(8,128)S(1)}, u32[]{:S(2)}, u32[]{:S(2)}) collective-permute-start(f32[272,512]{1,0:T(8,128)S(1)} %slice.13), channel_id=1, source_target_pairs={{0,2},{1,3},{2,0},{3,1},{4,6},{5,7},{6,4},{7,5},{8,10},{9,11},{10,... | collective-permute-start | bytes 1671176 | tf_op jit(solution)/shard_map/ppermute | solution.py:323
  4.1 1.8 %slice.12 = f32[240,512]{1,0:T(8,128)} slice(f32[512,512]{1,0:T(8,128)} %own_ref.1), slice={[0:240], [0:512]} | slice | bytes 983040 | tf_op jit(solution)/shard_map/slice | solution.py:358
  6.1 2.2 %copy-done.3 = f32[2048,512]{1,0:T(8,128)S(1)} copy-done((f32[2048,512]{1,0:T(8,128)S(1)}, f32[2048,512]{1,0:T(8,128)}, u32[]{:S(2)}) %copy-start.3) | copy-done | bytes 4194328
  8.2 1.2 %copy-done.4 = f32[512,512]{1,0:T(8,128)S(1)} copy-done((f32[512,512]{1,0:T(8,128)S(1)}, f32[512,512]{1,0:T(8,128)}, u32[]{:S(2)}) %copy-start.4) | copy-done | bytes 1048600
  9.5 0.9 %copy-done.7 = f32[2048,9]{0,1:T(8,128)S(1)} copy-done((f32[2048,9]{0,1:T(8,128)S(1)}, f32[2048,9]{0,1:T(8,128)}, u32[]{:S(2)}) %copy-start.7) | copy-done | bytes 73752
  10.4 1.4 %shard_map.82 = (bf16[2048,1280]{1,0:T(8,128)(2,1)S(1)}, bf16[512,1024]{1,0:T(8,128)(2,1)S(1)}) custom-call(f32[2048,512]{1,0:T(8,128)S(1)} %copy-done.3, f32[9,2048]{1,0:T(8,128)S(1)} %bitcast.15, f32[512,512]{1,0:T(8,128)S(1)} %copy-done.4), custom_call_target="tpu_custom_call" | custom-call | flops 3000000000 | bytes 1048576 | tf_op jit(solution)/shard_map/pallas_call | solution.py:304
  11.8 1.0 %copy-done.10 = bf16[512,1024]{1,0:T(8,128)(2,1)} copy-done((bf16[512,1024]{1,0:T(8,128)(2,1)}, bf16[512,1024]{1,0:T(8,128)(2,1)S(1)}, u32[]{:S(2)}) %copy-start.10) | copy-done | bytes 1048600
  12.8 1.0 %copy-done.5 = f32[512,512]{1,0:T(8,128)} copy-done((f32[512,512]{1,0:T(8,128)}, f32[512,512]{1,0:T(8,128)S(1)}, u32[]{:S(2)}) %copy-start.5) | copy-done | bytes 1048600
  13.8 2.0 %copy-done.6 = f32[512,512]{1,0:T(8,128)S(1)} copy-done((f32[512,512]{1,0:T(8,128)S(1)}, f32[512,512]{1,0:T(8,128)}, u32[]{:S(2)}) %copy-start.6) | copy-done | bytes 1048600
  15.8 3.0 %shard_map.83.refs_2_ = f32[512,640]{1,0:T(8,128)S(1)} custom-call(s32[4]{0:T(128)S(1)} %pad_add_fusion.index_ref, f32[512,512]{1,0:T(8,128)S(1)} %copy-done.2, f32[512,512]{1,0:T(8,128)S(1)} %copy-done.6, bf16[2048,1280]{1,0:T(8,128)(2,1)S(1)} %get-tuple-element.38.weight_ref.refs_3_), custom_call_target="tpu_custom_call" | custom-call | flops 3000000000 | bytes 1048576 | tf_op jit(solution)/shard_map/pallas_call | solution.py:304
  20.2 0.7 collective-permute-done.3.refs_1_
  20.8 1.9 %shard_map.84.raw_ref.refs_5_.refs_7_ = f32[272,640]{1,0:T(8,128)S(1)} custom-call(s32[4]{0:T(128)S(1)} %pad_add_fusion.index_ref, f32[272,512]{1,0:T(8,128)S(1)} %collective-permute-done.2.refs_0_, f32[272,512]{1,0:T(8,128)S(1)} %collective-permute-done.3.refs_1_, f32[512,640]{1,0:T(8,128)S(1)} %shard_map.83.refs_2_, ...), custom_call_target="tpu_custom_call" | custom-call | flops 2000000000 | bytes 1048576 | tf_op jit(solution)/shard_map/pallas_call | solution.py:304
  22.8 3.4 %collective-permute-start.4 = (f32[16,384]{1,0:T(8,128)S(1)}, f32[16,384]{1,0:T(8,128)S(1)}, u32[]{:S(2)}, u32[]{:S(2)}) collective-permute-start(f32[16,384]{1,0:T(8,128)S(1)} %slice.16), channel_id=1, source_target_pairs={{0,4},{4,8},{8,12},{12,16},{16,20},{20,24},{24,28},{1,5},{5,9},{9,... | collective-permute-start | bytes 73736 | tf_op jit(solution)/shard_map/ppermute | solution.py:366
  26.2 3.3 %shard_map.85 = (f32[256,128]{1,0:T(8,128)S(1)}, f32[256,128]{1,0:T(8,128)S(1)}, f32[256,128]{1,0:T(8,128)S(1)}, f32[256,128]{1,0:T(8,128)S(1)}, f32[256,128]{1,...) custom-call(f32[272,640]{1,0:T(8,128)S(1)} %shard_map.84.raw_ref.refs_5_.refs_7_, ...), custom_call_target="tpu_custom_call" | custom-call | flops 4000000000 | bytes 1048576 | tf_op jit(solution)/shard_map/pallas_call | solution.py:304
  32.1 0.7 copy-done.20
  33.3 1.9 %collective-permute-done.5.refs_1_ = f32[240,512]{1,0:T(8,128)S(1)} collective-permute-done((f32[240,512]{1,0:T(8,128)S(1)}, f32[240,512]{1,0:T(8,128)S(1)}, u32[]{:S(2)}, u32[]{:S(2)}) %collective-permute-start.5) | collective-permute-done | bytes 491552 | tf_op jit(solution)/shard_map/ppermute | solution.py:317
  35.2 2.5 %copy-done.1 = bf16[2048,1280]{1,0:T(8,128)(2,1)S(1)} copy-done((bf16[2048,1280]{1,0:T(8,128)(2,1)S(1)}, bf16[2048,1280]{1,0:T(8,128)(2,1)}, u32[]{:S(2)}) %copy-start.1) | copy-done | bytes 5242904
  37.7 5.1 %shard_map.86 = (f32[272,640]{1,0:T(8,128)S(1)}, f32[256,128]{1,0:T(8,128)S(1)}, f32[256,128]{1,0:T(8,128)S(1)}, f32[256,128]{1,0:T(8,128)S(1)}, f32[256,128]{1,...) custom-call(s32[4]{0:T(128)S(1)} %pad_add_fusion.index_ref, ...), custom_call_target="tpu_custom_call" | custom-call | flops 5000000000 | bytes 1048576 | tf_op jit(solution)/shard_map/pallas_call | solution.py:304
  42.8 1.6 %collective-permute-start.6 = (f32[2,128,128]{2,1,0:T(8,128)S(1)}, f32[2,128,128]{2,1,0:T(8,128)S(1)}, u32[]{:S(2)}, u32[]{:S(2)}) collective-permute-start(f32[2,128,128]{2,1,0:T(8,128)S(1)} %get-tuple-element.64.own_ref), channel_id=1, source_target_pairs={{0,4},{4,0},{8,12},{12,8},{16,20},{20,16},{24,28},{28,24},{1,5},{5... | collective-permute-start | bytes 393224 | tf_op jit(solution)/shard_map/ppermute | solution.py:390
  44.3 1.6 %collective-permute-start.7 = (f32[2,128,128]{2,1,0:T(8,128)S(1)}, f32[2,128,128]{2,1,0:T(8,128)S(1)}, u32[]{:S(2)}, u32[]{:S(2)}) collective-permute-start(f32[2,128,128]{2,1,0:T(8,128)S(1)} %get-tuple-element.64.own_ref), channel_id=1, source_target_pairs={{0,8},{4,12},{8,0},{12,4},{16,24},{20,28},{24,16},{28,20},{1,9},{5... | collective-permute-start | bytes 393224 | tf_op jit(solution)/shard_map/ppermute | solution.py:390
  46.4 2.0 %collective-permute-done.6.one_ref = f32[2,128,128]{2,1,0:T(8,128)S(1)} collective-permute-done((f32[2,128,128]{2,1,0:T(8,128)S(1)}, f32[2,128,128]{2,1,0:T(8,128)S(1)}, u32[]{:S(2)}, u32[]{:S(2)}) %collective-permute-start.6) | collective-permute-done | bytes 131104 | tf_op jit(solution)/shard_map/ppermute | solution.py:390
  48.4 2.3 %collective-permute-done.7.two_ref = f32[2,128,128]{2,1,0:T(8,128)S(1)} collective-permute-done((f32[2,128,128]{2,1,0:T(8,128)S(1)}, f32[2,128,128]{2,1,0:T(8,128)S(1)}, u32[]{:S(2)}, u32[]{:S(2)}) %collective-permute-start.7) | collective-permute-done | bytes 131104 | tf_op jit(solution)/shard_map/ppermute | solution.py:390
  50.7 1.7 %collective-permute-done.8.three_ref = f32[2,128,128]{2,1,0:T(8,128)S(1)} collective-permute-done((f32[2,128,128]{2,1,0:T(8,128)S(1)}, f32[2,128,128]{2,1,0:T(8,128)S(1)}, u32[]{:S(2)}, u32[]{:S(2)}) %collective-permute-start.8) | collective-permute-done | bytes 131104 | tf_op jit(solution)/shard_map/ppermute | solution.py:390
  52.4 1.1 %shard_map.88 = (f32[2,128,128]{2,1,0:T(8,128)S(1)}, f32[2,128,128]{2,1,0:T(8,128)S(1)}, f32[128,128]{1,0:T(8,128)S(1)}) custom-call(s32[2]{0:T(128)S(1)} %pad_add_fusion.1.bits_ref, f32[2,128,128]{2,1,0:T(8,128)S(1)} %get-tuple-element.64.own_ref, f32[2,128,128]{2,1,0:T(8,128)S(1)} %collective-permute-done.6.one_ref, ...), custom_call_target="tpu_custom_call" | custom-call | flops 1000000000 | bytes 1048576 | tf_op jit(solution)/shard_map/pallas_call | solution.py:304
  53.5 4.7 %collective-permute-start.9 = (f32[128,128]{1,0:T(8,128)S(1)}, f32[128,128]{1,0:T(8,128)S(1)}, u32[]{:S(2)}, u32[]{:S(2)}) collective-permute-start(f32[128,128]{1,0:T(8,128)S(1)} %slice_bitcast_fusion), channel_id=1, source_target_pairs={{0,16},{4,20},{8,24},{12,28},{1,17},{5,21},{9,25},{13,29},{2,18},{... | collective-permute-start | bytes 196616 | tf_op jit(solution)/shard_map/ppermute | solution.py:411
  58.2 1.5 %shard_map.87 = (f32[512,128]{1,0:T(8,128)S(1)}, f32[512,128]{1,0:T(8,128)S(1)}, f32[512,128]{1,0:T(8,128)S(1)}, f32[512,128]{1,0:T(8,128)S(1)}) custom-call(f32[272,640]{1,0:T(8,128)S(1)} %get-tuple-element.47.refs_0_, f32[256,128]{1,0:T(8,128)S(1)} %get-tuple-element.48.refs_1_, f32[256,128]{1,0:T(8,128)S(1)} %get-tuple-element.49.refs_2_, ...), custom_call_target="tpu_custom_call" | custom-call | flops 5000000000 | bytes 1048576 | tf_op jit(solution)/shard_map/pallas_call | solution.py:304
  61.1 0.9 %collective-permute-done.11.refs_1_ = f32[512,128]{1,0:T(8,128)S(1)} collective-permute-done((f32[512,128]{1,0:T(8,128)S(1)}, f32[512,128]{1,0:T(8,128)S(1)}, u32[]{:S(2)}, u32[]{:S(2)}) %collective-permute-start.11) | collective-permute-done | bytes 262176 | tf_op jit(solution)/shard_map/ppermute | solution.py:317
  62.0 1.5 %shard_map.90.refs_3_ = f32[512,512]{1,0:T(8,128)S(1)} custom-call(s32[4]{0:T(128)S(1)} %pad_add_fusion.index_ref, f32[512,128]{1,0:T(8,128)S(1)} %shard_map.89.refs_0_, f32[512,128]{1,0:T(8,128)S(1)} %collective-permute-done.11.refs_1_, bf16[512,1024]{1,0:T(8,128)(2,1)S(1)} %copy-done.11), custom_call_target="tpu_custom_call" | custom-call | flops 2000000000 | bytes 1048576 | tf_op jit(solution)/shard_map/pallas_call | solution.py:304
  63.5 5.7 %collective-permute-done.10.refs_0_ = f32[512,128]{1,0:T(8,128)S(1)} collective-permute-done((f32[512,128]{1,0:T(8,128)S(1)}, f32[512,128]{1,0:T(8,128)S(1)}, u32[]{:S(2)}, u32[]{:S(2)}) %collective-permute-start.10) | collective-permute-done | bytes 262176 | tf_op jit(solution)/shard_map/ppermute | solution.py:323
  69.2 1.5 %collective-permute-done.12.refs_1_ = f32[512,128]{1,0:T(8,128)S(1)} collective-permute-done((f32[512,128]{1,0:T(8,128)S(1)}, f32[512,128]{1,0:T(8,128)S(1)}, u32[]{:S(2)}, u32[]{:S(2)}) %collective-permute-start.12) | collective-permute-done | bytes 262176 | tf_op jit(solution)/shard_map/ppermute | solution.py:317
  70.8 2.5 %shard_map.91 = f32[512,512]{1,0:T(8,128)} custom-call(s32[4]{0:T(128)S(1)} %pad_add_fusion.index_ref, f32[512,128]{1,0:T(8,128)S(1)} %collective-permute-done.10.refs_0_, f32[512,128]{1,0:T(8,128)S(1)} %collective-permute-done.12.refs_1_, bf16[512,1024]{1,0:T(8,128)(2,1)S(1)} %copy-done.11, f32[512,512]{1,0:T(8,128)S(1)} %shard_map.90.refs_3_), custom_call_target="tpu_custom_call" | custom-call | flops 2000000000 | bytes 1048576 | tf_op jit(solution)/shard_map/pallas_call | solution.py:304
  (60 shorter events, 6.3 us)
Async XLA Ops:
  0.0 12.8 %collective-permute-start = (f32[512,512]{1,0:T(8,128)}, f32[512,512]{1,0:T(8,128)S(1)}, u32[]{:S(2)}, u32[]{:S(2)}) collective-permute-start(f32[512,512]{1,0:T(8,128)} %own_ref.1), channel_id=1, source_target_pairs={{0,1},{1,0},{2,3},{3,2},{4,5},{5,4},{6,7},{7,6},{8,9},{9,8},{10,11... | collective-permute-start | bytes 3145736 | tf_op jit(solution)/shard_map/ppermute | solution.py:317
  1.5 17.3 %collective-permute-start.2 = (f32[272,512]{1,0:T(8,128)S(1)}, f32[272,512]{1,0:T(8,128)S(1)}, u32[]{:S(2)}, u32[]{:S(2)}) collective-permute-start(f32[272,512]{1,0:T(8,128)S(1)} %slice.13), channel_id=1, source_target_pairs={{0,2},{1,3},{2,0},{3,1},{4,6},{5,7},{6,4},{7,5},{8,10},{9,11},{10,... | collective-permute-start | bytes 1671176 | tf_op jit(solution)/shard_map/ppermute | solution.py:323
  6.0 2.2 %copy-start.3 = (f32[2048,512]{1,0:T(8,128)S(1)}, f32[2048,512]{1,0:T(8,128)}, u32[]{:S(2)}) copy-start(f32[2048,512]{1,0:T(8,128)} %proj_ref.1) | copy-start | bytes 12582916
  8.2 1.2 %copy-start.4 = (f32[512,512]{1,0:T(8,128)S(1)}, f32[512,512]{1,0:T(8,128)}, u32[]{:S(2)}) copy-start(f32[512,512]{1,0:T(8,128)} %out_ref.1) | copy-start | bytes 3145732
  9.5 0.9 %copy-start.7 = (f32[2048,9]{0,1:T(8,128)S(1)}, f32[2048,9]{0,1:T(8,128)}, u32[]{:S(2)}) copy-start(f32[2048,9]{0,1:T(8,128)} %param.10) | copy-start | bytes 221188
  10.4 3.4 %copy-start.2 = (f32[512,512]{1,0:T(8,128)S(1)}, f32[512,512]{1,0:T(8,128)}, u32[]{:S(2)}) copy-start(f32[512,512]{1,0:T(8,128)} %own_ref.1) | copy-start | bytes 3145732
  11.8 1.0 %copy-start.10 = (bf16[512,1024]{1,0:T(8,128)(2,1)}, bf16[512,1024]{1,0:T(8,128)(2,1)S(1)}, u32[]{:S(2)}) copy-start(bf16[512,1024]{1,0:T(8,128)(2,1)S(1)} %get-tuple-element.68.refs_2_) | copy-start | bytes 3145732
  12.8 8.1 %copy-start = (bf16[2048,1280]{1,0:T(8,128)(2,1)}, bf16[2048,1280]{1,0:T(8,128)(2,1)S(1)}, u32[]{:S(2)}) copy-start(bf16[2048,1280]{1,0:T(8,128)(2,1)S(1)} %get-tuple-element.38.weight_ref.refs_3_) | copy-start | bytes 15728644
  12.8 1.0 %copy-start.5 = (f32[512,512]{1,0:T(8,128)}, f32[512,512]{1,0:T(8,128)S(1)}, u32[]{:S(2)}) copy-start(f32[512,512]{1,0:T(8,128)S(1)} %collective-permute-done.beside_ref) | copy-start | bytes 3145732
  13.8 2.0 %copy-start.6 = (f32[512,512]{1,0:T(8,128)S(1)}, f32[512,512]{1,0:T(8,128)}, u32[]{:S(2)}) copy-start(f32[512,512]{1,0:T(8,128)} %copy-done.5) | copy-start | bytes 3145732
  15.8 4.0 %copy-start.23 = (s32[512]{0:T(512)S(1)}, s32[512]{0:T(512)}, u32[]{:S(2)}) copy-start(s32[512]{0:T(512)} %param.13) | copy-start | bytes 6148
  15.8 4.0 %copy-start.22 = (f32[240,512]{1,0:T(8,128)S(1)}, f32[240,512]{1,0:T(8,128)}, u32[]{:S(2)}) copy-start(f32[240,512]{1,0:T(8,128)} %slice.12) | copy-start | bytes 1474564
  18.8 2.0 %collective-permute-start.3 = (f32[272,512]{1,0:T(8,128)S(1)}, f32[272,512]{1,0:T(8,128)S(1)}, u32[]{:S(2)}, u32[]{:S(2)}) collective-permute-start(f32[272,512]{1,0:T(8,128)S(1)} %collective-permute-done.2.refs_0_), channel_id=1, source_target_pairs={{0,1},{1,0},{2,3},{3,2},{4,5},{5,4},{6,7},{7,6},{8,9},{9,8},{10,11... | collective-permute-start | bytes 1671176 | tf_op jit(solution)/shard_map/ppermute | solution.py:317
  19.8 6.4 %copy-start.8 = (f32[4,384]{1,0:T(4,128)S(1)}, f32[4,384]{1,0:T(4,128)}, u32[]{:S(2)}) copy-start(f32[4,384]{1,0:T(4,128)} %refs_14_.1) | copy-start | bytes 18436
  19.8 13.5 %collective-permute-start.1 = (f32[240,512]{1,0:T(8,128)S(1)}, f32[240,512]{1,0:T(8,128)S(1)}, u32[]{:S(2)}, u32[]{:S(2)}) collective-permute-start(f32[240,512]{1,0:T(8,128)S(1)} %copy-done.22), channel_id=1, source_target_pairs={{0,2},{1,3},{2,0},{3,1},{4,6},{5,7},{6,4},{7,5},{8,10},{9,11},{10,... | collective-permute-start | bytes 1474568 | tf_op jit(solution)/shard_map/ppermute | solution.py:323
  22.8 10.5 %collective-permute-start.4 = (f32[16,384]{1,0:T(8,128)S(1)}, f32[16,384]{1,0:T(8,128)S(1)}, u32[]{:S(2)}, u32[]{:S(2)}) collective-permute-start(f32[16,384]{1,0:T(8,128)S(1)} %slice.16), channel_id=1, source_target_pairs={{0,4},{4,8},{8,12},{12,16},{16,20},{20,24},{24,28},{1,5},{5,9},{9,... | collective-permute-start | bytes 73736 | tf_op jit(solution)/shard_map/ppermute | solution.py:366
  33.3 1.9 %collective-permute-start.5 = (f32[240,512]{1,0:T(8,128)S(1)}, f32[240,512]{1,0:T(8,128)S(1)}, u32[]{:S(2)}, u32[]{:S(2)}) collective-permute-start(f32[240,512]{1,0:T(8,128)S(1)} %collective-permute-done.1.refs_0_), channel_id=1, source_target_pairs={{0,1},{1,0},{2,3},{3,2},{4,5},{5,4},{6,7},{7,6},{8,9},{9,8},{10,11... | collective-permute-start | bytes 1474568 | tf_op jit(solution)/shard_map/ppermute | solution.py:317
  35.2 2.5 %copy-start.1 = (bf16[2048,1280]{1,0:T(8,128)(2,1)S(1)}, bf16[2048,1280]{1,0:T(8,128)(2,1)}, u32[]{:S(2)}) copy-start(bf16[2048,1280]{1,0:T(8,128)(2,1)} %copy-done) | copy-start | bytes 15728644
  37.6 20.5 %copy-start.13 = (f32[256,128]{1,0:T(8,128)S(1)}, f32[256,128]{1,0:T(8,128)}, u32[]{:S(2)}) copy-start(f32[256,128]{1,0:T(8,128)} %copy-done.12) | copy-start | bytes 393220
  37.6 20.5 %copy-start.15 = (f32[256,128]{1,0:T(8,128)S(1)}, f32[256,128]{1,0:T(8,128)}, u32[]{:S(2)}) copy-start(f32[256,128]{1,0:T(8,128)} %copy-done.14) | copy-start | bytes 393220
  37.6 20.5 %copy-start.17 = (f32[256,128]{1,0:T(8,128)S(1)}, f32[256,128]{1,0:T(8,128)}, u32[]{:S(2)}) copy-start(f32[256,128]{1,0:T(8,128)} %copy-done.16) | copy-start | bytes 393220
  37.6 20.5 %copy-start.19 = (f32[256,128]{1,0:T(8,128)S(1)}, f32[256,128]{1,0:T(8,128)}, u32[]{:S(2)}) copy-start(f32[256,128]{1,0:T(8,128)} %copy-done.18) | copy-start | bytes 393220
  37.6 20.5 %copy-start.21 = (f32[256,128]{1,0:T(8,128)S(1)}, f32[256,128]{1,0:T(8,128)}, u32[]{:S(2)}) copy-start(f32[256,128]{1,0:T(8,128)} %copy-done.20) | copy-start | bytes 393220
  42.8 5.6 %collective-permute-start.6 = (f32[2,128,128]{2,1,0:T(8,128)S(1)}, f32[2,128,128]{2,1,0:T(8,128)S(1)}, u32[]{:S(2)}, u32[]{:S(2)}) collective-permute-start(f32[2,128,128]{2,1,0:T(8,128)S(1)} %get-tuple-element.64.own_ref), channel_id=1, source_target_pairs={{0,4},{4,0},{8,12},{12,8},{16,20},{20,16},{24,28},{28,24},{1,5},{5... | collective-permute-start | bytes 393224 | tf_op jit(solution)/shard_map/ppermute | solution.py:390
  44.3 6.4 %collective-permute-start.7 = (f32[2,128,128]{2,1,0:T(8,128)S(1)}, f32[2,128,128]{2,1,0:T(8,128)S(1)}, u32[]{:S(2)}, u32[]{:S(2)}) collective-permute-start(f32[2,128,128]{2,1,0:T(8,128)S(1)} %get-tuple-element.64.own_ref), channel_id=1, source_target_pairs={{0,8},{4,12},{8,0},{12,4},{16,24},{20,28},{24,16},{28,20},{1,9},{5... | collective-permute-start | bytes 393224 | tf_op jit(solution)/shard_map/ppermute | solution.py:390
  45.9 6.5 %collective-permute-start.8 = (f32[2,128,128]{2,1,0:T(8,128)S(1)}, f32[2,128,128]{2,1,0:T(8,128)S(1)}, u32[]{:S(2)}, u32[]{:S(2)}) collective-permute-start(f32[2,128,128]{2,1,0:T(8,128)S(1)} %get-tuple-element.64.own_ref), channel_id=1, source_target_pairs={{0,12},{4,8},{8,4},{12,0},{16,28},{20,24},{24,20},{28,16},{1,13},{... | collective-permute-start | bytes 393224 | tf_op jit(solution)/shard_map/ppermute | solution.py:390
  53.5 6.4 %collective-permute-start.9 = (f32[128,128]{1,0:T(8,128)S(1)}, f32[128,128]{1,0:T(8,128)S(1)}, u32[]{:S(2)}, u32[]{:S(2)}) collective-permute-start(f32[128,128]{1,0:T(8,128)S(1)} %slice_bitcast_fusion), channel_id=1, source_target_pairs={{0,16},{4,20},{8,24},{12,28},{1,17},{5,21},{9,25},{13,29},{2,18},{... | collective-permute-start | bytes 196616 | tf_op jit(solution)/shard_map/ppermute | solution.py:411
  58.2 1.7 %copy-start.9 = (f32[128]{0:T(128)S(1)}, f32[128]{0:T(128)}, u32[]{:S(2)}) copy-start(f32[128]{0:T(128)} %param.14) | copy-start | bytes 1540
  58.2 3.8 %copy-start.11 = (bf16[512,1024]{1,0:T(8,128)(2,1)S(1)}, bf16[512,1024]{1,0:T(8,128)(2,1)}, u32[]{:S(2)}) copy-start(bf16[512,1024]{1,0:T(8,128)(2,1)} %copy-done.10) | copy-start | bytes 3145732
  60.4 1.6 %collective-permute-start.11 = (f32[512,128]{1,0:T(8,128)S(1)}, f32[512,128]{1,0:T(8,128)S(1)}, u32[]{:S(2)}, u32[]{:S(2)}) collective-permute-start(f32[512,128]{1,0:T(8,128)S(1)} %shard_map.89.refs_0_), channel_id=1, source_target_pairs={{0,1},{1,0},{2,3},{3,2},{4,5},{5,4},{6,7},{7,6},{8,9},{9,8},{10,11... | collective-permute-start | bytes 786440 | tf_op jit(solution)/shard_map/ppermute | solution.py:317
  60.5 8.7 %collective-permute-start.10 = (f32[512,128]{1,0:T(8,128)S(1)}, f32[512,128]{1,0:T(8,128)S(1)}, u32[]{:S(2)}, u32[]{:S(2)}) collective-permute-start(f32[512,128]{1,0:T(8,128)S(1)} %shard_map.89.refs_0_), channel_id=1, source_target_pairs={{0,2},{1,3},{2,0},{3,1},{4,6},{5,7},{6,4},{7,5},{8,10},{9,11},{10,... | collective-permute-start | bytes 786440 | tf_op jit(solution)/shard_map/ppermute | solution.py:323
  69.2 1.5 %collective-permute-start.12 = (f32[512,128]{1,0:T(8,128)S(1)}, f32[512,128]{1,0:T(8,128)S(1)}, u32[]{:S(2)}, u32[]{:S(2)}) collective-permute-start(f32[512,128]{1,0:T(8,128)S(1)} %collective-permute-done.10.refs_0_), channel_id=1, source_target_pairs={{0,1},{1,0},{2,3},{3,2},{4,5},{5,4},{6,7},{7,6},{8,9},{9,8},{10,11... | collective-permute-start | bytes 786440 | tf_op jit(solution)/shard_map/ppermute | solution.py:317
  (5 other events, 3.3 us)

commit v4 on v3

--- a/solution.py
+++ b/solution.py
@@ -9,6 +9,7 @@
 
 CHUNK = 128
 RIM = 16
+VMEM_GRANT = 8 << 20
 F32 = jnp.float32
 BF16 = jnp.bfloat16
 
@@ -292,10 +293,22 @@
 
 def out_kernel(pieces, first, index_ref, *refs):
     weight_ref = refs[pieces]
-    total = refs[pieces + 1][...] if first else None
-    refs[-1][...] = add_products(
-        total, [ref[...] for ref in refs[:pieces]], index_ref, first, weight_ref
-    )
+    out_ref = refs[-1]
+    columns = out_ref.shape[1]
+    weights = []
+    for spot in range(pieces):
+        depth = refs[spot].shape[1]
+        rows = pl.ds(pl.multiple_of(index_ref[first + spot] * depth, depth), depth)
+        weights.append(weight_ref[rows, :])
+    weight = jnp.concatenate(weights, axis=0)
+    for base in range(0, out_ref.shape[0], CHUNK):
+        rows = slice(base, base + CHUNK)
+        parts = [halves(ref[rows, :]) for ref in refs[:pieces]]
+        high, low = (jnp.concatenate(part, axis=1) for part in zip(*parts))
+        both = jnp.dot(high, weight, preferred_element_type=F32)
+        rest = jnp.dot(low, weight[:, :columns], preferred_element_type=F32)
+        part = (both[:, :columns] + both[:, columns:]) + rest
+        out_ref[rows, :] = refs[pieces + 1][rows, :] + part if first else part
 
 
 def vmem_call(kernel, outs, scratch, cost, *args):
@@ -307,7 +320,7 @@
         in_specs=[small if arg.dtype == jnp.int32 else spec for arg in args],
         out_specs=jax.tree.map(lambda unused: spec, outs),
         scratch_shapes=scratch,
-        compiler_params=pltpu.CompilerParams(vmem_limit_bytes=40 << 20),
+        compiler_params=pltpu.CompilerParams(vmem_limit_bytes=VMEM_GRANT),
         cost_estimate=pl.CostEstimate(flops=int(cost * 1e9), bytes_accessed=1 << 20, transcendentals=0),
     )(*args)
 

time: 73.8 us -> 73.5 us (level)
  Pallas kernels: 21.8 us -> 21 us
where the time goes in v4:
time: 73.5 us; the launch traced here: 72.9 us
  Pallas kernels  21 us (29%)
  waiting for transfers between devices  17.7 us (24%)
  local copies, waits for them, and re-layouts  17.1 us (23%)
  starting transfers between devices  16 us (22%)
  between operations  0.92 us (1%)
    pallas_call x10, Pallas kernels, vmem_call(): pl.pallas_call(kernel, out_shape=outs, in_specs=[small if arg.dtype == jn...  21 us
    unnamed x48, local copies, waits for them, and re-layouts  14.1 us
    ppermute x3, waiting for transfers between devices, to_chips(): lax.ppermute(value, 'head', [(source, (source + 2 * step) % count) for so...  6.6 us
    ppermute x3, waiting for transfers between devices, shards(): lax.ppermute(pair, 'ctx', [(source, source ^ mask << bit) for source in r...  5.95 us
    ppermute x5, waiting for transfers between devices, to_sibling(): lax.ppermute(value, 'head', [(source, source ^ 1) for source in range(cou...  4.98 us
    ppermute x1, starting transfers between devices, shards(): lax.ppermute(pair[1], 'ctx', [(source, source + reach) for source in rang...  4.67 us
    ppermute x3, starting transfers between devices, to_chips(): lax.ppermute(value, 'head', [(source, (source + 2 * step) % count) for so...  3.56 us
    ppermute x3, starting transfers between devices, shards(): lax.ppermute(pair, 'ctx', [(source, source ^ mask << bit) for source in r...  3.55 us
  transfers between devices with their start and end apart: 13, of which 10 were waited for; matrix products, arithmetic and copies ran while one was open for 4% of the time, Pallas kernels for 17%

profile of v4, /device:TPU:0, one launch (start us, length us, event | category | flops | bytes accessed | tf_op | source)
XLA Modules:
  0.0 72.9 jit_solution(9601518925611593535)
XLA Ops:
  0.5 1.1 %slice.13 = f32[272,512]{1,0:T(8,128)S(1)} slice(f32[512,512]{1,0:T(8,128)} %own_ref.1), slice={[240:512], [0:512]} | slice | bytes 1114112 | tf_op jit(solution)/shard_map/slice | solution.py:362
  1.5 2.6 %collective-permute-start.2 = (f32[272,512]{1,0:T(8,128)S(1)}, f32[272,512]{1,0:T(8,128)S(1)}, u32[]{:S(2)}, u32[]{:S(2)}) collective-permute-start(f32[272,512]{1,0:T(8,128)S(1)} %slice.13), channel_id=1, source_target_pairs={{0,2},{1,3},{2,0},{3,1},{4,6},{5,7},{6,4},{7,5},{8,10},{9,11},{10,... | collective-permute-start | bytes 1671176 | tf_op jit(solution)/shard_map/ppermute | solution.py:336
  4.1 1.8 %slice.12 = f32[240,512]{1,0:T(8,128)} slice(f32[512,512]{1,0:T(8,128)} %own_ref.1), slice={[0:240], [0:512]} | slice | bytes 983040 | tf_op jit(solution)/shard_map/slice | solution.py:371
  6.1 2.2 %copy-done.3 = f32[2048,512]{1,0:T(8,128)S(1)} copy-done((f32[2048,512]{1,0:T(8,128)S(1)}, f32[2048,512]{1,0:T(8,128)}, u32[]{:S(2)}) %copy-start.3) | copy-done | bytes 4194328
  8.2 1.2 %copy-done.4 = f32[512,512]{1,0:T(8,128)S(1)} copy-done((f32[512,512]{1,0:T(8,128)S(1)}, f32[512,512]{1,0:T(8,128)}, u32[]{:S(2)}) %copy-start.4) | copy-done | bytes 1048600
  9.5 0.9 %copy-done.7 = f32[2048,9]{0,1:T(8,128)S(1)} copy-done((f32[2048,9]{0,1:T(8,128)S(1)}, f32[2048,9]{0,1:T(8,128)}, u32[]{:S(2)}) %copy-start.7) | copy-done | bytes 73752
  10.4 1.4 %shard_map.82 = (bf16[2048,1280]{1,0:T(8,128)(2,1)S(1)}, bf16[512,1024]{1,0:T(8,128)(2,1)S(1)}) custom-call(f32[2048,512]{1,0:T(8,128)S(1)} %copy-done.3, f32[9,2048]{1,0:T(8,128)S(1)} %bitcast.15, f32[512,512]{1,0:T(8,128)S(1)} %copy-done.4), custom_call_target="tpu_custom_call" | custom-call | flops 3000000000 | bytes 1048576 | tf_op jit(solution)/shard_map/pallas_call | solution.py:317
  11.8 1.0 %copy-done.10 = bf16[512,1024]{1,0:T(8,128)(2,1)} copy-done((bf16[512,1024]{1,0:T(8,128)(2,1)}, bf16[512,1024]{1,0:T(8,128)(2,1)S(1)}, u32[]{:S(2)}) %copy-start.10) | copy-done | bytes 1048600
  12.8 1.0 %copy-done.5 = f32[512,512]{1,0:T(8,128)} copy-done((f32[512,512]{1,0:T(8,128)}, f32[512,512]{1,0:T(8,128)S(1)}, u32[]{:S(2)}) %copy-start.5) | copy-done | bytes 1048600
  13.8 2.0 %copy-done.6 = f32[512,512]{1,0:T(8,128)S(1)} copy-done((f32[512,512]{1,0:T(8,128)S(1)}, f32[512,512]{1,0:T(8,128)}, u32[]{:S(2)}) %copy-start.6) | copy-done | bytes 1048600
  15.8 3.0 %shard_map.83.refs_2_ = f32[512,640]{1,0:T(8,128)S(1)} custom-call(s32[4]{0:T(128)S(1)} %pad_add_fusion.index_ref, f32[512,512]{1,0:T(8,128)S(1)} %copy-done.2, f32[512,512]{1,0:T(8,128)S(1)} %copy-done.6, bf16[2048,1280]{1,0:T(8,128)(2,1)S(1)} %get-tuple-element.38.weight_ref.refs_3_), custom_call_target="tpu_custom_call" | custom-call | flops 3000000000 | bytes 1048576 | tf_op jit(solution)/shard_map/pallas_call | solution.py:317
  20.2 0.7 collective-permute-done.3.refs_1_
  20.8 1.9 %shard_map.84.raw_ref.refs_5_.refs_7_ = f32[272,640]{1,0:T(8,128)S(1)} custom-call(s32[4]{0:T(128)S(1)} %pad_add_fusion.index_ref, f32[272,512]{1,0:T(8,128)S(1)} %collective-permute-done.2.refs_0_, f32[272,512]{1,0:T(8,128)S(1)} %collective-permute-done.3.refs_1_, f32[512,640]{1,0:T(8,128)S(1)} %shard_map.83.refs_2_, ...), custom_call_target="tpu_custom_call" | custom-call | flops 2000000000 | bytes 1048576 | tf_op jit(solution)/shard_map/pallas_call | solution.py:317
  22.8 3.4 %collective-permute-start.4 = (f32[16,384]{1,0:T(8,128)S(1)}, f32[16,384]{1,0:T(8,128)S(1)}, u32[]{:S(2)}, u32[]{:S(2)}) collective-permute-start(f32[16,384]{1,0:T(8,128)S(1)} %slice.16), channel_id=1, source_target_pairs={{0,4},{4,8},{8,12},{12,16},{16,20},{20,24},{24,28},{1,5},{5,9},{9,... | collective-permute-start | bytes 73736 | tf_op jit(solution)/shard_map/ppermute | solution.py:379
  26.2 3.3 %shard_map.85 = (f32[256,128]{1,0:T(8,128)S(1)}, f32[256,128]{1,0:T(8,128)S(1)}, f32[256,128]{1,0:T(8,128)S(1)}, f32[256,128]{1,0:T(8,128)S(1)}, f32[256,128]{1,...) custom-call(f32[272,640]{1,0:T(8,128)S(1)} %shard_map.84.raw_ref.refs_5_.refs_7_, ...), custom_call_target="tpu_custom_call" | custom-call | flops 4000000000 | bytes 1048576 | tf_op jit(solution)/shard_map/pallas_call | solution.py:317
  32.1 0.7 copy-done.20
  33.3 1.9 %collective-permute-done.5.refs_1_ = f32[240,512]{1,0:T(8,128)S(1)} collective-permute-done((f32[240,512]{1,0:T(8,128)S(1)}, f32[240,512]{1,0:T(8,128)S(1)}, u32[]{:S(2)}, u32[]{:S(2)}) %collective-permute-start.5) | collective-permute-done | bytes 491552 | tf_op jit(solution)/shard_map/ppermute | solution.py:330
  35.2 2.5 %copy-done.1 = bf16[2048,1280]{1,0:T(8,128)(2,1)S(1)} copy-done((bf16[2048,1280]{1,0:T(8,128)(2,1)S(1)}, bf16[2048,1280]{1,0:T(8,128)(2,1)}, u32[]{:S(2)}) %copy-start.1) | copy-done | bytes 5242904
  37.7 5.1 %shard_map.86 = (f32[272,640]{1,0:T(8,128)S(1)}, f32[256,128]{1,0:T(8,128)S(1)}, f32[256,128]{1,0:T(8,128)S(1)}, f32[256,128]{1,0:T(8,128)S(1)}, f32[256,128]{1,...) custom-call(s32[4]{0:T(128)S(1)} %pad_add_fusion.index_ref, ...), custom_call_target="tpu_custom_call" | custom-call | flops 5000000000 | bytes 1048576 | tf_op jit(solution)/shard_map/pallas_call | solution.py:317
  42.8 1.6 %collective-permute-start.6 = (f32[2,128,128]{2,1,0:T(8,128)S(1)}, f32[2,128,128]{2,1,0:T(8,128)S(1)}, u32[]{:S(2)}, u32[]{:S(2)}) collective-permute-start(f32[2,128,128]{2,1,0:T(8,128)S(1)} %get-tuple-element.64.own_ref), channel_id=1, source_target_pairs={{0,4},{4,0},{8,12},{12,8},{16,20},{20,16},{24,28},{28,24},{1,5},{5... | collective-permute-start | bytes 393224 | tf_op jit(solution)/shard_map/ppermute | solution.py:403
  44.3 1.6 %collective-permute-start.7 = (f32[2,128,128]{2,1,0:T(8,128)S(1)}, f32[2,128,128]{2,1,0:T(8,128)S(1)}, u32[]{:S(2)}, u32[]{:S(2)}) collective-permute-start(f32[2,128,128]{2,1,0:T(8,128)S(1)} %get-tuple-element.64.own_ref), channel_id=1, source_target_pairs={{0,8},{4,12},{8,0},{12,4},{16,24},{20,28},{24,16},{28,20},{1,9},{5... | collective-permute-start | bytes 393224 | tf_op jit(solution)/shard_map/ppermute | solution.py:403
  46.4 2.0 %collective-permute-done.6.one_ref = f32[2,128,128]{2,1,0:T(8,128)S(1)} collective-permute-done((f32[2,128,128]{2,1,0:T(8,128)S(1)}, f32[2,128,128]{2,1,0:T(8,128)S(1)}, u32[]{:S(2)}, u32[]{:S(2)}) %collective-permute-start.6) | collective-permute-done | bytes 131104 | tf_op jit(solution)/shard_map/ppermute | solution.py:403
  48.4 2.3 %collective-permute-done.7.two_ref = f32[2,128,128]{2,1,0:T(8,128)S(1)} collective-permute-done((f32[2,128,128]{2,1,0:T(8,128)S(1)}, f32[2,128,128]{2,1,0:T(8,128)S(1)}, u32[]{:S(2)}, u32[]{:S(2)}) %collective-permute-start.7) | collective-permute-done | bytes 131104 | tf_op jit(solution)/shard_map/ppermute | solution.py:403
  50.7 1.7 %collective-permute-done.8.three_ref = f32[2,128,128]{2,1,0:T(8,128)S(1)} collective-permute-done((f32[2,128,128]{2,1,0:T(8,128)S(1)}, f32[2,128,128]{2,1,0:T(8,128)S(1)}, u32[]{:S(2)}, u32[]{:S(2)}) %collective-permute-start.8) | collective-permute-done | bytes 131104 | tf_op jit(solution)/shard_map/ppermute | solution.py:403
  52.4 1.1 %shard_map.88 = (f32[2,128,128]{2,1,0:T(8,128)S(1)}, f32[2,128,128]{2,1,0:T(8,128)S(1)}, f32[128,128]{1,0:T(8,128)S(1)}) custom-call(s32[2]{0:T(128)S(1)} %pad_add_fusion.1.bits_ref, f32[2,128,128]{2,1,0:T(8,128)S(1)} %get-tuple-element.64.own_ref, f32[2,128,128]{2,1,0:T(8,128)S(1)} %collective-permute-done.6.one_ref, ...), custom_call_target="tpu_custom_call" | custom-call | flops 1000000000 | bytes 1048576 | tf_op jit(solution)/shard_map/pallas_call | solution.py:317
  53.5 4.7 %collective-permute-start.9 = (f32[128,128]{1,0:T(8,128)S(1)}, f32[128,128]{1,0:T(8,128)S(1)}, u32[]{:S(2)}, u32[]{:S(2)}) collective-permute-start(f32[128,128]{1,0:T(8,128)S(1)} %slice_bitcast_fusion), channel_id=1, source_target_pairs={{0,16},{4,20},{8,24},{12,28},{1,17},{5,21},{9,25},{13,29},{2,18},{... | collective-permute-start | bytes 196616 | tf_op jit(solution)/shard_map/ppermute | solution.py:424
  58.2 1.5 %shard_map.87 = (f32[512,128]{1,0:T(8,128)S(1)}, f32[512,128]{1,0:T(8,128)S(1)}, f32[512,128]{1,0:T(8,128)S(1)}, f32[512,128]{1,0:T(8,128)S(1)}) custom-call(f32[272,640]{1,0:T(8,128)S(1)} %get-tuple-element.47.refs_0_, f32[256,128]{1,0:T(8,128)S(1)} %get-tuple-element.48.refs_1_, f32[256,128]{1,0:T(8,128)S(1)} %get-tuple-element.49.refs_2_, ...), custom_call_target="tpu_custom_call" | custom-call | flops 5000000000 | bytes 1048576 | tf_op jit(solution)/shard_map/pallas_call | solution.py:317
  61.1 0.9 %collective-permute-done.11.refs_1_ = f32[512,128]{1,0:T(8,128)S(1)} collective-permute-done((f32[512,128]{1,0:T(8,128)S(1)}, f32[512,128]{1,0:T(8,128)S(1)}, u32[]{:S(2)}, u32[]{:S(2)}) %collective-permute-start.11) | collective-permute-done | bytes 262176 | tf_op jit(solution)/shard_map/ppermute | solution.py:330
  62.0 1.1 %shard_map.90.refs_3_ = f32[512,512]{1,0:T(8,128)S(1)} custom-call(s32[4]{0:T(128)S(1)} %pad_add_fusion.index_ref, f32[512,128]{1,0:T(8,128)S(1)} %shard_map.89.refs_0_, f32[512,128]{1,0:T(8,128)S(1)} %collective-permute-done.11.refs_1_, bf16[512,1024]{1,0:T(8,128)(2,1)S(1)} %copy-done.11), custom_call_target="tpu_custom_call" | custom-call | flops 2000000000 | bytes 1048576 | tf_op jit(solution)/shard_map/pallas_call | solution.py:317
  63.2 6.1 %collective-permute-done.10.refs_0_ = f32[512,128]{1,0:T(8,128)S(1)} collective-permute-done((f32[512,128]{1,0:T(8,128)S(1)}, f32[512,128]{1,0:T(8,128)S(1)}, u32[]{:S(2)}, u32[]{:S(2)}) %collective-permute-start.10) | collective-permute-done | bytes 262176 | tf_op jit(solution)/shard_map/ppermute | solution.py:336
  69.2 1.5 %collective-permute-done.12.refs_1_ = f32[512,128]{1,0:T(8,128)S(1)} collective-permute-done((f32[512,128]{1,0:T(8,128)S(1)}, f32[512,128]{1,0:T(8,128)S(1)}, u32[]{:S(2)}, u32[]{:S(2)}) %collective-permute-start.12) | collective-permute-done | bytes 262176 | tf_op jit(solution)/shard_map/ppermute | solution.py:330
  70.8 2.1 %shard_map.91 = f32[512,512]{1,0:T(8,128)} custom-call(s32[4]{0:T(128)S(1)} %pad_add_fusion.index_ref, f32[512,128]{1,0:T(8,128)S(1)} %collective-permute-done.10.refs_0_, f32[512,128]{1,0:T(8,128)S(1)} %collective-permute-done.12.refs_1_, bf16[512,1024]{1,0:T(8,128)(2,1)S(1)} %copy-done.11, f32[512,512]{1,0:T(8,128)S(1)} %shard_map.90.refs_3_), custom_call_target="tpu_custom_call" | custom-call | flops 2000000000 | bytes 1048576 | tf_op jit(solution)/shard_map/pallas_call | solution.py:317
  (60 shorter events, 6.3 us)
Async XLA Ops:
  0.0 12.8 %collective-permute-start = (f32[512,512]{1,0:T(8,128)}, f32[512,512]{1,0:T(8,128)S(1)}, u32[]{:S(2)}, u32[]{:S(2)}) collective-permute-start(f32[512,512]{1,0:T(8,128)} %own_ref.1), channel_id=1, source_target_pairs={{0,1},{1,0},{2,3},{3,2},{4,5},{5,4},{6,7},{7,6},{8,9},{9,8},{10,11... | collective-permute-start | bytes 3145736 | tf_op jit(solution)/shard_map/ppermute | solution.py:330
  1.5 17.3 %collective-permute-start.2 = (f32[272,512]{1,0:T(8,128)S(1)}, f32[272,512]{1,0:T(8,128)S(1)}, u32[]{:S(2)}, u32[]{:S(2)}) collective-permute-start(f32[272,512]{1,0:T(8,128)S(1)} %slice.13), channel_id=1, source_target_pairs={{0,2},{1,3},{2,0},{3,1},{4,6},{5,7},{6,4},{7,5},{8,10},{9,11},{10,... | collective-permute-start | bytes 1671176 | tf_op jit(solution)/shard_map/ppermute | solution.py:336
  6.0 2.2 %copy-start.3 = (f32[2048,512]{1,0:T(8,128)S(1)}, f32[2048,512]{1,0:T(8,128)}, u32[]{:S(2)}) copy-start(f32[2048,512]{1,0:T(8,128)} %proj_ref.1) | copy-start | bytes 12582916
  8.2 1.2 %copy-start.4 = (f32[512,512]{1,0:T(8,128)S(1)}, f32[512,512]{1,0:T(8,128)}, u32[]{:S(2)}) copy-start(f32[512,512]{1,0:T(8,128)} %out_ref.1) | copy-start | bytes 3145732
  9.5 0.9 %copy-start.7 = (f32[2048,9]{0,1:T(8,128)S(1)}, f32[2048,9]{0,1:T(8,128)}, u32[]{:S(2)}) copy-start(f32[2048,9]{0,1:T(8,128)} %param.10) | copy-start | bytes 221188
  10.4 3.4 %copy-start.2 = (f32[512,512]{1,0:T(8,128)S(1)}, f32[512,512]{1,0:T(8,128)}, u32[]{:S(2)}) copy-start(f32[512,512]{1,0:T(8,128)} %own_ref.1) | copy-start | bytes 3145732
  11.8 1.0 %copy-start.10 = (bf16[512,1024]{1,0:T(8,128)(2,1)}, bf16[512,1024]{1,0:T(8,128)(2,1)S(1)}, u32[]{:S(2)}) copy-start(bf16[512,1024]{1,0:T(8,128)(2,1)S(1)} %get-tuple-element.68.refs_2_) | copy-start | bytes 3145732
  12.8 8.1 %copy-start = (bf16[2048,1280]{1,0:T(8,128)(2,1)}, bf16[2048,1280]{1,0:T(8,128)(2,1)S(1)}, u32[]{:S(2)}) copy-start(bf16[2048,1280]{1,0:T(8,128)(2,1)S(1)} %get-tuple-element.38.weight_ref.refs_3_) | copy-start | bytes 15728644
  12.8 1.0 %copy-start.5 = (f32[512,512]{1,0:T(8,128)}, f32[512,512]{1,0:T(8,128)S(1)}, u32[]{:S(2)}) copy-start(f32[512,512]{1,0:T(8,128)S(1)} %collective-permute-done.beside_ref) | copy-start | bytes 3145732
  13.8 2.0 %copy-start.6 = (f32[512,512]{1,0:T(8,128)S(1)}, f32[512,512]{1,0:T(8,128)}, u32[]{:S(2)}) copy-start(f32[512,512]{1,0:T(8,128)} %copy-done.5) | copy-start | bytes 3145732
  15.8 4.0 %copy-start.23 = (s32[512]{0:T(512)S(1)}, s32[512]{0:T(512)}, u32[]{:S(2)}) copy-start(s32[512]{0:T(512)} %param.13) | copy-start | bytes 6148
  15.8 4.0 %copy-start.22 = (f32[240,512]{1,0:T(8,128)S(1)}, f32[240,512]{1,0:T(8,128)}, u32[]{:S(2)}) copy-start(f32[240,512]{1,0:T(8,128)} %slice.12) | copy-start | bytes 1474564
  18.8 2.0 %collective-permute-start.3 = (f32[272,512]{1,0:T(8,128)S(1)}, f32[272,512]{1,0:T(8,128)S(1)}, u32[]{:S(2)}, u32[]{:S(2)}) collective-permute-start(f32[272,512]{1,0:T(8,128)S(1)} %collective-permute-done.2.refs_0_), channel_id=1, source_target_pairs={{0,1},{1,0},{2,3},{3,2},{4,5},{5,4},{6,7},{7,6},{8,9},{9,8},{10,11... | collective-permute-start | bytes 1671176 | tf_op jit(solution)/shard_map/ppermute | solution.py:330
  19.8 6.4 %copy-start.8 = (f32[4,384]{1,0:T(4,128)S(1)}, f32[4,384]{1,0:T(4,128)}, u32[]{:S(2)}) copy-start(f32[4,384]{1,0:T(4,128)} %refs_14_.1) | copy-start | bytes 18436
  19.8 13.5 %collective-permute-start.1 = (f32[240,512]{1,0:T(8,128)S(1)}, f32[240,512]{1,0:T(8,128)S(1)}, u32[]{:S(2)}, u32[]{:S(2)}) collective-permute-start(f32[240,512]{1,0:T(8,128)S(1)} %copy-done.22), channel_id=1, source_target_pairs={{0,2},{1,3},{2,0},{3,1},{4,6},{5,7},{6,4},{7,5},{8,10},{9,11},{10,... | collective-permute-start | bytes 1474568 | tf_op jit(solution)/shard_map/ppermute | solution.py:336
  22.8 10.5 %collective-permute-start.4 = (f32[16,384]{1,0:T(8,128)S(1)}, f32[16,384]{1,0:T(8,128)S(1)}, u32[]{:S(2)}, u32[]{:S(2)}) collective-permute-start(f32[16,384]{1,0:T(8,128)S(1)} %slice.16), channel_id=1, source_target_pairs={{0,4},{4,8},{8,12},{12,16},{16,20},{20,24},{24,28},{1,5},{5,9},{9,... | collective-permute-start | bytes 73736 | tf_op jit(solution)/shard_map/ppermute | solution.py:379
  33.3 1.9 %collective-permute-start.5 = (f32[240,512]{1,0:T(8,128)S(1)}, f32[240,512]{1,0:T(8,128)S(1)}, u32[]{:S(2)}, u32[]{:S(2)}) collective-permute-start(f32[240,512]{1,0:T(8,128)S(1)} %collective-permute-done.1.refs_0_), channel_id=1, source_target_pairs={{0,1},{1,0},{2,3},{3,2},{4,5},{5,4},{6,7},{7,6},{8,9},{9,8},{10,11... | collective-permute-start | bytes 1474568 | tf_op jit(solution)/shard_map/ppermute | solution.py:330
  35.2 2.5 %copy-start.1 = (bf16[2048,1280]{1,0:T(8,128)(2,1)S(1)}, bf16[2048,1280]{1,0:T(8,128)(2,1)}, u32[]{:S(2)}) copy-start(bf16[2048,1280]{1,0:T(8,128)(2,1)} %copy-done) | copy-start | bytes 15728644
  37.6 20.5 %copy-start.13 = (f32[256,128]{1,0:T(8,128)S(1)}, f32[256,128]{1,0:T(8,128)}, u32[]{:S(2)}) copy-start(f32[256,128]{1,0:T(8,128)} %copy-done.12) | copy-start | bytes 393220
  37.6 20.5 %copy-start.15 = (f32[256,128]{1,0:T(8,128)S(1)}, f32[256,128]{1,0:T(8,128)}, u32[]{:S(2)}) copy-start(f32[256,128]{1,0:T(8,128)} %copy-done.14) | copy-start | bytes 393220
  37.6 20.5 %copy-start.17 = (f32[256,128]{1,0:T(8,128)S(1)}, f32[256,128]{1,0:T(8,128)}, u32[]{:S(2)}) copy-start(f32[256,128]{1,0:T(8,128)} %copy-done.16) | copy-start | bytes 393220
  37.6 20.5 %copy-start.19 = (f32[256,128]{1,0:T(8,128)S(1)}, f32[256,128]{1,0:T(8,128)}, u32[]{:S(2)}) copy-start(f32[256,128]{1,0:T(8,128)} %copy-done.18) | copy-start | bytes 393220
  37.6 20.5 %copy-start.21 = (f32[256,128]{1,0:T(8,128)S(1)}, f32[256,128]{1,0:T(8,128)}, u32[]{:S(2)}) copy-start(f32[256,128]{1,0:T(8,128)} %copy-done.20) | copy-start | bytes 393220
  42.8 5.6 %collective-permute-start.6 = (f32[2,128,128]{2,1,0:T(8,128)S(1)}, f32[2,128,128]{2,1,0:T(8,128)S(1)}, u32[]{:S(2)}, u32[]{:S(2)}) collective-permute-start(f32[2,128,128]{2,1,0:T(8,128)S(1)} %get-tuple-element.64.own_ref), channel_id=1, source_target_pairs={{0,4},{4,0},{8,12},{12,8},{16,20},{20,16},{24,28},{28,24},{1,5},{5... | collective-permute-start | bytes 393224 | tf_op jit(solution)/shard_map/ppermute | solution.py:403
  44.3 6.4 %collective-permute-start.7 = (f32[2,128,128]{2,1,0:T(8,128)S(1)}, f32[2,128,128]{2,1,0:T(8,128)S(1)}, u32[]{:S(2)}, u32[]{:S(2)}) collective-permute-start(f32[2,128,128]{2,1,0:T(8,128)S(1)} %get-tuple-element.64.own_ref), channel_id=1, source_target_pairs={{0,8},{4,12},{8,0},{12,4},{16,24},{20,28},{24,16},{28,20},{1,9},{5... | collective-permute-start | bytes 393224 | tf_op jit(solution)/shard_map/ppermute | solution.py:403
  45.9 6.5 %collective-permute-start.8 = (f32[2,128,128]{2,1,0:T(8,128)S(1)}, f32[2,128,128]{2,1,0:T(8,128)S(1)}, u32[]{:S(2)}, u32[]{:S(2)}) collective-permute-start(f32[2,128,128]{2,1,0:T(8,128)S(1)} %get-tuple-element.64.own_ref), channel_id=1, source_target_pairs={{0,12},{4,8},{8,4},{12,0},{16,28},{20,24},{24,20},{28,16},{1,13},{... | collective-permute-start | bytes 393224 | tf_op jit(solution)/shard_map/ppermute | solution.py:403
  53.5 6.4 %collective-permute-start.9 = (f32[128,128]{1,0:T(8,128)S(1)}, f32[128,128]{1,0:T(8,128)S(1)}, u32[]{:S(2)}, u32[]{:S(2)}) collective-permute-start(f32[128,128]{1,0:T(8,128)S(1)} %slice_bitcast_fusion), channel_id=1, source_target_pairs={{0,16},{4,20},{8,24},{12,28},{1,17},{5,21},{9,25},{13,29},{2,18},{... | collective-permute-start | bytes 196616 | tf_op jit(solution)/shard_map/ppermute | solution.py:424
  58.2 1.7 %copy-start.9 = (f32[128]{0:T(128)S(1)}, f32[128]{0:T(128)}, u32[]{:S(2)}) copy-start(f32[128]{0:T(128)} %param.14) | copy-start | bytes 1540
  58.2 3.8 %copy-start.11 = (bf16[512,1024]{1,0:T(8,128)(2,1)S(1)}, bf16[512,1024]{1,0:T(8,128)(2,1)}, u32[]{:S(2)}) copy-start(bf16[512,1024]{1,0:T(8,128)(2,1)} %copy-done.10) | copy-start | bytes 3145732
  60.4 1.6 %collective-permute-start.11 = (f32[512,128]{1,0:T(8,128)S(1)}, f32[512,128]{1,0:T(8,128)S(1)}, u32[]{:S(2)}, u32[]{:S(2)}) collective-permute-start(f32[512,128]{1,0:T(8,128)S(1)} %shard_map.89.refs_0_), channel_id=1, source_target_pairs={{0,1},{1,0},{2,3},{3,2},{4,5},{5,4},{6,7},{7,6},{8,9},{9,8},{10,11... | collective-permute-start | bytes 786440 | tf_op jit(solution)/shard_map/ppermute | solution.py:330
  60.5 8.7 %collective-permute-start.10 = (f32[512,128]{1,0:T(8,128)S(1)}, f32[512,128]{1,0:T(8,128)S(1)}, u32[]{:S(2)}, u32[]{:S(2)}) collective-permute-start(f32[512,128]{1,0:T(8,128)S(1)} %shard_map.89.refs_0_), channel_id=1, source_target_pairs={{0,2},{1,3},{2,0},{3,1},{4,6},{5,7},{6,4},{7,5},{8,10},{9,11},{10,... | collective-permute-start | bytes 786440 | tf_op jit(solution)/shard_map/ppermute | solution.py:336
  69.2 1.5 %collective-permute-start.12 = (f32[512,128]{1,0:T(8,128)S(1)}, f32[512,128]{1,0:T(8,128)S(1)}, u32[]{:S(2)}, u32[]{:S(2)}) collective-permute-start(f32[512,128]{1,0:T(8,128)S(1)} %collective-permute-done.10.refs_0_), channel_id=1, source_target_pairs={{0,1},{1,0},{2,3},{3,2},{4,5},{5,4},{6,7},{7,6},{8,9},{9,8},{10,11... | collective-permute-start | bytes 786440 | tf_op jit(solution)/shard_map/ppermute | solution.py:330
  (5 other events, 3.3 us)

commit v5 on v4

--- a/solution.py
+++ b/solution.py
@@ -9,7 +9,7 @@
 
 CHUNK = 128
 RIM = 16
-VMEM_GRANT = 8 << 20
+VMEM_GRANT = 16 << 20
 F32 = jnp.float32
 BF16 = jnp.bfloat16
 
@@ -70,31 +70,11 @@
     return inverses
 
 
-def prepare_kernel(proj_ref, mix_ref, out_ref, weight_ref, own_ref):
-    width = proj_ref.shape[1]
-    columns = weight_ref.shape[1] // 2
-    mixes = mix_ref.shape[0]
-    for base in range(0, proj_ref.shape[0], CHUNK):
-        rows = slice(base, base + CHUNK)
-        high, low = halves(proj_ref[rows, :])
-        weight_ref[rows, :width] = high
-        weight_ref[rows, columns : columns + width] = low
-        mixing = jnp.concatenate(
-            [mix_ref[:, rows], jnp.zeros((CHUNK - mixes, CHUNK), F32)], axis=0
-        )
-        high, low = halves(jnp.transpose(mixing))
-        weight_ref[rows, width:columns] = high
-        weight_ref[rows, columns + width :] = low
-    for base in range(0, out_ref.shape[0], CHUNK):
-        rows = slice(base, base + CHUNK)
-        own_ref[rows, :] = left_parts(out_ref[rows, :])
-
-
-def add_products(total, pieces, index_ref, first, weight_ref):
+def add_products(total, pieces, weight_ref, first):
     columns = weight_ref.shape[1] // 2
     for spot, piece in enumerate(pieces):
         depth = piece.shape[1]
-        rows = pl.ds(pl.multiple_of(index_ref[first + spot] * depth, depth), depth)
+        rows = slice((first + spot) * depth, (first + spot + 1) * depth)
         high, low = halves(piece)
         both = jnp.dot(high, weight_ref[rows, :], preferred_element_type=F32)
         rest = jnp.dot(low, weight_ref[rows, :columns], preferred_element_type=F32)
@@ -103,27 +83,70 @@
     return total
 
 
-def base_kernel(index_ref, own_ref, beside_ref, weight_ref, base_ref):
+def base_kernel(
+    index_ref, own_ref, beside_ref, mix_ref, proj_ref,
+    state_ref, query_ref, far_state_ref, far_query_ref, early_ref,
+    held, near_state, near_query, sems,
+):
+    sources, depth, across = held.shape
+    width = across // 4
+    copies = []
+    for source in range(sources):
+        rows = pl.ds(pl.multiple_of(index_ref[source] * depth, depth), depth)
+        copies.append(pltpu.make_async_copy(proj_ref.at[rows, :], held.at[source], sems.at[source]))
+        copies[-1].start()
+    early_ref[...] = own_ref[: early_ref.shape[0], :]
+    mixes = mix_ref.shape[0]
+
+    def split(source, state_out, query_out, base):
+        copies[source].wait()
+        lanes = pl.ds(pl.multiple_of(index_ref[source] * depth, depth), depth)
+        for begin in range(0, depth, CHUNK):
+            rows = slice(begin, begin + CHUNK)
+            out = slice(base + begin, base + begin + CHUNK)
+            value = held[source, rows, :]
+            mixing = mix_ref[:, lanes][:, rows]
+            mixing = jnp.concatenate([mixing, jnp.zeros((CHUNK - mixes, CHUNK), F32)], axis=0)
+            state = jnp.concatenate([value[:, width : 3 * width], jnp.transpose(mixing)], axis=1)
+            query = jnp.concatenate([value[:, :width], value[:, 3 * width :]], axis=1)
+            state_out[out, :] = left_parts(state)
+            query_out[out, :] = left_parts(query)
+
+    for source in range(2):
+        split(source, near_state, near_query, source * depth)
     half = own_ref.shape[0] // 2
     for rows in (slice(0, half), slice(half, 2 * half)):
-        base_ref[rows, :] = add_products(
-            None, [own_ref[rows, :], beside_ref[rows, :]], index_ref, 0, weight_ref
-        )
-
-
-def late_kernel(count, begin, index_ref, *refs):
-    base_ref, weight_ref, raw_ref = refs[count:]
-    raw_ref[...] = add_products(
-        base_ref[begin:, :], [ref[...] for ref in refs[:count]], index_ref, 2, weight_ref
-    )
-
-
-def convolve(raw, start, conv_ref, columns):
+        pieces = [own_ref[rows, :], beside_ref[rows, :]]
+        state_ref[rows, :] = add_products(None, pieces, near_state, 0)
+        query_ref[rows, :] = add_products(None, pieces, near_query, 0)
+    for source in range(2, sources):
+        split(source, far_state_ref, far_query_ref, (source - 2) * depth)
+
+
+def late_kernel(count, begin, *refs):
+    base_state, base_query, far_state, far_query, state_ref, query_ref, rim_ref = refs[count:]
+    pieces = [ref[...] for ref in refs[:count]]
+    width = base_query.shape[1] // 2
+    state_ref[...] = add_products(base_state[begin:, :], pieces, far_state, 0)
+    query_ref[...] = add_products(base_query[begin:, :], pieces, far_query, 0)
+    last = state_ref.shape[0] - RIM
+    rim_ref[:, :width] = query_ref[last:, :width]
+    rim_ref[:, width:] = state_ref[last:, : 2 * width]
+
+
+def partial_kernel(count, *refs):
+    base_state, far_state, out_ref = refs[count:]
+    out_ref[...] = add_products(
+        base_state[: out_ref.shape[0], :], [ref[...] for ref in refs[:count]], far_state, 0
+    )
+
+
+def convolve(raw, start, columns, conv_ref, taps_at):
     taps = conv_ref.shape[0]
     conv = 0.0
     for tap in range(taps):
         spot = start - taps + 1 + tap
-        conv = conv + conv_ref[tap : tap + 1, columns] * raw[spot : spot + CHUNK, columns]
+        conv = conv + conv_ref[tap : tap + 1, taps_at] * raw[spot : spot + CHUNK, columns]
     return conv * sigmoid(conv)
 
 
@@ -132,7 +155,7 @@
 
 
 def key_pass(raw, conv_ref, rate, doc_ref, first_chunk, outs, state):
-    key_ref, x_ref, y_ref, grid_ref, gamma_ref, chunk_ref, pair_ref = outs
+    key_ref, x_ref, y_ref, grid_ref, gamma_ref, plus_ref, chunk_ref, pair_ref = outs
     width = key_ref.shape[1]
     chunks = key_ref.shape[0] // CHUNK
     row = lax.broadcasted_iota(jnp.int32, (CHUNK, CHUNK), 0)
@@ -144,13 +167,16 @@
     for part in range(chunks):
         start = RIM + part * CHUNK
         rows = slice(part * CHUNK, (part + 1) * CHUNK)
-        keys.append(unit_rows(convolve(raw, start, conv_ref, slice(width, 2 * width))))
-        values.append(convolve(raw, start, conv_ref, slice(2 * width, 3 * width)))
-        mixing = raw[start : start + CHUNK, 4 * width :]
+        middle, last = slice(width, 2 * width), slice(2 * width, 3 * width)
+        keys.append(unit_rows(convolve(raw, start, slice(0, width), conv_ref, middle)))
+        values.append(convolve(raw, start, middle, conv_ref, last))
+        mixing = raw[start : start + CHUNK, last]
+        plus = softplus(mixing)
+        plus_ref[rows, :] = plus
         betas.append(sigmoid(mixing[:, 0:1]))
         spot = first_chunk + part
         docs = jnp.transpose(jnp.broadcast_to(doc_ref[spot : spot + 1, :], (CHUNK, CHUNK)))
-        steps = jnp.where(col == 1, -rate * softplus(mixing), jnp.where(col == 0, docs, 0.0))
+        steps = jnp.where(col == 1, -rate * plus, jnp.where(col == 0, docs, 0.0))
         sums = jnp.dot(tri, steps, precision=lax.Precision.HIGHEST, preferred_element_type=F32)
         across = jnp.transpose(sums)
         smooth, count = sums[:, 1:2], sums[:, 0:1]
@@ -200,38 +226,46 @@
     key_pass(raw_ref, conv_ref, rate_ref[0, 0], doc_ref, first_chunk, outs, None)
 
 
-def earlier_kernel(count, index_ref, *refs):
+def earlier_kernel(first, count, *refs):
     held, refs = refs[:count], refs[count:]
-    base_ref, weight_ref, rim_ref, next_ref, state_ref, conv_ref, rate_ref, doc_ref, raw = refs[:9]
+    part_ref, far_ref, rim_ref, next_ref, state_ref, conv_ref, rate_ref, doc_ref = refs[:8]
+    outs, raw = refs[8:-1], refs[-1]
+    rows, width = part_ref.shape[0], state_ref.shape[1]
+    raw[RIM : RIM + rows, :] = add_products(
+        part_ref[...], [ref[...] for ref in held], far_ref, first
+    )
+    raw[:RIM, : 2 * width] = rim_ref[:, width:]
+    raw[RIM + rows :, :] = next_ref[:RIM, :]
+    key_pass(raw, conv_ref, rate_ref[0, 0], doc_ref, 0, outs, (state_ref[0], state_ref[1]))
+
+
+def query_kernel(count, *refs):
+    held, refs = refs[:count], refs[count:]
+    base_ref, far_ref, rim_ref, next_ref, conv_ref = refs[:5]
+    fields = [(refs[5:11], 0), (refs[11:17], 1)]
+    carried_ref, local_ref, gate_ref, raw = refs[17:]
+    width = carried_ref.shape[1]
     rows = held[0].shape[0]
     raw[RIM : RIM + rows, :] = add_products(
-        base_ref[:rows, :], [ref[...] for ref in held], index_ref, 2, weight_ref
-    )
-    raw[:RIM, : rim_ref.shape[1]] = rim_ref[...]
+        base_ref[:rows, :], [ref[...] for ref in held], far_ref, 0
+    )
+    raw[:RIM, :width] = rim_ref[:, :width]
     raw[RIM + rows :, :] = next_ref[:RIM, :]
-    key_pass(
-        raw, conv_ref, rate_ref[0, 0], doc_ref, 0, refs[9:], (state_ref[0], state_ref[1])
-    )
-
-
-def query_kernel(pieces, *refs):
-    fields = [refs[7 * piece : 7 * piece + 7] for piece in range(pieces)]
-    conv_ref, carried_ref, local_ref, plus_ref, gate_ref = refs[7 * pieces :]
-    width = carried_ref.shape[1]
     row = lax.broadcasted_iota(jnp.int32, (CHUNK, CHUNK), 0)
     col = lax.broadcasted_iota(jnp.int32, (CHUNK, CHUNK), 1)
     state = None
     base = 0
-    for raw, key_ref, x_ref, y_ref, grid_ref, gamma_ref, chunk_ref in fields:
+    for (key_ref, x_ref, y_ref, grid_ref, gamma_ref, chunk_ref), later in fields:
+        source = next_ref if later else raw
         for part in range(key_ref.shape[0] // CHUNK):
             start = RIM + part * CHUNK
             rows = slice(part * CHUNK, (part + 1) * CHUNK)
             out = slice(base, base + CHUNK)
             base += CHUNK
-            query = unit_rows(convolve(raw, start, conv_ref, slice(0, width)))
-            gate = raw[start : start + CHUNK, 3 * width : 4 * width]
+            columns = slice(0, width)
+            query = unit_rows(convolve(source, start, columns, conv_ref, columns))
+            gate = source[start : start + CHUNK, width:]
             gate_ref[out, :] = gate * sigmoid(gate)
-            plus_ref[out, :] = softplus(raw[start : start + CHUNK, 4 * width :])
             overlap = product(query, jnp.transpose(key_ref[rows, :]))
             carried = gamma_ref[rows, :] * (
                 query - product(jnp.where(row >= col, overlap, 0.0), x_ref[rows, :])
@@ -276,14 +310,14 @@
     next_ref[...] = jnp.where(set_high, second[:, :width], carry)
 
 
-def mix_kernel(stages, single, carried_ref, local_ref, weight_ref, gate_ref, gain_ref, *refs):
+def mix_kernel(stages, single, carried_ref, local_ref, gate_ref, low_ref, high_ref, gain_ref, *refs):
     states = [ref[spot] for ref in refs[:stages] for spot in range(ref.shape[0])]
     if single:
         states.append(product(refs[stages][...], refs[stages + 1][...]))
     normed_ref = refs[-1]
     states = [right_parts(state) for state in states]
     carried = left_parts(carried_ref[...])
-    weights = weight_ref[...]
+    weights = jnp.concatenate([low_ref[...], high_ref[...]], axis=0)
     mixed = weights[:, 2:3] * local_ref[...]
     for level, state in enumerate(states):
         mixed = mixed + weights[:, level + 3 : level + 4] * parts_dot(carried, state)
@@ -293,32 +327,48 @@
 
 def out_kernel(pieces, first, index_ref, *refs):
     weight_ref = refs[pieces]
-    out_ref = refs[-1]
-    columns = out_ref.shape[1]
-    weights = []
+    parts = []
     for spot in range(pieces):
         depth = refs[spot].shape[1]
         rows = pl.ds(pl.multiple_of(index_ref[first + spot] * depth, depth), depth)
-        weights.append(weight_ref[rows, :])
-    weight = jnp.concatenate(weights, axis=0)
-    for base in range(0, out_ref.shape[0], CHUNK):
-        rows = slice(base, base + CHUNK)
+        parts.append(weight_ref[rows, :])
+    weight = left_parts(jnp.concatenate(parts, axis=0))
+    columns = weight.shape[1] // 2
+
+    def block(rows):
         parts = [halves(ref[rows, :]) for ref in refs[:pieces]]
         high, low = (jnp.concatenate(part, axis=1) for part in zip(*parts))
         both = jnp.dot(high, weight, preferred_element_type=F32)
         rest = jnp.dot(low, weight[:, :columns], preferred_element_type=F32)
-        part = (both[:, :columns] + both[:, columns:]) + rest
-        out_ref[rows, :] = refs[pieces + 1][rows, :] + part if first else part
-
-
-def vmem_call(kernel, outs, scratch, cost, *args):
+        return (both[:, :columns] + both[:, columns:]) + rest
+
+    blocks = [slice(base, base + CHUNK) for base in range(0, refs[0].shape[0], CHUNK)]
+    if not first:
+        for rows in blocks:
+            refs[-1][rows, :] = block(rows)
+        return
+    total_ref, out_ref, held, sems = refs[pieces + 1 :]
+    copies = []
+    for spot, rows in enumerate(blocks):
+        held[rows, :] = total_ref[rows, :] + block(rows)
+        copies.append(pltpu.make_async_copy(held.at[rows, :], out_ref.at[rows, :], sems.at[spot]))
+        copies[-1].start()
+    for copy in copies:
+        copy.wait()
+
+
+def vmem_call(kernel, outs, scratch, cost, *args, any_in=(), any_out=False):
     spec = pl.BlockSpec(memory_space=pltpu.VMEM)
     small = pl.BlockSpec(memory_space=pltpu.SMEM)
+    free = pl.BlockSpec(memory_space=pl.ANY)
     return pl.pallas_call(
         kernel,
         out_shape=outs,
-        in_specs=[small if arg.dtype == jnp.int32 else spec for arg in args],
-        out_specs=jax.tree.map(lambda unused: spec, outs),
+        in_specs=[
+            free if spot in any_in else small if arg.dtype == jnp.int32 else spec
+            for spot, arg in enumerate(args)
+        ],
+        out_specs=jax.tree.map(lambda unused: free if any_out else spec, outs),
         scratch_shapes=scratch,
         compiler_params=pltpu.CompilerParams(vmem_limit_bytes=VMEM_GRANT),
         cost_estimate=pl.CostEstimate(flops=int(cost * 1e9), bytes_accessed=1 << 20, transcendentals=0),
@@ -347,8 +397,7 @@
 def shards(tokens, w_proj, w_mix, conv_w, rates, doc_start, norm_gain, w_out):
     tok_rows, depth = tokens.shape
     width = w_proj.shape[1] // 4
-    features = w_proj.shape[0]
-    columns = 4 * width + CHUNK
+    state_columns, query_columns = 2 * width + CHUNK, 2 * width
     heads, me = lax.axis_size("head"), lax.axis_index("head")
     blocks, my_index = lax.axis_size("ctx"), lax.axis_index("ctx")
     remote = [(me + heads - 2 * step) % heads for step in range(1, heads // 2)]
@@ -356,48 +405,55 @@
     index = jnp.stack(order).astype(jnp.int32)
     count = heads - 2
     like = lambda *shape: jax.ShapeDtypeStruct(shape, F32)
+    parts = lambda *shape: jax.ShapeDtypeStruct(shape, BF16)
 
     half = tok_rows // 2
     cut = half - RIM
     late = to_chips(tokens[cut:])
     beside = to_sibling(tokens)
-    weight, own_weight = vmem_call(
-        prepare_kernel,
-        [jax.ShapeDtypeStruct((features, 2 * columns), BF16),
-         jax.ShapeDtypeStruct((w_out.shape[0], 2 * w_out.shape[1]), BF16)],
-        [], 3, w_proj, w_mix.T, w_out,
-    )
-    base = vmem_call(base_kernel, like(tok_rows, columns), [], 3, index, tokens, beside, weight)
-    early_rows, base = after(tokens[:cut], base)
+    base_state, base_query, far_state, far_query, early_rows = vmem_call(
+        base_kernel,
+        [like(tok_rows, state_columns), like(tok_rows, query_columns),
+         parts(count * depth, 2 * state_columns), parts(count * depth, 2 * query_columns),
+         like(cut, depth)],
+        [pltpu.VMEM((heads, depth, 4 * width), F32),
+         pltpu.VMEM((2 * depth, 2 * state_columns), BF16),
+         pltpu.VMEM((2 * depth, 2 * query_columns), BF16),
+         pltpu.SemaphoreType.DMA((heads,))],
+        3, index, tokens, beside, w_mix.T, w_proj, any_in=(4,),
+    )
     early = to_chips(early_rows)
-    late, base = after(late, base)
+    late, far_state = after(late, far_state)
     late_on = [to_sibling(value) for value in late]
-    raw_late = vmem_call(
-        functools.partial(late_kernel, count, cut), like(tok_rows - cut, columns), [], 2,
-        index, *late, *late_on, base, weight,
-    )
-    rim = lax.ppermute(
-        raw_late[tok_rows - cut - RIM :, : 3 * width], "ctx",
-        [(source, source + 1) for source in range(blocks - 1)],
-    )
+    late_state, late_query, rim = vmem_call(
+        functools.partial(late_kernel, count, cut),
+        [like(tok_rows - cut, state_columns), like(tok_rows - cut, query_columns),
+         like(RIM, 3 * width)],
+        [], 2, *late, *late_on, base_state, base_query, far_state, far_query,
+    )
+    rim = lax.ppermute(rim, "ctx", [(source, source + 1) for source in range(blocks - 1)])
     docs = doc_start.astype(F32).reshape(tok_rows // CHUNK, CHUNK)
     rate = rates[:, None]
-    outs = [like(half, width)] * 5 + [like(half // CHUNK, 2, width, width), like(2, width, width)]
+    outs = [like(half, width)] * 6 + [like(half // CHUNK, 2, width, width), like(2, width, width)]
     later = vmem_call(
-        functools.partial(later_kernel, half // CHUNK), outs, [], 4, raw_late, conv_w, rate, docs
-    )
-    early, pair_late, rim = after(early, later[6], rim)
+        functools.partial(later_kernel, half // CHUNK), outs, [], 4, late_state, conv_w, rate, docs
+    )
+    early, pair_late, rim = after(early, later[7], rim)
     early_on = [to_sibling(value) for value in early]
-    raw_early, *earlier = vmem_call(
-        functools.partial(earlier_kernel, count), [like(half + RIM, columns)] + outs, [], 5,
-        index, *early, *early_on, base, weight, rim, raw_late, pair_late, conv_w, rate, docs,
-    )
-
-    pair = earlier[6]
+    partial = vmem_call(
+        functools.partial(partial_kernel, len(early)), like(cut, state_columns), [], 1,
+        *early, base_state, far_state,
+    )
+    earlier = vmem_call(
+        functools.partial(earlier_kernel, len(early), len(early)), outs,
+        [pltpu.VMEM((half + RIM, state_columns), F32)], 5,
+        *early_on, partial, far_state, rim, late_state, pair_late, conv_w, rate, docs,
+    )
+
+    pair = earlier[7]
     carry = jnp.eye(width, dtype=F32)
     bits = blocks.bit_length() - 1
     levels = []
-    moved = None
     for bit in range(0, bits - 1, 2):
         others = [
             lax.ppermute(
@@ -413,8 +469,10 @@
         )
         levels.append(level)
     fields = vmem_call(
-        functools.partial(query_kernel, 2), [like(tok_rows, width)] * 4, [], 5,
-        raw_early, *earlier[:6], raw_late, *later[:6], conv_w,
+        functools.partial(query_kernel, count), [like(tok_rows, width)] * 3,
+        [pltpu.VMEM((half + RIM, query_columns), F32)], 5,
+        *early, *early_on, base_query, far_query, rim, late_query, conv_w,
+        *earlier[:5], earlier[6], *later[:5], later[6],
     )
     single = []
     if bits % 2:
@@ -425,19 +483,20 @@
         ]
     normed = vmem_call(
         functools.partial(mix_kernel, len(levels), bool(single)), like(tok_rows, width), [], 1,
-        *fields, norm_gain[None, :], *levels, *single,
+        *fields, earlier[5], later[5], norm_gain[None, :], *levels, *single,
     )
     far = to_chips(normed)
     near = to_sibling(normed)
     out_shape = like(tok_rows, w_out.shape[1])
     total = vmem_call(
-        functools.partial(out_kernel, 2, 0), out_shape, [], 2, index, normed, near, own_weight
+        functools.partial(out_kernel, 2, 0), out_shape, [], 2, index, normed, near, w_out
     )
     far, total = after(far, total)
     far_on = [to_sibling(value) for value in far]
     return vmem_call(
-        functools.partial(out_kernel, count, 2), out_shape, [], 2,
-        index, *far, *far_on, own_weight, total,
+        functools.partial(out_kernel, count, 2), out_shape,
+        [pltpu.VMEM(out_shape.shape, F32), pltpu.SemaphoreType.DMA((tok_rows // CHUNK,))], 2,
+        index, *far, *far_on, w_out, total, any_out=True,
     )
 
 

time: 73.5 us -> 73.4 us (level)
  local copies, waits for them, and re-layouts: 17.1 us -> 14.6 us
  starting transfers between devices: 16 us -> 17.8 us
  waiting for transfers between devices: 17.7 us -> 19.2 us
  Pallas kernels: 21 us -> 20.1 us
    ppermute x3, waiting for transfers between devices: 6.6 us -> 11.1 us  [to_chips(): lax.ppermute(value, 'head', [(source, (source + 2 * step) % count) for so...]
    ppermute x5, waiting for transfers between devices: 4.98 us -> 2 us  [to_sibling(): lax.ppermute(value, 'head', [(source, source ^ 1) for source in range(cou...]
    ppermute x3, starting transfers between devices: 3.56 us -> 5.61 us  [to_chips(): lax.ppermute(value, 'head', [(source, (source + 2 * step) % count) for so...]
    slice x2 -> x0, local copies, waits for them, and re-layouts: 1.85 us -> none  [the longest x1 1.84 us: shards(): early_rows, base = after(tokens[:cut], base)]
    unnamed x48 -> x62, local copies, waits for them, and re-layouts: 14.1 us -> 12.7 us
    pallas_call x10, Pallas kernels: 21 us -> 20.1 us  [vmem_call(): pl.pallas_call(kernel, out_shape=outs, in_specs=[free if spot in any_in e...]
    slice x1, local copies, waits for them, and re-layouts: 1.09 us -> 1.89 us  [shards(): late = to_chips(tokens[cut:])]
  transfers between devices with their start and end apart: 13 -> 13, of which waited for: 10 -> 8; matrix products, arithmetic and copies ran while one was open for 4% -> 3% of each run, Pallas kernels for 17% -> 17%
where the time goes in v5:
time: 73.4 us; the launch traced here: 73 us
  Pallas kernels  20.1 us (27%)
  waiting for transfers between devices  19.2 us (26%)
  starting transfers between devices  17.8 us (24%)
  local copies, waits for them, and re-layouts  14.6 us (20%)
  between operations  1.21 us (2%)
    pallas_call x10, Pallas kernels, vmem_call(): pl.pallas_call(kernel, out_shape=outs, in_specs=[free if spot in any_in e...  20.1 us
    unnamed x62, local copies, waits for them, and re-layouts  12.7 us
    ppermute x3, waiting for transfers between devices, to_chips(): lax.ppermute(value, 'head', [(source, (source + 2 * step) % count) for so...  11.1 us
    ppermute x3, waiting for transfers between devices, shards(): lax.ppermute(pair, 'ctx', [(source, source ^ mask << bit) for source in r...  6.1 us
    ppermute x3, starting transfers between devices, to_chips(): lax.ppermute(value, 'head', [(source, (source + 2 * step) % count) for so...  5.61 us
    ppermute x1, starting transfers between devices, shards(): lax.ppermute(pair[1], 'ctx', [(source, source + reach) for source in rang...  4.68 us
    ppermute x3, starting transfers between devices, shards(): lax.ppermute(pair, 'ctx', [(source, source ^ mask << bit) for source in r...  3.55 us
    ppermute x1, starting transfers between devices, shards(): lax.ppermute(rim, 'ctx', [(source, source + 1) for source in range(blocks...  3.4 us
  transfers between devices with their start and end apart: 13, of which 8 were waited for; matrix products, arithmetic and copies ran while one was open for 3% of the time, Pallas kernels for 17%

profile of v5, /device:TPU:0, one launch (start us, length us, event | category | flops | bytes accessed | tf_op | source)
XLA Modules:
  0.0 73.0 jit_solution(6212970388730009235)
XLA Ops:
  0.5 1.9 %slice.6 = f32[272,512]{1,0:T(8,128)} slice(f32[512,512]{1,0:T(8,128)} %own_ref.1), slice={[240:512], [0:512]} | slice | bytes 1114112 | tf_op jit(solution)/shard_map/slice | solution.py:412
  2.3 2.5 %collective-permute-start.2 = (f32[272,512]{1,0:T(8,128)}, f32[272,512]{1,0:T(8,128)S(1)}, u32[]{:S(2)}, u32[]{:S(2)}) collective-permute-start(f32[272,512]{1,0:T(8,128)} %slice.6), channel_id=1, source_target_pairs={{0,2},{1,3},{2,0},{3,1},{4,6},{5,7},{6,4},{7,5},{8,10},{9,11},{10,... | collective-permute-start | bytes 1671176 | tf_op jit(solution)/shard_map/ppermute | solution.py:386
  4.9 1.2 %copy-done = f32[512,512]{1,0:T(8,128)S(1)} copy-done((f32[512,512]{1,0:T(8,128)S(1)}, f32[512,512]{1,0:T(8,128)}, u32[]{:S(2)}) %copy-start) | copy-done | bytes 1048600
  6.2 2.2 %copy-done.1 = f32[2048,512]{1,0:T(8,128)S(1)} copy-done((f32[2048,512]{1,0:T(8,128)S(1)}, f32[2048,512]{1,0:T(8,128)}, u32[]{:S(2)}) %copy-start.1) | copy-done | bytes 4194328
  8.4 0.9 %copy-done.3 = f32[2048,9]{0,1:T(8,128)S(1)} copy-done((f32[2048,9]{0,1:T(8,128)S(1)}, f32[2048,9]{0,1:T(8,128)}, u32[]{:S(2)}) %copy-start.3) | copy-done | bytes 73752
  9.3 4.0 %shard_map.82 = (f32[512,384]{1,0:T(8,128)S(1)}, f32[512,256]{1,0:T(8,128)S(1)}, bf16[1024,768]{1,0:T(8,128)(2,1)S(1)}, bf16[1024,512]{1,0:T(8,128)(2,1)S(1)}, f32[240,512]{1,0:T(8,128)S(1)}) custom-call(s32[4]{0:T(128)S(1)} %pad_add_fusion.index_ref, f32[512,512]{1,0:T(8,128)S(1)} %copy-done, f32[512,512]{1,0:T(8,128)S(1)} %collective-permute-done.beside_ref, ...), custom_call_target="tpu_custom_call" | custom-call | flops 3000000000 | bytes 1048576 | tf_op jit(solution)/shard_map/pallas_call | solution.py:364
  13.3 5.0 %collective-permute-done.2.refs_0_ = f32[272,512]{1,0:T(8,128)S(1)} collective-permute-done((f32[272,512]{1,0:T(8,128)}, f32[272,512]{1,0:T(8,128)S(1)}, u32[]{:S(2)}, u32[]{:S(2)}) %collective-permute-start.2) | collective-permute-done | bytes 557088 | tf_op jit(solution)/shard_map/ppermute | solution.py:386
  19.0 1.8 %collective-permute-start.1 = (f32[240,512]{1,0:T(8,128)S(1)}, f32[240,512]{1,0:T(8,128)S(1)}, u32[]{:S(2)}, u32[]{:S(2)}) collective-permute-start(f32[240,512]{1,0:T(8,128)S(1)} %get-tuple-element.42), channel_id=1, source_target_pairs={{0,2},{1,3},{2,0},{3,1},{4,6},{5,7},{6,4},{7,5},{8,10},{9,11},{10,... | collective-permute-start | bytes 1474568 | tf_op jit(solution)/shard_map/ppermute | solution.py:386
  20.9 1.4 %shard_map.83 = (f32[272,384]{1,0:T(8,128)S(1)}, f32[272,256]{1,0:T(8,128)S(1)}, f32[16,384]{1,0:T(8,128)S(1)}) custom-call(f32[272,512]{1,0:T(8,128)S(1)} %collective-permute-done.2.refs_0_, f32[272,512]{1,0:T(8,128)S(1)} %collective-permute-done.3.refs_1_, f32[512,384]{1,0:T(8,128)S(1)} %get-tuple-element.45.refs_2_.refs_1_, ...), custom_call_target="tpu_custom_call" | custom-call | flops 2000000000 | bytes 1048576 | tf_op jit(solution)/shard_map/pallas_call | solution.py:364
  22.3 3.4 %collective-permute-start.4 = (f32[16,384]{1,0:T(8,128)S(1)}, f32[16,384]{1,0:T(8,128)S(1)}, u32[]{:S(2)}, u32[]{:S(2)}) collective-permute-start(f32[16,384]{1,0:T(8,128)S(1)} %get-tuple-element.51), channel_id=1, source_target_pairs={{0,4},{4,8},{8,12},{12,16},{16,20},{20,24},{24,28},{1,5},{5,9},{9,... | collective-permute-start | bytes 73736 | tf_op jit(solution)/shard_map/ppermute | solution.py:434
  25.7 3.3 %shard_map.84 = (f32[256,128]{1,0:T(8,128)S(1)}, f32[256,128]{1,0:T(8,128)S(1)}, f32[256,128]{1,0:T(8,128)S(1)}, f32[256,128]{1,0:T(8,128)S(1)}, f32[256,128]{1,...) custom-call(f32[272,384]{1,0:T(8,128)S(1)} %get-tuple-element.49.raw_ref.refs_4_,, ...), custom_call_target="tpu_custom_call" | custom-call | flops 4000000000 | bytes 1048576 | tf_op jit(solution)/shard_map/pallas_call | solution.py:364
  29.7 0.7 copy-done.16
  30.4 0.7 copy-done.18
  31.0 0.7 copy-done.20
  33.0 0.6 copy-done.26
  34.3 1.1 %copy-done.7 = f32[512,384]{1,0:T(8,128)S(1)} copy-done((f32[512,384]{1,0:T(8,128)S(1)}, f32[512,384]{1,0:T(8,128)}, u32[]{:S(2)}) %copy-start.7) | copy-done | bytes 786456
  36.1 1.0 %copy-done.13 = f32[272,384]{1,0:T(8,128)S(1)} copy-done((f32[272,384]{1,0:T(8,128)S(1)}, f32[272,384]{1,0:T(8,128)}, u32[]{:S(2)}) %copy-start.13) | copy-done | bytes 417816
  37.1 0.9 %copy-done.29 = f32[2,128,128]{2,1,0:T(8,128)S(1)} copy-done((f32[2,128,128]{2,1,0:T(8,128)S(1)}, f32[2,128,128]{2,1,0:T(8,128)}, u32[]{:S(2)}) %copy-start.29) | copy-done | bytes 131096
  38.1 3.8 %shard_map.86 = (f32[256,128]{1,0:T(8,128)S(1)}, f32[256,128]{1,0:T(8,128)S(1)}, f32[256,128]{1,0:T(8,128)S(1)}, f32[256,128]{1,0:T(8,128)S(1)}, f32[256,128]{1,...) custom-call(f32[240,512]{1,0:T(8,128)S(1)} %collective-permute-done.5.refs_0_.ref, ...), custom_call_target="tpu_custom_call" | custom-call | flops 5000000000 | bytes 1048576 | tf_op jit(solution)/shard_map/pallas_call | solution.py:364
  41.9 1.6 %collective-permute-start.6 = (f32[2,128,128]{2,1,0:T(8,128)S(1)}, f32[2,128,128]{2,1,0:T(8,128)S(1)}, u32[]{:S(2)}, u32[]{:S(2)}) collective-permute-start(f32[2,128,128]{2,1,0:T(8,128)S(1)} %get-tuple-element.73.own_ref), channel_id=1, source_target_pairs={{0,4},{4,0},{8,12},{12,8},{16,20},{20,16},{24,28},{28,24},{1,5},{5... | collective-permute-start | bytes 393224 | tf_op jit(solution)/shard_map/ppermute | solution.py:459
  43.5 1.6 %collective-permute-start.7 = (f32[2,128,128]{2,1,0:T(8,128)S(1)}, f32[2,128,128]{2,1,0:T(8,128)S(1)}, u32[]{:S(2)}, u32[]{:S(2)}) collective-permute-start(f32[2,128,128]{2,1,0:T(8,128)S(1)} %get-tuple-element.73.own_ref), channel_id=1, source_target_pairs={{0,8},{4,12},{8,0},{12,4},{16,24},{20,28},{24,16},{28,20},{1,9},{5... | collective-permute-start | bytes 393224 | tf_op jit(solution)/shard_map/ppermute | solution.py:459
  45.6 2.1 %collective-permute-done.6.one_ref = f32[2,128,128]{2,1,0:T(8,128)S(1)} collective-permute-done((f32[2,128,128]{2,1,0:T(8,128)S(1)}, f32[2,128,128]{2,1,0:T(8,128)S(1)}, u32[]{:S(2)}, u32[]{:S(2)}) %collective-permute-start.6) | collective-permute-done | bytes 131104 | tf_op jit(solution)/shard_map/ppermute | solution.py:459
  47.7 2.2 %collective-permute-done.7.two_ref = f32[2,128,128]{2,1,0:T(8,128)S(1)} collective-permute-done((f32[2,128,128]{2,1,0:T(8,128)S(1)}, f32[2,128,128]{2,1,0:T(8,128)S(1)}, u32[]{:S(2)}, u32[]{:S(2)}) %collective-permute-start.7) | collective-permute-done | bytes 131104 | tf_op jit(solution)/shard_map/ppermute | solution.py:459
  49.9 1.8 %collective-permute-done.8.three_ref = f32[2,128,128]{2,1,0:T(8,128)S(1)} collective-permute-done((f32[2,128,128]{2,1,0:T(8,128)S(1)}, f32[2,128,128]{2,1,0:T(8,128)S(1)}, u32[]{:S(2)}, u32[]{:S(2)}) %collective-permute-start.8) | collective-permute-done | bytes 131104 | tf_op jit(solution)/shard_map/ppermute | solution.py:459
  51.7 1.1 %shard_map.88 = (f32[2,128,128]{2,1,0:T(8,128)S(1)}, f32[2,128,128]{2,1,0:T(8,128)S(1)}, f32[128,128]{1,0:T(8,128)S(1)}) custom-call(s32[2]{0:T(128)S(1)} %pad_add_fusion.1.bits_ref, f32[2,128,128]{2,1,0:T(8,128)S(1)} %get-tuple-element.73.own_ref, f32[2,128,128]{2,1,0:T(8,128)S(1)} %collective-permute-done.6.one_ref, ...), custom_call_target="tpu_custom_call" | custom-call | flops 1000000000 | bytes 1048576 | tf_op jit(solution)/shard_map/pallas_call | solution.py:364
  52.7 4.7 %collective-permute-start.9 = (f32[128,128]{1,0:T(8,128)S(1)}, f32[128,128]{1,0:T(8,128)S(1)}, u32[]{:S(2)}, u32[]{:S(2)}) collective-permute-start(f32[128,128]{1,0:T(8,128)S(1)} %slice_bitcast_fusion), channel_id=1, source_target_pairs={{0,16},{4,20},{8,24},{12,28},{1,17},{5,21},{9,25},{13,29},{2,18},{... | collective-permute-start | bytes 196616 | tf_op jit(solution)/shard_map/ppermute | solution.py:482
  57.5 2.4 %shard_map.87 = (f32[512,128]{1,0:T(8,128)S(1)}, f32[512,128]{1,0:T(8,128)S(1)}, f32[512,128]{1,0:T(8,128)S(1)}) custom-call(f32[240,512]{1,0:T(8,128)S(1)} %collective-permute-done.1.refs_0_, f32[240,512]{1,0:T(8,128)S(1)} %collective-permute-done.5.refs_0_.refs_1_, f32[512,256]{1,0:T(8,128)S(1)} %copy-done.11, bf16[1024,512]{1,0:T(8,128)(2,1)S(1)} %copy-done.9, ...), custom_call_target="tpu_custom_call" | custom-call | flops 5000000000 | bytes 1048576 | tf_op jit(solution)/shard_map/pallas_call | solution.py:364
  60.6 1.3 %collective-permute-start.10 = (f32[512,128]{1,0:T(8,128)S(1)}, f32[512,128]{1,0:T(8,128)S(1)}, u32[]{:S(2)}, u32[]{:S(2)}) collective-permute-start(f32[512,128]{1,0:T(8,128)S(1)} %shard_map.89.refs_0_), channel_id=1, source_target_pairs={{0,2},{1,3},{2,0},{3,1},{4,6},{5,7},{6,4},{7,5},{8,10},{9,11},{10,... | collective-permute-start | bytes 786440 | tf_op jit(solution)/shard_map/ppermute | solution.py:386
  62.2 1.2 %shard_map.90.refs_3_ = f32[512,512]{1,0:T(8,128)S(1)} custom-call(s32[4]{0:T(128)S(1)} %pad_add_fusion.index_ref, f32[512,128]{1,0:T(8,128)S(1)} %shard_map.89.refs_0_, f32[512,128]{1,0:T(8,128)S(1)} %collective-permute-done.11.refs_1_, f32[512,512]{1,0:T(8,128)S(1)} %copy-done.2), custom_call_target="tpu_custom_call" | custom-call | flops 2000000000 | bytes 1048576 | tf_op jit(solution)/shard_map/pallas_call | solution.py:364
  63.3 6.0 %collective-permute-done.10.refs_0_ = f32[512,128]{1,0:T(8,128)S(1)} collective-permute-done((f32[512,128]{1,0:T(8,128)S(1)}, f32[512,128]{1,0:T(8,128)S(1)}, u32[]{:S(2)}, u32[]{:S(2)}) %collective-permute-start.10) | collective-permute-done | bytes 262176 | tf_op jit(solution)/shard_map/ppermute | solution.py:386
  69.4 1.5 %collective-permute-done.12.refs_1_ = f32[512,128]{1,0:T(8,128)S(1)} collective-permute-done((f32[512,128]{1,0:T(8,128)S(1)}, f32[512,128]{1,0:T(8,128)S(1)}, u32[]{:S(2)}, u32[]{:S(2)}) %collective-permute-start.12) | collective-permute-done | bytes 262176 | tf_op jit(solution)/shard_map/ppermute | solution.py:380
  70.9 1.9 %shard_map.91 = f32[512,512]{1,0:T(8,128)} custom-call(s32[4]{0:T(128)S(1)} %pad_add_fusion.index_ref, f32[512,128]{1,0:T(8,128)S(1)} %collective-permute-done.10.refs_0_, f32[512,128]{1,0:T(8,128)S(1)} %collective-permute-done.12.refs_1_, f32[512,512]{1,0:T(8,128)S(1)} %copy-done.2, f32[512,512]{1,0:T(8,128)S(1)} %shard_map.90.refs_3_), custom_call_target="tpu_custom_call" | custom-call | flops 2000000000 | bytes 1048576 | tf_op jit(solution)/shard_map/pallas_call | solution.py:364
  (72 shorter events, 5.3 us)
Async XLA Ops:
  0.0 4.9 %collective-permute-start = (f32[512,512]{1,0:T(8,128)}, f32[512,512]{1,0:T(8,128)S(1)}, u32[]{:S(2)}, u32[]{:S(2)}) collective-permute-start(f32[512,512]{1,0:T(8,128)} %own_ref.1), channel_id=1, source_target_pairs={{0,1},{1,0},{2,3},{3,2},{4,5},{5,4},{6,7},{7,6},{8,9},{9,8},{10,11... | collective-permute-start | bytes 3145736 | tf_op jit(solution)/shard_map/ppermute | solution.py:380
  2.3 16.0 %collective-permute-start.2 = (f32[272,512]{1,0:T(8,128)}, f32[272,512]{1,0:T(8,128)S(1)}, u32[]{:S(2)}, u32[]{:S(2)}) collective-permute-start(f32[272,512]{1,0:T(8,128)} %slice.6), channel_id=1, source_target_pairs={{0,2},{1,3},{2,0},{3,1},{4,6},{5,7},{6,4},{7,5},{8,10},{9,11},{10,... | collective-permute-start | bytes 1671176 | tf_op jit(solution)/shard_map/ppermute | solution.py:386
  4.9 1.2 %copy-start = (f32[512,512]{1,0:T(8,128)S(1)}, f32[512,512]{1,0:T(8,128)}, u32[]{:S(2)}) copy-start(f32[512,512]{1,0:T(8,128)} %own_ref.1) | copy-start | bytes 3145732
  6.2 2.2 %copy-start.1 = (f32[2048,512]{1,0:T(8,128)S(1)}, f32[2048,512]{1,0:T(8,128)}, u32[]{:S(2)}) copy-start(f32[2048,512]{1,0:T(8,128)} %proj_ref.1) | copy-start | bytes 12582916
  9.3 9.8 %copy-start.30 = (s32[512]{0:T(512)S(1)}, s32[512]{0:T(512)}, u32[]{:S(2)}) copy-start(s32[512]{0:T(512)} %param.13) | copy-start | bytes 6148
  13.3 15.7 %copy-start.6 = (f32[512,384]{1,0:T(8,128)}, f32[512,384]{1,0:T(8,128)S(1)}, u32[]{:S(2)}) copy-start(f32[512,384]{1,0:T(8,128)S(1)} %get-tuple-element.45.refs_2_.refs_1_) | copy-start | bytes 2359300
  13.3 15.7 %copy-start.8 = (bf16[1024,512]{1,0:T(8,128)(2,1)}, bf16[1024,512]{1,0:T(8,128)(2,1)S(1)}, u32[]{:S(2)}) copy-start(bf16[1024,512]{1,0:T(8,128)(2,1)S(1)} %get-tuple-element.48.refs_5_.refs_3_) | copy-start | bytes 3145732
  13.3 15.7 %copy-start.10 = (f32[512,256]{1,0:T(8,128)}, f32[512,256]{1,0:T(8,128)S(1)}, u32[]{:S(2)}) copy-start(f32[512,256]{1,0:T(8,128)S(1)} %get-tuple-element.46.refs_3_.refs_2_) | copy-start | bytes 1572868
  13.3 12.4 %copy-start.4 = (f32[4,384]{1,0:T(4,128)S(1)}, f32[4,384]{1,0:T(4,128)}, u32[]{:S(2)}) copy-start(f32[4,384]{1,0:T(4,128)} %refs_6_.3) | copy-start | bytes 18436
  18.4 2.5 %collective-permute-start.3 = (f32[272,512]{1,0:T(8,128)S(1)}, f32[272,512]{1,0:T(8,128)S(1)}, u32[]{:S(2)}, u32[]{:S(2)}) collective-permute-start(f32[272,512]{1,0:T(8,128)S(1)} %collective-permute-done.2.refs_0_), channel_id=1, source_target_pairs={{0,1},{1,0},{2,3},{3,2},{4,5},{5,4},{6,7},{7,6},{8,9},{9,8},{10,11... | collective-permute-start | bytes 1671176 | tf_op jit(solution)/shard_map/ppermute | solution.py:380
  19.0 15.2 %collective-permute-start.1 = (f32[240,512]{1,0:T(8,128)S(1)}, f32[240,512]{1,0:T(8,128)S(1)}, u32[]{:S(2)}, u32[]{:S(2)}) collective-permute-start(f32[240,512]{1,0:T(8,128)S(1)} %get-tuple-element.42), channel_id=1, source_target_pairs={{0,2},{1,3},{2,0},{3,1},{4,6},{5,7},{6,4},{7,5},{8,10},{9,11},{10,... | collective-permute-start | bytes 1474568 | tf_op jit(solution)/shard_map/ppermute | solution.py:386
  22.3 6.7 %copy-start.12 = (f32[272,384]{1,0:T(8,128)}, f32[272,384]{1,0:T(8,128)S(1)}, u32[]{:S(2)}) copy-start(f32[272,384]{1,0:T(8,128)S(1)} %get-tuple-element.49.raw_ref.refs_4_) | copy-start | bytes 1253380
  22.3 12.0 %collective-permute-start.4 = (f32[16,384]{1,0:T(8,128)S(1)}, f32[16,384]{1,0:T(8,128)S(1)}, u32[]{:S(2)}, u32[]{:S(2)}) collective-permute-start(f32[16,384]{1,0:T(8,128)S(1)} %get-tuple-element.51), channel_id=1, source_target_pairs={{0,4},{4,8},{8,12},{12,16},{16,20},{20,24},{24,28},{1,5},{5,9},{9,... | collective-permute-start | bytes 73736 | tf_op jit(solution)/shard_map/ppermute | solution.py:434
  34.3 1.9 %collective-permute-start.5 = (f32[240,512]{1,0:T(8,128)S(1)}, f32[240,512]{1,0:T(8,128)S(1)}, u32[]{:S(2)}, u32[]{:S(2)}) collective-permute-start(f32[240,512]{1,0:T(8,128)S(1)} %collective-permute-done.1.refs_0_), channel_id=1, source_target_pairs={{0,1},{1,0},{2,3},{3,2},{4,5},{5,4},{6,7},{7,6},{8,9},{9,8},{10,11... | collective-permute-start | bytes 1474568 | tf_op jit(solution)/shard_map/ppermute | solution.py:380
  38.0 19.4 %copy-start.9 = (bf16[1024,512]{1,0:T(8,128)(2,1)S(1)}, bf16[1024,512]{1,0:T(8,128)(2,1)}, u32[]{:S(2)}) copy-start(bf16[1024,512]{1,0:T(8,128)(2,1)} %copy-done.8) | copy-start | bytes 3145732
  38.0 19.4 %copy-start.11 = (f32[512,256]{1,0:T(8,128)S(1)}, f32[512,256]{1,0:T(8,128)}, u32[]{:S(2)}) copy-start(f32[512,256]{1,0:T(8,128)} %copy-done.10) | copy-start | bytes 1572868
  38.0 19.4 %copy-start.17 = (f32[2,2,128,128]{3,2,1,0:T(8,128)S(1)}, f32[2,2,128,128]{3,2,1,0:T(8,128)}, u32[]{:S(2)}) copy-start(f32[2,2,128,128]{3,2,1,0:T(8,128)} %copy-done.16) | copy-start | bytes 786436
  38.0 19.4 %copy-start.19 = (f32[256,128]{1,0:T(8,128)S(1)}, f32[256,128]{1,0:T(8,128)}, u32[]{:S(2)}) copy-start(f32[256,128]{1,0:T(8,128)} %copy-done.18) | copy-start | bytes 393220
  38.0 19.4 %copy-start.21 = (f32[256,128]{1,0:T(8,128)S(1)}, f32[256,128]{1,0:T(8,128)}, u32[]{:S(2)}) copy-start(f32[256,128]{1,0:T(8,128)} %copy-done.20) | copy-start | bytes 393220
  38.1 19.4 %copy-start.23 = (f32[256,128]{1,0:T(8,128)S(1)}, f32[256,128]{1,0:T(8,128)}, u32[]{:S(2)}) copy-start(f32[256,128]{1,0:T(8,128)} %copy-done.22) | copy-start | bytes 393220
  38.1 19.4 %copy-start.25 = (f32[256,128]{1,0:T(8,128)S(1)}, f32[256,128]{1,0:T(8,128)}, u32[]{:S(2)}) copy-start(f32[256,128]{1,0:T(8,128)} %copy-done.24) | copy-start | bytes 393220
  38.1 19.4 %copy-start.27 = (f32[256,128]{1,0:T(8,128)S(1)}, f32[256,128]{1,0:T(8,128)}, u32[]{:S(2)}) copy-start(f32[256,128]{1,0:T(8,128)} %copy-done.26) | copy-start | bytes 393220
  41.9 5.8 %collective-permute-start.6 = (f32[2,128,128]{2,1,0:T(8,128)S(1)}, f32[2,128,128]{2,1,0:T(8,128)S(1)}, u32[]{:S(2)}, u32[]{:S(2)}) collective-permute-start(f32[2,128,128]{2,1,0:T(8,128)S(1)} %get-tuple-element.73.own_ref), channel_id=1, source_target_pairs={{0,4},{4,0},{8,12},{12,8},{16,20},{20,16},{24,28},{28,24},{1,5},{5... | collective-permute-start | bytes 393224 | tf_op jit(solution)/shard_map/ppermute | solution.py:459
  43.5 6.4 %collective-permute-start.7 = (f32[2,128,128]{2,1,0:T(8,128)S(1)}, f32[2,128,128]{2,1,0:T(8,128)S(1)}, u32[]{:S(2)}, u32[]{:S(2)}) collective-permute-start(f32[2,128,128]{2,1,0:T(8,128)S(1)} %get-tuple-element.73.own_ref), channel_id=1, source_target_pairs={{0,8},{4,12},{8,0},{12,4},{16,24},{20,28},{24,16},{28,20},{1,9},{5... | collective-permute-start | bytes 393224 | tf_op jit(solution)/shard_map/ppermute | solution.py:459
  45.1 6.6 %collective-permute-start.8 = (f32[2,128,128]{2,1,0:T(8,128)S(1)}, f32[2,128,128]{2,1,0:T(8,128)S(1)}, u32[]{:S(2)}, u32[]{:S(2)}) collective-permute-start(f32[2,128,128]{2,1,0:T(8,128)S(1)} %get-tuple-element.73.own_ref), channel_id=1, source_target_pairs={{0,12},{4,8},{8,4},{12,0},{16,28},{20,24},{24,20},{28,16},{1,13},{... | collective-permute-start | bytes 393224 | tf_op jit(solution)/shard_map/ppermute | solution.py:459
  52.7 7.2 %collective-permute-start.9 = (f32[128,128]{1,0:T(8,128)S(1)}, f32[128,128]{1,0:T(8,128)S(1)}, u32[]{:S(2)}, u32[]{:S(2)}) collective-permute-start(f32[128,128]{1,0:T(8,128)S(1)} %slice_bitcast_fusion), channel_id=1, source_target_pairs={{0,16},{4,20},{8,24},{12,28},{1,17},{5,21},{9,25},{13,29},{2,18},{... | collective-permute-start | bytes 196616 | tf_op jit(solution)/shard_map/ppermute | solution.py:482
  57.5 2.4 %copy-start.5 = (f32[128]{0:T(128)S(1)}, f32[128]{0:T(128)}, u32[]{:S(2)}) copy-start(f32[128]{0:T(128)} %param.14) | copy-start | bytes 1540
  57.5 2.4 %copy-start.15 = (f32[256,128]{1,0:T(8,128)S(1)}, f32[256,128]{1,0:T(8,128)}, u32[]{:S(2)}) copy-start(f32[256,128]{1,0:T(8,128)} %copy-done.14) | copy-start | bytes 393220
  57.5 4.6 %copy-start.2 = (f32[512,512]{1,0:T(8,128)S(1)}, f32[512,512]{1,0:T(8,128)}, u32[]{:S(2)}) copy-start(f32[512,512]{1,0:T(8,128)} %refs_2_.3) | copy-start | bytes 3145732
  60.5 1.6 %collective-permute-start.11 = (f32[512,128]{1,0:T(8,128)S(1)}, f32[512,128]{1,0:T(8,128)S(1)}, u32[]{:S(2)}, u32[]{:S(2)}) collective-permute-start(f32[512,128]{1,0:T(8,128)S(1)} %shard_map.89.refs_0_), channel_id=1, source_target_pairs={{0,1},{1,0},{2,3},{3,2},{4,5},{5,4},{6,7},{7,6},{8,9},{9,8},{10,11... | collective-permute-start | bytes 786440 | tf_op jit(solution)/shard_map/ppermute | solution.py:380
  60.6 8.7 %collective-permute-start.10 = (f32[512,128]{1,0:T(8,128)S(1)}, f32[512,128]{1,0:T(8,128)S(1)}, u32[]{:S(2)}, u32[]{:S(2)}) collective-permute-start(f32[512,128]{1,0:T(8,128)S(1)} %shard_map.89.refs_0_), channel_id=1, source_target_pairs={{0,2},{1,3},{2,0},{3,1},{4,6},{5,7},{6,4},{7,5},{8,10},{9,11},{10,... | collective-permute-start | bytes 786440 | tf_op jit(solution)/shard_map/ppermute | solution.py:386
  69.3 1.5 %collective-permute-start.12 = (f32[512,128]{1,0:T(8,128)S(1)}, f32[512,128]{1,0:T(8,128)S(1)}, u32[]{:S(2)}, u32[]{:S(2)}) collective-permute-start(f32[512,128]{1,0:T(8,128)S(1)} %collective-permute-done.10.refs_0_), channel_id=1, source_target_pairs={{0,1},{1,0},{2,3},{3,2},{4,5},{5,4},{6,7},{7,6},{8,9},{9,8},{10,11... | collective-permute-start | bytes 786440 | tf_op jit(solution)/shard_map/ppermute | solution.py:380
  (12 other events, 9.2 us)

commit v6 on v5

--- a/solution.py
+++ b/solution.py
@@ -175,7 +175,8 @@
         plus_ref[rows, :] = plus
         betas.append(sigmoid(mixing[:, 0:1]))
         spot = first_chunk + part
-        docs = jnp.transpose(jnp.broadcast_to(doc_ref[spot : spot + 1, :], (CHUNK, CHUNK)))
+        docs = jnp.broadcast_to(doc_ref[spot : spot + 1, :].astype(F32), (CHUNK, CHUNK))
+        docs = jnp.transpose(docs)
         steps = jnp.where(col == 1, -rate * plus, jnp.where(col == 0, docs, 0.0))
         sums = jnp.dot(tri, steps, precision=lax.Precision.HIGHEST, preferred_element_type=F32)
         across = jnp.transpose(sums)
@@ -285,26 +286,37 @@
             local_ref[out, :] = local
 
 
-def four_kernel(bits_ref, own_ref, one_ref, two_ref, three_ref, carry_ref, group_ref, level_ref, next_ref, pairs):
-    low_bit, high_bit = bits_ref[0], bits_ref[1]
+def four_kernel(first_bit, carried, last, bits_ref, own_ref, one_ref, two_ref, three_ref, *refs):
+    group_ref, level_ref, next_ref, pairs = refs[-4:]
+    low_bit, high_bit = bits_ref[first_bit], bits_ref[first_bit + 1]
     place = 2 * high_bit + low_bit
     for mask, ref in enumerate((own_ref, one_ref, two_ref, three_ref)):
         pairs[place ^ mask] = ref[...]
-    width = carry_ref.shape[0]
+    width = next_ref.shape[0]
     joined = lambda spot: jnp.concatenate([pairs[spot, 0], pairs[spot, 1]], axis=1)
     onto_low = product(pairs[1, 0], joined(0))
     onto_high = product(pairs[3, 0], joined(2))
     low_a, low_s = onto_low[:, :width], onto_low[:, width:] + pairs[1, 1]
     high_a, high_s = onto_high[:, :width], onto_high[:, width:] + pairs[3, 1]
-    onto = product(high_a, jnp.concatenate([low_a, low_s], axis=1))
-    group_ref[0] = onto[:, :width]
-    group_ref[1] = onto[:, width:] + high_s
-    carry = carry_ref[...]
-    first = product(carry, jnp.concatenate([one_ref[0], one_ref[1]], axis=1))
+    if last:
+        group_ref[...] = product(high_a, low_s) + high_s
+    else:
+        onto = product(high_a, jnp.concatenate([low_a, low_s], axis=1))
+        group_ref[0] = onto[:, :width]
+        group_ref[1] = onto[:, width:] + high_s
     set_low = jnp.broadcast_to(low_bit, (width, width)) == 1
     set_high = jnp.broadcast_to(high_bit, (width, width)) == 1
-    level_ref[0] = jnp.where(set_low, first[:, width:], 0.0)
-    carry = jnp.where(set_low, first[:, :width], carry)
+    if carried:
+        carry = refs[0][...]
+        first = product(carry, jnp.concatenate([one_ref[0], one_ref[1]], axis=1))
+        first_a, first_s = first[:, :width], first[:, width:]
+    else:
+        row = lax.broadcasted_iota(jnp.int32, (width, width), 0)
+        col = lax.broadcasted_iota(jnp.int32, (width, width), 1)
+        carry = jnp.where(row == col, 1.0, 0.0).astype(F32)
+        first_a, first_s = one_ref[0], one_ref[1]
+    level_ref[0] = jnp.where(set_low, first_s, 0.0)
+    carry = jnp.where(set_low, first_a, carry)
     second = product(carry, jnp.concatenate([low_a, low_s], axis=1))
     level_ref[1] = jnp.where(set_high, second[:, width:], 0.0)
     next_ref[...] = jnp.where(set_high, second[:, :width], carry)
@@ -365,7 +377,7 @@
         kernel,
         out_shape=outs,
         in_specs=[
-            free if spot in any_in else small if arg.dtype == jnp.int32 else spec
+            free if spot in any_in else small if arg.dtype == jnp.int32 and arg.ndim == 1 else spec
             for spot, arg in enumerate(args)
         ],
         out_specs=jax.tree.map(lambda unused: free if any_out else spec, outs),
@@ -402,7 +414,9 @@
     blocks, my_index = lax.axis_size("ctx"), lax.axis_index("ctx")
     remote = [(me + heads - 2 * step) % heads for step in range(1, heads // 2)]
     order = [me, me ^ 1] + remote + [index ^ 1 for index in remote]
-    index = jnp.stack(order).astype(jnp.int32)
+    bits = blocks.bit_length() - 1
+    flags = [my_index >> bit & 1 for bit in range(bits)]
+    index = jnp.stack(order + flags).astype(jnp.int32)
     count = heads - 2
     like = lambda *shape: jax.ShapeDtypeStruct(shape, F32)
     parts = lambda *shape: jax.ShapeDtypeStruct(shape, BF16)
@@ -429,14 +443,14 @@
         functools.partial(late_kernel, count, cut),
         [like(tok_rows - cut, state_columns), like(tok_rows - cut, query_columns),
          like(RIM, 3 * width)],
-        [], 2, *late, *late_on, base_state, base_query, far_state, far_query,
+        [], 0.5, *late, *late_on, base_state, base_query, far_state, far_query,
     )
     rim = lax.ppermute(rim, "ctx", [(source, source + 1) for source in range(blocks - 1)])
-    docs = doc_start.astype(F32).reshape(tok_rows // CHUNK, CHUNK)
+    docs = doc_start.reshape(tok_rows // CHUNK, CHUNK)
     rate = rates[:, None]
     outs = [like(half, width)] * 6 + [like(half // CHUNK, 2, width, width), like(2, width, width)]
     later = vmem_call(
-        functools.partial(later_kernel, half // CHUNK), outs, [], 4, late_state, conv_w, rate, docs
+        functools.partial(later_kernel, half // CHUNK), outs, [], 0.5, late_state, conv_w, rate, docs
     )
     early, pair_late, rim = after(early, later[7], rim)
     early_on = [to_sibling(value) for value in early]
@@ -451,8 +465,7 @@
     )
 
     pair = earlier[7]
-    carry = jnp.eye(width, dtype=F32)
-    bits = blocks.bit_length() - 1
+    carry = ()
     levels = []
     for bit in range(0, bits - 1, 2):
         others = [
@@ -461,11 +474,13 @@
             )
             for mask in (1, 2, 3)
         ]
-        flags = jnp.stack([my_index >> bit & 1, my_index >> (bit + 1) & 1]).astype(jnp.int32)
-        pair, level, carry = vmem_call(
-            four_kernel, [like(2, width, width)] * 2 + [like(width, width)],
+        last = bit + 2 >= bits - 1 and bits % 2
+        group = [like(width, width)] if last else [like(2, width, width)]
+        pair, level, *carry = vmem_call(
+            functools.partial(four_kernel, heads + bit, bool(carry), last),
+            group + [like(2, width, width), like(width, width)],
             [pltpu.VMEM((4, 2, width, width), F32)], 1,
-            flags, pair, *others, carry,
+            index, pair, *others, *carry,
         )
         levels.append(level)
     fields = vmem_call(
@@ -478,8 +493,11 @@
     if bits % 2:
         reach = blocks // 2
         single = [
-            carry,
-            lax.ppermute(pair[1], "ctx", [(source, source + reach) for source in range(reach)]),
+            *(carry or [jnp.eye(width, dtype=F32)]),
+            lax.ppermute(
+                pair if carry else pair[1],
+                "ctx", [(source, source + reach) for source in range(reach)],
+            ),
         ]
     normed = vmem_call(
         functools.partial(mix_kernel, len(levels), bool(single)), like(tok_rows, width), [], 1,

time: 73.4 us -> 67.8 us (0.924)
  local copies, waits for them, and re-layouts: 14.6 us -> 5.52 us
  waiting for transfers between devices: 19.2 us -> 22.9 us
    unnamed x62 -> x14, local copies, waits for them, and re-layouts: 12.7 us -> 4.34 us
    ppermute x3, waiting for transfers between devices: 11.1 us -> 14 us  [to_chips(): lax.ppermute(value, 'head', [(source, (source + 2 * step) % count) for so...]
    ppermute x5, waiting for transfers between devices: 2 us -> 2.9 us  [to_sibling(): lax.ppermute(value, 'head', [(source, source ^ 1) for source in range(cou...]
    slice x1, local copies, waits for them, and re-layouts: 1.89 us -> 1.09 us  [shards(): late = to_chips(tokens[cut:])]
  transfers between devices with their start and end apart: 13 -> 13, of which waited for: 8 -> 7; matrix products, arithmetic and copies ran while one was open for 3% -> 2% of each run, Pallas kernels for 17% -> 19%
where the time goes in v6:
time: 67.8 us; the launch traced here: 67.5 us
  waiting for transfers between devices  22.9 us (34%)
  Pallas kernels  20 us (29%)
  starting transfers between devices  18.1 us (27%)
  local copies, waits for them, and re-layouts  5.52 us (8%)
  between operations  0.99 us (1%)
    pallas_call x10, Pallas kernels, vmem_call(): pl.pallas_call(kernel, out_shape=outs, in_specs=[free if spot in any_in e...  20 us
    ppermute x3, waiting for transfers between devices, to_chips(): lax.ppermute(value, 'head', [(source, (source + 2 * step) % count) for so...  14 us
    ppermute x3, waiting for transfers between devices, shards(): lax.ppermute(pair, 'ctx', [(source, source ^ mask << bit) for source in r...  6.01 us
    ppermute x3, starting transfers between devices, to_chips(): lax.ppermute(value, 'head', [(source, (source + 2 * step) % count) for so...  5.91 us
    ppermute x1, starting transfers between devices, shards(): lax.ppermute(pair if carry else pair[1], 'ctx', [(source, source + reach)...  4.67 us
    unnamed x14, local copies, waits for them, and re-layouts  4.34 us
    ppermute x3, starting transfers between devices, shards(): lax.ppermute(pair, 'ctx', [(source, source ^ mask << bit) for source in r...  3.55 us
    ppermute x1, starting transfers between devices, shards(): lax.ppermute(rim, 'ctx', [(source, source + 1) for source in range(blocks...  3.4 us
  transfers between devices with their start and end apart: 13, of which 7 were waited for; matrix products, arithmetic and copies ran while one was open for 2% of the time, Pallas kernels for 19%

profile of v6, /device:TPU:0, one launch (start us, length us, event | category | flops | bytes accessed | tf_op | source)
XLA Modules:
  0.0 67.5 jit_solution(10550239904077143057)
XLA Ops:
  0.0 0.5 collective-permute-start
  0.5 1.1 %slice.3 = f32[272,512]{1,0:T(8,128)S(1)} slice(f32[512,512]{1,0:T(8,128)} %own_ref.1), slice={[240:512], [0:512]} | slice | bytes 1114112 | tf_op jit(solution)/shard_map/slice | solution.py:426
  1.5 2.6 %collective-permute-start.2 = (f32[272,512]{1,0:T(8,128)S(1)}, f32[272,512]{1,0:T(8,128)S(1)}, u32[]{:S(2)}, u32[]{:S(2)}) collective-permute-start(f32[272,512]{1,0:T(8,128)S(1)} %slice.3), channel_id=1, source_target_pairs={{0,2},{1,3},{2,0},{3,1},{4,6},{5,7},{6,4},{7,5},{8,10},{9,11},{10,... | collective-permute-start | bytes 1671176 | tf_op jit(solution)/shard_map/ppermute | solution.py:398
  4.1 0.1 stack.31.index_ref.bits_ref
  4.2 1.2 %copy-done = f32[512,512]{1,0:T(8,128)S(1)} copy-done((f32[512,512]{1,0:T(8,128)S(1)}, f32[512,512]{1,0:T(8,128)}, u32[]{:S(2)}) %copy-start) | copy-done | bytes 1048600
  5.4 2.2 %copy-done.1 = f32[2048,512]{1,0:T(8,128)S(1)} copy-done((f32[2048,512]{1,0:T(8,128)S(1)}, f32[2048,512]{1,0:T(8,128)}, u32[]{:S(2)}) %copy-start.1) | copy-done | bytes 4194328
  7.6 0.9 %copy-done.3 = f32[2048,9]{0,1:T(8,128)S(1)} copy-done((f32[2048,9]{0,1:T(8,128)S(1)}, f32[2048,9]{0,1:T(8,128)}, u32[]{:S(2)}) %copy-start.3) | copy-done | bytes 73752
  8.5 4.0 %shard_map.82 = (f32[512,384]{1,0:T(8,128)S(1)}, f32[512,256]{1,0:T(8,128)S(1)}, bf16[1024,768]{1,0:T(8,128)(2,1)S(1)}, bf16[1024,512]{1,0:T(8,128)(2,1)S(1)}, f32[240,512]{1,0:T(8,128)S(1)}) custom-call(s32[7]{0:T(128)S(1)} %stack.31.index_ref.bits_ref, f32[512,512]{1,0:T(8,128)S(1)} %copy-done, f32[512,512]{1,0:T(8,128)S(1)} %collective-permute-done.beside_ref, ...), custom_call_target="tpu_custom_call" | custom-call | flops 3000000000 | bytes 1048576 | tf_op jit(solution)/shard_map/pallas_call | solution.py:376
  12.6 4.9 %collective-permute-done.2.refs_0_ = f32[272,512]{1,0:T(8,128)S(1)} collective-permute-done((f32[272,512]{1,0:T(8,128)S(1)}, f32[272,512]{1,0:T(8,128)S(1)}, u32[]{:S(2)}, u32[]{:S(2)}) %collective-permute-start.2) | collective-permute-done | bytes 557088 | tf_op jit(solution)/shard_map/ppermute | solution.py:398
  17.4 1.7 %collective-permute-start.1 = (f32[240,512]{1,0:T(8,128)S(1)}, f32[240,512]{1,0:T(8,128)S(1)}, u32[]{:S(2)}, u32[]{:S(2)}) collective-permute-start(f32[240,512]{1,0:T(8,128)S(1)} %get-tuple-element.42), channel_id=1, source_target_pairs={{0,2},{1,3},{2,0},{3,1},{4,6},{5,7},{6,4},{7,5},{8,10},{9,11},{10,... | collective-permute-start | bytes 1474568 | tf_op jit(solution)/shard_map/ppermute | solution.py:398
  19.8 1.4 %shard_map.83 = (f32[272,384]{1,0:T(8,128)S(1)}, f32[272,256]{1,0:T(8,128)S(1)}, f32[16,384]{1,0:T(8,128)S(1)}) custom-call(f32[272,512]{1,0:T(8,128)S(1)} %collective-permute-done.2.refs_0_, f32[272,512]{1,0:T(8,128)S(1)} %collective-permute-done.3.refs_1_, f32[512,384]{1,0:T(8,128)S(1)} %get-tuple-element.45.refs_2_.refs_1_, ...), custom_call_target="tpu_custom_call" | custom-call | flops 500000000 | bytes 1048576 | tf_op jit(solution)/shard_map/pallas_call | solution.py:376
  21.2 3.4 %collective-permute-start.4 = (f32[16,384]{1,0:T(8,128)S(1)}, f32[16,384]{1,0:T(8,128)S(1)}, u32[]{:S(2)}, u32[]{:S(2)}) collective-permute-start(f32[16,384]{1,0:T(8,128)S(1)} %get-tuple-element.51), channel_id=1, source_target_pairs={{0,4},{4,8},{8,12},{12,16},{16,20},{20,24},{24,28},{1,5},{5,9},{9,... | collective-permute-start | bytes 73736 | tf_op jit(solution)/shard_map/ppermute | solution.py:448
  24.7 3.3 %shard_map.84 = (f32[256,128]{1,0:T(8,128)S(1)}, f32[256,128]{1,0:T(8,128)S(1)}, f32[256,128]{1,0:T(8,128)S(1)}, f32[256,128]{1,0:T(8,128)S(1)}, f32[256,128]{1,...) custom-call(f32[272,384]{1,0:T(8,128)S(1)} %get-tuple-element.49.raw_ref.refs_4_,, ...), custom_call_target="tpu_custom_call" | custom-call | flops 500000000 | bytes 1048576 | tf_op jit(solution)/shard_map/pallas_call | solution.py:376
  27.9 3.1 %collective-permute-done.1.refs_0_ = f32[240,512]{1,0:T(8,128)S(1)} collective-permute-done((f32[240,512]{1,0:T(8,128)S(1)}, f32[240,512]{1,0:T(8,128)S(1)}, u32[]{:S(2)}, u32[]{:S(2)}) %collective-permute-start.1) | collective-permute-done | bytes 491552 | tf_op jit(solution)/shard_map/ppermute | solution.py:398
  31.1 0.5 shard_map.85.refs_1_
  31.6 1.4 %collective-permute-done.5.refs_0_.refs_1_ = f32[240,512]{1,0:T(8,128)S(1)} collective-permute-done((f32[240,512]{1,0:T(8,128)S(1)}, f32[240,512]{1,0:T(8,128)S(1)}, u32[]{:S(2)}, u32[]{:S(2)}) %collective-permute-start.5) | collective-permute-done | bytes 491552 | tf_op jit(solution)/shard_map/ppermute | solution.py:392
  32.9 3.8 %shard_map.86 = (f32[256,128]{1,0:T(8,128)S(1)}, f32[256,128]{1,0:T(8,128)S(1)}, f32[256,128]{1,0:T(8,128)S(1)}, f32[256,128]{1,0:T(8,128)S(1)}, f32[256,128]{1,...) custom-call(f32[240,512]{1,0:T(8,128)S(1)} %collective-permute-done.5.refs_0_.ref, ...), custom_call_target="tpu_custom_call" | custom-call | flops 5000000000 | bytes 1048576 | tf_op jit(solution)/shard_map/pallas_call | solution.py:376
  36.8 2.8 %collective-permute-start.8 = (f32[2,128,128]{2,1,0:T(8,128)S(1)}, f32[2,128,128]{2,1,0:T(8,128)S(1)}, u32[]{:S(2)}, u32[]{:S(2)}) collective-permute-start(f32[2,128,128]{2,1,0:T(8,128)S(1)} %get-tuple-element.73.own_ref), channel_id=1, source_target_pairs={{0,12},{4,8},{8,4},{12,0},{16,28},{20,24},{24,20},{28,16},{1,13},{... | collective-permute-start | bytes 393224 | tf_op jit(solution)/shard_map/ppermute | solution.py:472
  39.5 0.4 collective-permute-start.7
  40.0 0.3 collective-permute-start.6
  40.3 3.7 %collective-permute-done.8.three_ref = f32[2,128,128]{2,1,0:T(8,128)S(1)} collective-permute-done((f32[2,128,128]{2,1,0:T(8,128)S(1)}, f32[2,128,128]{2,1,0:T(8,128)S(1)}, u32[]{:S(2)}, u32[]{:S(2)}) %collective-permute-start.8) | collective-permute-done | bytes 131104 | tf_op jit(solution)/shard_map/ppermute | solution.py:472
  44.1 2.3 %collective-permute-done.7.two_ref = f32[2,128,128]{2,1,0:T(8,128)S(1)} collective-permute-done((f32[2,128,128]{2,1,0:T(8,128)S(1)}, f32[2,128,128]{2,1,0:T(8,128)S(1)}, u32[]{:S(2)}, u32[]{:S(2)}) %collective-permute-start.7) | collective-permute-done | bytes 131104 | tf_op jit(solution)/shard_map/ppermute | solution.py:472
  46.3 1.0 %shard_map.88 = (f32[128,128]{1,0:T(8,128)S(1)}, f32[2,128,128]{2,1,0:T(8,128)S(1)}, f32[128,128]{1,0:T(8,128)S(1)}) custom-call(s32[7]{0:T(128)S(1)} %stack.31.index_ref.bits_ref, f32[2,128,128]{2,1,0:T(8,128)S(1)} %get-tuple-element.73.own_ref, f32[2,128,128]{2,1,0:T(8,128)S(1)} %collective-permute-done.6.one_ref, ...), custom_call_target="tpu_custom_call" | custom-call | flops 1000000000 | bytes 1048576 | tf_op jit(solution)/shard_map/pallas_call | solution.py:376
  47.4 4.7 %collective-permute-start.9 = (f32[128,128]{1,0:T(8,128)S(1)}, f32[128,128]{1,0:T(8,128)S(1)}, u32[]{:S(2)}, u32[]{:S(2)}) collective-permute-start(f32[128,128]{1,0:T(8,128)S(1)} %get-tuple-element.76), channel_id=1, source_target_pairs={{0,16},{4,20},{8,24},{12,28},{1,17},{5,21},{9,25},{13,29},{2,18},{... | collective-permute-start | bytes 196616 | tf_op jit(solution)/shard_map/ppermute | solution.py:497
  52.1 2.4 %shard_map.87 = (f32[512,128]{1,0:T(8,128)S(1)}, f32[512,128]{1,0:T(8,128)S(1)}, f32[512,128]{1,0:T(8,128)S(1)}) custom-call(f32[240,512]{1,0:T(8,128)S(1)} %collective-permute-done.1.refs_0_, f32[240,512]{1,0:T(8,128)S(1)} %collective-permute-done.5.refs_0_.refs_1_, f32[512,256]{1,0:T(8,128)S(1)} %get-tuple-element.46.refs_3_.refs_2_, ...), custom_call_target="tpu_custom_call" | custom-call | flops 5000000000 | bytes 1048576 | tf_op jit(solution)/shard_map/pallas_call | solution.py:376
  54.5 0.6 shard_map.89.refs_0_
  55.1 0.1 collective-permute-start.11
  55.2 1.6 %collective-permute-start.10 = (f32[512,128]{1,0:T(8,128)S(1)}, f32[512,128]{1,0:T(8,128)S(1)}, u32[]{:S(2)}, u32[]{:S(2)}) collective-permute-start(f32[512,128]{1,0:T(8,128)S(1)} %shard_map.89.refs_0_), channel_id=1, source_target_pairs={{0,2},{1,3},{2,0},{3,1},{4,6},{5,7},{6,4},{7,5},{8,10},{9,11},{10,... | collective-permute-start | bytes 786440 | tf_op jit(solution)/shard_map/ppermute | solution.py:398
  56.7 1.2 %shard_map.90.refs_3_ = f32[512,512]{1,0:T(8,128)S(1)} custom-call(s32[7]{0:T(128)S(1)} %stack.31.index_ref.bits_ref, f32[512,128]{1,0:T(8,128)S(1)} %shard_map.89.refs_0_, f32[512,128]{1,0:T(8,128)S(1)} %collective-permute-done.11.refs_1_, f32[512,512]{1,0:T(8,128)S(1)} %copy-done.2), custom_call_target="tpu_custom_call" | custom-call | flops 2000000000 | bytes 1048576 | tf_op jit(solution)/shard_map/pallas_call | solution.py:376
  57.9 6.0 %collective-permute-done.10.refs_0_ = f32[512,128]{1,0:T(8,128)S(1)} collective-permute-done((f32[512,128]{1,0:T(8,128)S(1)}, f32[512,128]{1,0:T(8,128)S(1)}, u32[]{:S(2)}, u32[]{:S(2)}) %collective-permute-start.10) | collective-permute-done | bytes 262176 | tf_op jit(solution)/shard_map/ppermute | solution.py:398
  63.9 1.5 %collective-permute-done.12.refs_1_ = f32[512,128]{1,0:T(8,128)S(1)} collective-permute-done((f32[512,128]{1,0:T(8,128)S(1)}, f32[512,128]{1,0:T(8,128)S(1)}, u32[]{:S(2)}, u32[]{:S(2)}) %collective-permute-start.12) | collective-permute-done | bytes 262176 | tf_op jit(solution)/shard_map/ppermute | solution.py:392
  65.4 1.9 %shard_map.91 = f32[512,512]{1,0:T(8,128)} custom-call(s32[7]{0:T(128)S(1)} %stack.31.index_ref.bits_ref, f32[512,128]{1,0:T(8,128)S(1)} %collective-permute-done.10.refs_0_, f32[512,128]{1,0:T(8,128)S(1)} %collective-permute-done.12.refs_1_, f32[512,512]{1,0:T(8,128)S(1)} %copy-done.2, f32[512,512]{1,0:T(8,128)S(1)} %shard_map.90.refs_3_), custom_call_target="tpu_custom_call" | custom-call | flops 2000000000 | bytes 1048576 | tf_op jit(solution)/shard_map/pallas_call | solution.py:376
  (20 shorter events, 0.1 us)
Async XLA Ops:
  0.0 4.2 %collective-permute-start = (f32[512,512]{1,0:T(8,128)}, f32[512,512]{1,0:T(8,128)S(1)}, u32[]{:S(2)}, u32[]{:S(2)}) collective-permute-start(f32[512,512]{1,0:T(8,128)} %own_ref.1), channel_id=1, source_target_pairs={{0,1},{1,0},{2,3},{3,2},{4,5},{5,4},{6,7},{7,6},{8,9},{9,8},{10,11... | collective-permute-start | bytes 3145736 | tf_op jit(solution)/shard_map/ppermute | solution.py:392
  1.5 15.9 %collective-permute-start.2 = (f32[272,512]{1,0:T(8,128)S(1)}, f32[272,512]{1,0:T(8,128)S(1)}, u32[]{:S(2)}, u32[]{:S(2)}) collective-permute-start(f32[272,512]{1,0:T(8,128)S(1)} %slice.3), channel_id=1, source_target_pairs={{0,2},{1,3},{2,0},{3,1},{4,6},{5,7},{6,4},{7,5},{8,10},{9,11},{10,... | collective-permute-start | bytes 1671176 | tf_op jit(solution)/shard_map/ppermute | solution.py:398
  4.2 1.2 %copy-start = (f32[512,512]{1,0:T(8,128)S(1)}, f32[512,512]{1,0:T(8,128)}, u32[]{:S(2)}) copy-start(f32[512,512]{1,0:T(8,128)} %own_ref.1) | copy-start | bytes 3145732
  5.4 2.2 %copy-start.1 = (f32[2048,512]{1,0:T(8,128)S(1)}, f32[2048,512]{1,0:T(8,128)}, u32[]{:S(2)}) copy-start(f32[2048,512]{1,0:T(8,128)} %proj_ref.1) | copy-start | bytes 12582916
  7.6 0.9 %copy-start.3 = (f32[2048,9]{0,1:T(8,128)S(1)}, f32[2048,9]{0,1:T(8,128)}, u32[]{:S(2)}) copy-start(f32[2048,9]{0,1:T(8,128)} %param.10) | copy-start | bytes 221188
  12.5 12.1 %copy-start.4 = (f32[4,384]{1,0:T(4,128)S(1)}, f32[4,384]{1,0:T(4,128)}, u32[]{:S(2)}) copy-start(f32[4,384]{1,0:T(4,128)} %refs_6_.3) | copy-start | bytes 18436
  12.6 12.1 %copy-start.5 = (s32[512]{0:T(512)S(1)}, s32[512]{0:T(512)}, u32[]{:S(2)}) copy-start(s32[512]{0:T(512)} %param.13) | copy-start | bytes 6148
  17.4 2.4 %collective-permute-start.3 = (f32[272,512]{1,0:T(8,128)S(1)}, f32[272,512]{1,0:T(8,128)S(1)}, u32[]{:S(2)}, u32[]{:S(2)}) collective-permute-start(f32[272,512]{1,0:T(8,128)S(1)} %collective-permute-done.2.refs_0_), channel_id=1, source_target_pairs={{0,1},{1,0},{2,3},{3,2},{4,5},{5,4},{6,7},{7,6},{8,9},{9,8},{10,11... | collective-permute-start | bytes 1671176 | tf_op jit(solution)/shard_map/ppermute | solution.py:392
  17.4 13.6 %collective-permute-start.1 = (f32[240,512]{1,0:T(8,128)S(1)}, f32[240,512]{1,0:T(8,128)S(1)}, u32[]{:S(2)}, u32[]{:S(2)}) collective-permute-start(f32[240,512]{1,0:T(8,128)S(1)} %get-tuple-element.42), channel_id=1, source_target_pairs={{0,2},{1,3},{2,0},{3,1},{4,6},{5,7},{6,4},{7,5},{8,10},{9,11},{10,... | collective-permute-start | bytes 1474568 | tf_op jit(solution)/shard_map/ppermute | solution.py:398
  21.2 9.8 %collective-permute-start.4 = (f32[16,384]{1,0:T(8,128)S(1)}, f32[16,384]{1,0:T(8,128)S(1)}, u32[]{:S(2)}, u32[]{:S(2)}) collective-permute-start(f32[16,384]{1,0:T(8,128)S(1)} %get-tuple-element.51), channel_id=1, source_target_pairs={{0,4},{4,8},{8,12},{12,16},{16,20},{20,24},{24,28},{1,5},{5,9},{9,... | collective-permute-start | bytes 73736 | tf_op jit(solution)/shard_map/ppermute | solution.py:448
  31.1 1.9 %collective-permute-start.5 = (f32[240,512]{1,0:T(8,128)S(1)}, f32[240,512]{1,0:T(8,128)S(1)}, u32[]{:S(2)}, u32[]{:S(2)}) collective-permute-start(f32[240,512]{1,0:T(8,128)S(1)} %collective-permute-done.1.refs_0_), channel_id=1, source_target_pairs={{0,1},{1,0},{2,3},{3,2},{4,5},{5,4},{6,7},{7,6},{8,9},{9,8},{10,11... | collective-permute-start | bytes 1474568 | tf_op jit(solution)/shard_map/ppermute | solution.py:392
  36.8 7.3 %collective-permute-start.8 = (f32[2,128,128]{2,1,0:T(8,128)S(1)}, f32[2,128,128]{2,1,0:T(8,128)S(1)}, u32[]{:S(2)}, u32[]{:S(2)}) collective-permute-start(f32[2,128,128]{2,1,0:T(8,128)S(1)} %get-tuple-element.73.own_ref), channel_id=1, source_target_pairs={{0,12},{4,8},{8,4},{12,0},{16,28},{20,24},{24,20},{28,16},{1,13},{... | collective-permute-start | bytes 393224 | tf_op jit(solution)/shard_map/ppermute | solution.py:472
  39.5 6.8 %collective-permute-start.7 = (f32[2,128,128]{2,1,0:T(8,128)S(1)}, f32[2,128,128]{2,1,0:T(8,128)S(1)}, u32[]{:S(2)}, u32[]{:S(2)}) collective-permute-start(f32[2,128,128]{2,1,0:T(8,128)S(1)} %get-tuple-element.73.own_ref), channel_id=1, source_target_pairs={{0,8},{4,12},{8,0},{12,4},{16,24},{20,28},{24,16},{28,20},{1,9},{5... | collective-permute-start | bytes 393224 | tf_op jit(solution)/shard_map/ppermute | solution.py:472
  40.0 6.3 %collective-permute-start.6 = (f32[2,128,128]{2,1,0:T(8,128)S(1)}, f32[2,128,128]{2,1,0:T(8,128)S(1)}, u32[]{:S(2)}, u32[]{:S(2)}) collective-permute-start(f32[2,128,128]{2,1,0:T(8,128)S(1)} %get-tuple-element.73.own_ref), channel_id=1, source_target_pairs={{0,4},{4,0},{8,12},{12,8},{16,20},{20,16},{24,28},{28,24},{1,5},{5... | collective-permute-start | bytes 393224 | tf_op jit(solution)/shard_map/ppermute | solution.py:472
  47.4 7.1 %collective-permute-start.9 = (f32[128,128]{1,0:T(8,128)S(1)}, f32[128,128]{1,0:T(8,128)S(1)}, u32[]{:S(2)}, u32[]{:S(2)}) collective-permute-start(f32[128,128]{1,0:T(8,128)S(1)} %get-tuple-element.76), channel_id=1, source_target_pairs={{0,16},{4,20},{8,24},{12,28},{1,17},{5,21},{9,25},{13,29},{2,18},{... | collective-permute-start | bytes 196616 | tf_op jit(solution)/shard_map/ppermute | solution.py:497
  52.0 2.4 %copy-start.6 = (f32[128]{0:T(128)S(1)}, f32[128]{0:T(128)}, u32[]{:S(2)}) copy-start(f32[128]{0:T(128)} %param.14) | copy-start | bytes 1540
  52.0 4.7 %copy-start.2 = (f32[512,512]{1,0:T(8,128)S(1)}, f32[512,512]{1,0:T(8,128)}, u32[]{:S(2)}) copy-start(f32[512,512]{1,0:T(8,128)} %refs_2_.3) | copy-start | bytes 3145732
  55.1 1.7 %collective-permute-start.11 = (f32[512,128]{1,0:T(8,128)S(1)}, f32[512,128]{1,0:T(8,128)S(1)}, u32[]{:S(2)}, u32[]{:S(2)}) collective-permute-start(f32[512,128]{1,0:T(8,128)S(1)} %shard_map.89.refs_0_), channel_id=1, source_target_pairs={{0,1},{1,0},{2,3},{3,2},{4,5},{5,4},{6,7},{7,6},{8,9},{9,8},{10,11... | collective-permute-start | bytes 786440 | tf_op jit(solution)/shard_map/ppermute | solution.py:392
  55.2 8.7 %collective-permute-start.10 = (f32[512,128]{1,0:T(8,128)S(1)}, f32[512,128]{1,0:T(8,128)S(1)}, u32[]{:S(2)}, u32[]{:S(2)}) collective-permute-start(f32[512,128]{1,0:T(8,128)S(1)} %shard_map.89.refs_0_), channel_id=1, source_target_pairs={{0,2},{1,3},{2,0},{3,1},{4,6},{5,7},{6,4},{7,5},{8,10},{9,11},{10,... | collective-permute-start | bytes 786440 | tf_op jit(solution)/shard_map/ppermute | solution.py:398
  63.9 1.5 %collective-permute-start.12 = (f32[512,128]{1,0:T(8,128)S(1)}, f32[512,128]{1,0:T(8,128)S(1)}, u32[]{:S(2)}, u32[]{:S(2)}) collective-permute-start(f32[512,128]{1,0:T(8,128)S(1)} %collective-permute-done.10.refs_0_), channel_id=1, source_target_pairs={{0,1},{1,0},{2,3},{3,2},{4,5},{5,4},{6,7},{7,6},{8,9},{9,8},{10,11... | collective-permute-start | bytes 786440 | tf_op jit(solution)/shard_map/ppermute | solution.py:392

commit v7 on v6

--- a/solution.py
+++ b/solution.py
@@ -52,21 +52,21 @@
     inverses = [eye - jnp.where((row >> 1) == (col >> 1), lower, 0.0) for lower in lowers]
     lower_parts = [halves(lower) for lower in lowers]
     step = 1
-    while 2 << (step - 1) < size:
-        off = ((row >> (step + 1)) == (col >> (step + 1))) & ((row >> step) > (col >> step))
-        lefts = [left_parts(inverse) for inverse in inverses]
+    while 1 << step < size:
+        off = ((row >> (step + 2)) == (col >> (step + 2))) & ((row >> step) > (col >> step))
         offs = [
             jnp.concatenate([jnp.where(off, part, jnp.zeros_like(part)) for part in parts], axis=1)
             for parts in lower_parts
         ]
-        inner = [
-            parts_dot(offdiag, right_parts(inverse)) for offdiag, inverse in zip(offs, inverses)
+        onto = [parts_dot(left, right_parts(inverse)) for left, inverse in zip(offs, inverses)]
+        rights = [right_parts(value) for value in onto]
+        squares = [parts_dot(left_parts(value), right) for value, right in zip(onto, rights)]
+        firsts = [
+            inverse - parts_dot(left_parts(inverse), right)
+            for inverse, right in zip(inverses, rights)
         ]
-        inverses = [
-            inverse - parts_dot(left, right_parts(value))
-            for inverse, left, value in zip(inverses, lefts, inner)
-        ]
-        step += 1
+        inverses = [first + product(first, square) for first, square in zip(firsts, squares)]
+        step += 2
     return inverses
 
 
@@ -85,7 +85,7 @@
 
 def base_kernel(
     index_ref, own_ref, beside_ref, mix_ref, proj_ref,
-    state_ref, query_ref, far_state_ref, far_query_ref, early_ref,
+    state_ref, query_ref, far_state_ref, far_query_ref,
     held, near_state, near_query, sems,
 ):
     sources, depth, across = held.shape
@@ -95,7 +95,6 @@
         rows = pl.ds(pl.multiple_of(index_ref[source] * depth, depth), depth)
         copies.append(pltpu.make_async_copy(proj_ref.at[rows, :], held.at[source], sems.at[source]))
         copies[-1].start()
-    early_ref[...] = own_ref[: early_ref.shape[0], :]
     mixes = mix_ref.shape[0]
 
     def split(source, state_out, query_out, base):
@@ -210,11 +209,13 @@
         states.append((trans, onto[:, width:]))
         chunk_ref[part, 0] = trans
         chunk_ref[part, 1] = onto[:, width:]
-    for part in range(1, chunks):
-        states[0] = followed(states[0], states[part])
-    total = states[0] if state is None else followed(states[0], state)
-    pair_ref[0] = total[0]
-    pair_ref[1] = total[1]
+    if state is not None:
+        states.append(state)
+    while len(states) > 1:
+        joined = [followed(*states[at : at + 2]) for at in range(0, len(states) - 1, 2)]
+        states = joined + states[2 * len(joined) :]
+    pair_ref[0] = states[0][0]
+    pair_ref[1] = states[0][1]
 
 
 def followed(first, second):
@@ -337,7 +338,7 @@
     normed_ref[...] = mixed * scale * gain_ref[...] * gate_ref[...]
 
 
-def out_kernel(pieces, first, index_ref, *refs):
+def out_kernel(pieces, first, last, index_ref, *refs):
     weight_ref = refs[pieces]
     parts = []
     for spot in range(pieces):
@@ -355,9 +356,10 @@
         return (both[:, :columns] + both[:, columns:]) + rest
 
     blocks = [slice(base, base + CHUNK) for base in range(0, refs[0].shape[0], CHUNK)]
-    if not first:
+    if not last:
         for rows in blocks:
-            refs[-1][rows, :] = block(rows)
+            part = block(rows)
+            refs[-1][rows, :] = refs[pieces + 1][rows, :] + part if first else part
         return
     total_ref, out_ref, held, sems = refs[pieces + 1 :]
     copies = []
@@ -421,22 +423,22 @@
     like = lambda *shape: jax.ShapeDtypeStruct(shape, F32)
     parts = lambda *shape: jax.ShapeDtypeStruct(shape, BF16)
 
-    half = tok_rows // 2
-    cut = half - RIM
-    late = to_chips(tokens[cut:])
+    first = tok_rows - CHUNK
+    cut = first - RIM
+    late_rows, early_rows = after(tokens[cut:], tokens)
+    late = to_chips(late_rows)
+    early = to_chips(early_rows[:cut])
     beside = to_sibling(tokens)
-    base_state, base_query, far_state, far_query, early_rows = vmem_call(
+    base_state, base_query, far_state, far_query = vmem_call(
         base_kernel,
         [like(tok_rows, state_columns), like(tok_rows, query_columns),
-         parts(count * depth, 2 * state_columns), parts(count * depth, 2 * query_columns),
-         like(cut, depth)],
+         parts(count * depth, 2 * state_columns), parts(count * depth, 2 * query_columns)],
         [pltpu.VMEM((heads, depth, 4 * width), F32),
          pltpu.VMEM((2 * depth, 2 * state_columns), BF16),
          pltpu.VMEM((2 * depth, 2 * query_columns), BF16),
          pltpu.SemaphoreType.DMA((heads,))],
         3, index, tokens, beside, w_mix.T, w_proj, any_in=(4,),
     )
-    early = to_chips(early_rows)
     late, far_state = after(late, far_state)
     late_on = [to_sibling(value) for value in late]
     late_state, late_query, rim = vmem_call(
@@ -448,9 +450,14 @@
     rim = lax.ppermute(rim, "ctx", [(source, source + 1) for source in range(blocks - 1)])
     docs = doc_start.reshape(tok_rows // CHUNK, CHUNK)
     rate = rates[:, None]
-    outs = [like(half, width)] * 6 + [like(half // CHUNK, 2, width, width), like(2, width, width)]
+
+    def outs(rows):
+        chunks = like(rows // CHUNK, 2, width, width)
+        return [like(rows, width)] * 6 + [chunks, like(2, width, width)]
+
     later = vmem_call(
-        functools.partial(later_kernel, half // CHUNK), outs, [], 0.5, late_state, conv_w, rate, docs
+        functools.partial(later_kernel, first // CHUNK), outs(tok_rows - first), [], 0.5,
+        late_state, conv_w, rate, docs,
     )
     early, pair_late, rim = after(early, later[7], rim)
     early_on = [to_sibling(value) for value in early]
@@ -459,8 +466,8 @@
         *early, base_state, far_state,
     )
     earlier = vmem_call(
-        functools.partial(earlier_kernel, len(early), len(early)), outs,
-        [pltpu.VMEM((half + RIM, state_columns), F32)], 5,
+        functools.partial(earlier_kernel, len(early), len(early)), outs(first),
+        [pltpu.VMEM((first + RIM, state_columns), F32)], 5,
         *early_on, partial, far_state, rim, late_state, pair_late, conv_w, rate, docs,
     )
 
@@ -485,7 +492,7 @@
         levels.append(level)
     fields = vmem_call(
         functools.partial(query_kernel, count), [like(tok_rows, width)] * 3,
-        [pltpu.VMEM((half + RIM, query_columns), F32)], 5,
+        [pltpu.VMEM((first + RIM, query_columns), F32)], 5,
         *early, *early_on, base_query, far_query, rim, late_query, conv_w,
         *earlier[:5], earlier[6], *later[:5], later[6],
     )
@@ -507,14 +514,18 @@
     near = to_sibling(normed)
     out_shape = like(tok_rows, w_out.shape[1])
     total = vmem_call(
-        functools.partial(out_kernel, 2, 0), out_shape, [], 2, index, normed, near, w_out
+        functools.partial(out_kernel, 2, 0, False), out_shape, [], 2, index, normed, near, w_out
     )
     far, total = after(far, total)
     far_on = [to_sibling(value) for value in far]
+    total = vmem_call(
+        functools.partial(out_kernel, len(far), 2, False), out_shape, [], 1,
+        index, *far, w_out, total,
+    )
     return vmem_call(
-        functools.partial(out_kernel, count, 2), out_shape,
-        [pltpu.VMEM(out_shape.shape, F32), pltpu.SemaphoreType.DMA((tok_rows // CHUNK,))], 2,
-        index, *far, *far_on, w_out, total, any_out=True,
+        functools.partial(out_kernel, len(far), 2 + len(far), True), out_shape,
+        [pltpu.VMEM(out_shape.shape, F32), pltpu.SemaphoreType.DMA((tok_rows // CHUNK,))], 1,
+        index, *far_on, w_out, total, any_out=True,
     )
 
 

time: 67.8 us -> 75.3 us (1.11)
  waiting for transfers between devices: 22.9 us -> 29.7 us
  local copies, waits for them, and re-layouts: 5.52 us -> 6.58 us
    ppermute x3, waiting for transfers between devices: 14 us -> 21.3 us  [to_chips(): lax.ppermute(value, 'head', [(source, (source + 2 * step) % count) for so...]
    ppermute x3, starting transfers between devices: 5.91 us -> 4.24 us  [to_chips(): lax.ppermute(value, 'head', [(source, (source + 2 * step) % count) for so...]
    slice x1 -> x2, local copies, waits for them, and re-layouts: 1.09 us -> 2.15 us  [the longest x1 1.17 us: shards(): early = to_chips(early_rows[:cut])]
    pallas_call x10 -> x11, Pallas kernels: 20 us -> 19.9 us  [vmem_call(): pl.pallas_call(kernel, out_shape=outs, in_specs=[free if spot in any_in e...]
  transfers between devices with their start and end apart: 13 -> 13, of which waited for: 7 -> 7; matrix products, arithmetic and copies ran while one was open for 2% -> 3% of each run, Pallas kernels for 19% -> 17%
where the time goes in v7:
time: 75.3 us; the launch traced here: 75 us
  waiting for transfers between devices  29.7 us (39%)
  Pallas kernels  19.9 us (26%)
  starting transfers between devices  17.7 us (24%)
  local copies, waits for them, and re-layouts  6.58 us (9%)
  between operations  1.01 us (1%)
    ppermute x3, waiting for transfers between devices, to_chips(): lax.ppermute(value, 'head', [(source, (source + 2 * step) % count) for so...  21.3 us
    pallas_call x11, Pallas kernels, vmem_call(): pl.pallas_call(kernel, out_shape=outs, in_specs=[free if spot in any_in e...  19.9 us
    ppermute x3, waiting for transfers between devices, shards(): lax.ppermute(pair, 'ctx', [(source, source ^ mask << bit) for source in r...  5.5 us
    ppermute x1, starting transfers between devices, shards(): lax.ppermute(pair if carry else pair[1], 'ctx', [(source, source + reach)...  5.38 us
    unnamed x14, local copies, waits for them, and re-layouts  4.34 us
    ppermute x3, starting transfers between devices, to_chips(): lax.ppermute(value, 'head', [(source, (source + 2 * step) % count) for so...  4.24 us
    ppermute x3, starting transfers between devices, shards(): lax.ppermute(pair, 'ctx', [(source, source ^ mask << bit) for source in r...  3.89 us
    ppermute x1, starting transfers between devices, shards(): lax.ppermute(rim, 'ctx', [(source, source + 1) for source in range(blocks...  3.62 us
  transfers between devices with their start and end apart: 13, of which 7 were waited for; matrix products, arithmetic and copies ran while one was open for 3% of the time, Pallas kernels for 17%

profile of v7, /device:TPU:0, one launch (start us, length us, event | category | flops | bytes accessed | tf_op | source)
XLA Modules:
  0.0 75.0 jit_solution(4090601276345638109)
XLA Ops:
  0.0 0.5 collective-permute-start.2
  0.5 1.0 %slice.6 = f32[144,512]{1,0:T(8,128)S(1)} slice(f32[512,512]{1,0:T(8,128)} %own_ref.1), slice={[368:512], [0:512]} | slice | bytes 589824 | tf_op jit(solution)/shard_map/slice | solution.py:428
  1.4 1.2 %slice.7 = f32[368,512]{1,0:T(8,128)S(1)} slice(f32[512,512]{1,0:T(8,128)} %own_ref.1), slice={[0:368], [0:512]} | slice | bytes 1507328 | tf_op jit(solution)/shard_map/slice | solution.py:430
  2.6 2.6 %collective-permute-start = (f32[368,512]{1,0:T(8,128)S(1)}, f32[368,512]{1,0:T(8,128)S(1)}, u32[]{:S(2)}, u32[]{:S(2)}) collective-permute-start(f32[368,512]{1,0:T(8,128)S(1)} %slice.7), channel_id=1, source_target_pairs={{0,2},{1,3},{2,0},{3,1},{4,6},{5,7},{6,4},{7,5},{8,10},{9,11},{10,... | collective-permute-start | bytes 2261000 | tf_op jit(solution)/shard_map/ppermute | solution.py:400
  5.3 0.1 stack.31.index_ref.bits_ref
  5.4 1.2 %copy-done = f32[512,512]{1,0:T(8,128)S(1)} copy-done((f32[512,512]{1,0:T(8,128)S(1)}, f32[512,512]{1,0:T(8,128)}, u32[]{:S(2)}) %copy-start) | copy-done | bytes 1048600
  6.6 2.2 %copy-done.1 = f32[2048,512]{1,0:T(8,128)S(1)} copy-done((f32[2048,512]{1,0:T(8,128)S(1)}, f32[2048,512]{1,0:T(8,128)}, u32[]{:S(2)}) %copy-start.1) | copy-done | bytes 4194328
  8.8 0.9 %copy-done.3 = f32[2048,9]{0,1:T(8,128)S(1)} copy-done((f32[2048,9]{0,1:T(8,128)S(1)}, f32[2048,9]{0,1:T(8,128)}, u32[]{:S(2)}) %copy-start.3) | copy-done | bytes 73752
  9.7 4.0 %shard_map.82 = (f32[512,384]{1,0:T(8,128)S(1)}, f32[512,256]{1,0:T(8,128)S(1)}, bf16[1024,768]{1,0:T(8,128)(2,1)S(1)}, bf16[1024,512]{1,0:T(8,128)(2,1)S(1)}) custom-call(s32[7]{0:T(128)S(1)} %stack.31.index_ref.bits_ref, f32[512,512]{1,0:T(8,128)S(1)} %copy-done, f32[512,512]{1,0:T(8,128)S(1)} %collective-permute-done.2.beside_ref, ...), custom_call_target="tpu_custom_call" | custom-call | flops 3000000000 | bytes 1048576 | tf_op jit(solution)/shard_map/pallas_call | solution.py:378
  13.7 15.3 %collective-permute-done.1.refs_0_ = f32[144,512]{1,0:T(8,128)S(1)} collective-permute-done((f32[144,512]{1,0:T(8,128)S(1)}, f32[144,512]{1,0:T(8,128)S(1)}, u32[]{:S(2)}, u32[]{:S(2)}) %collective-permute-start.1) | collective-permute-done | bytes 294944 | tf_op jit(solution)/shard_map/ppermute | solution.py:400
  29.7 0.9 %collective-permute-done.3.refs_1_ = f32[144,512]{1,0:T(8,128)S(1)} collective-permute-done((f32[144,512]{1,0:T(8,128)S(1)}, f32[144,512]{1,0:T(8,128)S(1)}, u32[]{:S(2)}, u32[]{:S(2)}) %collective-permute-start.3) | collective-permute-done | bytes 294944 | tf_op jit(solution)/shard_map/ppermute | solution.py:394
  30.6 0.8 %shard_map.83 = (f32[144,384]{1,0:T(8,128)S(1)}, f32[144,256]{1,0:T(8,128)S(1)}, f32[16,384]{1,0:T(8,128)S(1)}) custom-call(f32[144,512]{1,0:T(8,128)S(1)} %collective-permute-done.1.refs_0_, f32[144,512]{1,0:T(8,128)S(1)} %collective-permute-done.3.refs_1_, f32[512,384]{1,0:T(8,128)S(1)} %get-tuple-element.47.refs_2_.refs_1_, ...), custom_call_target="tpu_custom_call" | custom-call | flops 500000000 | bytes 1048576 | tf_op jit(solution)/shard_map/pallas_call | solution.py:378
  31.4 3.6 %collective-permute-start.4 = (f32[16,384]{1,0:T(8,128)S(1)}, f32[16,384]{1,0:T(8,128)S(1)}, u32[]{:S(2)}, u32[]{:S(2)}) collective-permute-start(f32[16,384]{1,0:T(8,128)S(1)} %get-tuple-element.53), channel_id=1, source_target_pairs={{0,4},{4,8},{8,12},{12,16},{16,20},{20,24},{24,28},{1,5},{5,9},{9,... | collective-permute-start | bytes 73736 | tf_op jit(solution)/shard_map/ppermute | solution.py:450
  35.1 2.3 %shard_map.84 = (f32[128,128]{1,0:T(8,128)S(1)}, f32[128,128]{1,0:T(8,128)S(1)}, f32[128,128]{1,0:T(8,128)S(1)}, f32[128,128]{1,0:T(8,128)S(1)}, f32[128,128]{1,...) custom-call(f32[144,384]{1,0:T(8,128)S(1)} %get-tuple-element.51.raw_ref.refs_4_,, ...), custom_call_target="tpu_custom_call" | custom-call | flops 500000000 | bytes 1048576 | tf_op jit(solution)/shard_map/pallas_call | solution.py:378
  37.5 0.7 shard_map.85.refs_1_
  38.2 1.6 %collective-permute-done.5.refs_0_.refs_1_ = f32[368,512]{1,0:T(8,128)S(1)} collective-permute-done((f32[368,512]{1,0:T(8,128)S(1)}, f32[368,512]{1,0:T(8,128)S(1)}, u32[]{:S(2)}, u32[]{:S(2)}) %collective-permute-start.5) | collective-permute-done | bytes 753696 | tf_op jit(solution)/shard_map/ppermute | solution.py:394
  39.7 3.7 %shard_map.86 = (f32[384,128]{1,0:T(8,128)S(1)}, f32[384,128]{1,0:T(8,128)S(1)}, f32[384,128]{1,0:T(8,128)S(1)}, f32[384,128]{1,0:T(8,128)S(1)}, f32[384,128]{1,...) custom-call(f32[368,512]{1,0:T(8,128)S(1)} %collective-permute-done.5.refs_0_.ref, ...), custom_call_target="tpu_custom_call" | custom-call | flops 5000000000 | bytes 1048576 | tf_op jit(solution)/shard_map/pallas_call | solution.py:378
  43.5 2.6 %collective-permute-start.8 = (f32[2,128,128]{2,1,0:T(8,128)S(1)}, f32[2,128,128]{2,1,0:T(8,128)S(1)}, u32[]{:S(2)}, u32[]{:S(2)}) collective-permute-start(f32[2,128,128]{2,1,0:T(8,128)S(1)} %get-tuple-element.75.own_ref), channel_id=1, source_target_pairs={{0,12},{4,8},{8,4},{12,0},{16,28},{20,24},{24,20},{28,16},{1,13},{... | collective-permute-start | bytes 393224 | tf_op jit(solution)/shard_map/ppermute | solution.py:479
  46.1 0.4 collective-permute-start.7
  46.5 0.8 %collective-permute-start.6 = (f32[2,128,128]{2,1,0:T(8,128)S(1)}, f32[2,128,128]{2,1,0:T(8,128)S(1)}, u32[]{:S(2)}, u32[]{:S(2)}) collective-permute-start(f32[2,128,128]{2,1,0:T(8,128)S(1)} %get-tuple-element.75.own_ref), channel_id=1, source_target_pairs={{0,4},{4,0},{8,12},{12,8},{16,20},{20,16},{24,28},{28,24},{1,5},{5... | collective-permute-start | bytes 393224 | tf_op jit(solution)/shard_map/ppermute | solution.py:479
  47.3 3.3 %collective-permute-done.8.three_ref = f32[2,128,128]{2,1,0:T(8,128)S(1)} collective-permute-done((f32[2,128,128]{2,1,0:T(8,128)S(1)}, f32[2,128,128]{2,1,0:T(8,128)S(1)}, u32[]{:S(2)}, u32[]{:S(2)}) %collective-permute-start.8) | collective-permute-done | bytes 131104 | tf_op jit(solution)/shard_map/ppermute | solution.py:479
  50.6 2.2 %collective-permute-done.7.two_ref = f32[2,128,128]{2,1,0:T(8,128)S(1)} collective-permute-done((f32[2,128,128]{2,1,0:T(8,128)S(1)}, f32[2,128,128]{2,1,0:T(8,128)S(1)}, u32[]{:S(2)}, u32[]{:S(2)}) %collective-permute-start.7) | collective-permute-done | bytes 131104 | tf_op jit(solution)/shard_map/ppermute | solution.py:479
  52.9 1.0 %shard_map.88 = (f32[128,128]{1,0:T(8,128)S(1)}, f32[2,128,128]{2,1,0:T(8,128)S(1)}, f32[128,128]{1,0:T(8,128)S(1)}) custom-call(s32[7]{0:T(128)S(1)} %stack.31.index_ref.bits_ref, f32[2,128,128]{2,1,0:T(8,128)S(1)} %get-tuple-element.75.own_ref, f32[2,128,128]{2,1,0:T(8,128)S(1)} %collective-permute-done.6.one_ref, ...), custom_call_target="tpu_custom_call" | custom-call | flops 1000000000 | bytes 1048576 | tf_op jit(solution)/shard_map/pallas_call | solution.py:378
  53.9 5.4 %collective-permute-start.9 = (f32[128,128]{1,0:T(8,128)S(1)}, f32[128,128]{1,0:T(8,128)S(1)}, u32[]{:S(2)}, u32[]{:S(2)}) collective-permute-start(f32[128,128]{1,0:T(8,128)S(1)} %get-tuple-element.78), channel_id=1, source_target_pairs={{0,16},{4,20},{8,24},{12,28},{1,17},{5,21},{9,25},{13,29},{2,18},{... | collective-permute-start | bytes 196616 | tf_op jit(solution)/shard_map/ppermute | solution.py:504
  59.3 2.8 %shard_map.87 = (f32[512,128]{1,0:T(8,128)S(1)}, f32[512,128]{1,0:T(8,128)S(1)}, f32[512,128]{1,0:T(8,128)S(1)}) custom-call(f32[368,512]{1,0:T(8,128)S(1)} %collective-permute-done.refs_0_, f32[368,512]{1,0:T(8,128)S(1)} %collective-permute-done.5.refs_0_.refs_1_, f32[512,256]{1,0:T(8,128)S(1)} %get-tuple-element.48.refs_3_.refs_2_, ...), custom_call_target="tpu_custom_call" | custom-call | flops 5000000000 | bytes 1048576 | tf_op jit(solution)/shard_map/pallas_call | solution.py:378
  62.1 0.6 shard_map.89.refs_0_
  62.7 1.6 %collective-permute-start.10 = (f32[512,128]{1,0:T(8,128)S(1)}, f32[512,128]{1,0:T(8,128)S(1)}, u32[]{:S(2)}, u32[]{:S(2)}) collective-permute-start(f32[512,128]{1,0:T(8,128)S(1)} %shard_map.89.refs_0_), channel_id=1, source_target_pairs={{0,2},{1,3},{2,0},{3,1},{4,6},{5,7},{6,4},{7,5},{8,10},{9,11},{10,... | collective-permute-start | bytes 786440 | tf_op jit(solution)/shard_map/ppermute | solution.py:400
  64.3 1.2 %shard_map.90.refs_2_ = f32[512,512]{1,0:T(8,128)S(1)} custom-call(s32[7]{0:T(128)S(1)} %stack.31.index_ref.bits_ref, f32[512,128]{1,0:T(8,128)S(1)} %shard_map.89.refs_0_, f32[512,128]{1,0:T(8,128)S(1)} %collective-permute-done.11.refs_1_, f32[512,512]{1,0:T(8,128)S(1)} %copy-done.2), custom_call_target="tpu_custom_call" | custom-call | flops 2000000000 | bytes 1048576 | tf_op jit(solution)/shard_map/pallas_call | solution.py:378
  65.5 6.0 %collective-permute-done.10.refs_0_ = f32[512,128]{1,0:T(8,128)S(1)} collective-permute-done((f32[512,128]{1,0:T(8,128)S(1)}, f32[512,128]{1,0:T(8,128)S(1)}, u32[]{:S(2)}, u32[]{:S(2)}) %collective-permute-start.10) | collective-permute-done | bytes 262176 | tf_op jit(solution)/shard_map/ppermute | solution.py:400
  71.5 1.1 %shard_map.91.refs_2_ = f32[512,512]{1,0:T(8,128)S(1)} custom-call(s32[7]{0:T(128)S(1)} %stack.31.index_ref.bits_ref, f32[512,128]{1,0:T(8,128)S(1)} %collective-permute-done.10.refs_0_, f32[512,512]{1,0:T(8,128)S(1)} %copy-done.2, f32[512,512]{1,0:T(8,128)S(1)} %shard_map.90.refs_2_), custom_call_target="tpu_custom_call" | custom-call | flops 1000000000 | bytes 1048576 | tf_op jit(solution)/shard_map/pallas_call | solution.py:378
  72.6 0.4 collective-permute-done.12.refs_0_
  73.0 1.8 %shard_map.92 = f32[512,512]{1,0:T(8,128)} custom-call(s32[7]{0:T(128)S(1)} %stack.31.index_ref.bits_ref, f32[512,128]{1,0:T(8,128)S(1)} %collective-permute-done.12.refs_0_, f32[512,512]{1,0:T(8,128)S(1)} %copy-done.2, f32[512,512]{1,0:T(8,128)S(1)} %shard_map.91.refs_2_), custom_call_target="tpu_custom_call" | custom-call | flops 1000000000 | bytes 1048576 | tf_op jit(solution)/shard_map/pallas_call | solution.py:378
  (22 shorter events, 0.3 us)
Async XLA Ops:
  0.0 5.4 %collective-permute-start.2 = (f32[512,512]{1,0:T(8,128)}, f32[512,512]{1,0:T(8,128)S(1)}, u32[]{:S(2)}, u32[]{:S(2)}) collective-permute-start(f32[512,512]{1,0:T(8,128)} %own_ref.1), channel_id=1, source_target_pairs={{0,1},{1,0},{2,3},{3,2},{4,5},{5,4},{6,7},{7,6},{8,9},{9,8},{10,11... | collective-permute-start | bytes 3145736 | tf_op jit(solution)/shard_map/ppermute | solution.py:394
  2.6 34.8 %collective-permute-start = (f32[368,512]{1,0:T(8,128)S(1)}, f32[368,512]{1,0:T(8,128)S(1)}, u32[]{:S(2)}, u32[]{:S(2)}) collective-permute-start(f32[368,512]{1,0:T(8,128)S(1)} %slice.7), channel_id=1, source_target_pairs={{0,2},{1,3},{2,0},{3,1},{4,6},{5,7},{6,4},{7,5},{8,10},{9,11},{10,... | collective-permute-start | bytes 2261000 | tf_op jit(solution)/shard_map/ppermute | solution.py:400
  5.2 23.8 %collective-permute-start.1 = (f32[144,512]{1,0:T(8,128)S(1)}, f32[144,512]{1,0:T(8,128)S(1)}, u32[]{:S(2)}, u32[]{:S(2)}) collective-permute-start(f32[144,512]{1,0:T(8,128)S(1)} %slice.6), channel_id=1, source_target_pairs={{0,2},{1,3},{2,0},{3,1},{4,6},{5,7},{6,4},{7,5},{8,10},{9,11},{10,... | collective-permute-start | bytes 884744 | tf_op jit(solution)/shard_map/ppermute | solution.py:400
  5.4 1.2 %copy-start = (f32[512,512]{1,0:T(8,128)S(1)}, f32[512,512]{1,0:T(8,128)}, u32[]{:S(2)}) copy-start(f32[512,512]{1,0:T(8,128)} %own_ref.1) | copy-start | bytes 3145732
  6.6 2.2 %copy-start.1 = (f32[2048,512]{1,0:T(8,128)S(1)}, f32[2048,512]{1,0:T(8,128)}, u32[]{:S(2)}) copy-start(f32[2048,512]{1,0:T(8,128)} %proj_ref.1) | copy-start | bytes 12582916
  8.8 0.9 %copy-start.3 = (f32[2048,9]{0,1:T(8,128)S(1)}, f32[2048,9]{0,1:T(8,128)}, u32[]{:S(2)}) copy-start(f32[2048,9]{0,1:T(8,128)} %param.10) | copy-start | bytes 221188
  13.7 21.4 %copy-start.4 = (f32[4,384]{1,0:T(4,128)S(1)}, f32[4,384]{1,0:T(4,128)}, u32[]{:S(2)}) copy-start(f32[4,384]{1,0:T(4,128)} %refs_6_.3) | copy-start | bytes 18436
  13.7 21.4 %copy-start.5 = (s32[512]{0:T(512)S(1)}, s32[512]{0:T(512)}, u32[]{:S(2)}) copy-start(s32[512]{0:T(512)} %param.13) | copy-start | bytes 6148
  29.0 1.6 %collective-permute-start.3 = (f32[144,512]{1,0:T(8,128)S(1)}, f32[144,512]{1,0:T(8,128)S(1)}, u32[]{:S(2)}, u32[]{:S(2)}) collective-permute-start(f32[144,512]{1,0:T(8,128)S(1)} %collective-permute-done.1.refs_0_), channel_id=1, source_target_pairs={{0,1},{1,0},{2,3},{3,2},{4,5},{5,4},{6,7},{7,6},{8,9},{9,8},{10,11... | collective-permute-start | bytes 884744 | tf_op jit(solution)/shard_map/ppermute | solution.py:394
  31.4 6.0 %collective-permute-start.4 = (f32[16,384]{1,0:T(8,128)S(1)}, f32[16,384]{1,0:T(8,128)S(1)}, u32[]{:S(2)}, u32[]{:S(2)}) collective-permute-start(f32[16,384]{1,0:T(8,128)S(1)} %get-tuple-element.53), channel_id=1, source_target_pairs={{0,4},{4,8},{8,12},{12,16},{16,20},{20,24},{24,28},{1,5},{5,9},{9,... | collective-permute-start | bytes 73736 | tf_op jit(solution)/shard_map/ppermute | solution.py:450
  37.4 2.3 %collective-permute-start.5 = (f32[368,512]{1,0:T(8,128)S(1)}, f32[368,512]{1,0:T(8,128)S(1)}, u32[]{:S(2)}, u32[]{:S(2)}) collective-permute-start(f32[368,512]{1,0:T(8,128)S(1)} %collective-permute-done.refs_0_), channel_id=1, source_target_pairs={{0,1},{1,0},{2,3},{3,2},{4,5},{5,4},{6,7},{7,6},{8,9},{9,8},{10,11... | collective-permute-start | bytes 2261000 | tf_op jit(solution)/shard_map/ppermute | solution.py:394
  43.5 7.2 %collective-permute-start.8 = (f32[2,128,128]{2,1,0:T(8,128)S(1)}, f32[2,128,128]{2,1,0:T(8,128)S(1)}, u32[]{:S(2)}, u32[]{:S(2)}) collective-permute-start(f32[2,128,128]{2,1,0:T(8,128)S(1)} %get-tuple-element.75.own_ref), channel_id=1, source_target_pairs={{0,12},{4,8},{8,4},{12,0},{16,28},{20,24},{24,20},{28,16},{1,13},{... | collective-permute-start | bytes 393224 | tf_op jit(solution)/shard_map/ppermute | solution.py:479
  46.1 6.8 %collective-permute-start.7 = (f32[2,128,128]{2,1,0:T(8,128)S(1)}, f32[2,128,128]{2,1,0:T(8,128)S(1)}, u32[]{:S(2)}, u32[]{:S(2)}) collective-permute-start(f32[2,128,128]{2,1,0:T(8,128)S(1)} %get-tuple-element.75.own_ref), channel_id=1, source_target_pairs={{0,8},{4,12},{8,0},{12,4},{16,24},{20,28},{24,16},{28,20},{1,9},{5... | collective-permute-start | bytes 393224 | tf_op jit(solution)/shard_map/ppermute | solution.py:479
  46.5 6.3 %collective-permute-start.6 = (f32[2,128,128]{2,1,0:T(8,128)S(1)}, f32[2,128,128]{2,1,0:T(8,128)S(1)}, u32[]{:S(2)}, u32[]{:S(2)}) collective-permute-start(f32[2,128,128]{2,1,0:T(8,128)S(1)} %get-tuple-element.75.own_ref), channel_id=1, source_target_pairs={{0,4},{4,0},{8,12},{12,8},{16,20},{20,16},{24,28},{28,24},{1,5},{5... | collective-permute-start | bytes 393224 | tf_op jit(solution)/shard_map/ppermute | solution.py:479
  53.9 8.2 %collective-permute-start.9 = (f32[128,128]{1,0:T(8,128)S(1)}, f32[128,128]{1,0:T(8,128)S(1)}, u32[]{:S(2)}, u32[]{:S(2)}) collective-permute-start(f32[128,128]{1,0:T(8,128)S(1)} %get-tuple-element.78), channel_id=1, source_target_pairs={{0,16},{4,20},{8,24},{12,28},{1,17},{5,21},{9,25},{13,29},{2,18},{... | collective-permute-start | bytes 196616 | tf_op jit(solution)/shard_map/ppermute | solution.py:504
  59.3 2.8 %copy-start.6 = (f32[128]{0:T(128)S(1)}, f32[128]{0:T(128)}, u32[]{:S(2)}) copy-start(f32[128]{0:T(128)} %param.14) | copy-start | bytes 1540
  59.3 5.0 %copy-start.2 = (f32[512,512]{1,0:T(8,128)S(1)}, f32[512,512]{1,0:T(8,128)}, u32[]{:S(2)}) copy-start(f32[512,512]{1,0:T(8,128)} %refs_1_.3) | copy-start | bytes 3145732
  62.7 1.7 %collective-permute-start.11 = (f32[512,128]{1,0:T(8,128)S(1)}, f32[512,128]{1,0:T(8,128)S(1)}, u32[]{:S(2)}, u32[]{:S(2)}) collective-permute-start(f32[512,128]{1,0:T(8,128)S(1)} %shard_map.89.refs_0_), channel_id=1, source_target_pairs={{0,1},{1,0},{2,3},{3,2},{4,5},{5,4},{6,7},{7,6},{8,9},{9,8},{10,11... | collective-permute-start | bytes 786440 | tf_op jit(solution)/shard_map/ppermute | solution.py:394
  62.7 8.7 %collective-permute-start.10 = (f32[512,128]{1,0:T(8,128)S(1)}, f32[512,128]{1,0:T(8,128)S(1)}, u32[]{:S(2)}, u32[]{:S(2)}) collective-permute-start(f32[512,128]{1,0:T(8,128)S(1)} %shard_map.89.refs_0_), channel_id=1, source_target_pairs={{0,2},{1,3},{2,0},{3,1},{4,6},{5,7},{6,4},{7,5},{8,10},{9,11},{10,... | collective-permute-start | bytes 786440 | tf_op jit(solution)/shard_map/ppermute | solution.py:400
  71.5 1.5 %collective-permute-start.12 = (f32[512,128]{1,0:T(8,128)S(1)}, f32[512,128]{1,0:T(8,128)S(1)}, u32[]{:S(2)}, u32[]{:S(2)}) collective-permute-start(f32[512,128]{1,0:T(8,128)S(1)} %collective-permute-done.10.refs_0_), channel_id=1, source_target_pairs={{0,1},{1,0},{2,3},{3,2},{4,5},{5,4},{6,7},{7,6},{8,9},{9,8},{10,11... | collective-permute-start | bytes 786440 | tf_op jit(solution)/shard_map/ppermute | solution.py:394

commit v8 on v7

--- a/solution.py
+++ b/solution.py
@@ -122,12 +122,16 @@
         split(source, far_state_ref, far_query_ref, (source - 2) * depth)
 
 
-def late_kernel(count, begin, *refs):
-    base_state, base_query, far_state, far_query, state_ref, query_ref, rim_ref = refs[count:]
-    pieces = [ref[...] for ref in refs[:count]]
+def late_kernel(count, segments, *refs):
+    begin = segments[0].start
+    held, refs = refs[: count * len(segments)], refs[count * len(segments) :]
+    base_state, base_query, far_state, far_query, state_ref, query_ref, rim_ref = refs
     width = base_query.shape[1] // 2
-    state_ref[...] = add_products(base_state[begin:, :], pieces, far_state, 0)
-    query_ref[...] = add_products(base_query[begin:, :], pieces, far_query, 0)
+    for turn, rows in enumerate(segments):
+        pieces = [ref[...] for ref in held[turn * count : (turn + 1) * count]]
+        out = slice(rows.start - begin, rows.stop - begin)
+        state_ref[out, :] = add_products(base_state[rows, :], pieces, far_state, 0)
+        query_ref[out, :] = add_products(base_query[rows, :], pieces, far_query, 0)
     last = state_ref.shape[0] - RIM
     rim_ref[:, :width] = query_ref[last:, :width]
     rim_ref[:, width:] = state_ref[last:, : 2 * width]
@@ -423,12 +427,14 @@
     like = lambda *shape: jax.ShapeDtypeStruct(shape, F32)
     parts = lambda *shape: jax.ShapeDtypeStruct(shape, BF16)
 
-    first = tok_rows - CHUNK
+    first = tok_rows // 2
     cut = first - RIM
-    late_rows, early_rows = after(tokens[cut:], tokens)
-    late = to_chips(late_rows)
+    middle = tok_rows - CHUNK - RIM
+    segments = (slice(cut, middle), slice(middle, tok_rows))
+    late = [to_chips(tokens[rows]) for rows in segments]
+    beside = to_sibling(tokens)
+    early_rows, beside = after(tokens, beside)
     early = to_chips(early_rows[:cut])
-    beside = to_sibling(tokens)
     base_state, base_query, far_state, far_query = vmem_call(
         base_kernel,
         [like(tok_rows, state_columns), like(tok_rows, query_columns),
@@ -440,12 +446,13 @@
         3, index, tokens, beside, w_mix.T, w_proj, any_in=(4,),
     )
     late, far_state = after(late, far_state)
-    late_on = [to_sibling(value) for value in late]
+    late_on = [[to_sibling(value) for value in values] for values in late]
+    arrived = [value for pair in zip(late, late_on) for values in pair for value in values]
     late_state, late_query, rim = vmem_call(
-        functools.partial(late_kernel, count, cut),
+        functools.partial(late_kernel, count, segments),
         [like(tok_rows - cut, state_columns), like(tok_rows - cut, query_columns),
          like(RIM, 3 * width)],
-        [], 0.5, *late, *late_on, base_state, base_query, far_state, far_query,
+        [], 0.5, *arrived, base_state, base_query, far_state, far_query,
     )
     rim = lax.ppermute(rim, "ctx", [(source, source + 1) for source in range(blocks - 1)])
     docs = doc_start.reshape(tok_rows // CHUNK, CHUNK)

time: 75.3 us -> 64 us (0.85)
  waiting for transfers between devices: 29.7 us -> 15.8 us
  starting transfers between devices: 17.7 us -> 19.4 us
  local copies, waits for them, and re-layouts: 6.58 us -> 7.44 us
    ppermute x3 -> x4, waiting for transfers between devices: 21.3 us -> 7.15 us  [to_chips(): lax.ppermute(value, 'head', [(source, (source + 2 * step) % count) for so...]
    ppermute x3 -> x4, starting transfers between devices: 4.24 us -> 6.3 us  [to_chips(): lax.ppermute(value, 'head', [(source, (source + 2 * step) % count) for so...]
    slice x1 -> x2, local copies, waits for them, and re-layouts: 0.98 us -> 1.95 us  [shards(): late = [to_chips(tokens[rows]) for rows in segments]]
    ppermute x5 -> x6, waiting for transfers between devices: 2.91 us -> 2.59 us  [to_sibling(): lax.ppermute(value, 'head', [(source, source ^ 1) for source in range(cou...]
  transfers between devices with their start and end apart: 13 -> 15, of which waited for: 7 -> 8; matrix products, arithmetic and copies ran while one was open for 3% -> 5% of each run, Pallas kernels for 17% -> 21%
where the time goes in v8:
time: 64 us; the launch traced here: 63.7 us
  Pallas kernels  20.1 us (31%)
  starting transfers between devices  19.4 us (30%)
  waiting for transfers between devices  15.8 us (25%)
  local copies, waits for them, and re-layouts  7.44 us (12%)
  between operations  1.02 us (2%)
    pallas_call x11, Pallas kernels, vmem_call(): pl.pallas_call(kernel, out_shape=outs, in_specs=[free if spot in any_in e...  20.1 us
    ppermute x4, waiting for transfers between devices, to_chips(): lax.ppermute(value, 'head', [(source, (source + 2 * step) % count) for so...  7.15 us
    ppermute x4, starting transfers between devices, to_chips(): lax.ppermute(value, 'head', [(source, (source + 2 * step) % count) for so...  6.3 us
    ppermute x3, waiting for transfers between devices, shards(): lax.ppermute(pair, 'ctx', [(source, source ^ mask << bit) for source in r...  6.01 us
    ppermute x1, starting transfers between devices, shards(): lax.ppermute(pair if carry else pair[1], 'ctx', [(source, source + reach)...  4.67 us
    unnamed x14, local copies, waits for them, and re-layouts  4.34 us
    ppermute x1, starting transfers between devices, shards(): lax.ppermute(rim, 'ctx', [(source, source + 1) for source in range(blocks...  3.81 us
    ppermute x3, starting transfers between devices, shards(): lax.ppermute(pair, 'ctx', [(source, source ^ mask << bit) for source in r...  3.55 us
  transfers between devices with their start and end apart: 15, of which 8 were waited for; matrix products, arithmetic and copies ran while one was open for 5% of the time, Pallas kernels for 21%

profile of v8, /device:TPU:0, one launch (start us, length us, event | category | flops | bytes accessed | tf_op | source)
XLA Modules:
  0.0 63.7 jit_solution(16932299738394312138)
XLA Ops:
  0.0 0.5 collective-permute-start
  0.5 1.0 %slice.11 = f32[144,512]{1,0:T(8,128)S(1)} slice(f32[512,512]{1,0:T(8,128)} %own_ref.1), slice={[368:512], [0:512]} | slice | bytes 589824 | tf_op jit(solution)/shard_map/slice | solution.py:434
  1.4 2.6 %collective-permute-start.3 = (f32[144,512]{1,0:T(8,128)S(1)}, f32[144,512]{1,0:T(8,128)S(1)}, u32[]{:S(2)}, u32[]{:S(2)}) collective-permute-start(f32[144,512]{1,0:T(8,128)S(1)} %slice.11), channel_id=1, source_target_pairs={{0,2},{1,3},{2,0},{3,1},{4,6},{5,7},{6,4},{7,5},{8,10},{9,11},{10,... | collective-permute-start | bytes 884744 | tf_op jit(solution)/shard_map/ppermute | solution.py:404
  4.0 1.0 %slice.10 = f32[128,512]{1,0:T(8,128)S(1)} slice(f32[512,512]{1,0:T(8,128)} %own_ref.1), slice={[240:368], [0:512]} | slice | bytes 524288 | tf_op jit(solution)/shard_map/slice | solution.py:434
  5.2 1.1 %slice.9 = f32[240,512]{1,0:T(8,128)S(1)} slice(f32[512,512]{1,0:T(8,128)} %own_ref.1), slice={[0:240], [0:512]} | slice | bytes 983040 | tf_op jit(solution)/shard_map/slice | solution.py:437
  6.2 2.1 %collective-permute-start.1 = (f32[240,512]{1,0:T(8,128)S(1)}, f32[240,512]{1,0:T(8,128)S(1)}, u32[]{:S(2)}, u32[]{:S(2)}) collective-permute-start(f32[240,512]{1,0:T(8,128)S(1)} %slice.9), channel_id=1, source_target_pairs={{0,2},{1,3},{2,0},{3,1},{4,6},{5,7},{6,4},{7,5},{8,10},{9,11},{10,... | collective-permute-start | bytes 1474568 | tf_op jit(solution)/shard_map/ppermute | solution.py:404
  8.3 1.2 %copy-done = f32[512,512]{1,0:T(8,128)S(1)} copy-done((f32[512,512]{1,0:T(8,128)S(1)}, f32[512,512]{1,0:T(8,128)}, u32[]{:S(2)}) %copy-start) | copy-done | bytes 1048600
  9.5 2.2 %copy-done.1 = f32[2048,512]{1,0:T(8,128)S(1)} copy-done((f32[2048,512]{1,0:T(8,128)S(1)}, f32[2048,512]{1,0:T(8,128)}, u32[]{:S(2)}) %copy-start.1) | copy-done | bytes 4194328
  11.7 0.9 %copy-done.3 = f32[2048,9]{0,1:T(8,128)S(1)} copy-done((f32[2048,9]{0,1:T(8,128)S(1)}, f32[2048,9]{0,1:T(8,128)}, u32[]{:S(2)}) %copy-start.3) | copy-done | bytes 73752
  12.6 4.0 %shard_map.82 = (f32[512,384]{1,0:T(8,128)S(1)}, f32[512,256]{1,0:T(8,128)S(1)}, bf16[1024,768]{1,0:T(8,128)(2,1)S(1)}, bf16[1024,512]{1,0:T(8,128)(2,1)S(1)}) custom-call(s32[7]{0:T(128)S(1)} %stack.31.index_ref.bits_ref, f32[512,512]{1,0:T(8,128)S(1)} %copy-done, f32[512,512]{1,0:T(8,128)S(1)} %collective-permute-done.beside_ref, f32[9,2048]{1,0:T(8,128)S(1)} %bitcast.13, ...), custom_call_target="tpu_custom_call" | custom-call | flops 3000000000 | bytes 1048576 | tf_op jit(solution)/shard_map/pallas_call | solution.py:382
  16.6 0.9 %collective-permute-done.2.refs_0_ = f32[128,512]{1,0:T(8,128)S(1)} collective-permute-done((f32[128,512]{1,0:T(8,128)S(1)}, f32[128,512]{1,0:T(8,128)S(1)}, u32[]{:S(2)}, u32[]{:S(2)}) %collective-permute-start.2) | collective-permute-done | bytes 262176 | tf_op jit(solution)/shard_map/ppermute | solution.py:404
  17.5 0.5 collective-permute-start.4
  18.7 0.8 %collective-permute-done.4.refs_1_ = f32[128,512]{1,0:T(8,128)S(1)} collective-permute-done((f32[128,512]{1,0:T(8,128)S(1)}, f32[128,512]{1,0:T(8,128)S(1)}, u32[]{:S(2)}, u32[]{:S(2)}) %collective-permute-start.4) | collective-permute-done | bytes 262176 | tf_op jit(solution)/shard_map/ppermute | solution.py:398
  19.5 1.5 %shard_map.83 = (f32[272,384]{1,0:T(8,128)S(1)}, f32[272,256]{1,0:T(8,128)S(1)}, f32[16,384]{1,0:T(8,128)S(1)}) custom-call(f32[128,512]{1,0:T(8,128)S(1)} %collective-permute-done.2.refs_0_, f32[128,512]{1,0:T(8,128)S(1)} %collective-permute-done.4.refs_1_, f32[144,512]{1,0:T(8,128)S(1)} %collective-permute-done.3.refs_2_, ...), custom_call_target="tpu_custom_call" | custom-call | flops 500000000 | bytes 1048576 | tf_op jit(solution)/shard_map/pallas_call | solution.py:382
  20.9 3.8 %collective-permute-start.6 = (f32[16,384]{1,0:T(8,128)S(1)}, f32[16,384]{1,0:T(8,128)S(1)}, u32[]{:S(2)}, u32[]{:S(2)}) collective-permute-start(f32[16,384]{1,0:T(8,128)S(1)} %get-tuple-element.55), channel_id=1, source_target_pairs={{0,4},{4,8},{8,12},{12,16},{16,20},{20,24},{24,28},{1,5},{5,9},{9,... | collective-permute-start | bytes 73736 | tf_op jit(solution)/shard_map/ppermute | solution.py:457
  24.8 2.8 %shard_map.84 = (f32[256,128]{1,0:T(8,128)S(1)}, f32[256,128]{1,0:T(8,128)S(1)}, f32[256,128]{1,0:T(8,128)S(1)}, f32[256,128]{1,0:T(8,128)S(1)}, f32[256,128]{1,...) custom-call(f32[272,384]{1,0:T(8,128)S(1)} %get-tuple-element.53.raw_ref.refs_4_,, ...), custom_call_target="tpu_custom_call" | custom-call | flops 500000000 | bytes 1048576 | tf_op jit(solution)/shard_map/pallas_call | solution.py:382
  27.9 0.5 shard_map.85.refs_1_
  28.4 1.4 %collective-permute-done.7.refs_0_.refs_1_ = f32[240,512]{1,0:T(8,128)S(1)} collective-permute-done((f32[240,512]{1,0:T(8,128)S(1)}, f32[240,512]{1,0:T(8,128)S(1)}, u32[]{:S(2)}, u32[]{:S(2)}) %collective-permute-start.7) | collective-permute-done | bytes 491552 | tf_op jit(solution)/shard_map/ppermute | solution.py:398
  29.7 3.3 %shard_map.86 = (f32[256,128]{1,0:T(8,128)S(1)}, f32[256,128]{1,0:T(8,128)S(1)}, f32[256,128]{1,0:T(8,128)S(1)}, f32[256,128]{1,0:T(8,128)S(1)}, f32[256,128]{1,...) custom-call(f32[240,512]{1,0:T(8,128)S(1)} %collective-permute-done.7.refs_0_.ref, ...), custom_call_target="tpu_custom_call" | custom-call | flops 5000000000 | bytes 1048576 | tf_op jit(solution)/shard_map/pallas_call | solution.py:382
  33.0 2.8 %collective-permute-start.10 = (f32[2,128,128]{2,1,0:T(8,128)S(1)}, f32[2,128,128]{2,1,0:T(8,128)S(1)}, u32[]{:S(2)}, u32[]{:S(2)}) collective-permute-start(f32[2,128,128]{2,1,0:T(8,128)S(1)} %get-tuple-element.77.own_ref), channel_id=1, source_target_pairs={{0,12},{4,8},{8,4},{12,0},{16,28},{20,24},{24,20},{28,16},{1,13},{... | collective-permute-start | bytes 393224 | tf_op jit(solution)/shard_map/ppermute | solution.py:486
  35.8 0.5 collective-permute-start.9
  36.6 3.7 %collective-permute-done.10.three_ref = f32[2,128,128]{2,1,0:T(8,128)S(1)} collective-permute-done((f32[2,128,128]{2,1,0:T(8,128)S(1)}, f32[2,128,128]{2,1,0:T(8,128)S(1)}, u32[]{:S(2)}, u32[]{:S(2)}) %collective-permute-start.10) | collective-permute-done | bytes 131104 | tf_op jit(solution)/shard_map/ppermute | solution.py:486
  40.3 2.3 %collective-permute-done.9.two_ref = f32[2,128,128]{2,1,0:T(8,128)S(1)} collective-permute-done((f32[2,128,128]{2,1,0:T(8,128)S(1)}, f32[2,128,128]{2,1,0:T(8,128)S(1)}, u32[]{:S(2)}, u32[]{:S(2)}) %collective-permute-start.9) | collective-permute-done | bytes 131104 | tf_op jit(solution)/shard_map/ppermute | solution.py:486
  42.6 1.0 %shard_map.88 = (f32[128,128]{1,0:T(8,128)S(1)}, f32[2,128,128]{2,1,0:T(8,128)S(1)}, f32[128,128]{1,0:T(8,128)S(1)}) custom-call(s32[7]{0:T(128)S(1)} %stack.31.index_ref.bits_ref, f32[2,128,128]{2,1,0:T(8,128)S(1)} %get-tuple-element.77.own_ref, f32[2,128,128]{2,1,0:T(8,128)S(1)} %collective-permute-done.8.one_ref, ...), custom_call_target="tpu_custom_call" | custom-call | flops 1000000000 | bytes 1048576 | tf_op jit(solution)/shard_map/pallas_call | solution.py:382
  43.6 4.7 %collective-permute-start.11 = (f32[128,128]{1,0:T(8,128)S(1)}, f32[128,128]{1,0:T(8,128)S(1)}, u32[]{:S(2)}, u32[]{:S(2)}) collective-permute-start(f32[128,128]{1,0:T(8,128)S(1)} %get-tuple-element.80), channel_id=1, source_target_pairs={{0,16},{4,20},{8,24},{12,28},{1,17},{5,21},{9,25},{13,29},{2,18},{... | collective-permute-start | bytes 196616 | tf_op jit(solution)/shard_map/ppermute | solution.py:511
  48.3 2.4 %shard_map.87 = (f32[512,128]{1,0:T(8,128)S(1)}, f32[512,128]{1,0:T(8,128)S(1)}, f32[512,128]{1,0:T(8,128)S(1)}) custom-call(f32[240,512]{1,0:T(8,128)S(1)} %collective-permute-done.1.refs_0_, f32[240,512]{1,0:T(8,128)S(1)} %collective-permute-done.7.refs_0_.refs_1_, f32[512,256]{1,0:T(8,128)S(1)} %get-tuple-element.50.refs_5_.refs_2_, ...), custom_call_target="tpu_custom_call" | custom-call | flops 5000000000 | bytes 1048576 | tf_op jit(solution)/shard_map/pallas_call | solution.py:382
  50.8 0.6 shard_map.89.refs_0_
  51.4 1.6 %collective-permute-start.12 = (f32[512,128]{1,0:T(8,128)S(1)}, f32[512,128]{1,0:T(8,128)S(1)}, u32[]{:S(2)}, u32[]{:S(2)}) collective-permute-start(f32[512,128]{1,0:T(8,128)S(1)} %shard_map.89.refs_0_), channel_id=1, source_target_pairs={{0,2},{1,3},{2,0},{3,1},{4,6},{5,7},{6,4},{7,5},{8,10},{9,11},{10,... | collective-permute-start | bytes 786440 | tf_op jit(solution)/shard_map/ppermute | solution.py:404
  53.0 1.2 %shard_map.90.refs_2_ = f32[512,512]{1,0:T(8,128)S(1)} custom-call(s32[7]{0:T(128)S(1)} %stack.31.index_ref.bits_ref, f32[512,128]{1,0:T(8,128)S(1)} %shard_map.89.refs_0_, f32[512,128]{1,0:T(8,128)S(1)} %collective-permute-done.13.refs_1_, f32[512,512]{1,0:T(8,128)S(1)} %copy-done.2), custom_call_target="tpu_custom_call" | custom-call | flops 2000000000 | bytes 1048576 | tf_op jit(solution)/shard_map/pallas_call | solution.py:382
  54.2 6.0 %collective-permute-done.12.refs_0_ = f32[512,128]{1,0:T(8,128)S(1)} collective-permute-done((f32[512,128]{1,0:T(8,128)S(1)}, f32[512,128]{1,0:T(8,128)S(1)}, u32[]{:S(2)}, u32[]{:S(2)}) %collective-permute-start.12) | collective-permute-done | bytes 262176 | tf_op jit(solution)/shard_map/ppermute | solution.py:404
  60.1 1.1 %shard_map.91.refs_2_ = f32[512,512]{1,0:T(8,128)S(1)} custom-call(s32[7]{0:T(128)S(1)} %stack.31.index_ref.bits_ref, f32[512,128]{1,0:T(8,128)S(1)} %collective-permute-done.12.refs_0_, f32[512,512]{1,0:T(8,128)S(1)} %copy-done.2, f32[512,512]{1,0:T(8,128)S(1)} %shard_map.90.refs_2_), custom_call_target="tpu_custom_call" | custom-call | flops 1000000000 | bytes 1048576 | tf_op jit(solution)/shard_map/pallas_call | solution.py:382
  61.7 1.8 %shard_map.92 = f32[512,512]{1,0:T(8,128)} custom-call(s32[7]{0:T(128)S(1)} %stack.31.index_ref.bits_ref, f32[512,128]{1,0:T(8,128)S(1)} %collective-permute-done.14.refs_0_, f32[512,512]{1,0:T(8,128)S(1)} %copy-done.2, f32[512,512]{1,0:T(8,128)S(1)} %shard_map.91.refs_2_), custom_call_target="tpu_custom_call" | custom-call | flops 1000000000 | bytes 1048576 | tf_op jit(solution)/shard_map/pallas_call | solution.py:382
  (27 shorter events, 1.3 us)
Async XLA Ops:
  0.0 5.2 %collective-permute-start = (f32[512,512]{1,0:T(8,128)}, f32[512,512]{1,0:T(8,128)S(1)}, u32[]{:S(2)}, u32[]{:S(2)}) collective-permute-start(f32[512,512]{1,0:T(8,128)} %own_ref.1), channel_id=1, source_target_pairs={{0,1},{1,0},{2,3},{3,2},{4,5},{5,4},{6,7},{7,6},{8,9},{9,8},{10,11... | collective-permute-start | bytes 3145736 | tf_op jit(solution)/shard_map/ppermute | solution.py:398
  1.4 16.1 %collective-permute-start.3 = (f32[144,512]{1,0:T(8,128)S(1)}, f32[144,512]{1,0:T(8,128)S(1)}, u32[]{:S(2)}, u32[]{:S(2)}) collective-permute-start(f32[144,512]{1,0:T(8,128)S(1)} %slice.11), channel_id=1, source_target_pairs={{0,2},{1,3},{2,0},{3,1},{4,6},{5,7},{6,4},{7,5},{8,10},{9,11},{10,... | collective-permute-start | bytes 884744 | tf_op jit(solution)/shard_map/ppermute | solution.py:404
  5.0 12.5 %collective-permute-start.2 = (f32[128,512]{1,0:T(8,128)S(1)}, f32[128,512]{1,0:T(8,128)S(1)}, u32[]{:S(2)}, u32[]{:S(2)}) collective-permute-start(f32[128,512]{1,0:T(8,128)S(1)} %slice.10), channel_id=1, source_target_pairs={{0,2},{1,3},{2,0},{3,1},{4,6},{5,7},{6,4},{7,5},{8,10},{9,11},{10,... | collective-permute-start | bytes 786440 | tf_op jit(solution)/shard_map/ppermute | solution.py:404
  6.2 21.6 %collective-permute-start.1 = (f32[240,512]{1,0:T(8,128)S(1)}, f32[240,512]{1,0:T(8,128)S(1)}, u32[]{:S(2)}, u32[]{:S(2)}) collective-permute-start(f32[240,512]{1,0:T(8,128)S(1)} %slice.9), channel_id=1, source_target_pairs={{0,2},{1,3},{2,0},{3,1},{4,6},{5,7},{6,4},{7,5},{8,10},{9,11},{10,... | collective-permute-start | bytes 1474568 | tf_op jit(solution)/shard_map/ppermute | solution.py:404
  8.3 1.2 %copy-start = (f32[512,512]{1,0:T(8,128)S(1)}, f32[512,512]{1,0:T(8,128)}, u32[]{:S(2)}) copy-start(f32[512,512]{1,0:T(8,128)} %own_ref.1) | copy-start | bytes 3145732
  9.5 2.2 %copy-start.1 = (f32[2048,512]{1,0:T(8,128)S(1)}, f32[2048,512]{1,0:T(8,128)}, u32[]{:S(2)}) copy-start(f32[2048,512]{1,0:T(8,128)} %proj_ref.1) | copy-start | bytes 12582916
  11.7 0.9 %copy-start.3 = (f32[2048,9]{0,1:T(8,128)S(1)}, f32[2048,9]{0,1:T(8,128)}, u32[]{:S(2)}) copy-start(f32[2048,9]{0,1:T(8,128)} %param.10) | copy-start | bytes 221188
  16.6 8.2 %copy-start.4 = (f32[4,384]{1,0:T(4,128)S(1)}, f32[4,384]{1,0:T(4,128)}, u32[]{:S(2)}) copy-start(f32[4,384]{1,0:T(4,128)} %refs_6_.3) | copy-start | bytes 18436
  16.6 8.2 %copy-start.5 = (s32[512]{0:T(512)S(1)}, s32[512]{0:T(512)}, u32[]{:S(2)}) copy-start(s32[512]{0:T(512)} %param.13) | copy-start | bytes 6148
  17.5 2.0 %collective-permute-start.5 = (f32[144,512]{1,0:T(8,128)S(1)}, f32[144,512]{1,0:T(8,128)S(1)}, u32[]{:S(2)}, u32[]{:S(2)}) collective-permute-start(f32[144,512]{1,0:T(8,128)S(1)} %collective-permute-done.3.refs_2_), channel_id=1, source_target_pairs={{0,1},{1,0},{2,3},{3,2},{4,5},{5,4},{6,7},{7,6},{8,9},{9,8},{10,11... | collective-permute-start | bytes 884744 | tf_op jit(solution)/shard_map/ppermute | solution.py:398
  17.5 2.0 %collective-permute-start.4 = (f32[128,512]{1,0:T(8,128)S(1)}, f32[128,512]{1,0:T(8,128)S(1)}, u32[]{:S(2)}, u32[]{:S(2)}) collective-permute-start(f32[128,512]{1,0:T(8,128)S(1)} %collective-permute-done.2.refs_0_), channel_id=1, source_target_pairs={{0,1},{1,0},{2,3},{3,2},{4,5},{5,4},{6,7},{7,6},{8,9},{9,8},{10,11... | collective-permute-start | bytes 786440 | tf_op jit(solution)/shard_map/ppermute | solution.py:398
  20.9 6.6 %collective-permute-start.6 = (f32[16,384]{1,0:T(8,128)S(1)}, f32[16,384]{1,0:T(8,128)S(1)}, u32[]{:S(2)}, u32[]{:S(2)}) collective-permute-start(f32[16,384]{1,0:T(8,128)S(1)} %get-tuple-element.55), channel_id=1, source_target_pairs={{0,4},{4,8},{8,12},{12,16},{16,20},{20,24},{24,28},{1,5},{5,9},{9,... | collective-permute-start | bytes 73736 | tf_op jit(solution)/shard_map/ppermute | solution.py:457
  27.9 1.9 %collective-permute-start.7 = (f32[240,512]{1,0:T(8,128)S(1)}, f32[240,512]{1,0:T(8,128)S(1)}, u32[]{:S(2)}, u32[]{:S(2)}) collective-permute-start(f32[240,512]{1,0:T(8,128)S(1)} %collective-permute-done.1.refs_0_), channel_id=1, source_target_pairs={{0,1},{1,0},{2,3},{3,2},{4,5},{5,4},{6,7},{7,6},{8,9},{9,8},{10,11... | collective-permute-start | bytes 1474568 | tf_op jit(solution)/shard_map/ppermute | solution.py:398
  33.0 7.3 %collective-permute-start.10 = (f32[2,128,128]{2,1,0:T(8,128)S(1)}, f32[2,128,128]{2,1,0:T(8,128)S(1)}, u32[]{:S(2)}, u32[]{:S(2)}) collective-permute-start(f32[2,128,128]{2,1,0:T(8,128)S(1)} %get-tuple-element.77.own_ref), channel_id=1, source_target_pairs={{0,12},{4,8},{8,4},{12,0},{16,28},{20,24},{24,20},{28,16},{1,13},{... | collective-permute-start | bytes 393224 | tf_op jit(solution)/shard_map/ppermute | solution.py:486
  35.8 6.8 %collective-permute-start.9 = (f32[2,128,128]{2,1,0:T(8,128)S(1)}, f32[2,128,128]{2,1,0:T(8,128)S(1)}, u32[]{:S(2)}, u32[]{:S(2)}) collective-permute-start(f32[2,128,128]{2,1,0:T(8,128)S(1)} %get-tuple-element.77.own_ref), channel_id=1, source_target_pairs={{0,8},{4,12},{8,0},{12,4},{16,24},{20,28},{24,16},{28,20},{1,9},{5... | collective-permute-start | bytes 393224 | tf_op jit(solution)/shard_map/ppermute | solution.py:486
  36.3 6.3 %collective-permute-start.8 = (f32[2,128,128]{2,1,0:T(8,128)S(1)}, f32[2,128,128]{2,1,0:T(8,128)S(1)}, u32[]{:S(2)}, u32[]{:S(2)}) collective-permute-start(f32[2,128,128]{2,1,0:T(8,128)S(1)} %get-tuple-element.77.own_ref), channel_id=1, source_target_pairs={{0,4},{4,0},{8,12},{12,8},{16,20},{20,16},{24,28},{28,24},{1,5},{5... | collective-permute-start | bytes 393224 | tf_op jit(solution)/shard_map/ppermute | solution.py:486
  43.6 7.1 %collective-permute-start.11 = (f32[128,128]{1,0:T(8,128)S(1)}, f32[128,128]{1,0:T(8,128)S(1)}, u32[]{:S(2)}, u32[]{:S(2)}) collective-permute-start(f32[128,128]{1,0:T(8,128)S(1)} %get-tuple-element.80), channel_id=1, source_target_pairs={{0,16},{4,20},{8,24},{12,28},{1,17},{5,21},{9,25},{13,29},{2,18},{... | collective-permute-start | bytes 196616 | tf_op jit(solution)/shard_map/ppermute | solution.py:511
  48.3 2.4 %copy-start.6 = (f32[128]{0:T(128)S(1)}, f32[128]{0:T(128)}, u32[]{:S(2)}) copy-start(f32[128]{0:T(128)} %param.14) | copy-start | bytes 1540
  48.3 4.7 %copy-start.2 = (f32[512,512]{1,0:T(8,128)S(1)}, f32[512,512]{1,0:T(8,128)}, u32[]{:S(2)}) copy-start(f32[512,512]{1,0:T(8,128)} %refs_1_.3) | copy-start | bytes 3145732
  51.3 1.7 %collective-permute-start.13 = (f32[512,128]{1,0:T(8,128)S(1)}, f32[512,128]{1,0:T(8,128)S(1)}, u32[]{:S(2)}, u32[]{:S(2)}) collective-permute-start(f32[512,128]{1,0:T(8,128)S(1)} %shard_map.89.refs_0_), channel_id=1, source_target_pairs={{0,1},{1,0},{2,3},{3,2},{4,5},{5,4},{6,7},{7,6},{8,9},{9,8},{10,11... | collective-permute-start | bytes 786440 | tf_op jit(solution)/shard_map/ppermute | solution.py:398
  51.4 8.7 %collective-permute-start.12 = (f32[512,128]{1,0:T(8,128)S(1)}, f32[512,128]{1,0:T(8,128)S(1)}, u32[]{:S(2)}, u32[]{:S(2)}) collective-permute-start(f32[512,128]{1,0:T(8,128)S(1)} %shard_map.89.refs_0_), channel_id=1, source_target_pairs={{0,2},{1,3},{2,0},{3,1},{4,6},{5,7},{6,4},{7,5},{8,10},{9,11},{10,... | collective-permute-start | bytes 786440 | tf_op jit(solution)/shard_map/ppermute | solution.py:404
  60.1 1.5 %collective-permute-start.14 = (f32[512,128]{1,0:T(8,128)S(1)}, f32[512,128]{1,0:T(8,128)S(1)}, u32[]{:S(2)}, u32[]{:S(2)}) collective-permute-start(f32[512,128]{1,0:T(8,128)S(1)} %collective-permute-done.12.refs_0_), channel_id=1, source_target_pairs={{0,1},{1,0},{2,3},{3,2},{4,5},{5,4},{6,7},{7,6},{8,9},{9,8},{10,11... | collective-permute-start | bytes 786440 | tf_op jit(solution)/shard_map/ppermute | solution.py:398

commit v9 on v8

--- a/solution.py
+++ b/solution.py
@@ -327,11 +327,13 @@
     next_ref[...] = jnp.where(set_high, second[:, :width], carry)
 
 
-def mix_kernel(stages, single, carried_ref, local_ref, gate_ref, low_ref, high_ref, gain_ref, *refs):
+def mix_kernel(stages, single, bits_ref, carried_ref, local_ref, gate_ref, low_ref, high_ref, gain_ref, *refs):
     states = [ref[spot] for ref in refs[:stages] for spot in range(ref.shape[0])]
     if single:
-        states.append(product(refs[stages][...], refs[stages + 1][...]))
-    normed_ref = refs[-1]
+        carry_ref, other_ref = refs[stages : stages + 2]
+        upper = jnp.broadcast_to(bits_ref[single], other_ref.shape) == 1
+        states.append(product(carry_ref[...], jnp.where(upper, other_ref[...], 0.0)))
+    outs = refs[stages + (2 if single else 0) :]
     states = [right_parts(state) for state in states]
     carried = left_parts(carried_ref[...])
     weights = jnp.concatenate([low_ref[...], high_ref[...]], axis=0)
@@ -339,37 +341,70 @@
     for level, state in enumerate(states):
         mixed = mixed + weights[:, level + 3 : level + 4] * parts_dot(carried, state)
     scale = lax.rsqrt(jnp.mean(mixed * mixed, axis=1, keepdims=True) + 1e-05)
-    normed_ref[...] = mixed * scale * gain_ref[...] * gate_ref[...]
-
-
-def out_kernel(pieces, first, last, index_ref, *refs):
-    weight_ref = refs[pieces]
+    normed = mixed * scale * gain_ref[...] * gate_ref[...]
+    outs[0][...] = normed
+    base = 0
+    for out in outs[1:]:
+        out[...] = normed[base : base + out.shape[0]]
+        base += out.shape[0]
+
+
+def block_product(pieces, weight, rows):
+    parts = [halves(ref[rows, :]) for ref in pieces]
+    high, low = (jnp.concatenate(part, axis=1) for part in zip(*parts))
+    columns = weight.shape[1] // 2
+    both = jnp.dot(high, weight, preferred_element_type=F32)
+    rest = jnp.dot(low, weight[:, :columns], preferred_element_type=F32)
+    return (both[:, :columns] + both[:, columns:]) + rest
+
+
+def source_rows(index_ref, first, pieces, weight_ref):
     parts = []
-    for spot in range(pieces):
-        depth = refs[spot].shape[1]
+    for spot, piece in enumerate(pieces):
+        depth = piece.shape[1]
         rows = pl.ds(pl.multiple_of(index_ref[first + spot] * depth, depth), depth)
         parts.append(weight_ref[rows, :])
-    weight = left_parts(jnp.concatenate(parts, axis=0))
-    columns = weight.shape[1] // 2
-
-    def block(rows):
-        parts = [halves(ref[rows, :]) for ref in refs[:pieces]]
-        high, low = (jnp.concatenate(part, axis=1) for part in zip(*parts))
-        both = jnp.dot(high, weight, preferred_element_type=F32)
-        rest = jnp.dot(low, weight[:, :columns], preferred_element_type=F32)
-        return (both[:, :columns] + both[:, columns:]) + rest
-
-    blocks = [slice(base, base + CHUNK) for base in range(0, refs[0].shape[0], CHUNK)]
-    if not last:
-        for rows in blocks:
-            part = block(rows)
-            refs[-1][rows, :] = refs[pieces + 1][rows, :] + part if first else part
-        return
-    total_ref, out_ref, held, sems = refs[pieces + 1 :]
-    copies = []
-    for spot, rows in enumerate(blocks):
-        held[rows, :] = total_ref[rows, :] + block(rows)
-        copies.append(pltpu.make_async_copy(held.at[rows, :], out_ref.at[rows, :], sems.at[spot]))
+    return left_parts(jnp.concatenate(parts, axis=0))
+
+
+def row_blocks(rows):
+    return [slice(base, base + CHUNK) for base in range(0, rows, CHUNK)]
+
+
+def near_kernel(index_ref, own_ref, near_ref, weight_ref, low_ref, high_ref):
+    weight = source_rows(index_ref, 0, [own_ref, near_ref], weight_ref)
+    half = low_ref.shape[0]
+    for rows in row_blocks(half):
+        low_ref[rows, :] = block_product([own_ref, near_ref], weight, rows)
+        later = slice(half + rows.start, half + rows.stop)
+        high_ref[rows, :] = block_product([own_ref, near_ref], weight, later)
+
+
+def far_kernel(count, first, index_ref, *refs):
+    held, (weight_ref, total_ref, out_ref) = refs[:-3], refs[-3:]
+    weight = source_rows(index_ref, first, held[:count], weight_ref)
+    base = 0
+    for at in range(0, len(held), count):
+        pieces = held[at : at + count]
+        for rows in row_blocks(pieces[0].shape[0]):
+            out = slice(base + rows.start, base + rows.stop)
+            out_ref[out, :] = total_ref[out, :] + block_product(pieces, weight, rows)
+        base += pieces[0].shape[0]
+
+
+def last_kernel(count, first, index_ref, *refs):
+    pieces = refs[:count]
+    weight_ref, ready_ref, total_ref, out_ref, held, sems = refs[count:]
+    half = ready_ref.shape[0]
+    copies = [pltpu.make_async_copy(ready_ref, out_ref.at[:half, :], sems.at[0])]
+    copies[0].start()
+    weight = source_rows(index_ref, first, pieces, weight_ref)
+    for spot, rows in enumerate(row_blocks(total_ref.shape[0])):
+        held[rows, :] = total_ref[rows, :] + block_product(pieces, weight, rows)
+        out = slice(half + rows.start, half + rows.stop)
+        copies.append(
+            pltpu.make_async_copy(held.at[rows, :], out_ref.at[out, :], sems.at[spot + 1])
+        )
         copies[-1].start()
     for copy in copies:
         copy.wait()
@@ -510,29 +545,40 @@
             *(carry or [jnp.eye(width, dtype=F32)]),
             lax.ppermute(
                 pair if carry else pair[1],
-                "ctx", [(source, source + reach) for source in range(reach)],
+                "ctx", [(source, source ^ reach) for source in range(blocks)],
             ),
         ]
-    normed = vmem_call(
-        functools.partial(mix_kernel, len(levels), bool(single)), like(tok_rows, width), [], 1,
-        *fields, earlier[5], later[5], norm_gain[None, :], *levels, *single,
-    )
-    far = to_chips(normed)
+    half = tok_rows // 2
+    normed, *lows, high = vmem_call(
+        functools.partial(mix_kernel, len(levels), heads + bits - 1 if single else 0),
+        [like(tok_rows, width)] + [like(half // 2, width)] * 2 + [like(half, width)], [], 1,
+        index, *fields, earlier[5], later[5], norm_gain[None, :], *levels, *single,
+    )
+    columns = w_out.shape[1]
     near = to_sibling(normed)
-    out_shape = like(tok_rows, w_out.shape[1])
-    total = vmem_call(
-        functools.partial(out_kernel, 2, 0, False), out_shape, [], 2, index, normed, near, w_out
-    )
-    far, total = after(far, total)
-    far_on = [to_sibling(value) for value in far]
-    total = vmem_call(
-        functools.partial(out_kernel, len(far), 2, False), out_shape, [], 1,
-        index, *far, w_out, total,
+    far_lows = [to_chips(low) for low in lows]
+    high, near = after(high, near)
+    far_high = to_chips(high)
+    total_low, total_high = vmem_call(
+        near_kernel, [like(half, columns)] * 2, [], 2, index, normed, near, w_out
+    )
+    far_lows, total_low = after(far_lows, total_low)
+    far_lows_on = [[to_sibling(value) for value in values] for values in far_lows]
+    arrived = [value for pair in zip(far_lows, far_lows_on) for values in pair for value in values]
+    total_low = vmem_call(
+        functools.partial(far_kernel, count, 2), like(half, columns), [], 0.01,
+        index, *arrived, w_out, total_low,
+    )
+    far_high, total_low = after(far_high, total_low)
+    far_high_on = [to_sibling(value) for value in far_high]
+    total_high = vmem_call(
+        functools.partial(far_kernel, len(far_high), 2), like(half, columns), [], 1,
+        index, *far_high, w_out, total_high,
     )
     return vmem_call(
-        functools.partial(out_kernel, len(far), 2 + len(far), True), out_shape,
-        [pltpu.VMEM(out_shape.shape, F32), pltpu.SemaphoreType.DMA((tok_rows // CHUNK,))], 1,
-        index, *far_on, w_out, total, any_out=True,
+        functools.partial(last_kernel, len(far_high), 2 + len(far_high)), like(tok_rows, columns),
+        [pltpu.VMEM((half, columns), F32), pltpu.SemaphoreType.DMA((half // CHUNK + 1,))], 1,
+        index, *far_high_on, w_out, total_low, total_high, any_out=True,
     )
 
 

time: 64 us -> 63 us (0.984)
  waiting for transfers between devices: 15.8 us -> 12.4 us
  starting transfers between devices: 19.4 us -> 20.5 us
  Pallas kernels: 20.1 us -> 21.2 us
    ppermute x4 -> x6, waiting for transfers between devices: 7.15 us -> 2.74 us  [to_chips(): lax.ppermute(value, 'head', [(source, (source + 2 * step) % count) for so...]
    ppermute x4 -> x6, starting transfers between devices: 6.3 us -> 8.33 us  [to_chips(): lax.ppermute(value, 'head', [(source, (source + 2 * step) % count) for so...]
    ppermute x1, starting transfers between devices: 4.67 us -> 2.65 us  [shards(): lax.ppermute(pair if carry else pair[1], 'ctx', [(source, source ^ reach)...]
    pallas_call x11 -> x12, Pallas kernels: 20.1 us -> 21.2 us  [vmem_call(): pl.pallas_call(kernel, out_shape=outs, in_specs=[free if spot in any_in e...]
    ppermute x6 -> x8, starting transfers between devices: 1.04 us -> 1.96 us  [to_sibling(): lax.ppermute(value, 'head', [(source, source ^ 1) for source in range(cou...]
    ppermute x6 -> x8, waiting for transfers between devices: 2.59 us -> 3.16 us  [to_sibling(): lax.ppermute(value, 'head', [(source, source ^ 1) for source in range(cou...]
  transfers between devices with their start and end apart: 15 -> 19, of which waited for: 8 -> 11; matrix products, arithmetic and copies ran while one was open for 5% -> 5% of each run, Pallas kernels for 21% -> 22%
where the time goes in v9:
time: 63 us; the launch traced here: 62.5 us
  Pallas kernels  21.2 us (34%)
  starting transfers between devices  20.5 us (33%)
  waiting for transfers between devices  12.4 us (20%)
  local copies, waits for them, and re-layouts  7.43 us (12%)
  between operations  1.01 us (2%)
    pallas_call x12, Pallas kernels, vmem_call(): pl.pallas_call(kernel, out_shape=outs, in_specs=[free if spot in any_in e...  21.2 us
    ppermute x6, starting transfers between devices, to_chips(): lax.ppermute(value, 'head', [(source, (source + 2 * step) % count) for so...  8.33 us
    ppermute x3, waiting for transfers between devices, shards(): lax.ppermute(pair, 'ctx', [(source, source ^ mask << bit) for source in r...  6.01 us
    unnamed x14, local copies, waits for them, and re-layouts  4.34 us
    ppermute x1, starting transfers between devices, shards(): lax.ppermute(rim, 'ctx', [(source, source + 1) for source in range(blocks...  3.99 us
    ppermute x3, starting transfers between devices, shards(): lax.ppermute(pair, 'ctx', [(source, source ^ mask << bit) for source in r...  3.55 us
    ppermute x8, waiting for transfers between devices, to_sibling(): lax.ppermute(value, 'head', [(source, source ^ 1) for source in range(cou...  3.16 us
    ppermute x6, waiting for transfers between devices, to_chips(): lax.ppermute(value, 'head', [(source, (source + 2 * step) % count) for so...  2.74 us
  transfers between devices with their start and end apart: 19, of which 11 were waited for; matrix products, arithmetic and copies ran while one was open for 5% of the time, Pallas kernels for 22%

profile of v9, /device:TPU:0, one launch (start us, length us, event | category | flops | bytes accessed | tf_op | source)
XLA Modules:
  0.0 62.5 jit_solution(8413095744659946070)
XLA Ops:
  0.5 1.0 %slice.11 = f32[144,512]{1,0:T(8,128)S(1)} slice(f32[512,512]{1,0:T(8,128)} %own_ref.1), slice={[368:512], [0:512]} | slice | bytes 589824 | tf_op jit(solution)/shard_map/slice | solution.py:469
  1.4 2.6 %collective-permute-start.3 = (f32[144,512]{1,0:T(8,128)S(1)}, f32[144,512]{1,0:T(8,128)S(1)}, u32[]{:S(2)}, u32[]{:S(2)}) collective-permute-start(f32[144,512]{1,0:T(8,128)S(1)} %slice.11), channel_id=1, source_target_pairs={{0,2},{1,3},{2,0},{3,1},{4,6},{5,7},{6,4},{7,5},{8,10},{9,11},{10,... | collective-permute-start | bytes 884744 | tf_op jit(solution)/shard_map/ppermute | solution.py:439
  4.0 1.0 %slice.10 = f32[128,512]{1,0:T(8,128)S(1)} slice(f32[512,512]{1,0:T(8,128)} %own_ref.1), slice={[240:368], [0:512]} | slice | bytes 524288 | tf_op jit(solution)/shard_map/slice | solution.py:469
  5.2 1.1 %slice.9 = f32[240,512]{1,0:T(8,128)S(1)} slice(f32[512,512]{1,0:T(8,128)} %own_ref.1), slice={[0:240], [0:512]} | slice | bytes 983040 | tf_op jit(solution)/shard_map/slice | solution.py:472
  6.2 2.1 %collective-permute-start.1 = (f32[240,512]{1,0:T(8,128)S(1)}, f32[240,512]{1,0:T(8,128)S(1)}, u32[]{:S(2)}, u32[]{:S(2)}) collective-permute-start(f32[240,512]{1,0:T(8,128)S(1)} %slice.9), channel_id=1, source_target_pairs={{0,2},{1,3},{2,0},{3,1},{4,6},{5,7},{6,4},{7,5},{8,10},{9,11},{10,... | collective-permute-start | bytes 1474568 | tf_op jit(solution)/shard_map/ppermute | solution.py:439
  8.3 1.2 %copy-done.1 = f32[512,512]{1,0:T(8,128)S(1)} copy-done((f32[512,512]{1,0:T(8,128)S(1)}, f32[512,512]{1,0:T(8,128)}, u32[]{:S(2)}) %copy-start.1) | copy-done | bytes 1048600
  9.5 2.2 %copy-done.2 = f32[2048,512]{1,0:T(8,128)S(1)} copy-done((f32[2048,512]{1,0:T(8,128)S(1)}, f32[2048,512]{1,0:T(8,128)}, u32[]{:S(2)}) %copy-start.2) | copy-done | bytes 4194328
  11.7 0.9 %copy-done.3 = f32[2048,9]{0,1:T(8,128)S(1)} copy-done((f32[2048,9]{0,1:T(8,128)S(1)}, f32[2048,9]{0,1:T(8,128)}, u32[]{:S(2)}) %copy-start.3) | copy-done | bytes 73752
  12.6 4.0 %shard_map.82 = (f32[512,384]{1,0:T(8,128)S(1)}, f32[512,256]{1,0:T(8,128)S(1)}, bf16[1024,768]{1,0:T(8,128)(2,1)S(1)}, bf16[1024,512]{1,0:T(8,128)(2,1)S(1)}) custom-call(s32[7]{0:T(128)S(1)} %stack.31.index_ref.bits_ref, f32[512,512]{1,0:T(8,128)S(1)} %copy-done.1, f32[512,512]{1,0:T(8,128)S(1)} %collective-permute-done.beside_ref, ...), custom_call_target="tpu_custom_call" | custom-call | flops 3000000000 | bytes 1048576 | tf_op jit(solution)/shard_map/pallas_call | solution.py:417
  16.6 0.9 %collective-permute-done.2.refs_0_ = f32[128,512]{1,0:T(8,128)S(1)} collective-permute-done((f32[128,512]{1,0:T(8,128)S(1)}, f32[128,512]{1,0:T(8,128)S(1)}, u32[]{:S(2)}, u32[]{:S(2)}) %collective-permute-start.2) | collective-permute-done | bytes 262176 | tf_op jit(solution)/shard_map/ppermute | solution.py:439
  18.7 0.8 %collective-permute-done.4.refs_1_ = f32[128,512]{1,0:T(8,128)S(1)} collective-permute-done((f32[128,512]{1,0:T(8,128)S(1)}, f32[128,512]{1,0:T(8,128)S(1)}, u32[]{:S(2)}, u32[]{:S(2)}) %collective-permute-start.4) | collective-permute-done | bytes 262176 | tf_op jit(solution)/shard_map/ppermute | solution.py:433
  19.5 1.5 %shard_map.83 = (f32[272,384]{1,0:T(8,128)S(1)}, f32[272,256]{1,0:T(8,128)S(1)}, f32[16,384]{1,0:T(8,128)S(1)}) custom-call(f32[128,512]{1,0:T(8,128)S(1)} %collective-permute-done.2.refs_0_, f32[128,512]{1,0:T(8,128)S(1)} %collective-permute-done.4.refs_1_, f32[144,512]{1,0:T(8,128)S(1)} %collective-permute-done.3.refs_2_, ...), custom_call_target="tpu_custom_call" | custom-call | flops 500000000 | bytes 1048576 | tf_op jit(solution)/shard_map/pallas_call | solution.py:417
  20.9 4.0 %collective-permute-start.6 = (f32[16,384]{1,0:T(8,128)S(1)}, f32[16,384]{1,0:T(8,128)S(1)}, u32[]{:S(2)}, u32[]{:S(2)}) collective-permute-start(f32[16,384]{1,0:T(8,128)S(1)} %get-tuple-element.66), channel_id=1, source_target_pairs={{0,4},{4,8},{8,12},{12,16},{16,20},{20,24},{24,28},{1,5},{5,9},{9,... | collective-permute-start | bytes 73736 | tf_op jit(solution)/shard_map/ppermute | solution.py:492
  25.0 2.8 %shard_map.84 = (f32[256,128]{1,0:T(8,128)S(1)}, f32[256,128]{1,0:T(8,128)S(1)}, f32[256,128]{1,0:T(8,128)S(1)}, f32[256,128]{1,0:T(8,128)S(1)}, f32[256,128]{1,...) custom-call(f32[272,384]{1,0:T(8,128)S(1)} %get-tuple-element.64.raw_ref.refs_4_,, ...), custom_call_target="tpu_custom_call" | custom-call | flops 500000000 | bytes 1048576 | tf_op jit(solution)/shard_map/pallas_call | solution.py:417
  28.4 1.4 %collective-permute-done.7.refs_0_.refs_1_ = f32[240,512]{1,0:T(8,128)S(1)} collective-permute-done((f32[240,512]{1,0:T(8,128)S(1)}, f32[240,512]{1,0:T(8,128)S(1)}, u32[]{:S(2)}, u32[]{:S(2)}) %collective-permute-start.7) | collective-permute-done | bytes 491552 | tf_op jit(solution)/shard_map/ppermute | solution.py:433
  29.7 3.3 %shard_map.86 = (f32[256,128]{1,0:T(8,128)S(1)}, f32[256,128]{1,0:T(8,128)S(1)}, f32[256,128]{1,0:T(8,128)S(1)}, f32[256,128]{1,0:T(8,128)S(1)}, f32[256,128]{1,...) custom-call(f32[240,512]{1,0:T(8,128)S(1)} %collective-permute-done.7.refs_0_.ref, ...), custom_call_target="tpu_custom_call" | custom-call | flops 5000000000 | bytes 1048576 | tf_op jit(solution)/shard_map/pallas_call | solution.py:417
  33.0 2.8 %collective-permute-start.10 = (f32[2,128,128]{2,1,0:T(8,128)S(1)}, f32[2,128,128]{2,1,0:T(8,128)S(1)}, u32[]{:S(2)}, u32[]{:S(2)}) collective-permute-start(f32[2,128,128]{2,1,0:T(8,128)S(1)} %get-tuple-element.88.own_ref), channel_id=1, source_target_pairs={{0,12},{4,8},{8,4},{12,0},{16,28},{20,24},{24,20},{28,16},{1,13},{... | collective-permute-start | bytes 393224 | tf_op jit(solution)/shard_map/ppermute | solution.py:521
  36.6 3.7 %collective-permute-done.10.three_ref = f32[2,128,128]{2,1,0:T(8,128)S(1)} collective-permute-done((f32[2,128,128]{2,1,0:T(8,128)S(1)}, f32[2,128,128]{2,1,0:T(8,128)S(1)}, u32[]{:S(2)}, u32[]{:S(2)}) %collective-permute-start.10) | collective-permute-done | bytes 131104 | tf_op jit(solution)/shard_map/ppermute | solution.py:521
  40.3 2.3 %collective-permute-done.9.two_ref = f32[2,128,128]{2,1,0:T(8,128)S(1)} collective-permute-done((f32[2,128,128]{2,1,0:T(8,128)S(1)}, f32[2,128,128]{2,1,0:T(8,128)S(1)}, u32[]{:S(2)}, u32[]{:S(2)}) %collective-permute-start.9) | collective-permute-done | bytes 131104 | tf_op jit(solution)/shard_map/ppermute | solution.py:521
  42.6 1.0 %shard_map.88 = (f32[128,128]{1,0:T(8,128)S(1)}, f32[2,128,128]{2,1,0:T(8,128)S(1)}, f32[128,128]{1,0:T(8,128)S(1)}) custom-call(s32[7]{0:T(128)S(1)} %stack.31.index_ref.bits_ref, f32[2,128,128]{2,1,0:T(8,128)S(1)} %get-tuple-element.88.own_ref, f32[2,128,128]{2,1,0:T(8,128)S(1)} %collective-permute-done.8.one_ref, ...), custom_call_target="tpu_custom_call" | custom-call | flops 1000000000 | bytes 1048576 | tf_op jit(solution)/shard_map/pallas_call | solution.py:417
  43.6 2.6 %collective-permute-start.11 = (f32[128,128]{1,0:T(8,128)S(1)}, f32[128,128]{1,0:T(8,128)S(1)}, u32[]{:S(2)}, u32[]{:S(2)}) collective-permute-start(f32[128,128]{1,0:T(8,128)S(1)} %get-tuple-element.91), channel_id=1, source_target_pairs={{0,16},{4,20},{8,24},{12,28},{16,0},{20,4},{24,8},{28,12},{1,17},{... | collective-permute-start | bytes 196616 | tf_op jit(solution)/shard_map/ppermute | solution.py:546
  46.3 2.4 %shard_map.87 = (f32[512,128]{1,0:T(8,128)S(1)}, f32[512,128]{1,0:T(8,128)S(1)}, f32[512,128]{1,0:T(8,128)S(1)}) custom-call(f32[240,512]{1,0:T(8,128)S(1)} %collective-permute-done.1.refs_0_, f32[240,512]{1,0:T(8,128)S(1)} %collective-permute-done.7.refs_0_.refs_1_, f32[512,256]{1,0:T(8,128)S(1)} %get-tuple-element.61.refs_5_.refs_2_, ...), custom_call_target="tpu_custom_call" | custom-call | flops 5000000000 | bytes 1048576 | tf_op jit(solution)/shard_map/pallas_call | solution.py:417
  48.7 0.5 collective-permute-done.11.refs_2_
  49.2 1.1 %shard_map.89 = (f32[512,128]{1,0:T(8,128)S(1)}, f32[128,128]{1,0:T(8,128)S(1)}, f32[128,128]{1,0:T(8,128)S(1)}, f32[256,128]{1,0:T(8,128)S(1)}) custom-call(s32[7]{0:T(128)S(1)} %stack.31.index_ref.bits_ref, f32[512,128]{1,0:T(8,128)S(1)} %get-tuple-element.83.carried_ref, f32[512,128]{1,0:T(8,128)S(1)} %get-tuple-element.84.local_ref, ...), custom_call_target="tpu_custom_call" | custom-call | flops 1000000000 | bytes 1048576 | tf_op jit(solution)/shard_map/pallas_call | solution.py:417
  50.4 1.6 %collective-permute-start.14 = (f32[128,128]{1,0:T(8,128)S(1)}, f32[128,128]{1,0:T(8,128)S(1)}, u32[]{:S(2)}, u32[]{:S(2)}) collective-permute-start(f32[128,128]{1,0:T(8,128)S(1)} %get-tuple-element.95), channel_id=1, source_target_pairs={{0,2},{1,3},{2,0},{3,1},{4,6},{5,7},{6,4},{7,5},{8,10},{9,11},{10,... | collective-permute-start | bytes 196616 | tf_op jit(solution)/shard_map/ppermute | solution.py:439
  52.5 1.5 %collective-permute-start.13 = (f32[256,128]{1,0:T(8,128)S(1)}, f32[256,128]{1,0:T(8,128)S(1)}, u32[]{:S(2)}, u32[]{:S(2)}) collective-permute-start(f32[256,128]{1,0:T(8,128)S(1)} %get-tuple-element.94), channel_id=1, source_target_pairs={{0,2},{1,3},{2,0},{3,1},{4,6},{5,7},{6,4},{7,5},{8,10},{9,11},{10,... | collective-permute-start | bytes 393224 | tf_op jit(solution)/shard_map/ppermute | solution.py:439
  54.0 1.1 %shard_map.90 = (f32[256,512]{1,0:T(8,128)S(1)}, f32[256,512]{1,0:T(8,128)S(1)}) custom-call(s32[7]{0:T(128)S(1)} %stack.31.index_ref.bits_ref, f32[512,128]{1,0:T(8,128)S(1)} %get-tuple-element.93.own_ref, f32[512,128]{1,0:T(8,128)S(1)} %collective-permute-done.12.near_ref, f32[512,512]{1,0:T(8,128)S(1)} %copy-done), custom_call_target="tpu_custom_call" | custom-call | flops 2000000000 | bytes 1048576 | tf_op jit(solution)/shard_map/pallas_call | solution.py:417
  55.2 1.7 %collective-permute-done.15.refs_2_ = f32[128,128]{1,0:T(8,128)S(1)} collective-permute-done((f32[128,128]{1,0:T(8,128)S(1)}, f32[128,128]{1,0:T(8,128)S(1)}, u32[]{:S(2)}, u32[]{:S(2)}) %collective-permute-start.15) | collective-permute-done | bytes 65568 | tf_op jit(solution)/shard_map/ppermute | solution.py:439
  57.5 0.7 %collective-permute-done.16.refs_1_ = f32[128,128]{1,0:T(8,128)S(1)} collective-permute-done((f32[128,128]{1,0:T(8,128)S(1)}, f32[128,128]{1,0:T(8,128)S(1)}, u32[]{:S(2)}, u32[]{:S(2)}) %collective-permute-start.16) | collective-permute-done | bytes 65568 | tf_op jit(solution)/shard_map/ppermute | solution.py:433
  58.4 0.9 %shard_map.91.refs_2_ = f32[256,512]{1,0:T(8,128)S(1)} custom-call(s32[7]{0:T(128)S(1)} %stack.31.index_ref.bits_ref, f32[128,128]{1,0:T(8,128)S(1)} %collective-permute-done.14.refs_0_, f32[128,128]{1,0:T(8,128)S(1)} %collective-permute-done.16.refs_1_, f32[128,128]{1,0:T(8,128)S(1)} %collective-permute-done.15.refs_2_, ...), custom_call_target="tpu_custom_call" | custom-call | flops 10000000 | bytes 1048576 | tf_op jit(solution)/shard_map/pallas_call | solution.py:417
  59.7 0.9 %shard_map.92.refs_3_ = f32[256,512]{1,0:T(8,128)S(1)} custom-call(s32[7]{0:T(128)S(1)} %stack.31.index_ref.bits_ref, f32[256,128]{1,0:T(8,128)S(1)} %collective-permute-done.13.refs_0_, f32[512,512]{1,0:T(8,128)S(1)} %copy-done, f32[256,512]{1,0:T(8,128)S(1)} %get-tuple-element.104.refs_2_), custom_call_target="tpu_custom_call" | custom-call | flops 1000000000 | bytes 1048576 | tf_op jit(solution)/shard_map/pallas_call | solution.py:417
  60.7 1.6 %shard_map.93 = f32[512,512]{1,0:T(8,128)} custom-call(s32[7]{0:T(128)S(1)} %stack.31.index_ref.bits_ref, f32[256,128]{1,0:T(8,128)S(1)} %collective-permute-done.18.refs_0_, f32[512,512]{1,0:T(8,128)S(1)} %copy-done, f32[256,512]{1,0:T(8,128)S(1)} %shard_map.91.refs_2_, f32[256,512]{1,0:T(8,128)S(1)} %shard_map.92.refs_3_), custom_call_target="tpu_custom_call" | custom-call | flops 1000000000 | bytes 1048576 | tf_op jit(solution)/shard_map/pallas_call | solution.py:417
  (36 shorter events, 4.3 us)
Async XLA Ops:
  0.0 5.2 %collective-permute-start = (f32[512,512]{1,0:T(8,128)}, f32[512,512]{1,0:T(8,128)S(1)}, u32[]{:S(2)}, u32[]{:S(2)}) collective-permute-start(f32[512,512]{1,0:T(8,128)} %own_ref.1), channel_id=1, source_target_pairs={{0,1},{1,0},{2,3},{3,2},{4,5},{5,4},{6,7},{7,6},{8,9},{9,8},{10,11... | collective-permute-start | bytes 3145736 | tf_op jit(solution)/shard_map/ppermute | solution.py:433
  1.4 16.1 %collective-permute-start.3 = (f32[144,512]{1,0:T(8,128)S(1)}, f32[144,512]{1,0:T(8,128)S(1)}, u32[]{:S(2)}, u32[]{:S(2)}) collective-permute-start(f32[144,512]{1,0:T(8,128)S(1)} %slice.11), channel_id=1, source_target_pairs={{0,2},{1,3},{2,0},{3,1},{4,6},{5,7},{6,4},{7,5},{8,10},{9,11},{10,... | collective-permute-start | bytes 884744 | tf_op jit(solution)/shard_map/ppermute | solution.py:439
  5.0 12.5 %collective-permute-start.2 = (f32[128,512]{1,0:T(8,128)S(1)}, f32[128,512]{1,0:T(8,128)S(1)}, u32[]{:S(2)}, u32[]{:S(2)}) collective-permute-start(f32[128,512]{1,0:T(8,128)S(1)} %slice.10), channel_id=1, source_target_pairs={{0,2},{1,3},{2,0},{3,1},{4,6},{5,7},{6,4},{7,5},{8,10},{9,11},{10,... | collective-permute-start | bytes 786440 | tf_op jit(solution)/shard_map/ppermute | solution.py:439
  6.2 21.6 %collective-permute-start.1 = (f32[240,512]{1,0:T(8,128)S(1)}, f32[240,512]{1,0:T(8,128)S(1)}, u32[]{:S(2)}, u32[]{:S(2)}) collective-permute-start(f32[240,512]{1,0:T(8,128)S(1)} %slice.9), channel_id=1, source_target_pairs={{0,2},{1,3},{2,0},{3,1},{4,6},{5,7},{6,4},{7,5},{8,10},{9,11},{10,... | collective-permute-start | bytes 1474568 | tf_op jit(solution)/shard_map/ppermute | solution.py:439
  8.3 1.2 %copy-start.1 = (f32[512,512]{1,0:T(8,128)S(1)}, f32[512,512]{1,0:T(8,128)}, u32[]{:S(2)}) copy-start(f32[512,512]{1,0:T(8,128)} %own_ref.1) | copy-start | bytes 3145732
  9.5 2.2 %copy-start.2 = (f32[2048,512]{1,0:T(8,128)S(1)}, f32[2048,512]{1,0:T(8,128)}, u32[]{:S(2)}) copy-start(f32[2048,512]{1,0:T(8,128)} %proj_ref.1) | copy-start | bytes 12582916
  11.7 0.9 %copy-start.3 = (f32[2048,9]{0,1:T(8,128)S(1)}, f32[2048,9]{0,1:T(8,128)}, u32[]{:S(2)}) copy-start(f32[2048,9]{0,1:T(8,128)} %param.10) | copy-start | bytes 221188
  16.6 8.4 %copy-start.4 = (f32[4,384]{1,0:T(4,128)S(1)}, f32[4,384]{1,0:T(4,128)}, u32[]{:S(2)}) copy-start(f32[4,384]{1,0:T(4,128)} %refs_6_.3) | copy-start | bytes 18436
  16.6 8.4 %copy-start.5 = (s32[512]{0:T(512)S(1)}, s32[512]{0:T(512)}, u32[]{:S(2)}) copy-start(s32[512]{0:T(512)} %param.13) | copy-start | bytes 6148
  17.5 2.0 %collective-permute-start.5 = (f32[144,512]{1,0:T(8,128)S(1)}, f32[144,512]{1,0:T(8,128)S(1)}, u32[]{:S(2)}, u32[]{:S(2)}) collective-permute-start(f32[144,512]{1,0:T(8,128)S(1)} %collective-permute-done.3.refs_2_), channel_id=1, source_target_pairs={{0,1},{1,0},{2,3},{3,2},{4,5},{5,4},{6,7},{7,6},{8,9},{9,8},{10,11... | collective-permute-start | bytes 884744 | tf_op jit(solution)/shard_map/ppermute | solution.py:433
  17.5 2.0 %collective-permute-start.4 = (f32[128,512]{1,0:T(8,128)S(1)}, f32[128,512]{1,0:T(8,128)S(1)}, u32[]{:S(2)}, u32[]{:S(2)}) collective-permute-start(f32[128,512]{1,0:T(8,128)S(1)} %collective-permute-done.2.refs_0_), channel_id=1, source_target_pairs={{0,1},{1,0},{2,3},{3,2},{4,5},{5,4},{6,7},{7,6},{8,9},{9,8},{10,11... | collective-permute-start | bytes 786440 | tf_op jit(solution)/shard_map/ppermute | solution.py:433
  20.9 6.8 %collective-permute-start.6 = (f32[16,384]{1,0:T(8,128)S(1)}, f32[16,384]{1,0:T(8,128)S(1)}, u32[]{:S(2)}, u32[]{:S(2)}) collective-permute-start(f32[16,384]{1,0:T(8,128)S(1)} %get-tuple-element.66), channel_id=1, source_target_pairs={{0,4},{4,8},{8,12},{12,16},{16,20},{20,24},{24,28},{1,5},{5,9},{9,... | collective-permute-start | bytes 73736 | tf_op jit(solution)/shard_map/ppermute | solution.py:492
  27.9 1.9 %collective-permute-start.7 = (f32[240,512]{1,0:T(8,128)S(1)}, f32[240,512]{1,0:T(8,128)S(1)}, u32[]{:S(2)}, u32[]{:S(2)}) collective-permute-start(f32[240,512]{1,0:T(8,128)S(1)} %collective-permute-done.1.refs_0_), channel_id=1, source_target_pairs={{0,1},{1,0},{2,3},{3,2},{4,5},{5,4},{6,7},{7,6},{8,9},{9,8},{10,11... | collective-permute-start | bytes 1474568 | tf_op jit(solution)/shard_map/ppermute | solution.py:433
  33.0 7.3 %collective-permute-start.10 = (f32[2,128,128]{2,1,0:T(8,128)S(1)}, f32[2,128,128]{2,1,0:T(8,128)S(1)}, u32[]{:S(2)}, u32[]{:S(2)}) collective-permute-start(f32[2,128,128]{2,1,0:T(8,128)S(1)} %get-tuple-element.88.own_ref), channel_id=1, source_target_pairs={{0,12},{4,8},{8,4},{12,0},{16,28},{20,24},{24,20},{28,16},{1,13},{... | collective-permute-start | bytes 393224 | tf_op jit(solution)/shard_map/ppermute | solution.py:521
  35.8 6.8 %collective-permute-start.9 = (f32[2,128,128]{2,1,0:T(8,128)S(1)}, f32[2,128,128]{2,1,0:T(8,128)S(1)}, u32[]{:S(2)}, u32[]{:S(2)}) collective-permute-start(f32[2,128,128]{2,1,0:T(8,128)S(1)} %get-tuple-element.88.own_ref), channel_id=1, source_target_pairs={{0,8},{4,12},{8,0},{12,4},{16,24},{20,28},{24,16},{28,20},{1,9},{5... | collective-permute-start | bytes 393224 | tf_op jit(solution)/shard_map/ppermute | solution.py:521
  36.3 6.3 %collective-permute-start.8 = (f32[2,128,128]{2,1,0:T(8,128)S(1)}, f32[2,128,128]{2,1,0:T(8,128)S(1)}, u32[]{:S(2)}, u32[]{:S(2)}) collective-permute-start(f32[2,128,128]{2,1,0:T(8,128)S(1)} %get-tuple-element.88.own_ref), channel_id=1, source_target_pairs={{0,4},{4,0},{8,12},{12,8},{16,20},{20,16},{24,28},{28,24},{1,5},{5... | collective-permute-start | bytes 393224 | tf_op jit(solution)/shard_map/ppermute | solution.py:521
  43.6 5.6 %collective-permute-start.11 = (f32[128,128]{1,0:T(8,128)S(1)}, f32[128,128]{1,0:T(8,128)S(1)}, u32[]{:S(2)}, u32[]{:S(2)}) collective-permute-start(f32[128,128]{1,0:T(8,128)S(1)} %get-tuple-element.91), channel_id=1, source_target_pairs={{0,16},{4,20},{8,24},{12,28},{16,0},{20,4},{24,8},{28,12},{1,17},{... | collective-permute-start | bytes 196616 | tf_op jit(solution)/shard_map/ppermute | solution.py:546
  46.3 2.9 %copy-start.6 = (f32[128]{0:T(128)S(1)}, f32[128]{0:T(128)}, u32[]{:S(2)}) copy-start(f32[128]{0:T(128)} %param.14) | copy-start | bytes 1540
  46.3 7.8 %copy-start = (f32[512,512]{1,0:T(8,128)S(1)}, f32[512,512]{1,0:T(8,128)}, u32[]{:S(2)}) copy-start(f32[512,512]{1,0:T(8,128)} %refs_1_.3) | copy-start | bytes 3145732
  50.3 2.2 %collective-permute-start.12 = (f32[512,128]{1,0:T(8,128)S(1)}, f32[512,128]{1,0:T(8,128)S(1)}, u32[]{:S(2)}, u32[]{:S(2)}) collective-permute-start(f32[512,128]{1,0:T(8,128)S(1)} %get-tuple-element.93.own_ref), channel_id=1, source_target_pairs={{0,1},{1,0},{2,3},{3,2},{4,5},{5,4},{6,7},{7,6},{8,9},{9,8},{10,11... | collective-permute-start | bytes 786440 | tf_op jit(solution)/shard_map/ppermute | solution.py:433
  50.4 4.8 %collective-permute-start.14 = (f32[128,128]{1,0:T(8,128)S(1)}, f32[128,128]{1,0:T(8,128)S(1)}, u32[]{:S(2)}, u32[]{:S(2)}) collective-permute-start(f32[128,128]{1,0:T(8,128)S(1)} %get-tuple-element.95), channel_id=1, source_target_pairs={{0,2},{1,3},{2,0},{3,1},{4,6},{5,7},{6,4},{7,5},{8,10},{9,11},{10,... | collective-permute-start | bytes 196616 | tf_op jit(solution)/shard_map/ppermute | solution.py:439
  52.0 4.9 %collective-permute-start.15 = (f32[128,128]{1,0:T(8,128)S(1)}, f32[128,128]{1,0:T(8,128)S(1)}, u32[]{:S(2)}, u32[]{:S(2)}) collective-permute-start(f32[128,128]{1,0:T(8,128)S(1)} %get-tuple-element.96), channel_id=1, source_target_pairs={{0,2},{1,3},{2,0},{3,1},{4,6},{5,7},{6,4},{7,5},{8,10},{9,11},{10,... | collective-permute-start | bytes 196616 | tf_op jit(solution)/shard_map/ppermute | solution.py:439
  52.5 6.8 %collective-permute-start.13 = (f32[256,128]{1,0:T(8,128)S(1)}, f32[256,128]{1,0:T(8,128)S(1)}, u32[]{:S(2)}, u32[]{:S(2)}) collective-permute-start(f32[256,128]{1,0:T(8,128)S(1)} %get-tuple-element.94), channel_id=1, source_target_pairs={{0,2},{1,3},{2,0},{3,1},{4,6},{5,7},{6,4},{7,5},{8,10},{9,11},{10,... | collective-permute-start | bytes 393224 | tf_op jit(solution)/shard_map/ppermute | solution.py:439
  56.9 1.3 %collective-permute-start.16 = (f32[128,128]{1,0:T(8,128)S(1)}, f32[128,128]{1,0:T(8,128)S(1)}, u32[]{:S(2)}, u32[]{:S(2)}) collective-permute-start(f32[128,128]{1,0:T(8,128)S(1)} %collective-permute-done.14.refs_0_), channel_id=1, source_target_pairs={{0,1},{1,0},{2,3},{3,2},{4,5},{5,4},{6,7},{7,6},{8,9},{9,8},{10,11... | collective-permute-start | bytes 196616 | tf_op jit(solution)/shard_map/ppermute | solution.py:433
  56.9 1.4 %collective-permute-start.17 = (f32[128,128]{1,0:T(8,128)S(1)}, f32[128,128]{1,0:T(8,128)S(1)}, u32[]{:S(2)}, u32[]{:S(2)}) collective-permute-start(f32[128,128]{1,0:T(8,128)S(1)} %collective-permute-done.15.refs_2_), channel_id=1, source_target_pairs={{0,1},{1,0},{2,3},{3,2},{4,5},{5,4},{6,7},{7,6},{8,9},{9,8},{10,11... | collective-permute-start | bytes 196616 | tf_op jit(solution)/shard_map/ppermute | solution.py:433
  59.3 1.4 %collective-permute-start.18 = (f32[256,128]{1,0:T(8,128)S(1)}, f32[256,128]{1,0:T(8,128)S(1)}, u32[]{:S(2)}, u32[]{:S(2)}) collective-permute-start(f32[256,128]{1,0:T(8,128)S(1)} %collective-permute-done.13.refs_0_), channel_id=1, source_target_pairs={{0,1},{1,0},{2,3},{3,2},{4,5},{5,4},{6,7},{7,6},{8,9},{9,8},{10,11... | collective-permute-start | bytes 393224 | tf_op jit(solution)/shard_map/ppermute | solution.py:433

commit v10 on v9

--- a/solution.py
+++ b/solution.py
@@ -85,7 +85,7 @@
 
 def base_kernel(
     index_ref, own_ref, beside_ref, mix_ref, proj_ref,
-    state_ref, query_ref, far_state_ref, far_query_ref,
+    state_ref, query_ref, far_state_ref, far_query_ref, flag_ref,
     held, near_state, near_query, sems,
 ):
     sources, depth, across = held.shape
@@ -95,6 +95,8 @@
         rows = pl.ds(pl.multiple_of(index_ref[source] * depth, depth), depth)
         copies.append(pltpu.make_async_copy(proj_ref.at[rows, :], held.at[source], sems.at[source]))
         copies[-1].start()
+    for bit in range(flag_ref.shape[0]):
+        flag_ref[bit : bit + 1, :] = jnp.broadcast_to(index_ref[sources + bit], (1, CHUNK))
     mixes = mix_ref.shape[0]
 
     def split(source, state_out, query_out, base):
@@ -291,26 +293,29 @@
             local_ref[out, :] = local
 
 
-def four_kernel(first_bit, carried, last, bits_ref, own_ref, one_ref, two_ref, three_ref, *refs):
-    group_ref, level_ref, next_ref, pairs = refs[-4:]
-    low_bit, high_bit = bits_ref[first_bit], bits_ref[first_bit + 1]
-    place = 2 * high_bit + low_bit
-    for mask, ref in enumerate((own_ref, one_ref, two_ref, three_ref)):
-        pairs[place ^ mask] = ref[...]
+def four_kernel(bit, carried, last, flag_ref, own_ref, one_ref, two_ref, three_ref, *refs):
+    group_ref, level_ref, next_ref = refs[-3:]
     width = next_ref.shape[0]
-    joined = lambda spot: jnp.concatenate([pairs[spot, 0], pairs[spot, 1]], axis=1)
-    onto_low = product(pairs[1, 0], joined(0))
-    onto_high = product(pairs[3, 0], joined(2))
-    low_a, low_s = onto_low[:, :width], onto_low[:, width:] + pairs[1, 1]
-    high_a, high_s = onto_high[:, :width], onto_high[:, width:] + pairs[3, 1]
+    flag = lambda at: jnp.broadcast_to(flag_ref[at : at + 1, :], (width, width)) == 1
+    set_low, set_high = flag(bit), flag(bit + 1)
+    held = (own_ref, one_ref, two_ref, three_ref)
+
+    def placed(part):
+        by_low = [jnp.where(set_low, held[at ^ 1][part], held[at][part]) for at in range(4)]
+        return [jnp.where(set_high, by_low[at ^ 2], by_low[at]) for at in range(4)]
+
+    trans, memory = placed(0), placed(1)
+    joined = lambda at: jnp.concatenate([trans[at], memory[at]], axis=1)
+    onto_low = product(trans[1], joined(0))
+    onto_high = product(trans[3], joined(2))
+    low_a, low_s = onto_low[:, :width], onto_low[:, width:] + memory[1]
+    high_a, high_s = onto_high[:, :width], onto_high[:, width:] + memory[3]
     if last:
         group_ref[...] = product(high_a, low_s) + high_s
     else:
         onto = product(high_a, jnp.concatenate([low_a, low_s], axis=1))
         group_ref[0] = onto[:, :width]
         group_ref[1] = onto[:, width:] + high_s
-    set_low = jnp.broadcast_to(low_bit, (width, width)) == 1
-    set_high = jnp.broadcast_to(high_bit, (width, width)) == 1
     if carried:
         carry = refs[0][...]
         first = product(carry, jnp.concatenate([one_ref[0], one_ref[1]], axis=1))
@@ -324,15 +329,14 @@
     carry = jnp.where(set_low, first_a, carry)
     second = product(carry, jnp.concatenate([low_a, low_s], axis=1))
     level_ref[1] = jnp.where(set_high, second[:, width:], 0.0)
-    next_ref[...] = jnp.where(set_high, second[:, :width], carry)
-
-
-def mix_kernel(stages, single, bits_ref, carried_ref, local_ref, gate_ref, low_ref, high_ref, gain_ref, *refs):
+    carry = jnp.where(set_high, second[:, :width], carry)
+    next_ref[...] = jnp.where(flag(bit + 2), carry, 0.0) if last else carry
+
+
+def mix_kernel(stages, single, carried_ref, local_ref, gate_ref, low_ref, high_ref, gain_ref, *refs):
     states = [ref[spot] for ref in refs[:stages] for spot in range(ref.shape[0])]
     if single:
-        carry_ref, other_ref = refs[stages : stages + 2]
-        upper = jnp.broadcast_to(bits_ref[single], other_ref.shape) == 1
-        states.append(product(carry_ref[...], jnp.where(upper, other_ref[...], 0.0)))
+        states.append(product(refs[stages][...], refs[stages + 1][...]))
     outs = refs[stages + (2 if single else 0) :]
     states = [right_parts(state) for state in states]
     carried = left_parts(carried_ref[...])
@@ -358,21 +362,24 @@
     return (both[:, :columns] + both[:, columns:]) + rest
 
 
-def source_rows(index_ref, first, pieces, weight_ref):
-    parts = []
-    for spot, piece in enumerate(pieces):
-        depth = piece.shape[1]
-        rows = pl.ds(pl.multiple_of(index_ref[first + spot] * depth, depth), depth)
-        parts.append(weight_ref[rows, :])
-    return left_parts(jnp.concatenate(parts, axis=0))
+def order_kernel(sources, index_ref, weight_ref, out_ref):
+    depth = weight_ref.shape[0] // sources
+    for source in range(sources):
+        rows = pl.ds(pl.multiple_of(index_ref[source] * depth, depth), depth)
+        out_ref[source * depth : (source + 1) * depth, :] = left_parts(weight_ref[rows, :])
+
+
+def source_rows(first, pieces, weight_ref):
+    depth = pieces[0].shape[1]
+    return weight_ref[first * depth : (first + len(pieces)) * depth, :]
 
 
 def row_blocks(rows):
     return [slice(base, base + CHUNK) for base in range(0, rows, CHUNK)]
 
 
-def near_kernel(index_ref, own_ref, near_ref, weight_ref, low_ref, high_ref):
-    weight = source_rows(index_ref, 0, [own_ref, near_ref], weight_ref)
+def near_kernel(own_ref, near_ref, weight_ref, low_ref, high_ref):
+    weight = source_rows(0, [own_ref, near_ref], weight_ref)
     half = low_ref.shape[0]
     for rows in row_blocks(half):
         low_ref[rows, :] = block_product([own_ref, near_ref], weight, rows)
@@ -380,9 +387,9 @@
         high_ref[rows, :] = block_product([own_ref, near_ref], weight, later)
 
 
-def far_kernel(count, first, index_ref, *refs):
+def far_kernel(count, first, *refs):
     held, (weight_ref, total_ref, out_ref) = refs[:-3], refs[-3:]
-    weight = source_rows(index_ref, first, held[:count], weight_ref)
+    weight = source_rows(first, held[:count], weight_ref)
     base = 0
     for at in range(0, len(held), count):
         pieces = held[at : at + count]
@@ -392,13 +399,13 @@
         base += pieces[0].shape[0]
 
 
-def last_kernel(count, first, index_ref, *refs):
+def last_kernel(count, first, *refs):
     pieces = refs[:count]
     weight_ref, ready_ref, total_ref, out_ref, held, sems = refs[count:]
     half = ready_ref.shape[0]
     copies = [pltpu.make_async_copy(ready_ref, out_ref.at[:half, :], sems.at[0])]
     copies[0].start()
-    weight = source_rows(index_ref, first, pieces, weight_ref)
+    weight = source_rows(first, pieces, weight_ref)
     for spot, rows in enumerate(row_blocks(total_ref.shape[0])):
         held[rows, :] = total_ref[rows, :] + block_product(pieces, weight, rows)
         out = slice(half + rows.start, half + rows.stop)
@@ -456,8 +463,7 @@
     remote = [(me + heads - 2 * step) % heads for step in range(1, heads // 2)]
     order = [me, me ^ 1] + remote + [index ^ 1 for index in remote]
     bits = blocks.bit_length() - 1
-    flags = [my_index >> bit & 1 for bit in range(bits)]
-    index = jnp.stack(order + flags).astype(jnp.int32)
+    index = jnp.stack(order + [my_index >> bit & 1 for bit in range(bits)]).astype(jnp.int32)
     count = heads - 2
     like = lambda *shape: jax.ShapeDtypeStruct(shape, F32)
     parts = lambda *shape: jax.ShapeDtypeStruct(shape, BF16)
@@ -470,10 +476,11 @@
     beside = to_sibling(tokens)
     early_rows, beside = after(tokens, beside)
     early = to_chips(early_rows[:cut])
-    base_state, base_query, far_state, far_query = vmem_call(
+    base_state, base_query, far_state, far_query, flags = vmem_call(
         base_kernel,
         [like(tok_rows, state_columns), like(tok_rows, query_columns),
-         parts(count * depth, 2 * state_columns), parts(count * depth, 2 * query_columns)],
+         parts(count * depth, 2 * state_columns), parts(count * depth, 2 * query_columns),
+         jax.ShapeDtypeStruct((bits, CHUNK), jnp.int32)],
         [pltpu.VMEM((heads, depth, 4 * width), F32),
          pltpu.VMEM((2 * depth, 2 * state_columns), BF16),
          pltpu.VMEM((2 * depth, 2 * query_columns), BF16),
@@ -514,6 +521,16 @@
     )
 
     pair = earlier[7]
+    fields = vmem_call(
+        functools.partial(query_kernel, count), [like(tok_rows, width)] * 3,
+        [pltpu.VMEM((first + RIM, query_columns), F32)], 5,
+        *early, *early_on, base_query, far_query, rim, late_query, conv_w,
+        *earlier[:5], earlier[6], *later[:5], later[6],
+    )
+    own_weight = vmem_call(
+        functools.partial(order_kernel, heads), parts(w_out.shape[0], 2 * w_out.shape[1]), [], 1,
+        index, w_out,
+    )
     carry = ()
     levels = []
     for bit in range(0, bits - 1, 2):
@@ -523,26 +540,21 @@
             )
             for mask in (1, 2, 3)
         ]
+        if not bit:
+            others[0], *fields, own_weight = after(others[0], *fields, own_weight)
         last = bit + 2 >= bits - 1 and bits % 2
         group = [like(width, width)] if last else [like(2, width, width)]
         pair, level, *carry = vmem_call(
-            functools.partial(four_kernel, heads + bit, bool(carry), last),
-            group + [like(2, width, width), like(width, width)],
-            [pltpu.VMEM((4, 2, width, width), F32)], 1,
-            index, pair, *others, *carry,
+            functools.partial(four_kernel, bit, bool(carry), last),
+            group + [like(2, width, width), like(width, width)], [], 1,
+            flags, pair, *others, *carry,
         )
         levels.append(level)
-    fields = vmem_call(
-        functools.partial(query_kernel, count), [like(tok_rows, width)] * 3,
-        [pltpu.VMEM((first + RIM, query_columns), F32)], 5,
-        *early, *early_on, base_query, far_query, rim, late_query, conv_w,
-        *earlier[:5], earlier[6], *later[:5], later[6],
-    )
     single = []
     if bits % 2:
         reach = blocks // 2
         single = [
-            *(carry or [jnp.eye(width, dtype=F32)]),
+            *(carry or [jnp.where(my_index >= reach, jnp.eye(width, dtype=F32), 0.0)]),
             lax.ppermute(
                 pair if carry else pair[1],
                 "ctx", [(source, source ^ reach) for source in range(blocks)],
@@ -550,9 +562,9 @@
         ]
     half = tok_rows // 2
     normed, *lows, high = vmem_call(
-        functools.partial(mix_kernel, len(levels), heads + bits - 1 if single else 0),
+        functools.partial(mix_kernel, len(levels), bool(single)),
         [like(tok_rows, width)] + [like(half // 2, width)] * 2 + [like(half, width)], [], 1,
-        index, *fields, earlier[5], later[5], norm_gain[None, :], *levels, *single,
+        *fields, earlier[5], later[5], norm_gain[None, :], *levels, *single,
     )
     columns = w_out.shape[1]
     near = to_sibling(normed)
@@ -560,25 +572,25 @@
     high, near = after(high, near)
     far_high = to_chips(high)
     total_low, total_high = vmem_call(
-        near_kernel, [like(half, columns)] * 2, [], 2, index, normed, near, w_out
+        near_kernel, [like(half, columns)] * 2, [], 2, normed, near, own_weight
     )
     far_lows, total_low = after(far_lows, total_low)
     far_lows_on = [[to_sibling(value) for value in values] for values in far_lows]
     arrived = [value for pair in zip(far_lows, far_lows_on) for values in pair for value in values]
     total_low = vmem_call(
         functools.partial(far_kernel, count, 2), like(half, columns), [], 0.01,
-        index, *arrived, w_out, total_low,
+        *arrived, own_weight, total_low,
     )
     far_high, total_low = after(far_high, total_low)
     far_high_on = [to_sibling(value) for value in far_high]
     total_high = vmem_call(
         functools.partial(far_kernel, len(far_high), 2), like(half, columns), [], 1,
-        index, *far_high, w_out, total_high,
+        *far_high, own_weight, total_high,
     )
     return vmem_call(
         functools.partial(last_kernel, len(far_high), 2 + len(far_high)), like(tok_rows, columns),
         [pltpu.VMEM((half, columns), F32), pltpu.SemaphoreType.DMA((half // CHUNK + 1,))], 1,
-        index, *far_high_on, w_out, total_low, total_high, any_out=True,
+        *far_high_on, own_weight, total_low, total_high, any_out=True,
     )
 
 

time: 63 us -> 60.8 us (0.965)
  Pallas kernels: 21.2 us -> 18.5 us
    pallas_call x12 -> x13, Pallas kernels: 21.2 us -> 18.5 us  [vmem_call(): pl.pallas_call(kernel, out_shape=outs, in_specs=[free if spot in any_in e...]
    ppermute x3, waiting for transfers between devices: 6.01 us -> 3.76 us  [shards(): lax.ppermute(pair, 'ctx', [(source, source ^ mask << bit) for source in r...]
    ppermute x1, waiting for transfers between devices: 0.53 us -> 2.43 us  [shards(): lax.ppermute(pair if carry else pair[1], 'ctx', [(source, source ^ reach)...]
    ppermute x6, waiting for transfers between devices: 2.74 us -> 3.57 us  [to_chips(): lax.ppermute(value, 'head', [(source, (source + 2 * step) % count) for so...]
  transfers between devices with their start and end apart: 19 -> 19, of which waited for: 11 -> 14; matrix products, arithmetic and copies ran while one was open for 5% -> 5% of each run, Pallas kernels for 22% -> 22%
where the time goes in v10:
time: 60.8 us; the launch traced here: 60.4 us
  starting transfers between devices  20.5 us (34%)
  Pallas kernels  18.5 us (30%)
  waiting for transfers between devices  13 us (21%)
  local copies, waits for them, and re-layouts  7.44 us (12%)
  between operations  1 us (2%)
    pallas_call x13, Pallas kernels, vmem_call(): pl.pallas_call(kernel, out_shape=outs, in_specs=[free if spot in any_in e...  18.5 us
    ppermute x6, starting transfers between devices, to_chips(): lax.ppermute(value, 'head', [(source, (source + 2 * step) % count) for so...  8.47 us
    unnamed x14, local copies, waits for them, and re-layouts  4.34 us
    ppermute x1, starting transfers between devices, shards(): lax.ppermute(rim, 'ctx', [(source, source + 1) for source in range(blocks...  3.99 us
    ppermute x3, waiting for transfers between devices, shards(): lax.ppermute(pair, 'ctx', [(source, source ^ mask << bit) for source in r...  3.76 us
    ppermute x6, waiting for transfers between devices, to_chips(): lax.ppermute(value, 'head', [(source, (source + 2 * step) % count) for so...  3.57 us
    ppermute x3, starting transfers between devices, shards(): lax.ppermute(pair, 'ctx', [(source, source ^ mask << bit) for source in r...  3.55 us
    ppermute x8, waiting for transfers between devices, to_sibling(): lax.ppermute(value, 'head', [(source, source ^ 1) for source in range(cou...  3.21 us
  transfers between devices with their start and end apart: 19, of which 14 were waited for; matrix products, arithmetic and copies ran while one was open for 5% of the time, Pallas kernels for 22%

profile of v10, /device:TPU:0, one launch (start us, length us, event | category | flops | bytes accessed | tf_op | source)
XLA Modules:
  0.0 60.4 jit_solution(14540488193252848384)
XLA Ops:
  0.5 1.0 %slice.11 = f32[144,512]{1,0:T(8,128)S(1)} slice(f32[512,512]{1,0:T(8,128)} %own_ref.1), slice={[368:512], [0:512]} | slice | bytes 589824 | tf_op jit(solution)/shard_map/slice | solution.py:475
  1.4 2.6 %collective-permute-start.3 = (f32[144,512]{1,0:T(8,128)S(1)}, f32[144,512]{1,0:T(8,128)S(1)}, u32[]{:S(2)}, u32[]{:S(2)}) collective-permute-start(f32[144,512]{1,0:T(8,128)S(1)} %slice.11), channel_id=1, source_target_pairs={{0,2},{1,3},{2,0},{3,1},{4,6},{5,7},{6,4},{7,5},{8,10},{9,11},{10,... | collective-permute-start | bytes 884744 | tf_op jit(solution)/shard_map/ppermute | solution.py:446
  4.0 1.0 %slice.10 = f32[128,512]{1,0:T(8,128)S(1)} slice(f32[512,512]{1,0:T(8,128)} %own_ref.1), slice={[240:368], [0:512]} | slice | bytes 524288 | tf_op jit(solution)/shard_map/slice | solution.py:475
  5.2 1.1 %slice.9 = f32[240,512]{1,0:T(8,128)S(1)} slice(f32[512,512]{1,0:T(8,128)} %own_ref.1), slice={[0:240], [0:512]} | slice | bytes 983040 | tf_op jit(solution)/shard_map/slice | solution.py:478
  6.2 2.1 %collective-permute-start.1 = (f32[240,512]{1,0:T(8,128)S(1)}, f32[240,512]{1,0:T(8,128)S(1)}, u32[]{:S(2)}, u32[]{:S(2)}) collective-permute-start(f32[240,512]{1,0:T(8,128)S(1)} %slice.9), channel_id=1, source_target_pairs={{0,2},{1,3},{2,0},{3,1},{4,6},{5,7},{6,4},{7,5},{8,10},{9,11},{10,... | collective-permute-start | bytes 1474568 | tf_op jit(solution)/shard_map/ppermute | solution.py:446
  8.3 1.2 %copy-done = f32[512,512]{1,0:T(8,128)S(1)} copy-done((f32[512,512]{1,0:T(8,128)S(1)}, f32[512,512]{1,0:T(8,128)}, u32[]{:S(2)}) %copy-start) | copy-done | bytes 1048600
  9.5 2.2 %copy-done.1 = f32[2048,512]{1,0:T(8,128)S(1)} copy-done((f32[2048,512]{1,0:T(8,128)S(1)}, f32[2048,512]{1,0:T(8,128)}, u32[]{:S(2)}) %copy-start.1) | copy-done | bytes 4194328
  11.7 0.9 %copy-done.3 = f32[2048,9]{0,1:T(8,128)S(1)} copy-done((f32[2048,9]{0,1:T(8,128)S(1)}, f32[2048,9]{0,1:T(8,128)}, u32[]{:S(2)}) %copy-start.3) | copy-done | bytes 73752
  12.6 4.0 %shard_map.82 = (f32[512,384]{1,0:T(8,128)S(1)}, f32[512,256]{1,0:T(8,128)S(1)}, bf16[1024,768]{1,0:T(8,128)(2,1)S(1)}, bf16[1024,512]{1,0:T(8,128)(2,1)S(1)}, s32[3,128]{1,0:T(4,128)S(1)}) custom-call(s32[7]{0:T(128)S(1)} %stack.31.index_ref, f32[512,512]{1,0:T(8,128)S(1)} %copy-done, f32[512,512]{1,0:T(8,128)S(1)} %collective-permute-done.beside_ref, ...), custom_call_target="tpu_custom_call" | custom-call | flops 3000000000 | bytes 1048576 | tf_op jit(solution)/shard_map/pallas_call | solution.py:424
  16.6 0.9 %collective-permute-done.2.refs_0_ = f32[128,512]{1,0:T(8,128)S(1)} collective-permute-done((f32[128,512]{1,0:T(8,128)S(1)}, f32[128,512]{1,0:T(8,128)S(1)}, u32[]{:S(2)}, u32[]{:S(2)}) %collective-permute-start.2) | collective-permute-done | bytes 262176 | tf_op jit(solution)/shard_map/ppermute | solution.py:446
  18.7 0.8 %collective-permute-done.4.refs_1_ = f32[128,512]{1,0:T(8,128)S(1)} collective-permute-done((f32[128,512]{1,0:T(8,128)S(1)}, f32[128,512]{1,0:T(8,128)S(1)}, u32[]{:S(2)}, u32[]{:S(2)}) %collective-permute-start.4) | collective-permute-done | bytes 262176 | tf_op jit(solution)/shard_map/ppermute | solution.py:440
  19.5 1.5 %shard_map.83 = (f32[272,384]{1,0:T(8,128)S(1)}, f32[272,256]{1,0:T(8,128)S(1)}, f32[16,384]{1,0:T(8,128)S(1)}) custom-call(f32[128,512]{1,0:T(8,128)S(1)} %collective-permute-done.2.refs_0_, f32[128,512]{1,0:T(8,128)S(1)} %collective-permute-done.4.refs_1_, f32[144,512]{1,0:T(8,128)S(1)} %collective-permute-done.3.refs_2_, ...), custom_call_target="tpu_custom_call" | custom-call | flops 500000000 | bytes 1048576 | tf_op jit(solution)/shard_map/pallas_call | solution.py:424
  21.0 4.0 %collective-permute-start.6 = (f32[16,384]{1,0:T(8,128)S(1)}, f32[16,384]{1,0:T(8,128)S(1)}, u32[]{:S(2)}, u32[]{:S(2)}) collective-permute-start(f32[16,384]{1,0:T(8,128)S(1)} %get-tuple-element.72), channel_id=1, source_target_pairs={{0,4},{4,8},{8,12},{12,16},{16,20},{20,24},{24,28},{1,5},{5,9},{9,... | collective-permute-start | bytes 73736 | tf_op jit(solution)/shard_map/ppermute | solution.py:499
  25.0 2.8 %shard_map.84 = (f32[256,128]{1,0:T(8,128)S(1)}, f32[256,128]{1,0:T(8,128)S(1)}, f32[256,128]{1,0:T(8,128)S(1)}, f32[256,128]{1,0:T(8,128)S(1)}, f32[256,128]{1,...) custom-call(f32[272,384]{1,0:T(8,128)S(1)} %get-tuple-element.70.raw_ref.refs_4_,, ...), custom_call_target="tpu_custom_call" | custom-call | flops 500000000 | bytes 1048576 | tf_op jit(solution)/shard_map/pallas_call | solution.py:424
  27.9 0.7 %shard_map.88.weight_ref.refs_4_.refs_1_ = bf16[512,1024]{1,0:T(8,128)(2,1)S(1)} custom-call(s32[7]{0:T(128)S(1)} %stack.31.index_ref, f32[512,512]{1,0:T(8,128)S(1)} %copy-done.2), custom_call_target="tpu_custom_call" | custom-call | flops 1000000000 | bytes 1048576 | tf_op jit(solution)/shard_map/pallas_call | solution.py:424
  29.0 0.7 %collective-permute-done.7.refs_0_.refs_1_ = f32[240,512]{1,0:T(8,128)S(1)} collective-permute-done((f32[240,512]{1,0:T(8,128)S(1)}, f32[240,512]{1,0:T(8,128)S(1)}, u32[]{:S(2)}, u32[]{:S(2)}) %collective-permute-start.7) | collective-permute-done | bytes 491552 | tf_op jit(solution)/shard_map/ppermute | solution.py:440
  29.7 3.3 %shard_map.86 = (f32[256,128]{1,0:T(8,128)S(1)}, f32[256,128]{1,0:T(8,128)S(1)}, f32[256,128]{1,0:T(8,128)S(1)}, f32[256,128]{1,0:T(8,128)S(1)}, f32[256,128]{1,...) custom-call(f32[240,512]{1,0:T(8,128)S(1)} %collective-permute-done.7.refs_0_.ref, ...), custom_call_target="tpu_custom_call" | custom-call | flops 5000000000 | bytes 1048576 | tf_op jit(solution)/shard_map/pallas_call | solution.py:424
  33.0 1.8 %collective-permute-start.8 = (f32[2,128,128]{2,1,0:T(8,128)S(1)}, f32[2,128,128]{2,1,0:T(8,128)S(1)}, u32[]{:S(2)}, u32[]{:S(2)}) collective-permute-start(f32[2,128,128]{2,1,0:T(8,128)S(1)} %get-tuple-element.76.own_ref), channel_id=1, source_target_pairs={{0,4},{4,0},{8,12},{12,8},{16,20},{20,16},{24,28},{28,24},{1,5},{5... | collective-permute-start | bytes 393224 | tf_op jit(solution)/shard_map/ppermute | solution.py:538
  34.8 1.5 %collective-permute-start.10 = (f32[2,128,128]{2,1,0:T(8,128)S(1)}, f32[2,128,128]{2,1,0:T(8,128)S(1)}, u32[]{:S(2)}, u32[]{:S(2)}) collective-permute-start(f32[2,128,128]{2,1,0:T(8,128)S(1)} %get-tuple-element.76.own_ref), channel_id=1, source_target_pairs={{0,12},{4,8},{8,4},{12,0},{16,28},{20,24},{24,20},{28,16},{1,13},{... | collective-permute-start | bytes 393224 | tf_op jit(solution)/shard_map/ppermute | solution.py:538
  36.6 2.4 %shard_map.87 = (f32[512,128]{1,0:T(8,128)S(1)}, f32[512,128]{1,0:T(8,128)S(1)}, f32[512,128]{1,0:T(8,128)S(1)}) custom-call(f32[240,512]{1,0:T(8,128)S(1)} %collective-permute-done.1.refs_0_, f32[240,512]{1,0:T(8,128)S(1)} %collective-permute-done.7.refs_0_.refs_1_, f32[512,256]{1,0:T(8,128)S(1)} %get-tuple-element.67.refs_5_.refs_2_, ...), custom_call_target="tpu_custom_call" | custom-call | flops 5000000000 | bytes 1048576 | tf_op jit(solution)/shard_map/pallas_call | solution.py:424
  39.0 1.8 %collective-permute-done.8.one_ref = f32[2,128,128]{2,1,0:T(8,128)S(1)} collective-permute-done((f32[2,128,128]{2,1,0:T(8,128)S(1)}, f32[2,128,128]{2,1,0:T(8,128)S(1)}, u32[]{:S(2)}, u32[]{:S(2)}) %collective-permute-start.8) | collective-permute-done | bytes 131104 | tf_op jit(solution)/shard_map/ppermute | solution.py:538
  40.8 1.3 %collective-permute-done.10.three_ref = f32[2,128,128]{2,1,0:T(8,128)S(1)} collective-permute-done((f32[2,128,128]{2,1,0:T(8,128)S(1)}, f32[2,128,128]{2,1,0:T(8,128)S(1)}, u32[]{:S(2)}, u32[]{:S(2)}) %collective-permute-start.10) | collective-permute-done | bytes 131104 | tf_op jit(solution)/shard_map/ppermute | solution.py:538
  42.1 0.7 %collective-permute-done.9.two_ref = f32[2,128,128]{2,1,0:T(8,128)S(1)} collective-permute-done((f32[2,128,128]{2,1,0:T(8,128)S(1)}, f32[2,128,128]{2,1,0:T(8,128)S(1)}, u32[]{:S(2)}, u32[]{:S(2)}) %collective-permute-start.9) | collective-permute-done | bytes 131104 | tf_op jit(solution)/shard_map/ppermute | solution.py:538
  43.2 2.8 %collective-permute-start.11 = (f32[128,128]{1,0:T(8,128)S(1)}, f32[128,128]{1,0:T(8,128)S(1)}, u32[]{:S(2)}, u32[]{:S(2)}) collective-permute-start(f32[128,128]{1,0:T(8,128)S(1)} %get-tuple-element.102), channel_id=1, source_target_pairs={{0,16},{4,20},{8,24},{12,28},{16,0},{20,4},{24,8},{28,12},{1,17},{... | collective-permute-start | bytes 196616 | tf_op jit(solution)/shard_map/ppermute | solution.py:558
  46.0 2.4 %collective-permute-done.11.refs_2_ = f32[128,128]{1,0:T(8,128)S(1)} collective-permute-done((f32[128,128]{1,0:T(8,128)S(1)}, f32[128,128]{1,0:T(8,128)S(1)}, u32[]{:S(2)}, u32[]{:S(2)}) %collective-permute-start.11) | collective-permute-done | bytes 65568 | tf_op jit(solution)/shard_map/ppermute | solution.py:558
  49.1 1.7 %collective-permute-start.14 = (f32[128,128]{1,0:T(8,128)S(1)}, f32[128,128]{1,0:T(8,128)S(1)}, u32[]{:S(2)}, u32[]{:S(2)}) collective-permute-start(f32[128,128]{1,0:T(8,128)S(1)} %get-tuple-element.106), channel_id=1, source_target_pairs={{0,2},{1,3},{2,0},{3,1},{4,6},{5,7},{6,4},{7,5},{8,10},{9,11},{10,... | collective-permute-start | bytes 196616 | tf_op jit(solution)/shard_map/ppermute | solution.py:446
  51.2 1.7 %collective-permute-start.13 = (f32[256,128]{1,0:T(8,128)S(1)}, f32[256,128]{1,0:T(8,128)S(1)}, u32[]{:S(2)}, u32[]{:S(2)}) collective-permute-start(f32[256,128]{1,0:T(8,128)S(1)} %get-tuple-element.105), channel_id=1, source_target_pairs={{0,2},{1,3},{2,0},{3,1},{4,6},{5,7},{6,4},{7,5},{8,10},{9,11},{10,... | collective-permute-start | bytes 393224 | tf_op jit(solution)/shard_map/ppermute | solution.py:446
  52.9 0.6 shard_map.91
  53.7 2.1 %collective-permute-done.15.refs_2_ = f32[128,128]{1,0:T(8,128)S(1)} collective-permute-done((f32[128,128]{1,0:T(8,128)S(1)}, f32[128,128]{1,0:T(8,128)S(1)}, u32[]{:S(2)}, u32[]{:S(2)}) %collective-permute-start.15) | collective-permute-done | bytes 65568 | tf_op jit(solution)/shard_map/ppermute | solution.py:446
  56.3 0.7 %collective-permute-done.16.refs_1_ = f32[128,128]{1,0:T(8,128)S(1)} collective-permute-done((f32[128,128]{1,0:T(8,128)S(1)}, f32[128,128]{1,0:T(8,128)S(1)}, u32[]{:S(2)}, u32[]{:S(2)}) %collective-permute-start.16) | collective-permute-done | bytes 65568 | tf_op jit(solution)/shard_map/ppermute | solution.py:440
  58.4 0.8 %collective-permute-done.18.refs_0_ = f32[256,128]{1,0:T(8,128)S(1)} collective-permute-done((f32[256,128]{1,0:T(8,128)S(1)}, f32[256,128]{1,0:T(8,128)S(1)}, u32[]{:S(2)}, u32[]{:S(2)}) %collective-permute-start.18) | collective-permute-done | bytes 131104 | tf_op jit(solution)/shard_map/ppermute | solution.py:440
  59.2 1.1 %shard_map.94 = f32[512,512]{1,0:T(8,128)} custom-call(f32[256,128]{1,0:T(8,128)S(1)} %collective-permute-done.18.refs_0_, bf16[512,1024]{1,0:T(8,128)(2,1)S(1)} %shard_map.88.weight_ref.refs_4_.refs_1_, f32[256,512]{1,0:T(8,128)S(1)} %shard_map.92.refs_2_, f32[256,512]{1,0:T(8,128)S(1)} %shard_map.93.refs_3_), custom_call_target="tpu_custom_call" | custom-call | flops 1000000000 | bytes 1048576 | tf_op jit(solution)/shard_map/pallas_call | solution.py:424
  (37 shorter events, 5.5 us)
Async XLA Ops:
  0.0 5.2 %collective-permute-start = (f32[512,512]{1,0:T(8,128)}, f32[512,512]{1,0:T(8,128)S(1)}, u32[]{:S(2)}, u32[]{:S(2)}) collective-permute-start(f32[512,512]{1,0:T(8,128)} %own_ref.1), channel_id=1, source_target_pairs={{0,1},{1,0},{2,3},{3,2},{4,5},{5,4},{6,7},{7,6},{8,9},{9,8},{10,11... | collective-permute-start | bytes 3145736 | tf_op jit(solution)/shard_map/ppermute | solution.py:440
  1.4 16.1 %collective-permute-start.3 = (f32[144,512]{1,0:T(8,128)S(1)}, f32[144,512]{1,0:T(8,128)S(1)}, u32[]{:S(2)}, u32[]{:S(2)}) collective-permute-start(f32[144,512]{1,0:T(8,128)S(1)} %slice.11), channel_id=1, source_target_pairs={{0,2},{1,3},{2,0},{3,1},{4,6},{5,7},{6,4},{7,5},{8,10},{9,11},{10,... | collective-permute-start | bytes 884744 | tf_op jit(solution)/shard_map/ppermute | solution.py:446
  5.0 12.5 %collective-permute-start.2 = (f32[128,512]{1,0:T(8,128)S(1)}, f32[128,512]{1,0:T(8,128)S(1)}, u32[]{:S(2)}, u32[]{:S(2)}) collective-permute-start(f32[128,512]{1,0:T(8,128)S(1)} %slice.10), channel_id=1, source_target_pairs={{0,2},{1,3},{2,0},{3,1},{4,6},{5,7},{6,4},{7,5},{8,10},{9,11},{10,... | collective-permute-start | bytes 786440 | tf_op jit(solution)/shard_map/ppermute | solution.py:446
  6.2 21.6 %collective-permute-start.1 = (f32[240,512]{1,0:T(8,128)S(1)}, f32[240,512]{1,0:T(8,128)S(1)}, u32[]{:S(2)}, u32[]{:S(2)}) collective-permute-start(f32[240,512]{1,0:T(8,128)S(1)} %slice.9), channel_id=1, source_target_pairs={{0,2},{1,3},{2,0},{3,1},{4,6},{5,7},{6,4},{7,5},{8,10},{9,11},{10,... | collective-permute-start | bytes 1474568 | tf_op jit(solution)/shard_map/ppermute | solution.py:446
  8.3 1.2 %copy-start = (f32[512,512]{1,0:T(8,128)S(1)}, f32[512,512]{1,0:T(8,128)}, u32[]{:S(2)}) copy-start(f32[512,512]{1,0:T(8,128)} %own_ref.1) | copy-start | bytes 3145732
  9.5 2.2 %copy-start.1 = (f32[2048,512]{1,0:T(8,128)S(1)}, f32[2048,512]{1,0:T(8,128)}, u32[]{:S(2)}) copy-start(f32[2048,512]{1,0:T(8,128)} %proj_ref.1) | copy-start | bytes 12582916
  11.7 0.9 %copy-start.3 = (f32[2048,9]{0,1:T(8,128)S(1)}, f32[2048,9]{0,1:T(8,128)}, u32[]{:S(2)}) copy-start(f32[2048,9]{0,1:T(8,128)} %param.10) | copy-start | bytes 221188
  16.6 8.4 %copy-start.4 = (f32[4,384]{1,0:T(4,128)S(1)}, f32[4,384]{1,0:T(4,128)}, u32[]{:S(2)}) copy-start(f32[4,384]{1,0:T(4,128)} %refs_6_.3) | copy-start | bytes 18436
  16.6 8.4 %copy-start.5 = (s32[512]{0:T(512)S(1)}, s32[512]{0:T(512)}, u32[]{:S(2)}) copy-start(s32[512]{0:T(512)} %param.13) | copy-start | bytes 6148
  16.6 11.2 %copy-start.2 = (f32[512,512]{1,0:T(8,128)S(1)}, f32[512,512]{1,0:T(8,128)}, u32[]{:S(2)}) copy-start(f32[512,512]{1,0:T(8,128)} %weight_ref.1) | copy-start | bytes 3145732
  17.5 2.0 %collective-permute-start.5 = (f32[144,512]{1,0:T(8,128)S(1)}, f32[144,512]{1,0:T(8,128)S(1)}, u32[]{:S(2)}, u32[]{:S(2)}) collective-permute-start(f32[144,512]{1,0:T(8,128)S(1)} %collective-permute-done.3.refs_2_), channel_id=1, source_target_pairs={{0,1},{1,0},{2,3},{3,2},{4,5},{5,4},{6,7},{7,6},{8,9},{9,8},{10,11... | collective-permute-start | bytes 884744 | tf_op jit(solution)/shard_map/ppermute | solution.py:440
  17.5 2.0 %collective-permute-start.4 = (f32[128,512]{1,0:T(8,128)S(1)}, f32[128,512]{1,0:T(8,128)S(1)}, u32[]{:S(2)}, u32[]{:S(2)}) collective-permute-start(f32[128,512]{1,0:T(8,128)S(1)} %collective-permute-done.2.refs_0_), channel_id=1, source_target_pairs={{0,1},{1,0},{2,3},{3,2},{4,5},{5,4},{6,7},{7,6},{8,9},{9,8},{10,11... | collective-permute-start | bytes 786440 | tf_op jit(solution)/shard_map/ppermute | solution.py:440
  21.0 6.8 %collective-permute-start.6 = (f32[16,384]{1,0:T(8,128)S(1)}, f32[16,384]{1,0:T(8,128)S(1)}, u32[]{:S(2)}, u32[]{:S(2)}) collective-permute-start(f32[16,384]{1,0:T(8,128)S(1)} %get-tuple-element.72), channel_id=1, source_target_pairs={{0,4},{4,8},{8,12},{12,16},{16,20},{20,24},{24,28},{1,5},{5,9},{9,... | collective-permute-start | bytes 73736 | tf_op jit(solution)/shard_map/ppermute | solution.py:499
  27.9 1.9 %collective-permute-start.7 = (f32[240,512]{1,0:T(8,128)S(1)}, f32[240,512]{1,0:T(8,128)S(1)}, u32[]{:S(2)}, u32[]{:S(2)}) collective-permute-start(f32[240,512]{1,0:T(8,128)S(1)} %collective-permute-done.1.refs_0_), channel_id=1, source_target_pairs={{0,1},{1,0},{2,3},{3,2},{4,5},{5,4},{6,7},{7,6},{8,9},{9,8},{10,11... | collective-permute-start | bytes 1474568 | tf_op jit(solution)/shard_map/ppermute | solution.py:440
  33.0 7.8 %collective-permute-start.8 = (f32[2,128,128]{2,1,0:T(8,128)S(1)}, f32[2,128,128]{2,1,0:T(8,128)S(1)}, u32[]{:S(2)}, u32[]{:S(2)}) collective-permute-start(f32[2,128,128]{2,1,0:T(8,128)S(1)} %get-tuple-element.76.own_ref), channel_id=1, source_target_pairs={{0,4},{4,0},{8,12},{12,8},{16,20},{20,16},{24,28},{28,24},{1,5},{5... | collective-permute-start | bytes 393224 | tf_op jit(solution)/shard_map/ppermute | solution.py:538
  34.8 7.3 %collective-permute-start.10 = (f32[2,128,128]{2,1,0:T(8,128)S(1)}, f32[2,128,128]{2,1,0:T(8,128)S(1)}, u32[]{:S(2)}, u32[]{:S(2)}) collective-permute-start(f32[2,128,128]{2,1,0:T(8,128)S(1)} %get-tuple-element.76.own_ref), channel_id=1, source_target_pairs={{0,12},{4,8},{8,4},{12,0},{16,28},{20,24},{24,20},{28,16},{1,13},{... | collective-permute-start | bytes 393224 | tf_op jit(solution)/shard_map/ppermute | solution.py:538
  36.4 6.4 %collective-permute-start.9 = (f32[2,128,128]{2,1,0:T(8,128)S(1)}, f32[2,128,128]{2,1,0:T(8,128)S(1)}, u32[]{:S(2)}, u32[]{:S(2)}) collective-permute-start(f32[2,128,128]{2,1,0:T(8,128)S(1)} %get-tuple-element.76.own_ref), channel_id=1, source_target_pairs={{0,8},{4,12},{8,0},{12,4},{16,24},{20,28},{24,16},{28,20},{1,9},{5... | collective-permute-start | bytes 393224 | tf_op jit(solution)/shard_map/ppermute | solution.py:538
  36.6 11.9 %copy-start.6 = (f32[128]{0:T(128)S(1)}, f32[128]{0:T(128)}, u32[]{:S(2)}) copy-start(f32[128]{0:T(128)} %param.14) | copy-start | bytes 1540
  43.2 5.2 %collective-permute-start.11 = (f32[128,128]{1,0:T(8,128)S(1)}, f32[128,128]{1,0:T(8,128)S(1)}, u32[]{:S(2)}, u32[]{:S(2)}) collective-permute-start(f32[128,128]{1,0:T(8,128)S(1)} %get-tuple-element.102), channel_id=1, source_target_pairs={{0,16},{4,20},{8,24},{12,28},{16,0},{20,4},{24,8},{28,12},{1,17},{... | collective-permute-start | bytes 196616 | tf_op jit(solution)/shard_map/ppermute | solution.py:558
  49.0 2.2 %collective-permute-start.12 = (f32[512,128]{1,0:T(8,128)S(1)}, f32[512,128]{1,0:T(8,128)S(1)}, u32[]{:S(2)}, u32[]{:S(2)}) collective-permute-start(f32[512,128]{1,0:T(8,128)S(1)} %get-tuple-element.104.own_ref), channel_id=1, source_target_pairs={{0,1},{1,0},{2,3},{3,2},{4,5},{5,4},{6,7},{7,6},{8,9},{9,8},{10,11... | collective-permute-start | bytes 786440 | tf_op jit(solution)/shard_map/ppermute | solution.py:440
  49.1 4.6 %collective-permute-start.14 = (f32[128,128]{1,0:T(8,128)S(1)}, f32[128,128]{1,0:T(8,128)S(1)}, u32[]{:S(2)}, u32[]{:S(2)}) collective-permute-start(f32[128,128]{1,0:T(8,128)S(1)} %get-tuple-element.106), channel_id=1, source_target_pairs={{0,2},{1,3},{2,0},{3,1},{4,6},{5,7},{6,4},{7,5},{8,10},{9,11},{10,... | collective-permute-start | bytes 196616 | tf_op jit(solution)/shard_map/ppermute | solution.py:446
  50.8 4.9 %collective-permute-start.15 = (f32[128,128]{1,0:T(8,128)S(1)}, f32[128,128]{1,0:T(8,128)S(1)}, u32[]{:S(2)}, u32[]{:S(2)}) collective-permute-start(f32[128,128]{1,0:T(8,128)S(1)} %get-tuple-element.107), channel_id=1, source_target_pairs={{0,2},{1,3},{2,0},{3,1},{4,6},{5,7},{6,4},{7,5},{8,10},{9,11},{10,... | collective-permute-start | bytes 196616 | tf_op jit(solution)/shard_map/ppermute | solution.py:446
  51.2 6.6 %collective-permute-start.13 = (f32[256,128]{1,0:T(8,128)S(1)}, f32[256,128]{1,0:T(8,128)S(1)}, u32[]{:S(2)}, u32[]{:S(2)}) collective-permute-start(f32[256,128]{1,0:T(8,128)S(1)} %get-tuple-element.105), channel_id=1, source_target_pairs={{0,2},{1,3},{2,0},{3,1},{4,6},{5,7},{6,4},{7,5},{8,10},{9,11},{10,... | collective-permute-start | bytes 393224 | tf_op jit(solution)/shard_map/ppermute | solution.py:446
  55.8 1.3 %collective-permute-start.16 = (f32[128,128]{1,0:T(8,128)S(1)}, f32[128,128]{1,0:T(8,128)S(1)}, u32[]{:S(2)}, u32[]{:S(2)}) collective-permute-start(f32[128,128]{1,0:T(8,128)S(1)} %collective-permute-done.14.refs_0_), channel_id=1, source_target_pairs={{0,1},{1,0},{2,3},{3,2},{4,5},{5,4},{6,7},{7,6},{8,9},{9,8},{10,11... | collective-permute-start | bytes 196616 | tf_op jit(solution)/shard_map/ppermute | solution.py:440
  55.8 1.4 %collective-permute-start.17 = (f32[128,128]{1,0:T(8,128)S(1)}, f32[128,128]{1,0:T(8,128)S(1)}, u32[]{:S(2)}, u32[]{:S(2)}) collective-permute-start(f32[128,128]{1,0:T(8,128)S(1)} %collective-permute-done.15.refs_2_), channel_id=1, source_target_pairs={{0,1},{1,0},{2,3},{3,2},{4,5},{5,4},{6,7},{7,6},{8,9},{9,8},{10,11... | collective-permute-start | bytes 196616 | tf_op jit(solution)/shard_map/ppermute | solution.py:440
  57.8 1.3 %collective-permute-start.18 = (f32[256,128]{1,0:T(8,128)S(1)}, f32[256,128]{1,0:T(8,128)S(1)}, u32[]{:S(2)}, u32[]{:S(2)}) collective-permute-start(f32[256,128]{1,0:T(8,128)S(1)} %collective-permute-done.13.refs_0_), channel_id=1, source_target_pairs={{0,1},{1,0},{2,3},{3,2},{4,5},{5,4},{6,7},{7,6},{8,9},{9,8},{10,11... | collective-permute-start | bytes 393224 | tf_op jit(solution)/shard_map/ppermute | solution.py:440

commit v11 on v10

--- a/solution.py
+++ b/solution.py
@@ -293,18 +293,14 @@
             local_ref[out, :] = local
 
 
-def four_kernel(bit, carried, last, flag_ref, own_ref, one_ref, two_ref, three_ref, *refs):
+def four_kernel(bit, carried, last, flag_ref, four_ref, *refs):
     group_ref, level_ref, next_ref = refs[-3:]
     width = next_ref.shape[0]
     flag = lambda at: jnp.broadcast_to(flag_ref[at : at + 1, :], (width, width)) == 1
     set_low, set_high = flag(bit), flag(bit + 1)
-    held = (own_ref, one_ref, two_ref, three_ref)
-
-    def placed(part):
-        by_low = [jnp.where(set_low, held[at ^ 1][part], held[at][part]) for at in range(4)]
-        return [jnp.where(set_high, by_low[at ^ 2], by_low[at]) for at in range(4)]
-
-    trans, memory = placed(0), placed(1)
+    trans = [four_ref[2 * at] for at in range(4)]
+    memory = [four_ref[2 * at + 1] for at in range(4)]
+    one_a, one_s = (jnp.where(set_high, part[2], part[0]) for part in (trans, memory))
     joined = lambda at: jnp.concatenate([trans[at], memory[at]], axis=1)
     onto_low = product(trans[1], joined(0))
     onto_high = product(trans[3], joined(2))
@@ -318,13 +314,13 @@
         group_ref[1] = onto[:, width:] + high_s
     if carried:
         carry = refs[0][...]
-        first = product(carry, jnp.concatenate([one_ref[0], one_ref[1]], axis=1))
+        first = product(carry, jnp.concatenate([one_a, one_s], axis=1))
         first_a, first_s = first[:, :width], first[:, width:]
     else:
         row = lax.broadcasted_iota(jnp.int32, (width, width), 0)
         col = lax.broadcasted_iota(jnp.int32, (width, width), 1)
         carry = jnp.where(row == col, 1.0, 0.0).astype(F32)
-        first_a, first_s = one_ref[0], one_ref[1]
+        first_a, first_s = one_a, one_s
     level_ref[0] = jnp.where(set_low, first_s, 0.0)
     carry = jnp.where(set_low, first_a, carry)
     second = product(carry, jnp.concatenate([low_a, low_s], axis=1))
@@ -534,20 +530,20 @@
     carry = ()
     levels = []
     for bit in range(0, bits - 1, 2):
-        others = [
-            lax.ppermute(
-                pair, "ctx", [(source, source ^ (mask << bit)) for source in range(blocks)]
-            )
-            for mask in (1, 2, 3)
+        groups = [
+            [base + (at << bit) for at in range(4)]
+            for base in range(blocks)
+            if not base >> bit & 3
         ]
+        four = lax.all_gather(pair, "ctx", axis_index_groups=groups, tiled=True)
         if not bit:
-            others[0], *fields, own_weight = after(others[0], *fields, own_weight)
+            four, *fields, own_weight = after(four, *fields, own_weight)
         last = bit + 2 >= bits - 1 and bits % 2
         group = [like(width, width)] if last else [like(2, width, width)]
         pair, level, *carry = vmem_call(
             functools.partial(four_kernel, bit, bool(carry), last),
             group + [like(2, width, width), like(width, width)], [], 1,
-            flags, pair, *others, *carry,
+            flags, four, *carry,
         )
         levels.append(level)
     single = []

time: 60.8 us -> 68.5 us (1.13)
  blocking collectives: 0 us -> 14.4 us
  starting transfers between devices: 20.5 us -> 16.4 us
  waiting for transfers between devices: 13 us -> 10.5 us
    all_gather x0 -> x1, blocking collectives: none -> 14.4 us  [shards(): four = lax.all_gather(pair, 'ctx', axis_index_groups=groups, tiled=True)]
    ppermute x3 -> x0, waiting for transfers between devices: 3.76 us -> none  [shards(): lax.ppermute(pair, 'ctx', [(source, source ^ mask << bit) for source in r...]
    ppermute x3 -> x0, starting transfers between devices: 3.55 us -> none  [shards(): lax.ppermute(pair, 'ctx', [(source, source ^ mask << bit) for source in r...]
    ppermute x1, waiting for transfers between devices: 2.43 us -> 3.28 us  [shards(): lax.ppermute(pair if carry else pair[1], 'ctx', [(source, source ^ reach)...]
  transfers between devices with their start and end apart: 19 -> 16, of which waited for: 14 -> 11; matrix products, arithmetic and copies ran while one was open for 5% -> 5% of each run, Pallas kernels for 22% -> 16%
where the time goes in v11:
time: 68.5 us; the launch traced here: 68.2 us
  Pallas kernels  18.5 us (27%)
  starting transfers between devices  16.4 us (24%)
  blocking collectives  14.4 us (21%)
  waiting for transfers between devices  10.5 us (15%)
  local copies, waits for them, and re-layouts  7.44 us (11%)
  between operations  1 us (1%)
    pallas_call x13, Pallas kernels, vmem_call(): pl.pallas_call(kernel, out_shape=outs, in_specs=[free if spot in any_in e...  18.5 us
    all_gather x1, blocking collectives, shards(): four = lax.all_gather(pair, 'ctx', axis_index_groups=groups, tiled=True)  14.4 us
    ppermute x6, starting transfers between devices, to_chips(): lax.ppermute(value, 'head', [(source, (source + 2 * step) % count) for so...  8.33 us
    unnamed x14, local copies, waits for them, and re-layouts  4.34 us
    ppermute x6, waiting for transfers between devices, to_chips(): lax.ppermute(value, 'head', [(source, (source + 2 * step) % count) for so...  3.89 us
    ppermute x1, starting transfers between devices, shards(): lax.ppermute(rim, 'ctx', [(source, source + 1) for source in range(blocks...  3.81 us
    ppermute x8, waiting for transfers between devices, to_sibling(): lax.ppermute(value, 'head', [(source, source ^ 1) for source in range(cou...  3.35 us
    ppermute x1, waiting for transfers between devices, shards(): lax.ppermute(pair if carry else pair[1], 'ctx', [(source, source ^ reach)...  3.28 us
  transfers between devices with their start and end apart: 16, of which 11 were waited for; matrix products, arithmetic and copies ran while one was open for 5% of the time, Pallas kernels for 16%

profile of v11, /device:TPU:0, one launch (start us, length us, event | category | flops | bytes accessed | tf_op | source)
XLA Modules:
  0.0 68.2 jit_solution(15463718391104952402)
XLA Ops:
  0.5 1.0 %slice.11 = f32[144,512]{1,0:T(8,128)S(1)} slice(f32[512,512]{1,0:T(8,128)} %own_ref.1), slice={[368:512], [0:512]} | slice | bytes 589824 | tf_op jit(solution)/shard_map/slice | solution.py:471
  1.4 2.6 %collective-permute-start.3 = (f32[144,512]{1,0:T(8,128)S(1)}, f32[144,512]{1,0:T(8,128)S(1)}, u32[]{:S(2)}, u32[]{:S(2)}) collective-permute-start(f32[144,512]{1,0:T(8,128)S(1)} %slice.11), channel_id=1, source_target_pairs={{0,2},{1,3},{2,0},{3,1},{4,6},{5,7},{6,4},{7,5},{8,10},{9,11},{10,... | collective-permute-start | bytes 884744 | tf_op jit(solution)/shard_map/ppermute | solution.py:442
  4.0 1.0 %slice.10 = f32[128,512]{1,0:T(8,128)S(1)} slice(f32[512,512]{1,0:T(8,128)} %own_ref.1), slice={[240:368], [0:512]} | slice | bytes 524288 | tf_op jit(solution)/shard_map/slice | solution.py:471
  5.2 1.1 %slice.9 = f32[240,512]{1,0:T(8,128)S(1)} slice(f32[512,512]{1,0:T(8,128)} %own_ref.1), slice={[0:240], [0:512]} | slice | bytes 983040 | tf_op jit(solution)/shard_map/slice | solution.py:474
  6.2 2.1 %collective-permute-start.1 = (f32[240,512]{1,0:T(8,128)S(1)}, f32[240,512]{1,0:T(8,128)S(1)}, u32[]{:S(2)}, u32[]{:S(2)}) collective-permute-start(f32[240,512]{1,0:T(8,128)S(1)} %slice.9), channel_id=1, source_target_pairs={{0,2},{1,3},{2,0},{3,1},{4,6},{5,7},{6,4},{7,5},{8,10},{9,11},{10,... | collective-permute-start | bytes 1474568 | tf_op jit(solution)/shard_map/ppermute | solution.py:442
  8.3 1.2 %copy-done = f32[512,512]{1,0:T(8,128)S(1)} copy-done((f32[512,512]{1,0:T(8,128)S(1)}, f32[512,512]{1,0:T(8,128)}, u32[]{:S(2)}) %copy-start) | copy-done | bytes 1048600
  9.5 2.2 %copy-done.1 = f32[2048,512]{1,0:T(8,128)S(1)} copy-done((f32[2048,512]{1,0:T(8,128)S(1)}, f32[2048,512]{1,0:T(8,128)}, u32[]{:S(2)}) %copy-start.1) | copy-done | bytes 4194328
  11.7 0.9 %copy-done.3 = f32[2048,9]{0,1:T(8,128)S(1)} copy-done((f32[2048,9]{0,1:T(8,128)S(1)}, f32[2048,9]{0,1:T(8,128)}, u32[]{:S(2)}) %copy-start.3) | copy-done | bytes 73752
  12.6 4.0 %shard_map.82 = (f32[512,384]{1,0:T(8,128)S(1)}, f32[512,256]{1,0:T(8,128)S(1)}, bf16[1024,768]{1,0:T(8,128)(2,1)S(1)}, bf16[1024,512]{1,0:T(8,128)(2,1)S(1)}, s32[3,128]{1,0:T(4,128)S(1)}) custom-call(s32[7]{0:T(128)S(1)} %stack.31.index_ref, f32[512,512]{1,0:T(8,128)S(1)} %copy-done, f32[512,512]{1,0:T(8,128)S(1)} %collective-permute-done.beside_ref, ...), custom_call_target="tpu_custom_call" | custom-call | flops 3000000000 | bytes 1048576 | tf_op jit(solution)/shard_map/pallas_call | solution.py:420
  16.6 0.9 %collective-permute-done.2.refs_0_ = f32[128,512]{1,0:T(8,128)S(1)} collective-permute-done((f32[128,512]{1,0:T(8,128)S(1)}, f32[128,512]{1,0:T(8,128)S(1)}, u32[]{:S(2)}, u32[]{:S(2)}) %collective-permute-start.2) | collective-permute-done | bytes 262176 | tf_op jit(solution)/shard_map/ppermute | solution.py:442
  17.5 0.5 collective-permute-start.4
  18.7 0.8 %collective-permute-done.4.refs_1_ = f32[128,512]{1,0:T(8,128)S(1)} collective-permute-done((f32[128,512]{1,0:T(8,128)S(1)}, f32[128,512]{1,0:T(8,128)S(1)}, u32[]{:S(2)}, u32[]{:S(2)}) %collective-permute-start.4) | collective-permute-done | bytes 262176 | tf_op jit(solution)/shard_map/ppermute | solution.py:436
  19.5 1.5 %shard_map.83 = (f32[272,384]{1,0:T(8,128)S(1)}, f32[272,256]{1,0:T(8,128)S(1)}, f32[16,384]{1,0:T(8,128)S(1)}) custom-call(f32[128,512]{1,0:T(8,128)S(1)} %collective-permute-done.2.refs_0_, f32[128,512]{1,0:T(8,128)S(1)} %collective-permute-done.4.refs_1_, f32[144,512]{1,0:T(8,128)S(1)} %collective-permute-done.3.refs_2_, ...), custom_call_target="tpu_custom_call" | custom-call | flops 500000000 | bytes 1048576 | tf_op jit(solution)/shard_map/pallas_call | solution.py:420
  21.0 3.8 %collective-permute-start.6 = (f32[16,384]{1,0:T(8,128)S(1)}, f32[16,384]{1,0:T(8,128)S(1)}, u32[]{:S(2)}, u32[]{:S(2)}) collective-permute-start(f32[16,384]{1,0:T(8,128)S(1)} %get-tuple-element.72), channel_id=1, source_target_pairs={{0,4},{4,8},{8,12},{12,16},{16,20},{20,24},{24,28},{1,5},{5,9},{9,... | collective-permute-start | bytes 73736 | tf_op jit(solution)/shard_map/ppermute | solution.py:495
  24.8 2.8 %shard_map.84 = (f32[256,128]{1,0:T(8,128)S(1)}, f32[256,128]{1,0:T(8,128)S(1)}, f32[256,128]{1,0:T(8,128)S(1)}, f32[256,128]{1,0:T(8,128)S(1)}, f32[256,128]{1,...) custom-call(f32[272,384]{1,0:T(8,128)S(1)} %get-tuple-element.70.raw_ref.refs_4_,, ...), custom_call_target="tpu_custom_call" | custom-call | flops 500000000 | bytes 1048576 | tf_op jit(solution)/shard_map/pallas_call | solution.py:420
  27.9 0.7 shard_map.88.weight_ref.refs_4_.refs_1_
  29.0 0.7 collective-permute-done.7.refs_0_.refs_1_
  29.7 3.3 %shard_map.86 = (f32[256,128]{1,0:T(8,128)S(1)}, f32[256,128]{1,0:T(8,128)S(1)}, f32[256,128]{1,0:T(8,128)S(1)}, f32[256,128]{1,0:T(8,128)S(1)}, f32[256,128]{1,...) custom-call(f32[240,512]{1,0:T(8,128)S(1)} %collective-permute-done.7.refs_0_.ref, ...), custom_call_target="tpu_custom_call" | custom-call | flops 5000000000 | bytes 1048576 | tf_op jit(solution)/shard_map/pallas_call | solution.py:420
  33.0 14.4 %all_gather.3.four_ref = f32[8,128,128]{2,1,0:T(8,128)S(1)} all-gather(f32[2,128,128]{2,1,0:T(8,128)S(1)} %get-tuple-element.76), channel_id=1, replica_groups={{0,4,8,12},{16,20,24,28},{1,5,9,13},{17,21,25,29},{2,6,10,14},{18,22,26..., dimensions={0}, use_global_device_ids=true | all-gather | bytes 655360 | tf_op jit(solution)/shard_map/all_gather | solution.py:538
  47.4 2.4 %shard_map.87 = (f32[512,128]{1,0:T(8,128)S(1)}, f32[512,128]{1,0:T(8,128)S(1)}, f32[512,128]{1,0:T(8,128)S(1)}) custom-call(f32[240,512]{1,0:T(8,128)S(1)} %collective-permute-done.1.refs_0_, f32[240,512]{1,0:T(8,128)S(1)} %collective-permute-done.7.refs_0_.refs_1_, f32[512,256]{1,0:T(8,128)S(1)} %get-tuple-element.67.refs_5_.refs_2_, ...), custom_call_target="tpu_custom_call" | custom-call | flops 5000000000 | bytes 1048576 | tf_op jit(solution)/shard_map/pallas_call | solution.py:420
  50.3 2.7 %collective-permute-start.8 = (f32[128,128]{1,0:T(8,128)S(1)}, f32[128,128]{1,0:T(8,128)S(1)}, u32[]{:S(2)}, u32[]{:S(2)}) collective-permute-start(f32[128,128]{1,0:T(8,128)S(1)} %get-tuple-element.102), channel_id=1, source_target_pairs={{0,16},{4,20},{8,24},{12,28},{16,0},{20,4},{24,8},{28,12},{1,17},{... | collective-permute-start | bytes 196616 | tf_op jit(solution)/shard_map/ppermute | solution.py:554
  52.9 3.3 %collective-permute-done.8.refs_2_ = f32[128,128]{1,0:T(8,128)S(1)} collective-permute-done((f32[128,128]{1,0:T(8,128)S(1)}, f32[128,128]{1,0:T(8,128)S(1)}, u32[]{:S(2)}, u32[]{:S(2)}) %collective-permute-start.8) | collective-permute-done | bytes 65568 | tf_op jit(solution)/shard_map/ppermute | solution.py:554
  56.2 0.6 shard_map.90
  56.9 1.6 %collective-permute-start.11 = (f32[128,128]{1,0:T(8,128)S(1)}, f32[128,128]{1,0:T(8,128)S(1)}, u32[]{:S(2)}, u32[]{:S(2)}) collective-permute-start(f32[128,128]{1,0:T(8,128)S(1)} %get-tuple-element.106), channel_id=1, source_target_pairs={{0,2},{1,3},{2,0},{3,1},{4,6},{5,7},{6,4},{7,5},{8,10},{9,11},{10,... | collective-permute-start | bytes 196616 | tf_op jit(solution)/shard_map/ppermute | solution.py:442
  59.0 1.5 %collective-permute-start.10 = (f32[256,128]{1,0:T(8,128)S(1)}, f32[256,128]{1,0:T(8,128)S(1)}, u32[]{:S(2)}, u32[]{:S(2)}) collective-permute-start(f32[256,128]{1,0:T(8,128)S(1)} %get-tuple-element.105), channel_id=1, source_target_pairs={{0,2},{1,3},{2,0},{3,1},{4,6},{5,7},{6,4},{7,5},{8,10},{9,11},{10,... | collective-permute-start | bytes 393224 | tf_op jit(solution)/shard_map/ppermute | solution.py:442
  60.5 0.6 shard_map.91
  61.1 0.5 collective-permute-done.11.refs_0_
  61.6 1.8 %collective-permute-done.12.refs_2_ = f32[128,128]{1,0:T(8,128)S(1)} collective-permute-done((f32[128,128]{1,0:T(8,128)S(1)}, f32[128,128]{1,0:T(8,128)S(1)}, u32[]{:S(2)}, u32[]{:S(2)}) %collective-permute-start.12) | collective-permute-done | bytes 65568 | tf_op jit(solution)/shard_map/ppermute | solution.py:442
  63.4 0.5 collective-permute-start.14
  63.9 0.7 %collective-permute-done.13.refs_1_ = f32[128,128]{1,0:T(8,128)S(1)} collective-permute-done((f32[128,128]{1,0:T(8,128)S(1)}, f32[128,128]{1,0:T(8,128)S(1)}, u32[]{:S(2)}, u32[]{:S(2)}) %collective-permute-start.13) | collective-permute-done | bytes 65568 | tf_op jit(solution)/shard_map/ppermute | solution.py:436
  66.0 1.0 %collective-permute-done.15.refs_0_ = f32[256,128]{1,0:T(8,128)S(1)} collective-permute-done((f32[256,128]{1,0:T(8,128)S(1)}, f32[256,128]{1,0:T(8,128)S(1)}, u32[]{:S(2)}, u32[]{:S(2)}) %collective-permute-start.15) | collective-permute-done | bytes 131104 | tf_op jit(solution)/shard_map/ppermute | solution.py:436
  66.9 1.1 %shard_map.94 = f32[512,512]{1,0:T(8,128)} custom-call(f32[256,128]{1,0:T(8,128)S(1)} %collective-permute-done.15.refs_0_, bf16[512,1024]{1,0:T(8,128)(2,1)S(1)} %shard_map.88.weight_ref.refs_4_.refs_1_, f32[256,512]{1,0:T(8,128)S(1)} %shard_map.92.refs_2_, f32[256,512]{1,0:T(8,128)S(1)} %shard_map.93.refs_3_), custom_call_target="tpu_custom_call" | custom-call | flops 1000000000 | bytes 1048576 | tf_op jit(solution)/shard_map/pallas_call | solution.py:420
  (32 shorter events, 3.8 us)
Async XLA Ops:
  0.0 5.2 %collective-permute-start = (f32[512,512]{1,0:T(8,128)}, f32[512,512]{1,0:T(8,128)S(1)}, u32[]{:S(2)}, u32[]{:S(2)}) collective-permute-start(f32[512,512]{1,0:T(8,128)} %own_ref.1), channel_id=1, source_target_pairs={{0,1},{1,0},{2,3},{3,2},{4,5},{5,4},{6,7},{7,6},{8,9},{9,8},{10,11... | collective-permute-start | bytes 3145736 | tf_op jit(solution)/shard_map/ppermute | solution.py:436
  1.4 16.1 %collective-permute-start.3 = (f32[144,512]{1,0:T(8,128)S(1)}, f32[144,512]{1,0:T(8,128)S(1)}, u32[]{:S(2)}, u32[]{:S(2)}) collective-permute-start(f32[144,512]{1,0:T(8,128)S(1)} %slice.11), channel_id=1, source_target_pairs={{0,2},{1,3},{2,0},{3,1},{4,6},{5,7},{6,4},{7,5},{8,10},{9,11},{10,... | collective-permute-start | bytes 884744 | tf_op jit(solution)/shard_map/ppermute | solution.py:442
  5.0 12.5 %collective-permute-start.2 = (f32[128,512]{1,0:T(8,128)S(1)}, f32[128,512]{1,0:T(8,128)S(1)}, u32[]{:S(2)}, u32[]{:S(2)}) collective-permute-start(f32[128,512]{1,0:T(8,128)S(1)} %slice.10), channel_id=1, source_target_pairs={{0,2},{1,3},{2,0},{3,1},{4,6},{5,7},{6,4},{7,5},{8,10},{9,11},{10,... | collective-permute-start | bytes 786440 | tf_op jit(solution)/shard_map/ppermute | solution.py:442
  6.2 21.6 %collective-permute-start.1 = (f32[240,512]{1,0:T(8,128)S(1)}, f32[240,512]{1,0:T(8,128)S(1)}, u32[]{:S(2)}, u32[]{:S(2)}) collective-permute-start(f32[240,512]{1,0:T(8,128)S(1)} %slice.9), channel_id=1, source_target_pairs={{0,2},{1,3},{2,0},{3,1},{4,6},{5,7},{6,4},{7,5},{8,10},{9,11},{10,... | collective-permute-start | bytes 1474568 | tf_op jit(solution)/shard_map/ppermute | solution.py:442
  8.3 1.2 %copy-start = (f32[512,512]{1,0:T(8,128)S(1)}, f32[512,512]{1,0:T(8,128)}, u32[]{:S(2)}) copy-start(f32[512,512]{1,0:T(8,128)} %own_ref.1) | copy-start | bytes 3145732
  9.5 2.2 %copy-start.1 = (f32[2048,512]{1,0:T(8,128)S(1)}, f32[2048,512]{1,0:T(8,128)}, u32[]{:S(2)}) copy-start(f32[2048,512]{1,0:T(8,128)} %proj_ref.1) | copy-start | bytes 12582916
  11.7 0.9 %copy-start.3 = (f32[2048,9]{0,1:T(8,128)S(1)}, f32[2048,9]{0,1:T(8,128)}, u32[]{:S(2)}) copy-start(f32[2048,9]{0,1:T(8,128)} %param.10) | copy-start | bytes 221188
  16.6 8.2 %copy-start.4 = (f32[4,384]{1,0:T(4,128)S(1)}, f32[4,384]{1,0:T(4,128)}, u32[]{:S(2)}) copy-start(f32[4,384]{1,0:T(4,128)} %refs_6_.3) | copy-start | bytes 18436
  16.6 8.2 %copy-start.5 = (s32[512]{0:T(512)S(1)}, s32[512]{0:T(512)}, u32[]{:S(2)}) copy-start(s32[512]{0:T(512)} %param.13) | copy-start | bytes 6148
  16.6 11.2 %copy-start.2 = (f32[512,512]{1,0:T(8,128)S(1)}, f32[512,512]{1,0:T(8,128)}, u32[]{:S(2)}) copy-start(f32[512,512]{1,0:T(8,128)} %weight_ref.1) | copy-start | bytes 3145732
  17.5 2.0 %collective-permute-start.5 = (f32[144,512]{1,0:T(8,128)S(1)}, f32[144,512]{1,0:T(8,128)S(1)}, u32[]{:S(2)}, u32[]{:S(2)}) collective-permute-start(f32[144,512]{1,0:T(8,128)S(1)} %collective-permute-done.3.refs_2_), channel_id=1, source_target_pairs={{0,1},{1,0},{2,3},{3,2},{4,5},{5,4},{6,7},{7,6},{8,9},{9,8},{10,11... | collective-permute-start | bytes 884744 | tf_op jit(solution)/shard_map/ppermute | solution.py:436
  17.5 2.0 %collective-permute-start.4 = (f32[128,512]{1,0:T(8,128)S(1)}, f32[128,512]{1,0:T(8,128)S(1)}, u32[]{:S(2)}, u32[]{:S(2)}) collective-permute-start(f32[128,512]{1,0:T(8,128)S(1)} %collective-permute-done.2.refs_0_), channel_id=1, source_target_pairs={{0,1},{1,0},{2,3},{3,2},{4,5},{5,4},{6,7},{7,6},{8,9},{9,8},{10,11... | collective-permute-start | bytes 786440 | tf_op jit(solution)/shard_map/ppermute | solution.py:436
  21.0 6.6 %collective-permute-start.6 = (f32[16,384]{1,0:T(8,128)S(1)}, f32[16,384]{1,0:T(8,128)S(1)}, u32[]{:S(2)}, u32[]{:S(2)}) collective-permute-start(f32[16,384]{1,0:T(8,128)S(1)} %get-tuple-element.72), channel_id=1, source_target_pairs={{0,4},{4,8},{8,12},{12,16},{16,20},{20,24},{24,28},{1,5},{5,9},{9,... | collective-permute-start | bytes 73736 | tf_op jit(solution)/shard_map/ppermute | solution.py:495
  27.9 1.9 %collective-permute-start.7 = (f32[240,512]{1,0:T(8,128)S(1)}, f32[240,512]{1,0:T(8,128)S(1)}, u32[]{:S(2)}, u32[]{:S(2)}) collective-permute-start(f32[240,512]{1,0:T(8,128)S(1)} %collective-permute-done.1.refs_0_), channel_id=1, source_target_pairs={{0,1},{1,0},{2,3},{3,2},{4,5},{5,4},{6,7},{7,6},{8,9},{9,8},{10,11... | collective-permute-start | bytes 1474568 | tf_op jit(solution)/shard_map/ppermute | solution.py:436
  47.4 8.8 %copy-start.6 = (f32[128]{0:T(128)S(1)}, f32[128]{0:T(128)}, u32[]{:S(2)}) copy-start(f32[128]{0:T(128)} %param.14) | copy-start | bytes 1540
  50.3 5.9 %collective-permute-start.8 = (f32[128,128]{1,0:T(8,128)S(1)}, f32[128,128]{1,0:T(8,128)S(1)}, u32[]{:S(2)}, u32[]{:S(2)}) collective-permute-start(f32[128,128]{1,0:T(8,128)S(1)} %get-tuple-element.102), channel_id=1, source_target_pairs={{0,16},{4,20},{8,24},{12,28},{16,0},{20,4},{24,8},{28,12},{1,17},{... | collective-permute-start | bytes 196616 | tf_op jit(solution)/shard_map/ppermute | solution.py:554
  56.8 2.2 %collective-permute-start.9 = (f32[512,128]{1,0:T(8,128)S(1)}, f32[512,128]{1,0:T(8,128)S(1)}, u32[]{:S(2)}, u32[]{:S(2)}) collective-permute-start(f32[512,128]{1,0:T(8,128)S(1)} %get-tuple-element.104.own_ref), channel_id=1, source_target_pairs={{0,1},{1,0},{2,3},{3,2},{4,5},{5,4},{6,7},{7,6},{8,9},{9,8},{10,11... | collective-permute-start | bytes 786440 | tf_op jit(solution)/shard_map/ppermute | solution.py:436
  56.9 4.7 %collective-permute-start.11 = (f32[128,128]{1,0:T(8,128)S(1)}, f32[128,128]{1,0:T(8,128)S(1)}, u32[]{:S(2)}, u32[]{:S(2)}) collective-permute-start(f32[128,128]{1,0:T(8,128)S(1)} %get-tuple-element.106), channel_id=1, source_target_pairs={{0,2},{1,3},{2,0},{3,1},{4,6},{5,7},{6,4},{7,5},{8,10},{9,11},{10,... | collective-permute-start | bytes 196616 | tf_op jit(solution)/shard_map/ppermute | solution.py:442
  58.5 4.9 %collective-permute-start.12 = (f32[128,128]{1,0:T(8,128)S(1)}, f32[128,128]{1,0:T(8,128)S(1)}, u32[]{:S(2)}, u32[]{:S(2)}) collective-permute-start(f32[128,128]{1,0:T(8,128)S(1)} %get-tuple-element.107), channel_id=1, source_target_pairs={{0,2},{1,3},{2,0},{3,1},{4,6},{5,7},{6,4},{7,5},{8,10},{9,11},{10,... | collective-permute-start | bytes 196616 | tf_op jit(solution)/shard_map/ppermute | solution.py:442
  59.0 6.6 %collective-permute-start.10 = (f32[256,128]{1,0:T(8,128)S(1)}, f32[256,128]{1,0:T(8,128)S(1)}, u32[]{:S(2)}, u32[]{:S(2)}) collective-permute-start(f32[256,128]{1,0:T(8,128)S(1)} %get-tuple-element.105), channel_id=1, source_target_pairs={{0,2},{1,3},{2,0},{3,1},{4,6},{5,7},{6,4},{7,5},{8,10},{9,11},{10,... | collective-permute-start | bytes 393224 | tf_op jit(solution)/shard_map/ppermute | solution.py:442
  63.4 1.3 %collective-permute-start.13 = (f32[128,128]{1,0:T(8,128)S(1)}, f32[128,128]{1,0:T(8,128)S(1)}, u32[]{:S(2)}, u32[]{:S(2)}) collective-permute-start(f32[128,128]{1,0:T(8,128)S(1)} %collective-permute-done.11.refs_0_), channel_id=1, source_target_pairs={{0,1},{1,0},{2,3},{3,2},{4,5},{5,4},{6,7},{7,6},{8,9},{9,8},{10,11... | collective-permute-start | bytes 196616 | tf_op jit(solution)/shard_map/ppermute | solution.py:436
  63.4 1.4 %collective-permute-start.14 = (f32[128,128]{1,0:T(8,128)S(1)}, f32[128,128]{1,0:T(8,128)S(1)}, u32[]{:S(2)}, u32[]{:S(2)}) collective-permute-start(f32[128,128]{1,0:T(8,128)S(1)} %collective-permute-done.12.refs_2_), channel_id=1, source_target_pairs={{0,1},{1,0},{2,3},{3,2},{4,5},{5,4},{6,7},{7,6},{8,9},{9,8},{10,11... | collective-permute-start | bytes 196616 | tf_op jit(solution)/shard_map/ppermute | solution.py:436
  65.6 1.3 %collective-permute-start.15 = (f32[256,128]{1,0:T(8,128)S(1)}, f32[256,128]{1,0:T(8,128)S(1)}, u32[]{:S(2)}, u32[]{:S(2)}) collective-permute-start(f32[256,128]{1,0:T(8,128)S(1)} %collective-permute-done.10.refs_0_), channel_id=1, source_target_pairs={{0,1},{1,0},{2,3},{3,2},{4,5},{5,4},{6,7},{7,6},{8,9},{9,8},{10,11... | collective-permute-start | bytes 393224 | tf_op jit(solution)/shard_map/ppermute | solution.py:436

commit v12 on v10

--- a/solution.py
+++ b/solution.py
@@ -24,14 +24,14 @@
 
 
 def right_parts(value):
-    row = jnp.concatenate(halves(value), axis=1)
-    return jnp.concatenate([row, row], axis=0)
+    return jnp.concatenate(halves(value), axis=1)
 
 
 def parts_dot(left, right):
-    both = jnp.dot(left, right, preferred_element_type=F32)
-    half = both.shape[1] // 2
-    return both[:, :half] + both[:, half:]
+    depth, half = right.shape[0], right.shape[1] // 2
+    both = jnp.dot(left[:, :depth], right, preferred_element_type=F32)
+    rest = jnp.dot(left[:, depth:], right[:, :half], preferred_element_type=F32)
+    return (both[:, :half] + both[:, half:]) + rest
 
 
 def product(left, right):

time: 60.8 us -> 61.1 us (level)
  Pallas kernels: 18.5 us -> 19.3 us
    pallas_call x13, Pallas kernels: 18.5 us -> 19.3 us  [vmem_call(): pl.pallas_call(kernel, out_shape=outs, in_specs=[free if spot in any_in e...]
  transfers between devices with their start and end apart: 19 -> 19, of which waited for: 14 -> 13; matrix products, arithmetic and copies ran while one was open for 5% -> 5% of each run, Pallas kernels for 22% -> 22%
where the time goes in v12:
time: 61.1 us; the launch traced here: 60.7 us
  starting transfers between devices  20.5 us (34%)
  Pallas kernels  19.3 us (32%)
  waiting for transfers between devices  12.4 us (20%)
  local copies, waits for them, and re-layouts  7.44 us (12%)
  between operations  1.02 us (2%)
    pallas_call x13, Pallas kernels, vmem_call(): pl.pallas_call(kernel, out_shape=outs, in_specs=[free if spot in any_in e...  19.3 us
    ppermute x6, starting transfers between devices, to_chips(): lax.ppermute(value, 'head', [(source, (source + 2 * step) % count) for so...  8.46 us
    unnamed x14, local copies, waits for them, and re-layouts  4.34 us
    ppermute x1, starting transfers between devices, shards(): lax.ppermute(rim, 'ctx', [(source, source + 1) for source in range(blocks...  3.99 us
    ppermute x3, starting transfers between devices, shards(): lax.ppermute(pair, 'ctx', [(source, source ^ mask << bit) for source in r...  3.55 us
    ppermute x6, waiting for transfers between devices, to_chips(): lax.ppermute(value, 'head', [(source, (source + 2 * step) % count) for so...  3.48 us
    ppermute x3, waiting for transfers between devices, shards(): lax.ppermute(pair, 'ctx', [(source, source ^ mask << bit) for source in r...  3.27 us
    ppermute x8, waiting for transfers between devices, to_sibling(): lax.ppermute(value, 'head', [(source, source ^ 1) for source in range(cou...  3.21 us
  transfers between devices with their start and end apart: 19, of which 13 were waited for; matrix products, arithmetic and copies ran while one was open for 5% of the time, Pallas kernels for 22%

profile of v12, /device:TPU:0, one launch (start us, length us, event | category | flops | bytes accessed | tf_op | source)
XLA Modules:
  0.0 60.7 jit_solution(5247110206702484533)
XLA Ops:
  0.5 1.0 %slice.11 = f32[144,512]{1,0:T(8,128)S(1)} slice(f32[512,512]{1,0:T(8,128)} %own_ref.1), slice={[368:512], [0:512]} | slice | bytes 589824 | tf_op jit(solution)/shard_map/slice | solution.py:475
  1.4 2.6 %collective-permute-start.3 = (f32[144,512]{1,0:T(8,128)S(1)}, f32[144,512]{1,0:T(8,128)S(1)}, u32[]{:S(2)}, u32[]{:S(2)}) collective-permute-start(f32[144,512]{1,0:T(8,128)S(1)} %slice.11), channel_id=1, source_target_pairs={{0,2},{1,3},{2,0},{3,1},{4,6},{5,7},{6,4},{7,5},{8,10},{9,11},{10,... | collective-permute-start | bytes 884744 | tf_op jit(solution)/shard_map/ppermute | solution.py:446
  4.0 1.0 %slice.10 = f32[128,512]{1,0:T(8,128)S(1)} slice(f32[512,512]{1,0:T(8,128)} %own_ref.1), slice={[240:368], [0:512]} | slice | bytes 524288 | tf_op jit(solution)/shard_map/slice | solution.py:475
  5.2 1.1 %slice.9 = f32[240,512]{1,0:T(8,128)S(1)} slice(f32[512,512]{1,0:T(8,128)} %own_ref.1), slice={[0:240], [0:512]} | slice | bytes 983040 | tf_op jit(solution)/shard_map/slice | solution.py:478
  6.2 2.1 %collective-permute-start.1 = (f32[240,512]{1,0:T(8,128)S(1)}, f32[240,512]{1,0:T(8,128)S(1)}, u32[]{:S(2)}, u32[]{:S(2)}) collective-permute-start(f32[240,512]{1,0:T(8,128)S(1)} %slice.9), channel_id=1, source_target_pairs={{0,2},{1,3},{2,0},{3,1},{4,6},{5,7},{6,4},{7,5},{8,10},{9,11},{10,... | collective-permute-start | bytes 1474568 | tf_op jit(solution)/shard_map/ppermute | solution.py:446
  8.3 1.2 %copy-done = f32[512,512]{1,0:T(8,128)S(1)} copy-done((f32[512,512]{1,0:T(8,128)S(1)}, f32[512,512]{1,0:T(8,128)}, u32[]{:S(2)}) %copy-start) | copy-done | bytes 1048600
  9.5 2.2 %copy-done.1 = f32[2048,512]{1,0:T(8,128)S(1)} copy-done((f32[2048,512]{1,0:T(8,128)S(1)}, f32[2048,512]{1,0:T(8,128)}, u32[]{:S(2)}) %copy-start.1) | copy-done | bytes 4194328
  11.7 0.9 %copy-done.3 = f32[2048,9]{0,1:T(8,128)S(1)} copy-done((f32[2048,9]{0,1:T(8,128)S(1)}, f32[2048,9]{0,1:T(8,128)}, u32[]{:S(2)}) %copy-start.3) | copy-done | bytes 73752
  12.6 4.0 %shard_map.82 = (f32[512,384]{1,0:T(8,128)S(1)}, f32[512,256]{1,0:T(8,128)S(1)}, bf16[1024,768]{1,0:T(8,128)(2,1)S(1)}, bf16[1024,512]{1,0:T(8,128)(2,1)S(1)}, s32[3,128]{1,0:T(4,128)S(1)}) custom-call(s32[7]{0:T(128)S(1)} %stack.31.index_ref, f32[512,512]{1,0:T(8,128)S(1)} %copy-done, f32[512,512]{1,0:T(8,128)S(1)} %collective-permute-done.beside_ref, ...), custom_call_target="tpu_custom_call" | custom-call | flops 3000000000 | bytes 1048576 | tf_op jit(solution)/shard_map/pallas_call | solution.py:424
  16.6 0.9 %collective-permute-done.2.refs_0_ = f32[128,512]{1,0:T(8,128)S(1)} collective-permute-done((f32[128,512]{1,0:T(8,128)S(1)}, f32[128,512]{1,0:T(8,128)S(1)}, u32[]{:S(2)}, u32[]{:S(2)}) %collective-permute-start.2) | collective-permute-done | bytes 262176 | tf_op jit(solution)/shard_map/ppermute | solution.py:446
  18.7 0.8 %collective-permute-done.4.refs_1_ = f32[128,512]{1,0:T(8,128)S(1)} collective-permute-done((f32[128,512]{1,0:T(8,128)S(1)}, f32[128,512]{1,0:T(8,128)S(1)}, u32[]{:S(2)}, u32[]{:S(2)}) %collective-permute-start.4) | collective-permute-done | bytes 262176 | tf_op jit(solution)/shard_map/ppermute | solution.py:440
  19.5 1.5 %shard_map.83 = (f32[272,384]{1,0:T(8,128)S(1)}, f32[272,256]{1,0:T(8,128)S(1)}, f32[16,384]{1,0:T(8,128)S(1)}) custom-call(f32[128,512]{1,0:T(8,128)S(1)} %collective-permute-done.2.refs_0_, f32[128,512]{1,0:T(8,128)S(1)} %collective-permute-done.4.refs_1_, f32[144,512]{1,0:T(8,128)S(1)} %collective-permute-done.3.refs_2_, ...), custom_call_target="tpu_custom_call" | custom-call | flops 500000000 | bytes 1048576 | tf_op jit(solution)/shard_map/pallas_call | solution.py:424
  21.0 4.0 %collective-permute-start.6 = (f32[16,384]{1,0:T(8,128)S(1)}, f32[16,384]{1,0:T(8,128)S(1)}, u32[]{:S(2)}, u32[]{:S(2)}) collective-permute-start(f32[16,384]{1,0:T(8,128)S(1)} %get-tuple-element.72), channel_id=1, source_target_pairs={{0,4},{4,8},{8,12},{12,16},{16,20},{20,24},{24,28},{1,5},{5,9},{9,... | collective-permute-start | bytes 73736 | tf_op jit(solution)/shard_map/ppermute | solution.py:499
  25.0 2.9 %shard_map.84 = (f32[256,128]{1,0:T(8,128)S(1)}, f32[256,128]{1,0:T(8,128)S(1)}, f32[256,128]{1,0:T(8,128)S(1)}, f32[256,128]{1,0:T(8,128)S(1)}, f32[256,128]{1,...) custom-call(f32[272,384]{1,0:T(8,128)S(1)} %get-tuple-element.70.raw_ref.refs_4_,, ...), custom_call_target="tpu_custom_call" | custom-call | flops 500000000 | bytes 1048576 | tf_op jit(solution)/shard_map/pallas_call | solution.py:424
  28.0 0.7 %shard_map.88.weight_ref.refs_4_.refs_1_ = bf16[512,1024]{1,0:T(8,128)(2,1)S(1)} custom-call(s32[7]{0:T(128)S(1)} %stack.31.index_ref, f32[512,512]{1,0:T(8,128)S(1)} %copy-done.2), custom_call_target="tpu_custom_call" | custom-call | flops 1000000000 | bytes 1048576 | tf_op jit(solution)/shard_map/pallas_call | solution.py:424
  29.2 0.7 %collective-permute-done.7.refs_0_.refs_1_ = f32[240,512]{1,0:T(8,128)S(1)} collective-permute-done((f32[240,512]{1,0:T(8,128)S(1)}, f32[240,512]{1,0:T(8,128)S(1)}, u32[]{:S(2)}, u32[]{:S(2)}) %collective-permute-start.7) | collective-permute-done | bytes 491552 | tf_op jit(solution)/shard_map/ppermute | solution.py:440
  29.8 3.5 %shard_map.86 = (f32[256,128]{1,0:T(8,128)S(1)}, f32[256,128]{1,0:T(8,128)S(1)}, f32[256,128]{1,0:T(8,128)S(1)}, f32[256,128]{1,0:T(8,128)S(1)}, f32[256,128]{1,...) custom-call(f32[240,512]{1,0:T(8,128)S(1)} %collective-permute-done.7.refs_0_.ref, ...), custom_call_target="tpu_custom_call" | custom-call | flops 5000000000 | bytes 1048576 | tf_op jit(solution)/shard_map/pallas_call | solution.py:424
  33.4 1.7 %collective-permute-start.8 = (f32[2,128,128]{2,1,0:T(8,128)S(1)}, f32[2,128,128]{2,1,0:T(8,128)S(1)}, u32[]{:S(2)}, u32[]{:S(2)}) collective-permute-start(f32[2,128,128]{2,1,0:T(8,128)S(1)} %get-tuple-element.76.own_ref), channel_id=1, source_target_pairs={{0,4},{4,0},{8,12},{12,8},{16,20},{20,16},{24,28},{28,24},{1,5},{5... | collective-permute-start | bytes 393224 | tf_op jit(solution)/shard_map/ppermute | solution.py:538
  35.0 1.5 %collective-permute-start.10 = (f32[2,128,128]{2,1,0:T(8,128)S(1)}, f32[2,128,128]{2,1,0:T(8,128)S(1)}, u32[]{:S(2)}, u32[]{:S(2)}) collective-permute-start(f32[2,128,128]{2,1,0:T(8,128)S(1)} %get-tuple-element.76.own_ref), channel_id=1, source_target_pairs={{0,12},{4,8},{8,4},{12,0},{16,28},{20,24},{24,20},{28,16},{1,13},{... | collective-permute-start | bytes 393224 | tf_op jit(solution)/shard_map/ppermute | solution.py:538
  36.9 2.8 %shard_map.87 = (f32[512,128]{1,0:T(8,128)S(1)}, f32[512,128]{1,0:T(8,128)S(1)}, f32[512,128]{1,0:T(8,128)S(1)}) custom-call(f32[240,512]{1,0:T(8,128)S(1)} %collective-permute-done.1.refs_0_, f32[240,512]{1,0:T(8,128)S(1)} %collective-permute-done.7.refs_0_.refs_1_, f32[512,256]{1,0:T(8,128)S(1)} %get-tuple-element.67.refs_5_.refs_2_, ...), custom_call_target="tpu_custom_call" | custom-call | flops 5000000000 | bytes 1048576 | tf_op jit(solution)/shard_map/pallas_call | solution.py:424
  39.7 1.5 %collective-permute-done.8.one_ref = f32[2,128,128]{2,1,0:T(8,128)S(1)} collective-permute-done((f32[2,128,128]{2,1,0:T(8,128)S(1)}, f32[2,128,128]{2,1,0:T(8,128)S(1)}, u32[]{:S(2)}, u32[]{:S(2)}) %collective-permute-start.8) | collective-permute-done | bytes 131104 | tf_op jit(solution)/shard_map/ppermute | solution.py:538
  41.2 1.1 %collective-permute-done.10.three_ref = f32[2,128,128]{2,1,0:T(8,128)S(1)} collective-permute-done((f32[2,128,128]{2,1,0:T(8,128)S(1)}, f32[2,128,128]{2,1,0:T(8,128)S(1)}, u32[]{:S(2)}, u32[]{:S(2)}) %collective-permute-start.10) | collective-permute-done | bytes 131104 | tf_op jit(solution)/shard_map/ppermute | solution.py:538
  42.3 0.7 %collective-permute-done.9.two_ref = f32[2,128,128]{2,1,0:T(8,128)S(1)} collective-permute-done((f32[2,128,128]{2,1,0:T(8,128)S(1)}, f32[2,128,128]{2,1,0:T(8,128)S(1)}, u32[]{:S(2)}, u32[]{:S(2)}) %collective-permute-start.9) | collective-permute-done | bytes 131104 | tf_op jit(solution)/shard_map/ppermute | solution.py:538
  43.5 2.8 %collective-permute-start.11 = (f32[128,128]{1,0:T(8,128)S(1)}, f32[128,128]{1,0:T(8,128)S(1)}, u32[]{:S(2)}, u32[]{:S(2)}) collective-permute-start(f32[128,128]{1,0:T(8,128)S(1)} %get-tuple-element.102), channel_id=1, source_target_pairs={{0,16},{4,20},{8,24},{12,28},{16,0},{20,4},{24,8},{28,12},{1,17},{... | collective-permute-start | bytes 196616 | tf_op jit(solution)/shard_map/ppermute | solution.py:558
  46.3 2.5 %collective-permute-done.11.refs_2_ = f32[128,128]{1,0:T(8,128)S(1)} collective-permute-done((f32[128,128]{1,0:T(8,128)S(1)}, f32[128,128]{1,0:T(8,128)S(1)}, u32[]{:S(2)}, u32[]{:S(2)}) %collective-permute-start.11) | collective-permute-done | bytes 65568 | tf_op jit(solution)/shard_map/ppermute | solution.py:558
  49.4 1.7 %collective-permute-start.14 = (f32[128,128]{1,0:T(8,128)S(1)}, f32[128,128]{1,0:T(8,128)S(1)}, u32[]{:S(2)}, u32[]{:S(2)}) collective-permute-start(f32[128,128]{1,0:T(8,128)S(1)} %get-tuple-element.106), channel_id=1, source_target_pairs={{0,2},{1,3},{2,0},{3,1},{4,6},{5,7},{6,4},{7,5},{8,10},{9,11},{10,... | collective-permute-start | bytes 196616 | tf_op jit(solution)/shard_map/ppermute | solution.py:446
  51.5 1.6 %collective-permute-start.13 = (f32[256,128]{1,0:T(8,128)S(1)}, f32[256,128]{1,0:T(8,128)S(1)}, u32[]{:S(2)}, u32[]{:S(2)}) collective-permute-start(f32[256,128]{1,0:T(8,128)S(1)} %get-tuple-element.105), channel_id=1, source_target_pairs={{0,2},{1,3},{2,0},{3,1},{4,6},{5,7},{6,4},{7,5},{8,10},{9,11},{10,... | collective-permute-start | bytes 393224 | tf_op jit(solution)/shard_map/ppermute | solution.py:446
  53.2 0.6 shard_map.91
  54.0 2.1 %collective-permute-done.15.refs_2_ = f32[128,128]{1,0:T(8,128)S(1)} collective-permute-done((f32[128,128]{1,0:T(8,128)S(1)}, f32[128,128]{1,0:T(8,128)S(1)}, u32[]{:S(2)}, u32[]{:S(2)}) %collective-permute-start.15) | collective-permute-done | bytes 65568 | tf_op jit(solution)/shard_map/ppermute | solution.py:446
  56.6 0.7 %collective-permute-done.16.refs_1_ = f32[128,128]{1,0:T(8,128)S(1)} collective-permute-done((f32[128,128]{1,0:T(8,128)S(1)}, f32[128,128]{1,0:T(8,128)S(1)}, u32[]{:S(2)}, u32[]{:S(2)}) %collective-permute-start.16) | collective-permute-done | bytes 65568 | tf_op jit(solution)/shard_map/ppermute | solution.py:440
  58.7 0.8 %collective-permute-done.18.refs_0_ = f32[256,128]{1,0:T(8,128)S(1)} collective-permute-done((f32[256,128]{1,0:T(8,128)S(1)}, f32[256,128]{1,0:T(8,128)S(1)}, u32[]{:S(2)}, u32[]{:S(2)}) %collective-permute-start.18) | collective-permute-done | bytes 131104 | tf_op jit(solution)/shard_map/ppermute | solution.py:440
  59.5 1.1 %shard_map.94 = f32[512,512]{1,0:T(8,128)} custom-call(f32[256,128]{1,0:T(8,128)S(1)} %collective-permute-done.18.refs_0_, bf16[512,1024]{1,0:T(8,128)(2,1)S(1)} %shard_map.88.weight_ref.refs_4_.refs_1_, f32[256,512]{1,0:T(8,128)S(1)} %shard_map.92.refs_2_, f32[256,512]{1,0:T(8,128)S(1)} %shard_map.93.refs_3_), custom_call_target="tpu_custom_call" | custom-call | flops 1000000000 | bytes 1048576 | tf_op jit(solution)/shard_map/pallas_call | solution.py:424
  (37 shorter events, 5.7 us)
Async XLA Ops:
  0.0 5.2 %collective-permute-start = (f32[512,512]{1,0:T(8,128)}, f32[512,512]{1,0:T(8,128)S(1)}, u32[]{:S(2)}, u32[]{:S(2)}) collective-permute-start(f32[512,512]{1,0:T(8,128)} %own_ref.1), channel_id=1, source_target_pairs={{0,1},{1,0},{2,3},{3,2},{4,5},{5,4},{6,7},{7,6},{8,9},{9,8},{10,11... | collective-permute-start | bytes 3145736 | tf_op jit(solution)/shard_map/ppermute | solution.py:440
  1.4 16.1 %collective-permute-start.3 = (f32[144,512]{1,0:T(8,128)S(1)}, f32[144,512]{1,0:T(8,128)S(1)}, u32[]{:S(2)}, u32[]{:S(2)}) collective-permute-start(f32[144,512]{1,0:T(8,128)S(1)} %slice.11), channel_id=1, source_target_pairs={{0,2},{1,3},{2,0},{3,1},{4,6},{5,7},{6,4},{7,5},{8,10},{9,11},{10,... | collective-permute-start | bytes 884744 | tf_op jit(solution)/shard_map/ppermute | solution.py:446
  5.0 12.5 %collective-permute-start.2 = (f32[128,512]{1,0:T(8,128)S(1)}, f32[128,512]{1,0:T(8,128)S(1)}, u32[]{:S(2)}, u32[]{:S(2)}) collective-permute-start(f32[128,512]{1,0:T(8,128)S(1)} %slice.10), channel_id=1, source_target_pairs={{0,2},{1,3},{2,0},{3,1},{4,6},{5,7},{6,4},{7,5},{8,10},{9,11},{10,... | collective-permute-start | bytes 786440 | tf_op jit(solution)/shard_map/ppermute | solution.py:446
  6.2 21.6 %collective-permute-start.1 = (f32[240,512]{1,0:T(8,128)S(1)}, f32[240,512]{1,0:T(8,128)S(1)}, u32[]{:S(2)}, u32[]{:S(2)}) collective-permute-start(f32[240,512]{1,0:T(8,128)S(1)} %slice.9), channel_id=1, source_target_pairs={{0,2},{1,3},{2,0},{3,1},{4,6},{5,7},{6,4},{7,5},{8,10},{9,11},{10,... | collective-permute-start | bytes 1474568 | tf_op jit(solution)/shard_map/ppermute | solution.py:446
  8.3 1.2 %copy-start = (f32[512,512]{1,0:T(8,128)S(1)}, f32[512,512]{1,0:T(8,128)}, u32[]{:S(2)}) copy-start(f32[512,512]{1,0:T(8,128)} %own_ref.1) | copy-start | bytes 3145732
  9.5 2.2 %copy-start.1 = (f32[2048,512]{1,0:T(8,128)S(1)}, f32[2048,512]{1,0:T(8,128)}, u32[]{:S(2)}) copy-start(f32[2048,512]{1,0:T(8,128)} %proj_ref.1) | copy-start | bytes 12582916
  11.7 0.9 %copy-start.3 = (f32[2048,9]{0,1:T(8,128)S(1)}, f32[2048,9]{0,1:T(8,128)}, u32[]{:S(2)}) copy-start(f32[2048,9]{0,1:T(8,128)} %param.10) | copy-start | bytes 221188
  16.6 8.4 %copy-start.4 = (f32[4,384]{1,0:T(4,128)S(1)}, f32[4,384]{1,0:T(4,128)}, u32[]{:S(2)}) copy-start(f32[4,384]{1,0:T(4,128)} %refs_6_.3) | copy-start | bytes 18436
  16.6 8.4 %copy-start.5 = (s32[512]{0:T(512)S(1)}, s32[512]{0:T(512)}, u32[]{:S(2)}) copy-start(s32[512]{0:T(512)} %param.13) | copy-start | bytes 6148
  16.6 11.4 %copy-start.2 = (f32[512,512]{1,0:T(8,128)S(1)}, f32[512,512]{1,0:T(8,128)}, u32[]{:S(2)}) copy-start(f32[512,512]{1,0:T(8,128)} %weight_ref.1) | copy-start | bytes 3145732
  17.5 2.0 %collective-permute-start.5 = (f32[144,512]{1,0:T(8,128)S(1)}, f32[144,512]{1,0:T(8,128)S(1)}, u32[]{:S(2)}, u32[]{:S(2)}) collective-permute-start(f32[144,512]{1,0:T(8,128)S(1)} %collective-permute-done.3.refs_2_), channel_id=1, source_target_pairs={{0,1},{1,0},{2,3},{3,2},{4,5},{5,4},{6,7},{7,6},{8,9},{9,8},{10,11... | collective-permute-start | bytes 884744 | tf_op jit(solution)/shard_map/ppermute | solution.py:440
  17.5 2.0 %collective-permute-start.4 = (f32[128,512]{1,0:T(8,128)S(1)}, f32[128,512]{1,0:T(8,128)S(1)}, u32[]{:S(2)}, u32[]{:S(2)}) collective-permute-start(f32[128,512]{1,0:T(8,128)S(1)} %collective-permute-done.2.refs_0_), channel_id=1, source_target_pairs={{0,1},{1,0},{2,3},{3,2},{4,5},{5,4},{6,7},{7,6},{8,9},{9,8},{10,11... | collective-permute-start | bytes 786440 | tf_op jit(solution)/shard_map/ppermute | solution.py:440
  21.0 6.9 %collective-permute-start.6 = (f32[16,384]{1,0:T(8,128)S(1)}, f32[16,384]{1,0:T(8,128)S(1)}, u32[]{:S(2)}, u32[]{:S(2)}) collective-permute-start(f32[16,384]{1,0:T(8,128)S(1)} %get-tuple-element.72), channel_id=1, source_target_pairs={{0,4},{4,8},{8,12},{12,16},{16,20},{20,24},{24,28},{1,5},{5,9},{9,... | collective-permute-start | bytes 73736 | tf_op jit(solution)/shard_map/ppermute | solution.py:499
  27.9 1.9 %collective-permute-start.7 = (f32[240,512]{1,0:T(8,128)S(1)}, f32[240,512]{1,0:T(8,128)S(1)}, u32[]{:S(2)}, u32[]{:S(2)}) collective-permute-start(f32[240,512]{1,0:T(8,128)S(1)} %collective-permute-done.1.refs_0_), channel_id=1, source_target_pairs={{0,1},{1,0},{2,3},{3,2},{4,5},{5,4},{6,7},{7,6},{8,9},{9,8},{10,11... | collective-permute-start | bytes 1474568 | tf_op jit(solution)/shard_map/ppermute | solution.py:440
  33.4 7.8 %collective-permute-start.8 = (f32[2,128,128]{2,1,0:T(8,128)S(1)}, f32[2,128,128]{2,1,0:T(8,128)S(1)}, u32[]{:S(2)}, u32[]{:S(2)}) collective-permute-start(f32[2,128,128]{2,1,0:T(8,128)S(1)} %get-tuple-element.76.own_ref), channel_id=1, source_target_pairs={{0,4},{4,0},{8,12},{12,8},{16,20},{20,16},{24,28},{28,24},{1,5},{5... | collective-permute-start | bytes 393224 | tf_op jit(solution)/shard_map/ppermute | solution.py:538
  35.0 7.3 %collective-permute-start.10 = (f32[2,128,128]{2,1,0:T(8,128)S(1)}, f32[2,128,128]{2,1,0:T(8,128)S(1)}, u32[]{:S(2)}, u32[]{:S(2)}) collective-permute-start(f32[2,128,128]{2,1,0:T(8,128)S(1)} %get-tuple-element.76.own_ref), channel_id=1, source_target_pairs={{0,12},{4,8},{8,4},{12,0},{16,28},{20,24},{24,20},{28,16},{1,13},{... | collective-permute-start | bytes 393224 | tf_op jit(solution)/shard_map/ppermute | solution.py:538
  36.6 6.4 %collective-permute-start.9 = (f32[2,128,128]{2,1,0:T(8,128)S(1)}, f32[2,128,128]{2,1,0:T(8,128)S(1)}, u32[]{:S(2)}, u32[]{:S(2)}) collective-permute-start(f32[2,128,128]{2,1,0:T(8,128)S(1)} %get-tuple-element.76.own_ref), channel_id=1, source_target_pairs={{0,8},{4,12},{8,0},{12,4},{16,24},{20,28},{24,16},{28,20},{1,9},{5... | collective-permute-start | bytes 393224 | tf_op jit(solution)/shard_map/ppermute | solution.py:538
  36.9 11.9 %copy-start.6 = (f32[128]{0:T(128)S(1)}, f32[128]{0:T(128)}, u32[]{:S(2)}) copy-start(f32[128]{0:T(128)} %param.14) | copy-start | bytes 1540
  43.5 5.2 %collective-permute-start.11 = (f32[128,128]{1,0:T(8,128)S(1)}, f32[128,128]{1,0:T(8,128)S(1)}, u32[]{:S(2)}, u32[]{:S(2)}) collective-permute-start(f32[128,128]{1,0:T(8,128)S(1)} %get-tuple-element.102), channel_id=1, source_target_pairs={{0,16},{4,20},{8,24},{12,28},{16,0},{20,4},{24,8},{28,12},{1,17},{... | collective-permute-start | bytes 196616 | tf_op jit(solution)/shard_map/ppermute | solution.py:558
  49.3 2.2 %collective-permute-start.12 = (f32[512,128]{1,0:T(8,128)S(1)}, f32[512,128]{1,0:T(8,128)S(1)}, u32[]{:S(2)}, u32[]{:S(2)}) collective-permute-start(f32[512,128]{1,0:T(8,128)S(1)} %get-tuple-element.104.own_ref), channel_id=1, source_target_pairs={{0,1},{1,0},{2,3},{3,2},{4,5},{5,4},{6,7},{7,6},{8,9},{9,8},{10,11... | collective-permute-start | bytes 786440 | tf_op jit(solution)/shard_map/ppermute | solution.py:440
  49.4 4.6 %collective-permute-start.14 = (f32[128,128]{1,0:T(8,128)S(1)}, f32[128,128]{1,0:T(8,128)S(1)}, u32[]{:S(2)}, u32[]{:S(2)}) collective-permute-start(f32[128,128]{1,0:T(8,128)S(1)} %get-tuple-element.106), channel_id=1, source_target_pairs={{0,2},{1,3},{2,0},{3,1},{4,6},{5,7},{6,4},{7,5},{8,10},{9,11},{10,... | collective-permute-start | bytes 196616 | tf_op jit(solution)/shard_map/ppermute | solution.py:446
  51.1 4.9 %collective-permute-start.15 = (f32[128,128]{1,0:T(8,128)S(1)}, f32[128,128]{1,0:T(8,128)S(1)}, u32[]{:S(2)}, u32[]{:S(2)}) collective-permute-start(f32[128,128]{1,0:T(8,128)S(1)} %get-tuple-element.107), channel_id=1, source_target_pairs={{0,2},{1,3},{2,0},{3,1},{4,6},{5,7},{6,4},{7,5},{8,10},{9,11},{10,... | collective-permute-start | bytes 196616 | tf_op jit(solution)/shard_map/ppermute | solution.py:446
  51.5 6.6 %collective-permute-start.13 = (f32[256,128]{1,0:T(8,128)S(1)}, f32[256,128]{1,0:T(8,128)S(1)}, u32[]{:S(2)}, u32[]{:S(2)}) collective-permute-start(f32[256,128]{1,0:T(8,128)S(1)} %get-tuple-element.105), channel_id=1, source_target_pairs={{0,2},{1,3},{2,0},{3,1},{4,6},{5,7},{6,4},{7,5},{8,10},{9,11},{10,... | collective-permute-start | bytes 393224 | tf_op jit(solution)/shard_map/ppermute | solution.py:446
  56.1 1.3 %collective-permute-start.16 = (f32[128,128]{1,0:T(8,128)S(1)}, f32[128,128]{1,0:T(8,128)S(1)}, u32[]{:S(2)}, u32[]{:S(2)}) collective-permute-start(f32[128,128]{1,0:T(8,128)S(1)} %collective-permute-done.14.refs_0_), channel_id=1, source_target_pairs={{0,1},{1,0},{2,3},{3,2},{4,5},{5,4},{6,7},{7,6},{8,9},{9,8},{10,11... | collective-permute-start | bytes 196616 | tf_op jit(solution)/shard_map/ppermute | solution.py:440
  56.1 1.4 %collective-permute-start.17 = (f32[128,128]{1,0:T(8,128)S(1)}, f32[128,128]{1,0:T(8,128)S(1)}, u32[]{:S(2)}, u32[]{:S(2)}) collective-permute-start(f32[128,128]{1,0:T(8,128)S(1)} %collective-permute-done.15.refs_2_), channel_id=1, source_target_pairs={{0,1},{1,0},{2,3},{3,2},{4,5},{5,4},{6,7},{7,6},{8,9},{9,8},{10,11... | collective-permute-start | bytes 196616 | tf_op jit(solution)/shard_map/ppermute | solution.py:440
  58.1 1.3 %collective-permute-start.18 = (f32[256,128]{1,0:T(8,128)S(1)}, f32[256,128]{1,0:T(8,128)S(1)}, u32[]{:S(2)}, u32[]{:S(2)}) collective-permute-start(f32[256,128]{1,0:T(8,128)S(1)} %collective-permute-done.13.refs_0_), channel_id=1, source_target_pairs={{0,1},{1,0},{2,3},{3,2},{4,5},{5,4},{6,7},{7,6},{8,9},{9,8},{10,11... | collective-permute-start | bytes 393224 | tf_op jit(solution)/shard_map/ppermute | solution.py:440

commit v13 on v10

--- a/solution.py
+++ b/solution.py
@@ -201,6 +201,8 @@
     lowers = [jnp.where(row > col, beta * gram, 0.0) for beta, gram in zip(betas, grams)]
     inverses = unit_lower_inverse(lowers, row, col)
     states = []
+    if state is not None:
+        later_keys = product(state[0], across_keys[-1])
     for part in range(chunks):
         rows = slice(part * CHUNK, (part + 1) * CHUNK)
         inverse, beta = inverses[part], betas[part]
@@ -208,15 +210,17 @@
         factor_y = product(grids[part] * inverse, beta * values[part])
         x_ref[rows, :] = factor_x
         y_ref[rows, :] = factor_y
-        onto = product(
-            across_keys[part], jnp.concatenate([factor_x, tails[part] * factor_y], axis=1)
-        )
+        factors = jnp.concatenate([factor_x, tails[part] * factor_y], axis=1)
+        onto = product(across_keys[part], factors)
+        if state is not None and part == chunks - 1:
+            behind = product(later_keys, factors)
         trans = gammas[part][CHUNK - 1 : CHUNK, :] * (eye - onto[:, :width])
         states.append((trans, onto[:, width:]))
         chunk_ref[part, 0] = trans
         chunk_ref[part, 1] = onto[:, width:]
     if state is not None:
-        states.append(state)
+        decay = gammas[-1][CHUNK - 1 : CHUNK, :]
+        states[-1] = (decay * (state[0] - behind[:, :width]), behind[:, width:] + state[1])
     while len(states) > 1:
         joined = [followed(*states[at : at + 2]) for at in range(0, len(states) - 1, 2)]
         states = joined + states[2 * len(joined) :]
@@ -399,25 +403,36 @@
         base += pieces[0].shape[0]
 
 
+def flush_kernel(count, first, *refs):
+    pieces = refs[:count]
+    weight_ref, ready_ref, total_ref, out_ref, next_ref, sem = refs[count:]
+    half = ready_ref.shape[0]
+    copy = pltpu.make_async_copy(ready_ref, out_ref.at[:half, :], sem)
+    copy.start()
+    weight = source_rows(first, pieces, weight_ref)
+    for rows in row_blocks(half):
+        next_ref[rows, :] = total_ref[rows, :] + block_product(pieces, weight, rows)
+    copy.wait()
+
+
 def last_kernel(count, first, *refs):
     pieces = refs[:count]
-    weight_ref, ready_ref, total_ref, out_ref, held, sems = refs[count:]
-    half = ready_ref.shape[0]
-    copies = [pltpu.make_async_copy(ready_ref, out_ref.at[:half, :], sems.at[0])]
-    copies[0].start()
+    weight_ref, total_ref, begun_ref, out_ref, held, sems = refs[count:]
+    half = total_ref.shape[0]
+    copies = []
     weight = source_rows(first, pieces, weight_ref)
-    for spot, rows in enumerate(row_blocks(total_ref.shape[0])):
+    for spot, rows in enumerate(row_blocks(half)):
         held[rows, :] = total_ref[rows, :] + block_product(pieces, weight, rows)
         out = slice(half + rows.start, half + rows.stop)
         copies.append(
-            pltpu.make_async_copy(held.at[rows, :], out_ref.at[out, :], sems.at[spot + 1])
+            pltpu.make_async_copy(held.at[rows, :], out_ref.at[out, :], sems.at[spot])
         )
         copies[-1].start()
     for copy in copies:
         copy.wait()
 
 
-def vmem_call(kernel, outs, scratch, cost, *args, any_in=(), any_out=False):
+def vmem_call(kernel, outs, scratch, cost, *args, any_in=(), any_out=(), aliases=()):
     spec = pl.BlockSpec(memory_space=pltpu.VMEM)
     small = pl.BlockSpec(memory_space=pltpu.SMEM)
     free = pl.BlockSpec(memory_space=pl.ANY)
@@ -428,7 +443,10 @@
             free if spot in any_in else small if arg.dtype == jnp.int32 and arg.ndim == 1 else spec
             for spot, arg in enumerate(args)
         ],
-        out_specs=jax.tree.map(lambda unused: free if any_out else spec, outs),
+        out_specs=[free if spot in any_out else spec for spot in range(len(outs))]
+        if isinstance(outs, list)
+        else (free if any_out else spec),
+        input_output_aliases=dict(aliases),
         scratch_shapes=scratch,
         compiler_params=pltpu.CompilerParams(vmem_limit_bytes=VMEM_GRANT),
         cost_estimate=pl.CostEstimate(flops=int(cost * 1e9), bytes_accessed=1 << 20, transcendentals=0),
@@ -583,14 +601,18 @@
     )
     far_high, total_low = after(far_high, total_low)
     far_high_on = [to_sibling(value) for value in far_high]
-    total_high = vmem_call(
-        functools.partial(far_kernel, len(far_high), 2), like(half, columns), [], 1,
-        *far_high, own_weight, total_high,
-    )
+    whole = like(tok_rows, columns)
+    begun, total_high = vmem_call(
+        functools.partial(flush_kernel, len(far_high), 2), [whole, like(half, columns)],
+        [pltpu.SemaphoreType.DMA], 1,
+        *far_high, own_weight, total_low, total_high, any_out=(0,),
+    )
+    args = [*far_high_on, own_weight, total_high, begun]
+    last = len(args) - 1
     return vmem_call(
-        functools.partial(last_kernel, len(far_high), 2 + len(far_high)), like(tok_rows, columns),
-        [pltpu.VMEM((half, columns), F32), pltpu.SemaphoreType.DMA((half // CHUNK + 1,))], 1,
-        *far_high_on, own_weight, total_low, total_high, any_out=True,
+        functools.partial(last_kernel, len(far_high), 2 + len(far_high)), whole,
+        [pltpu.VMEM((half, columns), F32), pltpu.SemaphoreType.DMA((half // CHUNK,))], 1,
+        *args, any_in=(last,), any_out=True, aliases=((last, 0),),
     )
 
 

time: 60.8 us -> 60.7 us (level)
  no operation moved by 1% of the time
where the time goes in v13:
time: 60.7 us; the launch traced here: 60.4 us
  starting transfers between devices  20.5 us (34%)
  Pallas kernels  18.9 us (31%)
  waiting for transfers between devices  12.5 us (21%)
  local copies, waits for them, and re-layouts  7.44 us (12%)
  between operations  1 us (2%)
    pallas_call x13, Pallas kernels, vmem_call(): pl.pallas_call(kernel, out_shape=outs, in_specs=[free if spot in any_in e...  18.9 us
    ppermute x6, starting transfers between devices, to_chips(): lax.ppermute(value, 'head', [(source, (source + 2 * step) % count) for so...  8.47 us
    unnamed x14, local copies, waits for them, and re-layouts  4.34 us
    ppermute x1, starting transfers between devices, shards(): lax.ppermute(rim, 'ctx', [(source, source + 1) for source in range(blocks...  3.99 us
    ppermute x3, waiting for transfers between devices, shards(): lax.ppermute(pair, 'ctx', [(source, source ^ mask << bit) for source in r...  3.76 us
    ppermute x6, waiting for transfers between devices, to_chips(): lax.ppermute(value, 'head', [(source, (source + 2 * step) % count) for so...  3.57 us
    ppermute x3, starting transfers between devices, shards(): lax.ppermute(pair, 'ctx', [(source, source ^ mask << bit) for source in r...  3.55 us
    ppermute x1, starting transfers between devices, shards(): lax.ppermute(pair if carry else pair[1], 'ctx', [(source, source ^ reach)...  2.79 us
  transfers between devices with their start and end apart: 19, of which 14 were waited for; matrix products, arithmetic and copies ran while one was open for 5% of the time, Pallas kernels for 22%

profile of v13, /device:TPU:0, one launch (start us, length us, event | category | flops | bytes accessed | tf_op | source)
XLA Modules:
  0.0 60.4 jit_solution(13200311111765815926)
XLA Ops:
  0.5 1.0 %slice.11 = f32[144,512]{1,0:T(8,128)S(1)} slice(f32[512,512]{1,0:T(8,128)} %own_ref.1), slice={[368:512], [0:512]} | slice | bytes 589824 | tf_op jit(solution)/shard_map/slice | solution.py:493
  1.4 2.6 %collective-permute-start.3 = (f32[144,512]{1,0:T(8,128)S(1)}, f32[144,512]{1,0:T(8,128)S(1)}, u32[]{:S(2)}, u32[]{:S(2)}) collective-permute-start(f32[144,512]{1,0:T(8,128)S(1)} %slice.11), channel_id=1, source_target_pairs={{0,2},{1,3},{2,0},{3,1},{4,6},{5,7},{6,4},{7,5},{8,10},{9,11},{10,... | collective-permute-start | bytes 884744 | tf_op jit(solution)/shard_map/ppermute | solution.py:464
  4.0 1.0 %slice.10 = f32[128,512]{1,0:T(8,128)S(1)} slice(f32[512,512]{1,0:T(8,128)} %own_ref.1), slice={[240:368], [0:512]} | slice | bytes 524288 | tf_op jit(solution)/shard_map/slice | solution.py:493
  5.2 1.1 %slice.9 = f32[240,512]{1,0:T(8,128)S(1)} slice(f32[512,512]{1,0:T(8,128)} %own_ref.1), slice={[0:240], [0:512]} | slice | bytes 983040 | tf_op jit(solution)/shard_map/slice | solution.py:496
  6.2 2.1 %collective-permute-start.1 = (f32[240,512]{1,0:T(8,128)S(1)}, f32[240,512]{1,0:T(8,128)S(1)}, u32[]{:S(2)}, u32[]{:S(2)}) collective-permute-start(f32[240,512]{1,0:T(8,128)S(1)} %slice.9), channel_id=1, source_target_pairs={{0,2},{1,3},{2,0},{3,1},{4,6},{5,7},{6,4},{7,5},{8,10},{9,11},{10,... | collective-permute-start | bytes 1474568 | tf_op jit(solution)/shard_map/ppermute | solution.py:464
  8.3 1.2 %copy-done = f32[512,512]{1,0:T(8,128)S(1)} copy-done((f32[512,512]{1,0:T(8,128)S(1)}, f32[512,512]{1,0:T(8,128)}, u32[]{:S(2)}) %copy-start) | copy-done | bytes 1048600
  9.5 2.2 %copy-done.1 = f32[2048,512]{1,0:T(8,128)S(1)} copy-done((f32[2048,512]{1,0:T(8,128)S(1)}, f32[2048,512]{1,0:T(8,128)}, u32[]{:S(2)}) %copy-start.1) | copy-done | bytes 4194328
  11.7 0.9 %copy-done.3 = f32[2048,9]{0,1:T(8,128)S(1)} copy-done((f32[2048,9]{0,1:T(8,128)S(1)}, f32[2048,9]{0,1:T(8,128)}, u32[]{:S(2)}) %copy-start.3) | copy-done | bytes 73752
  12.6 4.0 %shard_map.82 = (f32[512,384]{1,0:T(8,128)S(1)}, f32[512,256]{1,0:T(8,128)S(1)}, bf16[1024,768]{1,0:T(8,128)(2,1)S(1)}, bf16[1024,512]{1,0:T(8,128)(2,1)S(1)}, s32[3,128]{1,0:T(4,128)S(1)}) custom-call(s32[7]{0:T(128)S(1)} %stack.31.index_ref, f32[512,512]{1,0:T(8,128)S(1)} %copy-done, f32[512,512]{1,0:T(8,128)S(1)} %collective-permute-done.beside_ref, ...), custom_call_target="tpu_custom_call" | custom-call | flops 3000000000 | bytes 1048576 | tf_op jit(solution)/shard_map/pallas_call | solution.py:439
  16.6 0.9 %collective-permute-done.2.refs_0_ = f32[128,512]{1,0:T(8,128)S(1)} collective-permute-done((f32[128,512]{1,0:T(8,128)S(1)}, f32[128,512]{1,0:T(8,128)S(1)}, u32[]{:S(2)}, u32[]{:S(2)}) %collective-permute-start.2) | collective-permute-done | bytes 262176 | tf_op jit(solution)/shard_map/ppermute | solution.py:464
  18.7 0.8 %collective-permute-done.4.refs_1_ = f32[128,512]{1,0:T(8,128)S(1)} collective-permute-done((f32[128,512]{1,0:T(8,128)S(1)}, f32[128,512]{1,0:T(8,128)S(1)}, u32[]{:S(2)}, u32[]{:S(2)}) %collective-permute-start.4) | collective-permute-done | bytes 262176 | tf_op jit(solution)/shard_map/ppermute | solution.py:458
  19.5 1.5 %shard_map.83 = (f32[272,384]{1,0:T(8,128)S(1)}, f32[272,256]{1,0:T(8,128)S(1)}, f32[16,384]{1,0:T(8,128)S(1)}) custom-call(f32[128,512]{1,0:T(8,128)S(1)} %collective-permute-done.2.refs_0_, f32[128,512]{1,0:T(8,128)S(1)} %collective-permute-done.4.refs_1_, f32[144,512]{1,0:T(8,128)S(1)} %collective-permute-done.3.refs_2_, ...), custom_call_target="tpu_custom_call" | custom-call | flops 500000000 | bytes 1048576 | tf_op jit(solution)/shard_map/pallas_call | solution.py:439
  21.0 4.0 %collective-permute-start.6 = (f32[16,384]{1,0:T(8,128)S(1)}, f32[16,384]{1,0:T(8,128)S(1)}, u32[]{:S(2)}, u32[]{:S(2)}) collective-permute-start(f32[16,384]{1,0:T(8,128)S(1)} %get-tuple-element.74), channel_id=1, source_target_pairs={{0,4},{4,8},{8,12},{12,16},{16,20},{20,24},{24,28},{1,5},{5,9},{9,... | collective-permute-start | bytes 73736 | tf_op jit(solution)/shard_map/ppermute | solution.py:517
  25.0 2.8 %shard_map.84 = (f32[256,128]{1,0:T(8,128)S(1)}, f32[256,128]{1,0:T(8,128)S(1)}, f32[256,128]{1,0:T(8,128)S(1)}, f32[256,128]{1,0:T(8,128)S(1)}, f32[256,128]{1,...) custom-call(f32[272,384]{1,0:T(8,128)S(1)} %get-tuple-element.72.raw_ref.refs_4_,, ...), custom_call_target="tpu_custom_call" | custom-call | flops 500000000 | bytes 1048576 | tf_op jit(solution)/shard_map/pallas_call | solution.py:439
  27.9 0.7 %shard_map.88.weight_ref.refs_4_.refs_1_ = bf16[512,1024]{1,0:T(8,128)(2,1)S(1)} custom-call(s32[7]{0:T(128)S(1)} %stack.31.index_ref, f32[512,512]{1,0:T(8,128)S(1)} %copy-done.2), custom_call_target="tpu_custom_call" | custom-call | flops 1000000000 | bytes 1048576 | tf_op jit(solution)/shard_map/pallas_call | solution.py:439
  29.0 0.7 %collective-permute-done.7.refs_0_.refs_1_ = f32[240,512]{1,0:T(8,128)S(1)} collective-permute-done((f32[240,512]{1,0:T(8,128)S(1)}, f32[240,512]{1,0:T(8,128)S(1)}, u32[]{:S(2)}, u32[]{:S(2)}) %collective-permute-start.7) | collective-permute-done | bytes 491552 | tf_op jit(solution)/shard_map/ppermute | solution.py:458
  29.7 3.2 %shard_map.86 = (f32[256,128]{1,0:T(8,128)S(1)}, f32[256,128]{1,0:T(8,128)S(1)}, f32[256,128]{1,0:T(8,128)S(1)}, f32[256,128]{1,0:T(8,128)S(1)}, f32[256,128]{1,...) custom-call(f32[240,512]{1,0:T(8,128)S(1)} %collective-permute-done.7.refs_0_.ref, ...), custom_call_target="tpu_custom_call" | custom-call | flops 5000000000 | bytes 1048576 | tf_op jit(solution)/shard_map/pallas_call | solution.py:439
  33.0 1.8 %collective-permute-start.8 = (f32[2,128,128]{2,1,0:T(8,128)S(1)}, f32[2,128,128]{2,1,0:T(8,128)S(1)}, u32[]{:S(2)}, u32[]{:S(2)}) collective-permute-start(f32[2,128,128]{2,1,0:T(8,128)S(1)} %get-tuple-element.78.own_ref), channel_id=1, source_target_pairs={{0,4},{4,0},{8,12},{12,8},{16,20},{20,16},{24,28},{28,24},{1,5},{5... | collective-permute-start | bytes 393224 | tf_op jit(solution)/shard_map/ppermute | solution.py:556
  34.7 1.5 %collective-permute-start.10 = (f32[2,128,128]{2,1,0:T(8,128)S(1)}, f32[2,128,128]{2,1,0:T(8,128)S(1)}, u32[]{:S(2)}, u32[]{:S(2)}) collective-permute-start(f32[2,128,128]{2,1,0:T(8,128)S(1)} %get-tuple-element.78.own_ref), channel_id=1, source_target_pairs={{0,12},{4,8},{8,4},{12,0},{16,28},{20,24},{24,20},{28,16},{1,13},{... | collective-permute-start | bytes 393224 | tf_op jit(solution)/shard_map/ppermute | solution.py:556
  36.5 2.4 %shard_map.87 = (f32[512,128]{1,0:T(8,128)S(1)}, f32[512,128]{1,0:T(8,128)S(1)}, f32[512,128]{1,0:T(8,128)S(1)}) custom-call(f32[240,512]{1,0:T(8,128)S(1)} %collective-permute-done.1.refs_0_, f32[240,512]{1,0:T(8,128)S(1)} %collective-permute-done.7.refs_0_.refs_1_, f32[512,256]{1,0:T(8,128)S(1)} %get-tuple-element.69.refs_5_.refs_2_, ...), custom_call_target="tpu_custom_call" | custom-call | flops 5000000000 | bytes 1048576 | tf_op jit(solution)/shard_map/pallas_call | solution.py:439
  38.9 1.8 %collective-permute-done.8.one_ref = f32[2,128,128]{2,1,0:T(8,128)S(1)} collective-permute-done((f32[2,128,128]{2,1,0:T(8,128)S(1)}, f32[2,128,128]{2,1,0:T(8,128)S(1)}, u32[]{:S(2)}, u32[]{:S(2)}) %collective-permute-start.8) | collective-permute-done | bytes 131104 | tf_op jit(solution)/shard_map/ppermute | solution.py:556
  40.7 1.3 %collective-permute-done.10.three_ref = f32[2,128,128]{2,1,0:T(8,128)S(1)} collective-permute-done((f32[2,128,128]{2,1,0:T(8,128)S(1)}, f32[2,128,128]{2,1,0:T(8,128)S(1)}, u32[]{:S(2)}, u32[]{:S(2)}) %collective-permute-start.10) | collective-permute-done | bytes 131104 | tf_op jit(solution)/shard_map/ppermute | solution.py:556
  42.0 0.7 %collective-permute-done.9.two_ref = f32[2,128,128]{2,1,0:T(8,128)S(1)} collective-permute-done((f32[2,128,128]{2,1,0:T(8,128)S(1)}, f32[2,128,128]{2,1,0:T(8,128)S(1)}, u32[]{:S(2)}, u32[]{:S(2)}) %collective-permute-start.9) | collective-permute-done | bytes 131104 | tf_op jit(solution)/shard_map/ppermute | solution.py:556
  43.2 2.8 %collective-permute-start.11 = (f32[128,128]{1,0:T(8,128)S(1)}, f32[128,128]{1,0:T(8,128)S(1)}, u32[]{:S(2)}, u32[]{:S(2)}) collective-permute-start(f32[128,128]{1,0:T(8,128)S(1)} %get-tuple-element.104), channel_id=1, source_target_pairs={{0,16},{4,20},{8,24},{12,28},{16,0},{20,4},{24,8},{28,12},{1,17},{... | collective-permute-start | bytes 196616 | tf_op jit(solution)/shard_map/ppermute | solution.py:576
  45.9 2.4 %collective-permute-done.11.refs_2_ = f32[128,128]{1,0:T(8,128)S(1)} collective-permute-done((f32[128,128]{1,0:T(8,128)S(1)}, f32[128,128]{1,0:T(8,128)S(1)}, u32[]{:S(2)}, u32[]{:S(2)}) %collective-permute-start.11) | collective-permute-done | bytes 65568 | tf_op jit(solution)/shard_map/ppermute | solution.py:576
  49.0 1.7 %collective-permute-start.14 = (f32[128,128]{1,0:T(8,128)S(1)}, f32[128,128]{1,0:T(8,128)S(1)}, u32[]{:S(2)}, u32[]{:S(2)}) collective-permute-start(f32[128,128]{1,0:T(8,128)S(1)} %get-tuple-element.108), channel_id=1, source_target_pairs={{0,2},{1,3},{2,0},{3,1},{4,6},{5,7},{6,4},{7,5},{8,10},{9,11},{10,... | collective-permute-start | bytes 196616 | tf_op jit(solution)/shard_map/ppermute | solution.py:464
  51.1 1.7 %collective-permute-start.13 = (f32[256,128]{1,0:T(8,128)S(1)}, f32[256,128]{1,0:T(8,128)S(1)}, u32[]{:S(2)}, u32[]{:S(2)}) collective-permute-start(f32[256,128]{1,0:T(8,128)S(1)} %get-tuple-element.107), channel_id=1, source_target_pairs={{0,2},{1,3},{2,0},{3,1},{4,6},{5,7},{6,4},{7,5},{8,10},{9,11},{10,... | collective-permute-start | bytes 393224 | tf_op jit(solution)/shard_map/ppermute | solution.py:464
  52.8 0.6 shard_map.91
  53.6 2.1 %collective-permute-done.15.refs_2_ = f32[128,128]{1,0:T(8,128)S(1)} collective-permute-done((f32[128,128]{1,0:T(8,128)S(1)}, f32[128,128]{1,0:T(8,128)S(1)}, u32[]{:S(2)}, u32[]{:S(2)}) %collective-permute-start.15) | collective-permute-done | bytes 65568 | tf_op jit(solution)/shard_map/ppermute | solution.py:464
  56.2 0.7 %collective-permute-done.16.refs_1_ = f32[128,128]{1,0:T(8,128)S(1)} collective-permute-done((f32[128,128]{1,0:T(8,128)S(1)}, f32[128,128]{1,0:T(8,128)S(1)}, u32[]{:S(2)}, u32[]{:S(2)}) %collective-permute-start.16) | collective-permute-done | bytes 65568 | tf_op jit(solution)/shard_map/ppermute | solution.py:458
  57.9 0.8 %shard_map.93 = (f32[512,512]{1,0:T(8,128)}, f32[256,512]{1,0:T(8,128)S(1)}) custom-call(f32[256,128]{1,0:T(8,128)S(1)} %collective-permute-done.13.refs_0_, bf16[512,1024]{1,0:T(8,128)(2,1)S(1)} %shard_map.88.weight_ref.refs_4_.refs_1_, f32[256,512]{1,0:T(8,128)S(1)} %shard_map.92.refs_2_, f32[256,512]{1,0:T(8,128)S(1)} %get-tuple-element.118.refs_3_), custom_call_target="tpu_custom_call" | custom-call | flops 1000000000 | bytes 1048576 | tf_op jit(solution)/shard_map/pallas_call | solution.py:439
  59.1 1.1 %shard_map.94 = f32[512,512]{1,0:T(8,128)} custom-call(f32[256,128]{1,0:T(8,128)S(1)} %collective-permute-done.18.refs_0_, bf16[512,1024]{1,0:T(8,128)(2,1)S(1)} %shard_map.88.weight_ref.refs_4_.refs_1_, f32[256,512]{1,0:T(8,128)S(1)} %get-tuple-element.119.refs_2_, f32[512,512]{1,0:T(8,128)} %get-tuple-element.120.refs_3_), custom_call_target="tpu_custom_call", output_to_operand_aliasing={{}: (3, {})} | custom-call | flops 1000000000 | bytes 1048576 | tf_op jit(solution)/shard_map/pallas_call | solution.py:439
  (37 shorter events, 5.6 us)
Async XLA Ops:
  0.0 5.2 %collective-permute-start = (f32[512,512]{1,0:T(8,128)}, f32[512,512]{1,0:T(8,128)S(1)}, u32[]{:S(2)}, u32[]{:S(2)}) collective-permute-start(f32[512,512]{1,0:T(8,128)} %own_ref.1), channel_id=1, source_target_pairs={{0,1},{1,0},{2,3},{3,2},{4,5},{5,4},{6,7},{7,6},{8,9},{9,8},{10,11... | collective-permute-start | bytes 3145736 | tf_op jit(solution)/shard_map/ppermute | solution.py:458
  1.4 16.1 %collective-permute-start.3 = (f32[144,512]{1,0:T(8,128)S(1)}, f32[144,512]{1,0:T(8,128)S(1)}, u32[]{:S(2)}, u32[]{:S(2)}) collective-permute-start(f32[144,512]{1,0:T(8,128)S(1)} %slice.11), channel_id=1, source_target_pairs={{0,2},{1,3},{2,0},{3,1},{4,6},{5,7},{6,4},{7,5},{8,10},{9,11},{10,... | collective-permute-start | bytes 884744 | tf_op jit(solution)/shard_map/ppermute | solution.py:464
  5.0 12.5 %collective-permute-start.2 = (f32[128,512]{1,0:T(8,128)S(1)}, f32[128,512]{1,0:T(8,128)S(1)}, u32[]{:S(2)}, u32[]{:S(2)}) collective-permute-start(f32[128,512]{1,0:T(8,128)S(1)} %slice.10), channel_id=1, source_target_pairs={{0,2},{1,3},{2,0},{3,1},{4,6},{5,7},{6,4},{7,5},{8,10},{9,11},{10,... | collective-permute-start | bytes 786440 | tf_op jit(solution)/shard_map/ppermute | solution.py:464
  6.2 21.6 %collective-permute-start.1 = (f32[240,512]{1,0:T(8,128)S(1)}, f32[240,512]{1,0:T(8,128)S(1)}, u32[]{:S(2)}, u32[]{:S(2)}) collective-permute-start(f32[240,512]{1,0:T(8,128)S(1)} %slice.9), channel_id=1, source_target_pairs={{0,2},{1,3},{2,0},{3,1},{4,6},{5,7},{6,4},{7,5},{8,10},{9,11},{10,... | collective-permute-start | bytes 1474568 | tf_op jit(solution)/shard_map/ppermute | solution.py:464
  8.3 1.2 %copy-start = (f32[512,512]{1,0:T(8,128)S(1)}, f32[512,512]{1,0:T(8,128)}, u32[]{:S(2)}) copy-start(f32[512,512]{1,0:T(8,128)} %own_ref.1) | copy-start | bytes 3145732
  9.5 2.2 %copy-start.1 = (f32[2048,512]{1,0:T(8,128)S(1)}, f32[2048,512]{1,0:T(8,128)}, u32[]{:S(2)}) copy-start(f32[2048,512]{1,0:T(8,128)} %proj_ref.1) | copy-start | bytes 12582916
  11.7 0.9 %copy-start.3 = (f32[2048,9]{0,1:T(8,128)S(1)}, f32[2048,9]{0,1:T(8,128)}, u32[]{:S(2)}) copy-start(f32[2048,9]{0,1:T(8,128)} %param.10) | copy-start | bytes 221188
  16.6 8.4 %copy-start.4 = (f32[4,384]{1,0:T(4,128)S(1)}, f32[4,384]{1,0:T(4,128)}, u32[]{:S(2)}) copy-start(f32[4,384]{1,0:T(4,128)} %refs_6_.3) | copy-start | bytes 18436
  16.6 8.4 %copy-start.5 = (s32[512]{0:T(512)S(1)}, s32[512]{0:T(512)}, u32[]{:S(2)}) copy-start(s32[512]{0:T(512)} %param.13) | copy-start | bytes 6148
  16.6 11.2 %copy-start.2 = (f32[512,512]{1,0:T(8,128)S(1)}, f32[512,512]{1,0:T(8,128)}, u32[]{:S(2)}) copy-start(f32[512,512]{1,0:T(8,128)} %weight_ref.1) | copy-start | bytes 3145732
  17.5 2.0 %collective-permute-start.5 = (f32[144,512]{1,0:T(8,128)S(1)}, f32[144,512]{1,0:T(8,128)S(1)}, u32[]{:S(2)}, u32[]{:S(2)}) collective-permute-start(f32[144,512]{1,0:T(8,128)S(1)} %collective-permute-done.3.refs_2_), channel_id=1, source_target_pairs={{0,1},{1,0},{2,3},{3,2},{4,5},{5,4},{6,7},{7,6},{8,9},{9,8},{10,11... | collective-permute-start | bytes 884744 | tf_op jit(solution)/shard_map/ppermute | solution.py:458
  17.5 2.0 %collective-permute-start.4 = (f32[128,512]{1,0:T(8,128)S(1)}, f32[128,512]{1,0:T(8,128)S(1)}, u32[]{:S(2)}, u32[]{:S(2)}) collective-permute-start(f32[128,512]{1,0:T(8,128)S(1)} %collective-permute-done.2.refs_0_), channel_id=1, source_target_pairs={{0,1},{1,0},{2,3},{3,2},{4,5},{5,4},{6,7},{7,6},{8,9},{9,8},{10,11... | collective-permute-start | bytes 786440 | tf_op jit(solution)/shard_map/ppermute | solution.py:458
  21.0 6.8 %collective-permute-start.6 = (f32[16,384]{1,0:T(8,128)S(1)}, f32[16,384]{1,0:T(8,128)S(1)}, u32[]{:S(2)}, u32[]{:S(2)}) collective-permute-start(f32[16,384]{1,0:T(8,128)S(1)} %get-tuple-element.74), channel_id=1, source_target_pairs={{0,4},{4,8},{8,12},{12,16},{16,20},{20,24},{24,28},{1,5},{5,9},{9,... | collective-permute-start | bytes 73736 | tf_op jit(solution)/shard_map/ppermute | solution.py:517
  27.9 1.9 %collective-permute-start.7 = (f32[240,512]{1,0:T(8,128)S(1)}, f32[240,512]{1,0:T(8,128)S(1)}, u32[]{:S(2)}, u32[]{:S(2)}) collective-permute-start(f32[240,512]{1,0:T(8,128)S(1)} %collective-permute-done.1.refs_0_), channel_id=1, source_target_pairs={{0,1},{1,0},{2,3},{3,2},{4,5},{5,4},{6,7},{7,6},{8,9},{9,8},{10,11... | collective-permute-start | bytes 1474568 | tf_op jit(solution)/shard_map/ppermute | solution.py:458
  33.0 7.7 %collective-permute-start.8 = (f32[2,128,128]{2,1,0:T(8,128)S(1)}, f32[2,128,128]{2,1,0:T(8,128)S(1)}, u32[]{:S(2)}, u32[]{:S(2)}) collective-permute-start(f32[2,128,128]{2,1,0:T(8,128)S(1)} %get-tuple-element.78.own_ref), channel_id=1, source_target_pairs={{0,4},{4,0},{8,12},{12,8},{16,20},{20,16},{24,28},{28,24},{1,5},{5... | collective-permute-start | bytes 393224 | tf_op jit(solution)/shard_map/ppermute | solution.py:556
  34.7 7.3 %collective-permute-start.10 = (f32[2,128,128]{2,1,0:T(8,128)S(1)}, f32[2,128,128]{2,1,0:T(8,128)S(1)}, u32[]{:S(2)}, u32[]{:S(2)}) collective-permute-start(f32[2,128,128]{2,1,0:T(8,128)S(1)} %get-tuple-element.78.own_ref), channel_id=1, source_target_pairs={{0,12},{4,8},{8,4},{12,0},{16,28},{20,24},{24,20},{28,16},{1,13},{... | collective-permute-start | bytes 393224 | tf_op jit(solution)/shard_map/ppermute | solution.py:556
  36.3 6.4 %collective-permute-start.9 = (f32[2,128,128]{2,1,0:T(8,128)S(1)}, f32[2,128,128]{2,1,0:T(8,128)S(1)}, u32[]{:S(2)}, u32[]{:S(2)}) collective-permute-start(f32[2,128,128]{2,1,0:T(8,128)S(1)} %get-tuple-element.78.own_ref), channel_id=1, source_target_pairs={{0,8},{4,12},{8,0},{12,4},{16,24},{20,28},{24,16},{28,20},{1,9},{5... | collective-permute-start | bytes 393224 | tf_op jit(solution)/shard_map/ppermute | solution.py:556
  36.5 11.9 %copy-start.6 = (f32[128]{0:T(128)S(1)}, f32[128]{0:T(128)}, u32[]{:S(2)}) copy-start(f32[128]{0:T(128)} %param.14) | copy-start | bytes 1540
  43.2 5.2 %collective-permute-start.11 = (f32[128,128]{1,0:T(8,128)S(1)}, f32[128,128]{1,0:T(8,128)S(1)}, u32[]{:S(2)}, u32[]{:S(2)}) collective-permute-start(f32[128,128]{1,0:T(8,128)S(1)} %get-tuple-element.104), channel_id=1, source_target_pairs={{0,16},{4,20},{8,24},{12,28},{16,0},{20,4},{24,8},{28,12},{1,17},{... | collective-permute-start | bytes 196616 | tf_op jit(solution)/shard_map/ppermute | solution.py:576
  49.0 2.2 %collective-permute-start.12 = (f32[512,128]{1,0:T(8,128)S(1)}, f32[512,128]{1,0:T(8,128)S(1)}, u32[]{:S(2)}, u32[]{:S(2)}) collective-permute-start(f32[512,128]{1,0:T(8,128)S(1)} %get-tuple-element.106.own_ref), channel_id=1, source_target_pairs={{0,1},{1,0},{2,3},{3,2},{4,5},{5,4},{6,7},{7,6},{8,9},{9,8},{10,11... | collective-permute-start | bytes 786440 | tf_op jit(solution)/shard_map/ppermute | solution.py:458
  49.0 4.6 %collective-permute-start.14 = (f32[128,128]{1,0:T(8,128)S(1)}, f32[128,128]{1,0:T(8,128)S(1)}, u32[]{:S(2)}, u32[]{:S(2)}) collective-permute-start(f32[128,128]{1,0:T(8,128)S(1)} %get-tuple-element.108), channel_id=1, source_target_pairs={{0,2},{1,3},{2,0},{3,1},{4,6},{5,7},{6,4},{7,5},{8,10},{9,11},{10,... | collective-permute-start | bytes 196616 | tf_op jit(solution)/shard_map/ppermute | solution.py:464
  50.8 4.9 %collective-permute-start.15 = (f32[128,128]{1,0:T(8,128)S(1)}, f32[128,128]{1,0:T(8,128)S(1)}, u32[]{:S(2)}, u32[]{:S(2)}) collective-permute-start(f32[128,128]{1,0:T(8,128)S(1)} %get-tuple-element.109), channel_id=1, source_target_pairs={{0,2},{1,3},{2,0},{3,1},{4,6},{5,7},{6,4},{7,5},{8,10},{9,11},{10,... | collective-permute-start | bytes 196616 | tf_op jit(solution)/shard_map/ppermute | solution.py:464
  51.1 6.6 %collective-permute-start.13 = (f32[256,128]{1,0:T(8,128)S(1)}, f32[256,128]{1,0:T(8,128)S(1)}, u32[]{:S(2)}, u32[]{:S(2)}) collective-permute-start(f32[256,128]{1,0:T(8,128)S(1)} %get-tuple-element.107), channel_id=1, source_target_pairs={{0,2},{1,3},{2,0},{3,1},{4,6},{5,7},{6,4},{7,5},{8,10},{9,11},{10,... | collective-permute-start | bytes 393224 | tf_op jit(solution)/shard_map/ppermute | solution.py:464
  55.7 1.3 %collective-permute-start.16 = (f32[128,128]{1,0:T(8,128)S(1)}, f32[128,128]{1,0:T(8,128)S(1)}, u32[]{:S(2)}, u32[]{:S(2)}) collective-permute-start(f32[128,128]{1,0:T(8,128)S(1)} %collective-permute-done.14.refs_0_), channel_id=1, source_target_pairs={{0,1},{1,0},{2,3},{3,2},{4,5},{5,4},{6,7},{7,6},{8,9},{9,8},{10,11... | collective-permute-start | bytes 196616 | tf_op jit(solution)/shard_map/ppermute | solution.py:458
  55.7 1.4 %collective-permute-start.17 = (f32[128,128]{1,0:T(8,128)S(1)}, f32[128,128]{1,0:T(8,128)S(1)}, u32[]{:S(2)}, u32[]{:S(2)}) collective-permute-start(f32[128,128]{1,0:T(8,128)S(1)} %collective-permute-done.15.refs_2_), channel_id=1, source_target_pairs={{0,1},{1,0},{2,3},{3,2},{4,5},{5,4},{6,7},{7,6},{8,9},{9,8},{10,11... | collective-permute-start | bytes 196616 | tf_op jit(solution)/shard_map/ppermute | solution.py:458
  57.8 1.3 %collective-permute-start.18 = (f32[256,128]{1,0:T(8,128)S(1)}, f32[256,128]{1,0:T(8,128)S(1)}, u32[]{:S(2)}, u32[]{:S(2)}) collective-permute-start(f32[256,128]{1,0:T(8,128)S(1)} %collective-permute-done.13.refs_0_), channel_id=1, source_target_pairs={{0,1},{1,0},{2,3},{3,2},{4,5},{5,4},{6,7},{7,6},{8,9},{9,8},{10,11... | collective-permute-start | bytes 393224 | tf_op jit(solution)/shard_map/ppermute | solution.py:458

commit v14 on v13

--- a/solution.py
+++ b/solution.py
@@ -337,17 +337,29 @@
     next_ref[...] = jnp.where(flag(bit + 2), carry, 0.0) if last else carry
 
 
-def mix_kernel(stages, single, carried_ref, local_ref, gate_ref, low_ref, high_ref, gain_ref, *refs):
+def level_kernel(stages, single, carried_ref, local_ref, low_ref, high_ref, *refs):
     states = [ref[spot] for ref in refs[:stages] for spot in range(ref.shape[0])]
-    if single:
-        states.append(product(refs[stages][...], refs[stages + 1][...]))
-    outs = refs[stages + (2 if single else 0) :]
-    states = [right_parts(state) for state in states]
     carried = left_parts(carried_ref[...])
     weights = jnp.concatenate([low_ref[...], high_ref[...]], axis=0)
     mixed = weights[:, 2:3] * local_ref[...]
     for level, state in enumerate(states):
-        mixed = mixed + weights[:, level + 3 : level + 4] * parts_dot(carried, state)
+        mixed = mixed + weights[:, level + 3 : level + 4] * parts_dot(carried, right_parts(state))
+    if single:
+        carry_ref, mixed_ref, reach_ref = refs[stages:]
+        level = len(states) + 3
+        reach_ref[...] = weights[:, level : level + 1] * parts_dot(
+            carried, right_parts(carry_ref[...])
+        )
+    else:
+        (mixed_ref,) = refs[stages:]
+    mixed_ref[...] = mixed
+
+
+def mix_kernel(single, mixed_ref, gate_ref, gain_ref, *refs):
+    mixed = mixed_ref[...]
+    if single:
+        mixed = mixed + product(refs[0][...], refs[1][...])
+    outs = refs[2 if single else 0 :]
     scale = lax.rsqrt(jnp.mean(mixed * mixed, axis=1, keepdims=True) + 1e-05)
     normed = mixed * scale * gain_ref[...] * gate_ref[...]
     outs[0][...] = normed
@@ -568,21 +580,28 @@
             flags, pair, *others, *carry,
         )
         levels.append(level)
-    single = []
-    if bits % 2:
-        reach = blocks // 2
-        single = [
-            *(carry or [jnp.where(my_index >= reach, jnp.eye(width, dtype=F32), 0.0)]),
-            lax.ppermute(
-                pair if carry else pair[1],
-                "ctx", [(source, source ^ reach) for source in range(blocks)],
-            ),
-        ]
+    carried, local, gate = fields
+    lone = bool(bits % 2)
+    reach = blocks // 2
+    if lone:
+        other = lax.ppermute(
+            pair if carry else pair[1],
+            "ctx", [(source, source ^ reach) for source in range(blocks)],
+        )
+        if not carry:
+            carry = [jnp.where(my_index >= reach, jnp.eye(width, dtype=F32), 0.0)]
+    rows_shape = like(tok_rows, width)
+    mixed, *reached = vmem_call(
+        functools.partial(level_kernel, len(levels), lone), [rows_shape] * (2 if lone else 1), [], 1,
+        carried, local, earlier[5], later[5], *levels, *(carry if lone else ()),
+    )
+    if lone:
+        reached.append(other)
     half = tok_rows // 2
     normed, *lows, high = vmem_call(
-        functools.partial(mix_kernel, len(levels), bool(single)),
-        [like(tok_rows, width)] + [like(half // 2, width)] * 2 + [like(half, width)], [], 1,
-        *fields, earlier[5], later[5], norm_gain[None, :], *levels, *single,
+        functools.partial(mix_kernel, lone),
+        [rows_shape] + [like(half // 2, width)] * 2 + [like(half, width)], [], 1,
+        mixed, gate, norm_gain[None, :], *reached,
     )
     columns = w_out.shape[1]
     near = to_sibling(normed)

time: 60.7 us -> 60.4 us (level)
    pallas_call x13 -> x14, Pallas kernels: 18.9 us -> 19 us  [vmem_call(): pl.pallas_call(kernel, out_shape=outs, in_specs=[free if spot in any_in e...]
  transfers between devices with their start and end apart: 19 -> 19, of which waited for: 14 -> 14; matrix products, arithmetic and copies ran while one was open for 5% -> 5% of each run, Pallas kernels for 22% -> 23%
where the time goes in v14:
time: 60.4 us; the launch traced here: 60.1 us
  starting transfers between devices  20.5 us (34%)
  Pallas kernels  19 us (31%)
  waiting for transfers between devices  12.1 us (20%)
  local copies, waits for them, and re-layouts  7.44 us (12%)
  between operations  1.02 us (2%)
    pallas_call x14, Pallas kernels, vmem_call(): pl.pallas_call(kernel, out_shape=outs, in_specs=[free if spot in any_in e...  19 us
    ppermute x6, starting transfers between devices, to_chips(): lax.ppermute(value, 'head', [(source, (source + 2 * step) % count) for so...  8.47 us
    unnamed x14, local copies, waits for them, and re-layouts  4.34 us
    ppermute x1, starting transfers between devices, shards(): lax.ppermute(rim, 'ctx', [(source, source + 1) for source in range(blocks...  3.99 us
    ppermute x3, waiting for transfers between devices, shards(): lax.ppermute(pair, 'ctx', [(source, source ^ mask << bit) for source in r...  3.75 us
    ppermute x6, waiting for transfers between devices, to_chips(): lax.ppermute(value, 'head', [(source, (source + 2 * step) % count) for so...  3.55 us
    ppermute x3, starting transfers between devices, shards(): lax.ppermute(pair, 'ctx', [(source, source ^ mask << bit) for source in r...  3.55 us
    ppermute x1, starting transfers between devices, shards(): lax.ppermute(pair if carry else pair[1], 'ctx', [(source, source ^ reach)...  2.79 us
  transfers between devices with their start and end apart: 19, of which 14 were waited for; matrix products, arithmetic and copies ran while one was open for 5% of the time, Pallas kernels for 23%

profile of v14, /device:TPU:0, one launch (start us, length us, event | category | flops | bytes accessed | tf_op | source)
XLA Modules:
  0.0 60.1 jit_solution(11215748071635301186)
XLA Ops:
  0.5 1.0 %slice.11 = f32[144,512]{1,0:T(8,128)S(1)} slice(f32[512,512]{1,0:T(8,128)} %own_ref.1), slice={[368:512], [0:512]} | slice | bytes 589824 | tf_op jit(solution)/shard_map/slice | solution.py:505
  1.4 2.6 %collective-permute-start.3 = (f32[144,512]{1,0:T(8,128)S(1)}, f32[144,512]{1,0:T(8,128)S(1)}, u32[]{:S(2)}, u32[]{:S(2)}) collective-permute-start(f32[144,512]{1,0:T(8,128)S(1)} %slice.11), channel_id=1, source_target_pairs={{0,2},{1,3},{2,0},{3,1},{4,6},{5,7},{6,4},{7,5},{8,10},{9,11},{10,... | collective-permute-start | bytes 884744 | tf_op jit(solution)/shard_map/ppermute | solution.py:476
  4.0 1.0 %slice.10 = f32[128,512]{1,0:T(8,128)S(1)} slice(f32[512,512]{1,0:T(8,128)} %own_ref.1), slice={[240:368], [0:512]} | slice | bytes 524288 | tf_op jit(solution)/shard_map/slice | solution.py:505
  5.2 1.1 %slice.9 = f32[240,512]{1,0:T(8,128)S(1)} slice(f32[512,512]{1,0:T(8,128)} %own_ref.1), slice={[0:240], [0:512]} | slice | bytes 983040 | tf_op jit(solution)/shard_map/slice | solution.py:508
  6.2 2.1 %collective-permute-start.1 = (f32[240,512]{1,0:T(8,128)S(1)}, f32[240,512]{1,0:T(8,128)S(1)}, u32[]{:S(2)}, u32[]{:S(2)}) collective-permute-start(f32[240,512]{1,0:T(8,128)S(1)} %slice.9), channel_id=1, source_target_pairs={{0,2},{1,3},{2,0},{3,1},{4,6},{5,7},{6,4},{7,5},{8,10},{9,11},{10,... | collective-permute-start | bytes 1474568 | tf_op jit(solution)/shard_map/ppermute | solution.py:476
  8.3 1.2 %copy-done = f32[512,512]{1,0:T(8,128)S(1)} copy-done((f32[512,512]{1,0:T(8,128)S(1)}, f32[512,512]{1,0:T(8,128)}, u32[]{:S(2)}) %copy-start) | copy-done | bytes 1048600
  9.5 2.2 %copy-done.1 = f32[2048,512]{1,0:T(8,128)S(1)} copy-done((f32[2048,512]{1,0:T(8,128)S(1)}, f32[2048,512]{1,0:T(8,128)}, u32[]{:S(2)}) %copy-start.1) | copy-done | bytes 4194328
  11.7 0.9 %copy-done.3 = f32[2048,9]{0,1:T(8,128)S(1)} copy-done((f32[2048,9]{0,1:T(8,128)S(1)}, f32[2048,9]{0,1:T(8,128)}, u32[]{:S(2)}) %copy-start.3) | copy-done | bytes 73752
  12.6 4.0 %shard_map.82 = (f32[512,384]{1,0:T(8,128)S(1)}, f32[512,256]{1,0:T(8,128)S(1)}, bf16[1024,768]{1,0:T(8,128)(2,1)S(1)}, bf16[1024,512]{1,0:T(8,128)(2,1)S(1)}, s32[3,128]{1,0:T(4,128)S(1)}) custom-call(s32[7]{0:T(128)S(1)} %stack.31.index_ref, f32[512,512]{1,0:T(8,128)S(1)} %copy-done, f32[512,512]{1,0:T(8,128)S(1)} %collective-permute-done.beside_ref, ...), custom_call_target="tpu_custom_call" | custom-call | flops 3000000000 | bytes 1048576 | tf_op jit(solution)/shard_map/pallas_call | solution.py:451
  16.6 0.9 %collective-permute-done.2.refs_0_ = f32[128,512]{1,0:T(8,128)S(1)} collective-permute-done((f32[128,512]{1,0:T(8,128)S(1)}, f32[128,512]{1,0:T(8,128)S(1)}, u32[]{:S(2)}, u32[]{:S(2)}) %collective-permute-start.2) | collective-permute-done | bytes 262176 | tf_op jit(solution)/shard_map/ppermute | solution.py:476
  18.7 0.8 %collective-permute-done.4.refs_1_ = f32[128,512]{1,0:T(8,128)S(1)} collective-permute-done((f32[128,512]{1,0:T(8,128)S(1)}, f32[128,512]{1,0:T(8,128)S(1)}, u32[]{:S(2)}, u32[]{:S(2)}) %collective-permute-start.4) | collective-permute-done | bytes 262176 | tf_op jit(solution)/shard_map/ppermute | solution.py:470
  19.5 1.5 %shard_map.83 = (f32[272,384]{1,0:T(8,128)S(1)}, f32[272,256]{1,0:T(8,128)S(1)}, f32[16,384]{1,0:T(8,128)S(1)}) custom-call(f32[128,512]{1,0:T(8,128)S(1)} %collective-permute-done.2.refs_0_, f32[128,512]{1,0:T(8,128)S(1)} %collective-permute-done.4.refs_1_, f32[144,512]{1,0:T(8,128)S(1)} %collective-permute-done.3.refs_2_, ...), custom_call_target="tpu_custom_call" | custom-call | flops 500000000 | bytes 1048576 | tf_op jit(solution)/shard_map/pallas_call | solution.py:451
  21.0 4.0 %collective-permute-start.6 = (f32[16,384]{1,0:T(8,128)S(1)}, f32[16,384]{1,0:T(8,128)S(1)}, u32[]{:S(2)}, u32[]{:S(2)}) collective-permute-start(f32[16,384]{1,0:T(8,128)S(1)} %get-tuple-element.76), channel_id=1, source_target_pairs={{0,4},{4,8},{8,12},{12,16},{16,20},{20,24},{24,28},{1,5},{5,9},{9,... | collective-permute-start | bytes 73736 | tf_op jit(solution)/shard_map/ppermute | solution.py:529
  25.0 2.8 %shard_map.84 = (f32[256,128]{1,0:T(8,128)S(1)}, f32[256,128]{1,0:T(8,128)S(1)}, f32[256,128]{1,0:T(8,128)S(1)}, f32[256,128]{1,0:T(8,128)S(1)}, f32[256,128]{1,...) custom-call(f32[272,384]{1,0:T(8,128)S(1)} %get-tuple-element.74.raw_ref.refs_4_,, ...), custom_call_target="tpu_custom_call" | custom-call | flops 500000000 | bytes 1048576 | tf_op jit(solution)/shard_map/pallas_call | solution.py:451
  27.9 0.7 %shard_map.88.weight_ref.refs_4_.refs_1_ = bf16[512,1024]{1,0:T(8,128)(2,1)S(1)} custom-call(s32[7]{0:T(128)S(1)} %stack.31.index_ref, f32[512,512]{1,0:T(8,128)S(1)} %copy-done.2), custom_call_target="tpu_custom_call" | custom-call | flops 1000000000 | bytes 1048576 | tf_op jit(solution)/shard_map/pallas_call | solution.py:451
  29.0 0.7 %collective-permute-done.7.refs_0_.refs_1_ = f32[240,512]{1,0:T(8,128)S(1)} collective-permute-done((f32[240,512]{1,0:T(8,128)S(1)}, f32[240,512]{1,0:T(8,128)S(1)}, u32[]{:S(2)}, u32[]{:S(2)}) %collective-permute-start.7) | collective-permute-done | bytes 491552 | tf_op jit(solution)/shard_map/ppermute | solution.py:470
  29.7 3.2 %shard_map.86 = (f32[256,128]{1,0:T(8,128)S(1)}, f32[256,128]{1,0:T(8,128)S(1)}, f32[256,128]{1,0:T(8,128)S(1)}, f32[256,128]{1,0:T(8,128)S(1)}, f32[256,128]{1,...) custom-call(f32[240,512]{1,0:T(8,128)S(1)} %collective-permute-done.7.refs_0_.ref, ...), custom_call_target="tpu_custom_call" | custom-call | flops 5000000000 | bytes 1048576 | tf_op jit(solution)/shard_map/pallas_call | solution.py:451
  33.0 1.8 %collective-permute-start.8 = (f32[2,128,128]{2,1,0:T(8,128)S(1)}, f32[2,128,128]{2,1,0:T(8,128)S(1)}, u32[]{:S(2)}, u32[]{:S(2)}) collective-permute-start(f32[2,128,128]{2,1,0:T(8,128)S(1)} %get-tuple-element.80.own_ref), channel_id=1, source_target_pairs={{0,4},{4,0},{8,12},{12,8},{16,20},{20,16},{24,28},{28,24},{1,5},{5... | collective-permute-start | bytes 393224 | tf_op jit(solution)/shard_map/ppermute | solution.py:568
  34.7 1.5 %collective-permute-start.10 = (f32[2,128,128]{2,1,0:T(8,128)S(1)}, f32[2,128,128]{2,1,0:T(8,128)S(1)}, u32[]{:S(2)}, u32[]{:S(2)}) collective-permute-start(f32[2,128,128]{2,1,0:T(8,128)S(1)} %get-tuple-element.80.own_ref), channel_id=1, source_target_pairs={{0,12},{4,8},{8,4},{12,0},{16,28},{20,24},{24,20},{28,16},{1,13},{... | collective-permute-start | bytes 393224 | tf_op jit(solution)/shard_map/ppermute | solution.py:568
  36.5 2.4 %shard_map.87 = (f32[512,128]{1,0:T(8,128)S(1)}, f32[512,128]{1,0:T(8,128)S(1)}, f32[512,128]{1,0:T(8,128)S(1)}) custom-call(f32[240,512]{1,0:T(8,128)S(1)} %collective-permute-done.1.refs_0_, f32[240,512]{1,0:T(8,128)S(1)} %collective-permute-done.7.refs_0_.refs_1_, f32[512,256]{1,0:T(8,128)S(1)} %get-tuple-element.71.refs_5_.refs_2_, ...), custom_call_target="tpu_custom_call" | custom-call | flops 5000000000 | bytes 1048576 | tf_op jit(solution)/shard_map/pallas_call | solution.py:451
  38.9 1.8 %collective-permute-done.8.one_ref = f32[2,128,128]{2,1,0:T(8,128)S(1)} collective-permute-done((f32[2,128,128]{2,1,0:T(8,128)S(1)}, f32[2,128,128]{2,1,0:T(8,128)S(1)}, u32[]{:S(2)}, u32[]{:S(2)}) %collective-permute-start.8) | collective-permute-done | bytes 131104 | tf_op jit(solution)/shard_map/ppermute | solution.py:568
  40.7 1.3 %collective-permute-done.10.three_ref = f32[2,128,128]{2,1,0:T(8,128)S(1)} collective-permute-done((f32[2,128,128]{2,1,0:T(8,128)S(1)}, f32[2,128,128]{2,1,0:T(8,128)S(1)}, u32[]{:S(2)}, u32[]{:S(2)}) %collective-permute-start.10) | collective-permute-done | bytes 131104 | tf_op jit(solution)/shard_map/ppermute | solution.py:568
  42.0 0.7 %collective-permute-done.9.two_ref = f32[2,128,128]{2,1,0:T(8,128)S(1)} collective-permute-done((f32[2,128,128]{2,1,0:T(8,128)S(1)}, f32[2,128,128]{2,1,0:T(8,128)S(1)}, u32[]{:S(2)}, u32[]{:S(2)}) %collective-permute-start.9) | collective-permute-done | bytes 131104 | tf_op jit(solution)/shard_map/ppermute | solution.py:568
  43.2 2.8 %collective-permute-start.11 = (f32[128,128]{1,0:T(8,128)S(1)}, f32[128,128]{1,0:T(8,128)S(1)}, u32[]{:S(2)}, u32[]{:S(2)}) collective-permute-start(f32[128,128]{1,0:T(8,128)S(1)} %get-tuple-element.108), channel_id=1, source_target_pairs={{0,16},{4,20},{8,24},{12,28},{16,0},{20,4},{24,8},{28,12},{1,17},{... | collective-permute-start | bytes 196616 | tf_op jit(solution)/shard_map/ppermute | solution.py:587
  46.3 2.0 %collective-permute-done.11.refs_1_ = f32[128,128]{1,0:T(8,128)S(1)} collective-permute-done((f32[128,128]{1,0:T(8,128)S(1)}, f32[128,128]{1,0:T(8,128)S(1)}, u32[]{:S(2)}, u32[]{:S(2)}) %collective-permute-start.11) | collective-permute-done | bytes 65568 | tf_op jit(solution)/shard_map/ppermute | solution.py:587
  48.8 1.7 %collective-permute-start.14 = (f32[128,128]{1,0:T(8,128)S(1)}, f32[128,128]{1,0:T(8,128)S(1)}, u32[]{:S(2)}, u32[]{:S(2)}) collective-permute-start(f32[128,128]{1,0:T(8,128)S(1)} %get-tuple-element.112), channel_id=1, source_target_pairs={{0,2},{1,3},{2,0},{3,1},{4,6},{5,7},{6,4},{7,5},{8,10},{9,11},{10,... | collective-permute-start | bytes 196616 | tf_op jit(solution)/shard_map/ppermute | solution.py:476
  50.9 1.7 %collective-permute-start.13 = (f32[256,128]{1,0:T(8,128)S(1)}, f32[256,128]{1,0:T(8,128)S(1)}, u32[]{:S(2)}, u32[]{:S(2)}) collective-permute-start(f32[256,128]{1,0:T(8,128)S(1)} %get-tuple-element.111), channel_id=1, source_target_pairs={{0,2},{1,3},{2,0},{3,1},{4,6},{5,7},{6,4},{7,5},{8,10},{9,11},{10,... | collective-permute-start | bytes 393224 | tf_op jit(solution)/shard_map/ppermute | solution.py:476
  52.6 0.6 shard_map.92
  53.4 2.1 %collective-permute-done.15.refs_2_ = f32[128,128]{1,0:T(8,128)S(1)} collective-permute-done((f32[128,128]{1,0:T(8,128)S(1)}, f32[128,128]{1,0:T(8,128)S(1)}, u32[]{:S(2)}, u32[]{:S(2)}) %collective-permute-start.15) | collective-permute-done | bytes 65568 | tf_op jit(solution)/shard_map/ppermute | solution.py:476
  56.0 0.7 %collective-permute-done.16.refs_1_ = f32[128,128]{1,0:T(8,128)S(1)} collective-permute-done((f32[128,128]{1,0:T(8,128)S(1)}, f32[128,128]{1,0:T(8,128)S(1)}, u32[]{:S(2)}, u32[]{:S(2)}) %collective-permute-start.16) | collective-permute-done | bytes 65568 | tf_op jit(solution)/shard_map/ppermute | solution.py:470
  57.7 0.8 %shard_map.94 = (f32[512,512]{1,0:T(8,128)}, f32[256,512]{1,0:T(8,128)S(1)}) custom-call(f32[256,128]{1,0:T(8,128)S(1)} %collective-permute-done.13.refs_0_, bf16[512,1024]{1,0:T(8,128)(2,1)S(1)} %shard_map.88.weight_ref.refs_4_.refs_1_, f32[256,512]{1,0:T(8,128)S(1)} %shard_map.93.refs_2_, f32[256,512]{1,0:T(8,128)S(1)} %get-tuple-element.122.refs_3_), custom_call_target="tpu_custom_call" | custom-call | flops 1000000000 | bytes 1048576 | tf_op jit(solution)/shard_map/pallas_call | solution.py:451
  58.9 1.1 %shard_map.95 = f32[512,512]{1,0:T(8,128)} custom-call(f32[256,128]{1,0:T(8,128)S(1)} %collective-permute-done.18.refs_0_, bf16[512,1024]{1,0:T(8,128)(2,1)S(1)} %shard_map.88.weight_ref.refs_4_.refs_1_, f32[256,512]{1,0:T(8,128)S(1)} %get-tuple-element.123.refs_2_, f32[512,512]{1,0:T(8,128)} %get-tuple-element.124.refs_3_), custom_call_target="tpu_custom_call", output_to_operand_aliasing={{}: (3, {})} | custom-call | flops 1000000000 | bytes 1048576 | tf_op jit(solution)/shard_map/pallas_call | solution.py:451
  (38 shorter events, 5.7 us)
Async XLA Ops:
  0.0 5.2 %collective-permute-start = (f32[512,512]{1,0:T(8,128)}, f32[512,512]{1,0:T(8,128)S(1)}, u32[]{:S(2)}, u32[]{:S(2)}) collective-permute-start(f32[512,512]{1,0:T(8,128)} %own_ref.1), channel_id=1, source_target_pairs={{0,1},{1,0},{2,3},{3,2},{4,5},{5,4},{6,7},{7,6},{8,9},{9,8},{10,11... | collective-permute-start | bytes 3145736 | tf_op jit(solution)/shard_map/ppermute | solution.py:470
  1.4 16.1 %collective-permute-start.3 = (f32[144,512]{1,0:T(8,128)S(1)}, f32[144,512]{1,0:T(8,128)S(1)}, u32[]{:S(2)}, u32[]{:S(2)}) collective-permute-start(f32[144,512]{1,0:T(8,128)S(1)} %slice.11), channel_id=1, source_target_pairs={{0,2},{1,3},{2,0},{3,1},{4,6},{5,7},{6,4},{7,5},{8,10},{9,11},{10,... | collective-permute-start | bytes 884744 | tf_op jit(solution)/shard_map/ppermute | solution.py:476
  5.0 12.5 %collective-permute-start.2 = (f32[128,512]{1,0:T(8,128)S(1)}, f32[128,512]{1,0:T(8,128)S(1)}, u32[]{:S(2)}, u32[]{:S(2)}) collective-permute-start(f32[128,512]{1,0:T(8,128)S(1)} %slice.10), channel_id=1, source_target_pairs={{0,2},{1,3},{2,0},{3,1},{4,6},{5,7},{6,4},{7,5},{8,10},{9,11},{10,... | collective-permute-start | bytes 786440 | tf_op jit(solution)/shard_map/ppermute | solution.py:476
  6.2 21.6 %collective-permute-start.1 = (f32[240,512]{1,0:T(8,128)S(1)}, f32[240,512]{1,0:T(8,128)S(1)}, u32[]{:S(2)}, u32[]{:S(2)}) collective-permute-start(f32[240,512]{1,0:T(8,128)S(1)} %slice.9), channel_id=1, source_target_pairs={{0,2},{1,3},{2,0},{3,1},{4,6},{5,7},{6,4},{7,5},{8,10},{9,11},{10,... | collective-permute-start | bytes 1474568 | tf_op jit(solution)/shard_map/ppermute | solution.py:476
  8.3 1.2 %copy-start = (f32[512,512]{1,0:T(8,128)S(1)}, f32[512,512]{1,0:T(8,128)}, u32[]{:S(2)}) copy-start(f32[512,512]{1,0:T(8,128)} %own_ref.1) | copy-start | bytes 3145732
  9.5 2.2 %copy-start.1 = (f32[2048,512]{1,0:T(8,128)S(1)}, f32[2048,512]{1,0:T(8,128)}, u32[]{:S(2)}) copy-start(f32[2048,512]{1,0:T(8,128)} %proj_ref.1) | copy-start | bytes 12582916
  11.7 0.9 %copy-start.3 = (f32[2048,9]{0,1:T(8,128)S(1)}, f32[2048,9]{0,1:T(8,128)}, u32[]{:S(2)}) copy-start(f32[2048,9]{0,1:T(8,128)} %param.10) | copy-start | bytes 221188
  16.6 8.4 %copy-start.4 = (f32[4,384]{1,0:T(4,128)S(1)}, f32[4,384]{1,0:T(4,128)}, u32[]{:S(2)}) copy-start(f32[4,384]{1,0:T(4,128)} %refs_6_.3) | copy-start | bytes 18436
  16.6 8.4 %copy-start.5 = (s32[512]{0:T(512)S(1)}, s32[512]{0:T(512)}, u32[]{:S(2)}) copy-start(s32[512]{0:T(512)} %param.13) | copy-start | bytes 6148
  16.6 11.2 %copy-start.2 = (f32[512,512]{1,0:T(8,128)S(1)}, f32[512,512]{1,0:T(8,128)}, u32[]{:S(2)}) copy-start(f32[512,512]{1,0:T(8,128)} %weight_ref.1) | copy-start | bytes 3145732
  17.5 2.0 %collective-permute-start.5 = (f32[144,512]{1,0:T(8,128)S(1)}, f32[144,512]{1,0:T(8,128)S(1)}, u32[]{:S(2)}, u32[]{:S(2)}) collective-permute-start(f32[144,512]{1,0:T(8,128)S(1)} %collective-permute-done.3.refs_2_), channel_id=1, source_target_pairs={{0,1},{1,0},{2,3},{3,2},{4,5},{5,4},{6,7},{7,6},{8,9},{9,8},{10,11... | collective-permute-start | bytes 884744 | tf_op jit(solution)/shard_map/ppermute | solution.py:470
  17.5 2.0 %collective-permute-start.4 = (f32[128,512]{1,0:T(8,128)S(1)}, f32[128,512]{1,0:T(8,128)S(1)}, u32[]{:S(2)}, u32[]{:S(2)}) collective-permute-start(f32[128,512]{1,0:T(8,128)S(1)} %collective-permute-done.2.refs_0_), channel_id=1, source_target_pairs={{0,1},{1,0},{2,3},{3,2},{4,5},{5,4},{6,7},{7,6},{8,9},{9,8},{10,11... | collective-permute-start | bytes 786440 | tf_op jit(solution)/shard_map/ppermute | solution.py:470
  21.0 6.8 %collective-permute-start.6 = (f32[16,384]{1,0:T(8,128)S(1)}, f32[16,384]{1,0:T(8,128)S(1)}, u32[]{:S(2)}, u32[]{:S(2)}) collective-permute-start(f32[16,384]{1,0:T(8,128)S(1)} %get-tuple-element.76), channel_id=1, source_target_pairs={{0,4},{4,8},{8,12},{12,16},{16,20},{20,24},{24,28},{1,5},{5,9},{9,... | collective-permute-start | bytes 73736 | tf_op jit(solution)/shard_map/ppermute | solution.py:529
  27.9 1.9 %collective-permute-start.7 = (f32[240,512]{1,0:T(8,128)S(1)}, f32[240,512]{1,0:T(8,128)S(1)}, u32[]{:S(2)}, u32[]{:S(2)}) collective-permute-start(f32[240,512]{1,0:T(8,128)S(1)} %collective-permute-done.1.refs_0_), channel_id=1, source_target_pairs={{0,1},{1,0},{2,3},{3,2},{4,5},{5,4},{6,7},{7,6},{8,9},{9,8},{10,11... | collective-permute-start | bytes 1474568 | tf_op jit(solution)/shard_map/ppermute | solution.py:470
  33.0 7.7 %collective-permute-start.8 = (f32[2,128,128]{2,1,0:T(8,128)S(1)}, f32[2,128,128]{2,1,0:T(8,128)S(1)}, u32[]{:S(2)}, u32[]{:S(2)}) collective-permute-start(f32[2,128,128]{2,1,0:T(8,128)S(1)} %get-tuple-element.80.own_ref), channel_id=1, source_target_pairs={{0,4},{4,0},{8,12},{12,8},{16,20},{20,16},{24,28},{28,24},{1,5},{5... | collective-permute-start | bytes 393224 | tf_op jit(solution)/shard_map/ppermute | solution.py:568
  34.7 7.3 %collective-permute-start.10 = (f32[2,128,128]{2,1,0:T(8,128)S(1)}, f32[2,128,128]{2,1,0:T(8,128)S(1)}, u32[]{:S(2)}, u32[]{:S(2)}) collective-permute-start(f32[2,128,128]{2,1,0:T(8,128)S(1)} %get-tuple-element.80.own_ref), channel_id=1, source_target_pairs={{0,12},{4,8},{8,4},{12,0},{16,28},{20,24},{24,20},{28,16},{1,13},{... | collective-permute-start | bytes 393224 | tf_op jit(solution)/shard_map/ppermute | solution.py:568
  36.3 6.4 %collective-permute-start.9 = (f32[2,128,128]{2,1,0:T(8,128)S(1)}, f32[2,128,128]{2,1,0:T(8,128)S(1)}, u32[]{:S(2)}, u32[]{:S(2)}) collective-permute-start(f32[2,128,128]{2,1,0:T(8,128)S(1)} %get-tuple-element.80.own_ref), channel_id=1, source_target_pairs={{0,8},{4,12},{8,0},{12,4},{16,24},{20,28},{24,16},{28,20},{1,9},{5... | collective-permute-start | bytes 393224 | tf_op jit(solution)/shard_map/ppermute | solution.py:568
  38.9 9.5 %copy-start.6 = (f32[128]{0:T(128)S(1)}, f32[128]{0:T(128)}, u32[]{:S(2)}) copy-start(f32[128]{0:T(128)} %param.14) | copy-start | bytes 1540
  43.2 5.2 %collective-permute-start.11 = (f32[128,128]{1,0:T(8,128)S(1)}, f32[128,128]{1,0:T(8,128)S(1)}, u32[]{:S(2)}, u32[]{:S(2)}) collective-permute-start(f32[128,128]{1,0:T(8,128)S(1)} %get-tuple-element.108), channel_id=1, source_target_pairs={{0,16},{4,20},{8,24},{12,28},{16,0},{20,4},{24,8},{28,12},{1,17},{... | collective-permute-start | bytes 196616 | tf_op jit(solution)/shard_map/ppermute | solution.py:587
  48.7 2.2 %collective-permute-start.12 = (f32[512,128]{1,0:T(8,128)S(1)}, f32[512,128]{1,0:T(8,128)S(1)}, u32[]{:S(2)}, u32[]{:S(2)}) collective-permute-start(f32[512,128]{1,0:T(8,128)S(1)} %get-tuple-element.110.own_ref), channel_id=1, source_target_pairs={{0,1},{1,0},{2,3},{3,2},{4,5},{5,4},{6,7},{7,6},{8,9},{9,8},{10,11... | collective-permute-start | bytes 786440 | tf_op jit(solution)/shard_map/ppermute | solution.py:470
  48.8 4.6 %collective-permute-start.14 = (f32[128,128]{1,0:T(8,128)S(1)}, f32[128,128]{1,0:T(8,128)S(1)}, u32[]{:S(2)}, u32[]{:S(2)}) collective-permute-start(f32[128,128]{1,0:T(8,128)S(1)} %get-tuple-element.112), channel_id=1, source_target_pairs={{0,2},{1,3},{2,0},{3,1},{4,6},{5,7},{6,4},{7,5},{8,10},{9,11},{10,... | collective-permute-start | bytes 196616 | tf_op jit(solution)/shard_map/ppermute | solution.py:476
  50.5 4.9 %collective-permute-start.15 = (f32[128,128]{1,0:T(8,128)S(1)}, f32[128,128]{1,0:T(8,128)S(1)}, u32[]{:S(2)}, u32[]{:S(2)}) collective-permute-start(f32[128,128]{1,0:T(8,128)S(1)} %get-tuple-element.113), channel_id=1, source_target_pairs={{0,2},{1,3},{2,0},{3,1},{4,6},{5,7},{6,4},{7,5},{8,10},{9,11},{10,... | collective-permute-start | bytes 196616 | tf_op jit(solution)/shard_map/ppermute | solution.py:476
  50.9 6.6 %collective-permute-start.13 = (f32[256,128]{1,0:T(8,128)S(1)}, f32[256,128]{1,0:T(8,128)S(1)}, u32[]{:S(2)}, u32[]{:S(2)}) collective-permute-start(f32[256,128]{1,0:T(8,128)S(1)} %get-tuple-element.111), channel_id=1, source_target_pairs={{0,2},{1,3},{2,0},{3,1},{4,6},{5,7},{6,4},{7,5},{8,10},{9,11},{10,... | collective-permute-start | bytes 393224 | tf_op jit(solution)/shard_map/ppermute | solution.py:476
  55.5 1.3 %collective-permute-start.16 = (f32[128,128]{1,0:T(8,128)S(1)}, f32[128,128]{1,0:T(8,128)S(1)}, u32[]{:S(2)}, u32[]{:S(2)}) collective-permute-start(f32[128,128]{1,0:T(8,128)S(1)} %collective-permute-done.14.refs_0_), channel_id=1, source_target_pairs={{0,1},{1,0},{2,3},{3,2},{4,5},{5,4},{6,7},{7,6},{8,9},{9,8},{10,11... | collective-permute-start | bytes 196616 | tf_op jit(solution)/shard_map/ppermute | solution.py:470
  55.5 1.4 %collective-permute-start.17 = (f32[128,128]{1,0:T(8,128)S(1)}, f32[128,128]{1,0:T(8,128)S(1)}, u32[]{:S(2)}, u32[]{:S(2)}) collective-permute-start(f32[128,128]{1,0:T(8,128)S(1)} %collective-permute-done.15.refs_2_), channel_id=1, source_target_pairs={{0,1},{1,0},{2,3},{3,2},{4,5},{5,4},{6,7},{7,6},{8,9},{9,8},{10,11... | collective-permute-start | bytes 196616 | tf_op jit(solution)/shard_map/ppermute | solution.py:470
  57.5 1.3 %collective-permute-start.18 = (f32[256,128]{1,0:T(8,128)S(1)}, f32[256,128]{1,0:T(8,128)S(1)}, u32[]{:S(2)}, u32[]{:S(2)}) collective-permute-start(f32[256,128]{1,0:T(8,128)S(1)} %collective-permute-done.13.refs_0_), channel_id=1, source_target_pairs={{0,1},{1,0},{2,3},{3,2},{4,5},{5,4},{6,7},{7,6},{8,9},{9,8},{10,11... | collective-permute-start | bytes 393224 | tf_op jit(solution)/shard_map/ppermute | solution.py:470

commit v15 on v14

--- a/solution.py
+++ b/solution.py
@@ -81,6 +81,18 @@
         part = (both[:, :columns] + both[:, columns:]) + rest
         total = part if total is None else total + part
     return total
+
+
+def stage_kernel(spans, tokens_ref, *refs):
+    outs, sems = refs[:-1], refs[-1]
+    copies = [
+        pltpu.make_async_copy(tokens_ref.at[rows, :], out, sems.at[spot])
+        for spot, (rows, out) in enumerate(zip(spans, outs))
+    ]
+    for copy in copies:
+        copy.start()
+    for copy in copies:
+        copy.wait()
 
 
 def base_kernel(
@@ -502,10 +514,17 @@
     cut = first - RIM
     middle = tok_rows - CHUNK - RIM
     segments = (slice(cut, middle), slice(middle, tok_rows))
-    late = [to_chips(tokens[rows]) for rows in segments]
-    beside = to_sibling(tokens)
-    early_rows, beside = after(tokens, beside)
-    early = to_chips(early_rows[:cut])
+    spans = (segments[1], segments[0], slice(0, cut), slice(0, tok_rows))
+    tokens, index = after(tokens, index)
+    last_rows, next_rows, early_rows, own = vmem_call(
+        functools.partial(stage_kernel, spans),
+        [like(rows.stop - rows.start, depth) for rows in spans],
+        [pltpu.SemaphoreType.DMA((len(spans),))], 1, tokens, any_in=(0,),
+    )
+    late = [to_chips(next_rows), to_chips(last_rows)]
+    beside = to_sibling(own)
+    early_rows, beside = after(early_rows, beside)
+    early = to_chips(early_rows)
     base_state, base_query, far_state, far_query, flags = vmem_call(
         base_kernel,
         [like(tok_rows, state_columns), like(tok_rows, query_columns),
@@ -515,7 +534,7 @@
          pltpu.VMEM((2 * depth, 2 * state_columns), BF16),
          pltpu.VMEM((2 * depth, 2 * query_columns), BF16),
          pltpu.SemaphoreType.DMA((heads,))],
-        3, index, tokens, beside, w_mix.T, w_proj, any_in=(4,),
+        3, index, own, beside, w_mix.T, w_proj, any_in=(4,),
     )
     late, far_state = after(late, far_state)
     late_on = [[to_sibling(value) for value in values] for values in late]

time: 60.4 us -> 61.2 us (1.013)
  local copies, waits for them, and re-layouts: 7.44 us -> 4.43 us
  waiting for transfers between devices: 12.1 us -> 14.9 us
    slice x3 -> x0, local copies, waits for them, and re-layouts: 3.01 us -> none  [the longest x2 1.95 us: shards(): late = [to_chips(tokens[rows]) for rows in segments]]
    ppermute x6, waiting for transfers between devices: 3.55 us -> 6.44 us  [to_chips(): lax.ppermute(value, 'head', [(source, (source + 2 * step) % count) for so...]
    pallas_call x14 -> x15, Pallas kernels: 19 us -> 19.5 us  [vmem_call(): pl.pallas_call(kernel, out_shape=outs, in_specs=[free if spot in any_in e...]
  transfers between devices with their start and end apart: 19 -> 19, of which waited for: 14 -> 13; matrix products, arithmetic and copies ran while one was open for 5% -> 0% of each run, Pallas kernels for 23% -> 23%
where the time goes in v15:
time: 61.2 us; the launch traced here: 61 us
  starting transfers between devices  21.1 us (34%)
  Pallas kernels  19.5 us (32%)
  waiting for transfers between devices  14.9 us (24%)
  local copies, waits for them, and re-layouts  4.43 us (7%)
  between operations  1.02 us (2%)
    pallas_call x15, Pallas kernels, vmem_call(): pl.pallas_call(kernel, out_shape=outs, in_specs=[free if spot in any_in e...  19.5 us
    ppermute x6, starting transfers between devices, to_chips(): lax.ppermute(value, 'head', [(source, (source + 2 * step) % count) for so...  8.92 us
    ppermute x6, waiting for transfers between devices, to_chips(): lax.ppermute(value, 'head', [(source, (source + 2 * step) % count) for so...  6.44 us
    unnamed x14, local copies, waits for them, and re-layouts  4.34 us
    ppermute x1, starting transfers between devices, shards(): lax.ppermute(rim, 'ctx', [(source, source + 1) for source in range(blocks...  4.01 us
    ppermute x3, waiting for transfers between devices, shards(): lax.ppermute(pair, 'ctx', [(source, source ^ mask << bit) for source in r...  3.71 us
    ppermute x3, starting transfers between devices, shards(): lax.ppermute(pair, 'ctx', [(source, source ^ mask << bit) for source in r...  3.55 us
    ppermute x1, starting transfers between devices, shards(): lax.ppermute(pair if carry else pair[1], 'ctx', [(source, source ^ reach)...  2.8 us
  transfers between devices with their start and end apart: 19, of which 13 were waited for; matrix products, arithmetic and copies ran while one was open for 0% of the time, Pallas kernels for 23%

profile of v15, /device:TPU:0, one launch (start us, length us, event | category | flops | bytes accessed | tf_op | source)
XLA Modules:
  0.0 61.0 jit_solution(6845767910373092152)
XLA Ops:
  0.1 1.2 %copy-done.1 = f32[512,512]{1,0:T(8,128)S(1)} copy-done((f32[512,512]{1,0:T(8,128)S(1)}, f32[512,512]{1,0:T(8,128)}, u32[]{:S(2)}) %copy-start.1) | copy-done | bytes 1048600
  1.8 0.5 collective-permute-start
  2.3 2.6 %collective-permute-start.3 = (f32[144,512]{1,0:T(8,128)S(1)}, f32[144,512]{1,0:T(8,128)S(1)}, u32[]{:S(2)}, u32[]{:S(2)}) collective-permute-start(f32[144,512]{1,0:T(8,128)S(1)} %get-tuple-element.76), channel_id=1, source_target_pairs={{0,2},{1,3},{2,0},{3,1},{4,6},{5,7},{6,4},{7,5},{8,10},{9,11},{10,... | collective-permute-start | bytes 884744 | tf_op jit(solution)/shard_map/ppermute | solution.py:488
  5.0 2.5 %collective-permute-start.1 = (f32[240,512]{1,0:T(8,128)S(1)}, f32[240,512]{1,0:T(8,128)S(1)}, u32[]{:S(2)}, u32[]{:S(2)}) collective-permute-start(f32[240,512]{1,0:T(8,128)S(1)} %get-tuple-element.74), channel_id=1, source_target_pairs={{0,2},{1,3},{2,0},{3,1},{4,6},{5,7},{6,4},{7,5},{8,10},{9,11},{10,... | collective-permute-start | bytes 1474568 | tf_op jit(solution)/shard_map/ppermute | solution.py:488
  7.5 2.2 %copy-done = f32[2048,512]{1,0:T(8,128)S(1)} copy-done((f32[2048,512]{1,0:T(8,128)S(1)}, f32[2048,512]{1,0:T(8,128)}, u32[]{:S(2)}) %copy-start) | copy-done | bytes 4194328
  9.7 0.9 %copy-done.3 = f32[2048,9]{0,1:T(8,128)S(1)} copy-done((f32[2048,9]{0,1:T(8,128)S(1)}, f32[2048,9]{0,1:T(8,128)}, u32[]{:S(2)}) %copy-start.3) | copy-done | bytes 73752
  10.6 3.9 %shard_map.83 = (f32[512,384]{1,0:T(8,128)S(1)}, f32[512,256]{1,0:T(8,128)S(1)}, bf16[1024,768]{1,0:T(8,128)(2,1)S(1)}, bf16[1024,512]{1,0:T(8,128)(2,1)S(1)}, s32[3,128]{1,0:T(4,128)S(1)}) custom-call(s32[7]{0:T(128)S(1)} %stack.31.index_ref, f32[512,512]{1,0:T(8,128)S(1)} %get-tuple-element.73.own_ref, f32[512,512]{1,0:T(8,128)S(1)} %collective-permute-done.beside_ref, ...), custom_call_target="tpu_custom_call" | custom-call | flops 3000000000 | bytes 1048576 | tf_op jit(solution)/shard_map/pallas_call | solution.py:463
  14.6 3.8 %collective-permute-done.2.refs_0_ = f32[128,512]{1,0:T(8,128)S(1)} collective-permute-done((f32[128,512]{1,0:T(8,128)S(1)}, f32[128,512]{1,0:T(8,128)S(1)}, u32[]{:S(2)}, u32[]{:S(2)}) %collective-permute-start.2) | collective-permute-done | bytes 262176 | tf_op jit(solution)/shard_map/ppermute | solution.py:488
  18.4 0.5 collective-permute-start.4
  19.6 0.8 %collective-permute-done.4.refs_1_ = f32[128,512]{1,0:T(8,128)S(1)} collective-permute-done((f32[128,512]{1,0:T(8,128)S(1)}, f32[128,512]{1,0:T(8,128)S(1)}, u32[]{:S(2)}, u32[]{:S(2)}) %collective-permute-start.4) | collective-permute-done | bytes 262176 | tf_op jit(solution)/shard_map/ppermute | solution.py:482
  20.4 1.5 %shard_map.84 = (f32[272,384]{1,0:T(8,128)S(1)}, f32[272,256]{1,0:T(8,128)S(1)}, f32[16,384]{1,0:T(8,128)S(1)}) custom-call(f32[128,512]{1,0:T(8,128)S(1)} %collective-permute-done.2.refs_0_, f32[128,512]{1,0:T(8,128)S(1)} %collective-permute-done.4.refs_1_, f32[144,512]{1,0:T(8,128)S(1)} %collective-permute-done.3.refs_2_, ...), custom_call_target="tpu_custom_call" | custom-call | flops 500000000 | bytes 1048576 | tf_op jit(solution)/shard_map/pallas_call | solution.py:463
  21.9 4.0 %collective-permute-start.6 = (f32[16,384]{1,0:T(8,128)S(1)}, f32[16,384]{1,0:T(8,128)S(1)}, u32[]{:S(2)}, u32[]{:S(2)}) collective-permute-start(f32[16,384]{1,0:T(8,128)S(1)} %get-tuple-element.88), channel_id=1, source_target_pairs={{0,4},{4,8},{8,12},{12,16},{16,20},{20,24},{24,28},{1,5},{5,9},{9,... | collective-permute-start | bytes 73736 | tf_op jit(solution)/shard_map/ppermute | solution.py:548
  25.9 2.8 %shard_map.85 = (f32[256,128]{1,0:T(8,128)S(1)}, f32[256,128]{1,0:T(8,128)S(1)}, f32[256,128]{1,0:T(8,128)S(1)}, f32[256,128]{1,0:T(8,128)S(1)}, f32[256,128]{1,...) custom-call(f32[272,384]{1,0:T(8,128)S(1)} %get-tuple-element.86.raw_ref.refs_4_,, ...), custom_call_target="tpu_custom_call" | custom-call | flops 500000000 | bytes 1048576 | tf_op jit(solution)/shard_map/pallas_call | solution.py:463
  28.8 0.7 %shard_map.89.weight_ref.refs_4_.refs_1_ = bf16[512,1024]{1,0:T(8,128)(2,1)S(1)} custom-call(s32[7]{0:T(128)S(1)} %stack.31.index_ref, f32[512,512]{1,0:T(8,128)S(1)} %copy-done.2), custom_call_target="tpu_custom_call" | custom-call | flops 1000000000 | bytes 1048576 | tf_op jit(solution)/shard_map/pallas_call | solution.py:463
  29.9 0.7 %collective-permute-done.7.refs_0_.refs_1_ = f32[240,512]{1,0:T(8,128)S(1)} collective-permute-done((f32[240,512]{1,0:T(8,128)S(1)}, f32[240,512]{1,0:T(8,128)S(1)}, u32[]{:S(2)}, u32[]{:S(2)}) %collective-permute-start.7) | collective-permute-done | bytes 491552 | tf_op jit(solution)/shard_map/ppermute | solution.py:482
  30.6 3.2 %shard_map.87 = (f32[256,128]{1,0:T(8,128)S(1)}, f32[256,128]{1,0:T(8,128)S(1)}, f32[256,128]{1,0:T(8,128)S(1)}, f32[256,128]{1,0:T(8,128)S(1)}, f32[256,128]{1,...) custom-call(f32[240,512]{1,0:T(8,128)S(1)} %collective-permute-done.7.refs_0_.ref, ...), custom_call_target="tpu_custom_call" | custom-call | flops 5000000000 | bytes 1048576 | tf_op jit(solution)/shard_map/pallas_call | solution.py:463
  33.9 1.7 %collective-permute-start.8 = (f32[2,128,128]{2,1,0:T(8,128)S(1)}, f32[2,128,128]{2,1,0:T(8,128)S(1)}, u32[]{:S(2)}, u32[]{:S(2)}) collective-permute-start(f32[2,128,128]{2,1,0:T(8,128)S(1)} %get-tuple-element.92.own_ref), channel_id=1, source_target_pairs={{0,4},{4,0},{8,12},{12,8},{16,20},{20,16},{24,28},{28,24},{1,5},{5... | collective-permute-start | bytes 393224 | tf_op jit(solution)/shard_map/ppermute | solution.py:587
  35.6 1.6 %collective-permute-start.10 = (f32[2,128,128]{2,1,0:T(8,128)S(1)}, f32[2,128,128]{2,1,0:T(8,128)S(1)}, u32[]{:S(2)}, u32[]{:S(2)}) collective-permute-start(f32[2,128,128]{2,1,0:T(8,128)S(1)} %get-tuple-element.92.own_ref), channel_id=1, source_target_pairs={{0,12},{4,8},{8,4},{12,0},{16,28},{20,24},{24,20},{28,16},{1,13},{... | collective-permute-start | bytes 393224 | tf_op jit(solution)/shard_map/ppermute | solution.py:587
  37.4 2.4 %shard_map.88 = (f32[512,128]{1,0:T(8,128)S(1)}, f32[512,128]{1,0:T(8,128)S(1)}, f32[512,128]{1,0:T(8,128)S(1)}) custom-call(f32[240,512]{1,0:T(8,128)S(1)} %collective-permute-done.1.refs_0_, f32[240,512]{1,0:T(8,128)S(1)} %collective-permute-done.7.refs_0_.refs_1_, f32[512,256]{1,0:T(8,128)S(1)} %get-tuple-element.83.refs_5_.refs_2_, ...), custom_call_target="tpu_custom_call" | custom-call | flops 5000000000 | bytes 1048576 | tf_op jit(solution)/shard_map/pallas_call | solution.py:463
  39.8 1.8 %collective-permute-done.8.one_ref = f32[2,128,128]{2,1,0:T(8,128)S(1)} collective-permute-done((f32[2,128,128]{2,1,0:T(8,128)S(1)}, f32[2,128,128]{2,1,0:T(8,128)S(1)}, u32[]{:S(2)}, u32[]{:S(2)}) %collective-permute-start.8) | collective-permute-done | bytes 131104 | tf_op jit(solution)/shard_map/ppermute | solution.py:587
  41.7 1.2 %collective-permute-done.10.three_ref = f32[2,128,128]{2,1,0:T(8,128)S(1)} collective-permute-done((f32[2,128,128]{2,1,0:T(8,128)S(1)}, f32[2,128,128]{2,1,0:T(8,128)S(1)}, u32[]{:S(2)}, u32[]{:S(2)}) %collective-permute-start.10) | collective-permute-done | bytes 131104 | tf_op jit(solution)/shard_map/ppermute | solution.py:587
  42.9 0.7 %collective-permute-done.9.two_ref = f32[2,128,128]{2,1,0:T(8,128)S(1)} collective-permute-done((f32[2,128,128]{2,1,0:T(8,128)S(1)}, f32[2,128,128]{2,1,0:T(8,128)S(1)}, u32[]{:S(2)}, u32[]{:S(2)}) %collective-permute-start.9) | collective-permute-done | bytes 131104 | tf_op jit(solution)/shard_map/ppermute | solution.py:587
  44.0 2.8 %collective-permute-start.11 = (f32[128,128]{1,0:T(8,128)S(1)}, f32[128,128]{1,0:T(8,128)S(1)}, u32[]{:S(2)}, u32[]{:S(2)}) collective-permute-start(f32[128,128]{1,0:T(8,128)S(1)} %get-tuple-element.120), channel_id=1, source_target_pairs={{0,16},{4,20},{8,24},{12,28},{16,0},{20,4},{24,8},{28,12},{1,17},{... | collective-permute-start | bytes 196616 | tf_op jit(solution)/shard_map/ppermute | solution.py:606
  47.2 2.0 %collective-permute-done.11.refs_1_ = f32[128,128]{1,0:T(8,128)S(1)} collective-permute-done((f32[128,128]{1,0:T(8,128)S(1)}, f32[128,128]{1,0:T(8,128)S(1)}, u32[]{:S(2)}, u32[]{:S(2)}) %collective-permute-start.11) | collective-permute-done | bytes 65568 | tf_op jit(solution)/shard_map/ppermute | solution.py:606
  49.6 1.7 %collective-permute-start.14 = (f32[128,128]{1,0:T(8,128)S(1)}, f32[128,128]{1,0:T(8,128)S(1)}, u32[]{:S(2)}, u32[]{:S(2)}) collective-permute-start(f32[128,128]{1,0:T(8,128)S(1)} %get-tuple-element.124), channel_id=1, source_target_pairs={{0,2},{1,3},{2,0},{3,1},{4,6},{5,7},{6,4},{7,5},{8,10},{9,11},{10,... | collective-permute-start | bytes 196616 | tf_op jit(solution)/shard_map/ppermute | solution.py:488
  51.7 1.7 %collective-permute-start.13 = (f32[256,128]{1,0:T(8,128)S(1)}, f32[256,128]{1,0:T(8,128)S(1)}, u32[]{:S(2)}, u32[]{:S(2)}) collective-permute-start(f32[256,128]{1,0:T(8,128)S(1)} %get-tuple-element.123), channel_id=1, source_target_pairs={{0,2},{1,3},{2,0},{3,1},{4,6},{5,7},{6,4},{7,5},{8,10},{9,11},{10,... | collective-permute-start | bytes 393224 | tf_op jit(solution)/shard_map/ppermute | solution.py:488
  53.4 0.6 shard_map.93
  54.2 2.1 %collective-permute-done.15.refs_2_ = f32[128,128]{1,0:T(8,128)S(1)} collective-permute-done((f32[128,128]{1,0:T(8,128)S(1)}, f32[128,128]{1,0:T(8,128)S(1)}, u32[]{:S(2)}, u32[]{:S(2)}) %collective-permute-start.15) | collective-permute-done | bytes 65568 | tf_op jit(solution)/shard_map/ppermute | solution.py:488
  56.3 0.5 collective-permute-start.17
  56.8 0.7 %collective-permute-done.16.refs_1_ = f32[128,128]{1,0:T(8,128)S(1)} collective-permute-done((f32[128,128]{1,0:T(8,128)S(1)}, f32[128,128]{1,0:T(8,128)S(1)}, u32[]{:S(2)}, u32[]{:S(2)}) %collective-permute-start.16) | collective-permute-done | bytes 65568 | tf_op jit(solution)/shard_map/ppermute | solution.py:482
  58.5 0.8 %shard_map.95 = (f32[512,512]{1,0:T(8,128)}, f32[256,512]{1,0:T(8,128)S(1)}) custom-call(f32[256,128]{1,0:T(8,128)S(1)} %collective-permute-done.13.refs_0_, bf16[512,1024]{1,0:T(8,128)(2,1)S(1)} %shard_map.89.weight_ref.refs_4_.refs_1_, f32[256,512]{1,0:T(8,128)S(1)} %shard_map.94.refs_2_, f32[256,512]{1,0:T(8,128)S(1)} %get-tuple-element.134.refs_3_), custom_call_target="tpu_custom_call" | custom-call | flops 1000000000 | bytes 1048576 | tf_op jit(solution)/shard_map/pallas_call | solution.py:463
  59.7 1.1 %shard_map.96 = f32[512,512]{1,0:T(8,128)} custom-call(f32[256,128]{1,0:T(8,128)S(1)} %collective-permute-done.18.refs_0_, bf16[512,1024]{1,0:T(8,128)(2,1)S(1)} %shard_map.89.weight_ref.refs_4_.refs_1_, f32[256,512]{1,0:T(8,128)S(1)} %get-tuple-element.135.refs_2_, f32[512,512]{1,0:T(8,128)} %get-tuple-element.136.refs_3_), custom_call_target="tpu_custom_call", output_to_operand_aliasing={{}: (3, {})} | custom-call | flops 1000000000 | bytes 1048576 | tf_op jit(solution)/shard_map/pallas_call | solution.py:463
  (36 shorter events, 4.7 us)
Async XLA Ops:
  0.1 1.2 %copy-start.1 = (f32[512,512]{1,0:T(8,128)S(1)}, f32[512,512]{1,0:T(8,128)}, u32[]{:S(2)}) copy-start(f32[512,512]{1,0:T(8,128)} %tokens_ref) | copy-start | bytes 3145732
  1.8 3.2 %collective-permute-start = (f32[512,512]{1,0:T(8,128)S(1)}, f32[512,512]{1,0:T(8,128)S(1)}, u32[]{:S(2)}, u32[]{:S(2)}) collective-permute-start(f32[512,512]{1,0:T(8,128)S(1)} %get-tuple-element.73.own_ref), channel_id=1, source_target_pairs={{0,1},{1,0},{2,3},{3,2},{4,5},{5,4},{6,7},{7,6},{8,9},{9,8},{10,11... | collective-permute-start | bytes 3145736 | tf_op jit(solution)/shard_map/ppermute | solution.py:482
  2.3 16.1 %collective-permute-start.3 = (f32[144,512]{1,0:T(8,128)S(1)}, f32[144,512]{1,0:T(8,128)S(1)}, u32[]{:S(2)}, u32[]{:S(2)}) collective-permute-start(f32[144,512]{1,0:T(8,128)S(1)} %get-tuple-element.76), channel_id=1, source_target_pairs={{0,2},{1,3},{2,0},{3,1},{4,6},{5,7},{6,4},{7,5},{8,10},{9,11},{10,... | collective-permute-start | bytes 884744 | tf_op jit(solution)/shard_map/ppermute | solution.py:488
  4.9 13.5 %collective-permute-start.2 = (f32[128,512]{1,0:T(8,128)S(1)}, f32[128,512]{1,0:T(8,128)S(1)}, u32[]{:S(2)}, u32[]{:S(2)}) collective-permute-start(f32[128,512]{1,0:T(8,128)S(1)} %get-tuple-element.75), channel_id=1, source_target_pairs={{0,2},{1,3},{2,0},{3,1},{4,6},{5,7},{6,4},{7,5},{8,10},{9,11},{10,... | collective-permute-start | bytes 786440 | tf_op jit(solution)/shard_map/ppermute | solution.py:488
  5.0 23.7 %collective-permute-start.1 = (f32[240,512]{1,0:T(8,128)S(1)}, f32[240,512]{1,0:T(8,128)S(1)}, u32[]{:S(2)}, u32[]{:S(2)}) collective-permute-start(f32[240,512]{1,0:T(8,128)S(1)} %get-tuple-element.74), channel_id=1, source_target_pairs={{0,2},{1,3},{2,0},{3,1},{4,6},{5,7},{6,4},{7,5},{8,10},{9,11},{10,... | collective-permute-start | bytes 1474568 | tf_op jit(solution)/shard_map/ppermute | solution.py:488
  7.5 2.2 %copy-start = (f32[2048,512]{1,0:T(8,128)S(1)}, f32[2048,512]{1,0:T(8,128)}, u32[]{:S(2)}) copy-start(f32[2048,512]{1,0:T(8,128)} %proj_ref.1) | copy-start | bytes 12582916
  9.7 0.9 %copy-start.3 = (f32[2048,9]{0,1:T(8,128)S(1)}, f32[2048,9]{0,1:T(8,128)}, u32[]{:S(2)}) copy-start(f32[2048,9]{0,1:T(8,128)} %param.10) | copy-start | bytes 221188
  14.5 11.3 %copy-start.4 = (f32[4,384]{1,0:T(4,128)S(1)}, f32[4,384]{1,0:T(4,128)}, u32[]{:S(2)}) copy-start(f32[4,384]{1,0:T(4,128)} %refs_6_.3) | copy-start | bytes 18436
  14.6 11.3 %copy-start.5 = (s32[512]{0:T(512)S(1)}, s32[512]{0:T(512)}, u32[]{:S(2)}) copy-start(s32[512]{0:T(512)} %param.13) | copy-start | bytes 6148
  14.6 14.2 %copy-start.2 = (f32[512,512]{1,0:T(8,128)S(1)}, f32[512,512]{1,0:T(8,128)}, u32[]{:S(2)}) copy-start(f32[512,512]{1,0:T(8,128)} %weight_ref.1) | copy-start | bytes 3145732
  18.4 2.0 %collective-permute-start.5 = (f32[144,512]{1,0:T(8,128)S(1)}, f32[144,512]{1,0:T(8,128)S(1)}, u32[]{:S(2)}, u32[]{:S(2)}) collective-permute-start(f32[144,512]{1,0:T(8,128)S(1)} %collective-permute-done.3.refs_2_), channel_id=1, source_target_pairs={{0,1},{1,0},{2,3},{3,2},{4,5},{5,4},{6,7},{7,6},{8,9},{9,8},{10,11... | collective-permute-start | bytes 884744 | tf_op jit(solution)/shard_map/ppermute | solution.py:482
  18.4 2.0 %collective-permute-start.4 = (f32[128,512]{1,0:T(8,128)S(1)}, f32[128,512]{1,0:T(8,128)S(1)}, u32[]{:S(2)}, u32[]{:S(2)}) collective-permute-start(f32[128,512]{1,0:T(8,128)S(1)} %collective-permute-done.2.refs_0_), channel_id=1, source_target_pairs={{0,1},{1,0},{2,3},{3,2},{4,5},{5,4},{6,7},{7,6},{8,9},{9,8},{10,11... | collective-permute-start | bytes 786440 | tf_op jit(solution)/shard_map/ppermute | solution.py:482
  21.9 6.8 %collective-permute-start.6 = (f32[16,384]{1,0:T(8,128)S(1)}, f32[16,384]{1,0:T(8,128)S(1)}, u32[]{:S(2)}, u32[]{:S(2)}) collective-permute-start(f32[16,384]{1,0:T(8,128)S(1)} %get-tuple-element.88), channel_id=1, source_target_pairs={{0,4},{4,8},{8,12},{12,16},{16,20},{20,24},{24,28},{1,5},{5,9},{9,... | collective-permute-start | bytes 73736 | tf_op jit(solution)/shard_map/ppermute | solution.py:548
  28.7 1.9 %collective-permute-start.7 = (f32[240,512]{1,0:T(8,128)S(1)}, f32[240,512]{1,0:T(8,128)S(1)}, u32[]{:S(2)}, u32[]{:S(2)}) collective-permute-start(f32[240,512]{1,0:T(8,128)S(1)} %collective-permute-done.1.refs_0_), channel_id=1, source_target_pairs={{0,1},{1,0},{2,3},{3,2},{4,5},{5,4},{6,7},{7,6},{8,9},{9,8},{10,11... | collective-permute-start | bytes 1474568 | tf_op jit(solution)/shard_map/ppermute | solution.py:482
  33.9 7.8 %collective-permute-start.8 = (f32[2,128,128]{2,1,0:T(8,128)S(1)}, f32[2,128,128]{2,1,0:T(8,128)S(1)}, u32[]{:S(2)}, u32[]{:S(2)}) collective-permute-start(f32[2,128,128]{2,1,0:T(8,128)S(1)} %get-tuple-element.92.own_ref), channel_id=1, source_target_pairs={{0,4},{4,0},{8,12},{12,8},{16,20},{20,16},{24,28},{28,24},{1,5},{5... | collective-permute-start | bytes 393224 | tf_op jit(solution)/shard_map/ppermute | solution.py:587
  35.6 7.3 %collective-permute-start.10 = (f32[2,128,128]{2,1,0:T(8,128)S(1)}, f32[2,128,128]{2,1,0:T(8,128)S(1)}, u32[]{:S(2)}, u32[]{:S(2)}) collective-permute-start(f32[2,128,128]{2,1,0:T(8,128)S(1)} %get-tuple-element.92.own_ref), channel_id=1, source_target_pairs={{0,12},{4,8},{8,4},{12,0},{16,28},{20,24},{24,20},{28,16},{1,13},{... | collective-permute-start | bytes 393224 | tf_op jit(solution)/shard_map/ppermute | solution.py:587
  37.1 6.4 %collective-permute-start.9 = (f32[2,128,128]{2,1,0:T(8,128)S(1)}, f32[2,128,128]{2,1,0:T(8,128)S(1)}, u32[]{:S(2)}, u32[]{:S(2)}) collective-permute-start(f32[2,128,128]{2,1,0:T(8,128)S(1)} %get-tuple-element.92.own_ref), channel_id=1, source_target_pairs={{0,8},{4,12},{8,0},{12,4},{16,24},{20,28},{24,16},{28,20},{1,9},{5... | collective-permute-start | bytes 393224 | tf_op jit(solution)/shard_map/ppermute | solution.py:587
  39.8 9.4 %copy-start.6 = (f32[128]{0:T(128)S(1)}, f32[128]{0:T(128)}, u32[]{:S(2)}) copy-start(f32[128]{0:T(128)} %param.14) | copy-start | bytes 1540
  44.0 5.2 %collective-permute-start.11 = (f32[128,128]{1,0:T(8,128)S(1)}, f32[128,128]{1,0:T(8,128)S(1)}, u32[]{:S(2)}, u32[]{:S(2)}) collective-permute-start(f32[128,128]{1,0:T(8,128)S(1)} %get-tuple-element.120), channel_id=1, source_target_pairs={{0,16},{4,20},{8,24},{12,28},{16,0},{20,4},{24,8},{28,12},{1,17},{... | collective-permute-start | bytes 196616 | tf_op jit(solution)/shard_map/ppermute | solution.py:606
  49.6 2.2 %collective-permute-start.12 = (f32[512,128]{1,0:T(8,128)S(1)}, f32[512,128]{1,0:T(8,128)S(1)}, u32[]{:S(2)}, u32[]{:S(2)}) collective-permute-start(f32[512,128]{1,0:T(8,128)S(1)} %get-tuple-element.122.own_ref), channel_id=1, source_target_pairs={{0,1},{1,0},{2,3},{3,2},{4,5},{5,4},{6,7},{7,6},{8,9},{9,8},{10,11... | collective-permute-start | bytes 786440 | tf_op jit(solution)/shard_map/ppermute | solution.py:482
  49.6 4.6 %collective-permute-start.14 = (f32[128,128]{1,0:T(8,128)S(1)}, f32[128,128]{1,0:T(8,128)S(1)}, u32[]{:S(2)}, u32[]{:S(2)}) collective-permute-start(f32[128,128]{1,0:T(8,128)S(1)} %get-tuple-element.124), channel_id=1, source_target_pairs={{0,2},{1,3},{2,0},{3,1},{4,6},{5,7},{6,4},{7,5},{8,10},{9,11},{10,... | collective-permute-start | bytes 196616 | tf_op jit(solution)/shard_map/ppermute | solution.py:488
  51.4 4.9 %collective-permute-start.15 = (f32[128,128]{1,0:T(8,128)S(1)}, f32[128,128]{1,0:T(8,128)S(1)}, u32[]{:S(2)}, u32[]{:S(2)}) collective-permute-start(f32[128,128]{1,0:T(8,128)S(1)} %get-tuple-element.125), channel_id=1, source_target_pairs={{0,2},{1,3},{2,0},{3,1},{4,6},{5,7},{6,4},{7,5},{8,10},{9,11},{10,... | collective-permute-start | bytes 196616 | tf_op jit(solution)/shard_map/ppermute | solution.py:488
  51.7 6.6 %collective-permute-start.13 = (f32[256,128]{1,0:T(8,128)S(1)}, f32[256,128]{1,0:T(8,128)S(1)}, u32[]{:S(2)}, u32[]{:S(2)}) collective-permute-start(f32[256,128]{1,0:T(8,128)S(1)} %get-tuple-element.123), channel_id=1, source_target_pairs={{0,2},{1,3},{2,0},{3,1},{4,6},{5,7},{6,4},{7,5},{8,10},{9,11},{10,... | collective-permute-start | bytes 393224 | tf_op jit(solution)/shard_map/ppermute | solution.py:488
  56.3 1.3 %collective-permute-start.16 = (f32[128,128]{1,0:T(8,128)S(1)}, f32[128,128]{1,0:T(8,128)S(1)}, u32[]{:S(2)}, u32[]{:S(2)}) collective-permute-start(f32[128,128]{1,0:T(8,128)S(1)} %collective-permute-done.14.refs_0_), channel_id=1, source_target_pairs={{0,1},{1,0},{2,3},{3,2},{4,5},{5,4},{6,7},{7,6},{8,9},{9,8},{10,11... | collective-permute-start | bytes 196616 | tf_op jit(solution)/shard_map/ppermute | solution.py:482
  56.3 1.4 %collective-permute-start.17 = (f32[128,128]{1,0:T(8,128)S(1)}, f32[128,128]{1,0:T(8,128)S(1)}, u32[]{:S(2)}, u32[]{:S(2)}) collective-permute-start(f32[128,128]{1,0:T(8,128)S(1)} %collective-permute-done.15.refs_2_), channel_id=1, source_target_pairs={{0,1},{1,0},{2,3},{3,2},{4,5},{5,4},{6,7},{7,6},{8,9},{9,8},{10,11... | collective-permute-start | bytes 196616 | tf_op jit(solution)/shard_map/ppermute | solution.py:482
  58.4 1.3 %collective-permute-start.18 = (f32[256,128]{1,0:T(8,128)S(1)}, f32[256,128]{1,0:T(8,128)S(1)}, u32[]{:S(2)}, u32[]{:S(2)}) collective-permute-start(f32[256,128]{1,0:T(8,128)S(1)} %collective-permute-done.13.refs_0_), channel_id=1, source_target_pairs={{0,1},{1,0},{2,3},{3,2},{4,5},{5,4},{6,7},{7,6},{8,9},{9,8},{10,11... | collective-permute-start | bytes 393224 | tf_op jit(solution)/shard_map/ppermute | solution.py:482

commit v16 on v15

--- a/solution.py
+++ b/solution.py
@@ -10,6 +10,7 @@
 CHUNK = 128
 RIM = 16
 VMEM_GRANT = 16 << 20
+STAGE_GRANT = 61 << 20
 F32 = jnp.float32
 BF16 = jnp.bfloat16
 
@@ -456,7 +457,7 @@
         copy.wait()
 
 
-def vmem_call(kernel, outs, scratch, cost, *args, any_in=(), any_out=(), aliases=()):
+def vmem_call(kernel, outs, scratch, cost, *args, any_in=(), any_out=(), aliases=(), grant=VMEM_GRANT):
     spec = pl.BlockSpec(memory_space=pltpu.VMEM)
     small = pl.BlockSpec(memory_space=pltpu.SMEM)
     free = pl.BlockSpec(memory_space=pl.ANY)
@@ -472,7 +473,7 @@
         else (free if any_out else spec),
         input_output_aliases=dict(aliases),
         scratch_shapes=scratch,
-        compiler_params=pltpu.CompilerParams(vmem_limit_bytes=VMEM_GRANT),
+        compiler_params=pltpu.CompilerParams(vmem_limit_bytes=grant),
         cost_estimate=pl.CostEstimate(flops=int(cost * 1e9), bytes_accessed=1 << 20, transcendentals=0),
     )(*args)
 
@@ -519,7 +520,7 @@
     last_rows, next_rows, early_rows, own = vmem_call(
         functools.partial(stage_kernel, spans),
         [like(rows.stop - rows.start, depth) for rows in spans],
-        [pltpu.SemaphoreType.DMA((len(spans),))], 1, tokens, any_in=(0,),
+        [pltpu.SemaphoreType.DMA((len(spans),))], 1, tokens, any_in=(0,), any_out=(0, 1, 2, 3), grant=STAGE_GRANT,
     )
     late = [to_chips(next_rows), to_chips(last_rows)]
     beside = to_sibling(own)
@@ -534,7 +535,7 @@
          pltpu.VMEM((2 * depth, 2 * state_columns), BF16),
          pltpu.VMEM((2 * depth, 2 * query_columns), BF16),
          pltpu.SemaphoreType.DMA((heads,))],
-        3, index, own, beside, w_mix.T, w_proj, any_in=(4,),
+        3, index, tokens, beside, w_mix.T, w_proj, any_in=(4,),
     )
     late, far_state = after(late, far_state)
     late_on = [[to_sibling(value) for value in values] for values in late]

time: 61.2 us -> 124 us (2.03)
  Pallas kernels: 19.5 us -> 83.6 us
    pallas_call x15, Pallas kernels: 19.5 us -> 83.6 us  [vmem_call(): pl.pallas_call(kernel, out_shape=outs, in_specs=[free if spot in any_in e...]
  transfers between devices with their start and end apart: 19 -> 19, of which waited for: 13 -> 13; matrix products, arithmetic and copies ran while one was open for 0% -> 0% of each run, Pallas kernels for 23% -> 11%
where the time goes in v16:
time: 124 us
  Pallas kernels  83.6 us (67%)
  starting transfers between devices  21.3 us (17%)
  waiting for transfers between devices  13.7 us (11%)
  local copies, waits for them, and re-layouts  4.42 us (4%)
    pallas_call x15, Pallas kernels, vmem_call(): pl.pallas_call(kernel, out_shape=outs, in_specs=[free if spot in any_in e...  83.6 us
    ppermute x6, starting transfers between devices, to_chips(): lax.ppermute(value, 'head', [(source, (source + 2 * step) % count) for so...  9.13 us
    ppermute x6, waiting for transfers between devices, to_chips(): lax.ppermute(value, 'head', [(source, (source + 2 * step) % count) for so...  5.22 us
    unnamed x14, local copies, waits for them, and re-layouts  4.34 us
    ppermute x1, starting transfers between devices, shards(): lax.ppermute(rim, 'ctx', [(source, source + 1) for source in range(blocks...  4.01 us
    ppermute x3, waiting for transfers between devices, shards(): lax.ppermute(pair, 'ctx', [(source, source ^ mask << bit) for source in r...  3.71 us
    ppermute x3, starting transfers between devices, shards(): lax.ppermute(pair, 'ctx', [(source, source ^ mask << bit) for source in r...  3.55 us
    ppermute x1, starting transfers between devices, shards(): lax.ppermute(pair if carry else pair[1], 'ctx', [(source, source ^ reach)...  2.8 us
  transfers between devices with their start and end apart: 19, of which 13 were waited for; matrix products, arithmetic and copies ran while one was open for 0% of the time, Pallas kernels for 11%

profile of v16, /device:TPU:0, one launch (start us, length us, event | category | flops | bytes accessed | tf_op | source)
XLA Modules:
  0.0 124.1 jit_solution(2588654965742609313)
XLA Ops:
  0.1 64.7 %shard_map.82 = (f32[144,512]{1,0:T(8,128)}, f32[128,512]{1,0:T(8,128)}, f32[240,512]{1,0:T(8,128)}, f32[512,512]{1,0:T(8,128)}) custom-call(f32[512,512]{1,0:T(8,128)} %own_ref), custom_call_target="tpu_custom_call" | custom-call | flops 1000000000 | bytes 1048576 | tf_op jit(solution)/shard_map/pallas_call | solution.py:464
  64.8 0.5 collective-permute-start
  65.3 2.6 %collective-permute-start.3 = (f32[144,512]{1,0:T(8,128)}, f32[144,512]{1,0:T(8,128)S(1)}, u32[]{:S(2)}, u32[]{:S(2)}) collective-permute-start(f32[144,512]{1,0:T(8,128)} %get-tuple-element.76), channel_id=1, source_target_pairs={{0,2},{1,3},{2,0},{3,1},{4,6},{5,7},{6,4},{7,5},{8,10},{9,11},{10,... | collective-permute-start | bytes 884744 | tf_op jit(solution)/shard_map/ppermute | solution.py:489
  68.0 2.7 %collective-permute-start.1 = (f32[240,512]{1,0:T(8,128)}, f32[240,512]{1,0:T(8,128)S(1)}, u32[]{:S(2)}, u32[]{:S(2)}) collective-permute-start(f32[240,512]{1,0:T(8,128)} %get-tuple-element.74), channel_id=1, source_target_pairs={{0,2},{1,3},{2,0},{3,1},{4,6},{5,7},{6,4},{7,5},{8,10},{9,11},{10,... | collective-permute-start | bytes 1474568 | tf_op jit(solution)/shard_map/ppermute | solution.py:489
  70.7 2.2 %copy-done = f32[2048,512]{1,0:T(8,128)S(1)} copy-done((f32[2048,512]{1,0:T(8,128)S(1)}, f32[2048,512]{1,0:T(8,128)}, u32[]{:S(2)}) %copy-start) | copy-done | bytes 4194328
  72.9 1.2 copy-done.1
  74.1 0.9 copy-done.3
  75.0 3.9 %shard_map.83 = (f32[512,384]{1,0:T(8,128)S(1)}, f32[512,256]{1,0:T(8,128)S(1)}, bf16[1024,768]{1,0:T(8,128)(2,1)S(1)}, bf16[1024,512]{1,0:T(8,128)(2,1)S(1)}, s32[3,128]{1,0:T(4,128)S(1)}) custom-call(s32[7]{0:T(128)S(1)} %stack.31.index_ref, f32[512,512]{1,0:T(8,128)S(1)} %copy-done.1, f32[512,512]{1,0:T(8,128)S(1)} %collective-permute-done.beside_ref, ...), custom_call_target="tpu_custom_call" | custom-call | flops 3000000000 | bytes 1048576 | tf_op jit(solution)/shard_map/pallas_call | solution.py:464
  79.0 2.6 %collective-permute-done.2.refs_0_ = f32[128,512]{1,0:T(8,128)S(1)} collective-permute-done((f32[128,512]{1,0:T(8,128)}, f32[128,512]{1,0:T(8,128)S(1)}, u32[]{:S(2)}, u32[]{:S(2)}) %collective-permute-start.2) | collective-permute-done | bytes 262176 | tf_op jit(solution)/shard_map/ppermute | solution.py:489
  81.6 0.5 collective-permute-start.4
  82.7 0.8 collective-permute-done.4.refs_1_
  83.5 1.5 %shard_map.84 = (f32[272,384]{1,0:T(8,128)S(1)}, f32[272,256]{1,0:T(8,128)S(1)}, f32[16,384]{1,0:T(8,128)S(1)}) custom-call(f32[128,512]{1,0:T(8,128)S(1)} %collective-permute-done.2.refs_0_, f32[128,512]{1,0:T(8,128)S(1)} %collective-permute-done.4.refs_1_, f32[144,512]{1,0:T(8,128)S(1)} %collective-permute-done.3.refs_2_, ...), custom_call_target="tpu_custom_call" | custom-call | flops 500000000 | bytes 1048576 | tf_op jit(solution)/shard_map/pallas_call | solution.py:464
  85.0 4.0 %collective-permute-start.6 = (f32[16,384]{1,0:T(8,128)S(1)}, f32[16,384]{1,0:T(8,128)S(1)}, u32[]{:S(2)}, u32[]{:S(2)}) collective-permute-start(f32[16,384]{1,0:T(8,128)S(1)} %get-tuple-element.88), channel_id=1, source_target_pairs={{0,4},{4,8},{8,12},{12,16},{16,20},{20,24},{24,28},{1,5},{5,9},{9,... | collective-permute-start | bytes 73736 | tf_op jit(solution)/shard_map/ppermute | solution.py:549
  89.0 2.8 %shard_map.85 = (f32[256,128]{1,0:T(8,128)S(1)}, f32[256,128]{1,0:T(8,128)S(1)}, f32[256,128]{1,0:T(8,128)S(1)}, f32[256,128]{1,0:T(8,128)S(1)}, f32[256,128]{1,...) custom-call(f32[272,384]{1,0:T(8,128)S(1)} %get-tuple-element.86.raw_ref.refs_4_,, ...), custom_call_target="tpu_custom_call" | custom-call | flops 500000000 | bytes 1048576 | tf_op jit(solution)/shard_map/pallas_call | solution.py:464
  91.9 0.7 shard_map.89.weight_ref.refs_4_.refs_1_
  93.1 0.7 collective-permute-done.7.refs_0_.refs_1_
  93.8 3.2 %shard_map.87 = (f32[256,128]{1,0:T(8,128)S(1)}, f32[256,128]{1,0:T(8,128)S(1)}, f32[256,128]{1,0:T(8,128)S(1)}, f32[256,128]{1,0:T(8,128)S(1)}, f32[256,128]{1,...) custom-call(f32[240,512]{1,0:T(8,128)S(1)} %collective-permute-done.7.refs_0_.ref, ...), custom_call_target="tpu_custom_call" | custom-call | flops 5000000000 | bytes 1048576 | tf_op jit(solution)/shard_map/pallas_call | solution.py:464
  97.0 1.7 %collective-permute-start.8 = (f32[2,128,128]{2,1,0:T(8,128)S(1)}, f32[2,128,128]{2,1,0:T(8,128)S(1)}, u32[]{:S(2)}, u32[]{:S(2)}) collective-permute-start(f32[2,128,128]{2,1,0:T(8,128)S(1)} %get-tuple-element.92.own_ref), channel_id=1, source_target_pairs={{0,4},{4,0},{8,12},{12,8},{16,20},{20,16},{24,28},{28,24},{1,5},{5... | collective-permute-start | bytes 393224 | tf_op jit(solution)/shard_map/ppermute | solution.py:588
  98.7 1.6 %collective-permute-start.10 = (f32[2,128,128]{2,1,0:T(8,128)S(1)}, f32[2,128,128]{2,1,0:T(8,128)S(1)}, u32[]{:S(2)}, u32[]{:S(2)}) collective-permute-start(f32[2,128,128]{2,1,0:T(8,128)S(1)} %get-tuple-element.92.own_ref), channel_id=1, source_target_pairs={{0,12},{4,8},{8,4},{12,0},{16,28},{20,24},{24,20},{28,16},{1,13},{... | collective-permute-start | bytes 393224 | tf_op jit(solution)/shard_map/ppermute | solution.py:588
  100.6 2.4 %shard_map.88 = (f32[512,128]{1,0:T(8,128)S(1)}, f32[512,128]{1,0:T(8,128)S(1)}, f32[512,128]{1,0:T(8,128)S(1)}) custom-call(f32[240,512]{1,0:T(8,128)S(1)} %collective-permute-done.1.refs_0_, f32[240,512]{1,0:T(8,128)S(1)} %collective-permute-done.7.refs_0_.refs_1_, f32[512,256]{1,0:T(8,128)S(1)} %get-tuple-element.83.refs_5_.refs_2_, ...), custom_call_target="tpu_custom_call" | custom-call | flops 5000000000 | bytes 1048576 | tf_op jit(solution)/shard_map/pallas_call | solution.py:464
  103.0 1.8 %collective-permute-done.8.one_ref = f32[2,128,128]{2,1,0:T(8,128)S(1)} collective-permute-done((f32[2,128,128]{2,1,0:T(8,128)S(1)}, f32[2,128,128]{2,1,0:T(8,128)S(1)}, u32[]{:S(2)}, u32[]{:S(2)}) %collective-permute-start.8) | collective-permute-done | bytes 131104 | tf_op jit(solution)/shard_map/ppermute | solution.py:588
  104.8 1.2 collective-permute-done.10.three_ref
  106.0 0.7 collective-permute-done.9.two_ref
  107.2 2.8 %collective-permute-start.11 = (f32[128,128]{1,0:T(8,128)S(1)}, f32[128,128]{1,0:T(8,128)S(1)}, u32[]{:S(2)}, u32[]{:S(2)}) collective-permute-start(f32[128,128]{1,0:T(8,128)S(1)} %get-tuple-element.120), channel_id=1, source_target_pairs={{0,16},{4,20},{8,24},{12,28},{16,0},{20,4},{24,8},{28,12},{1,17},{... | collective-permute-start | bytes 196616 | tf_op jit(solution)/shard_map/ppermute | solution.py:607
  110.3 2.0 %collective-permute-done.11.refs_1_ = f32[128,128]{1,0:T(8,128)S(1)} collective-permute-done((f32[128,128]{1,0:T(8,128)S(1)}, f32[128,128]{1,0:T(8,128)S(1)}, u32[]{:S(2)}, u32[]{:S(2)}) %collective-permute-start.11) | collective-permute-done | bytes 65568 | tf_op jit(solution)/shard_map/ppermute | solution.py:607
  112.8 1.7 %collective-permute-start.14 = (f32[128,128]{1,0:T(8,128)S(1)}, f32[128,128]{1,0:T(8,128)S(1)}, u32[]{:S(2)}, u32[]{:S(2)}) collective-permute-start(f32[128,128]{1,0:T(8,128)S(1)} %get-tuple-element.124), channel_id=1, source_target_pairs={{0,2},{1,3},{2,0},{3,1},{4,6},{5,7},{6,4},{7,5},{8,10},{9,11},{10,... | collective-permute-start | bytes 196616 | tf_op jit(solution)/shard_map/ppermute | solution.py:489
  114.9 1.7 %collective-permute-start.13 = (f32[256,128]{1,0:T(8,128)S(1)}, f32[256,128]{1,0:T(8,128)S(1)}, u32[]{:S(2)}, u32[]{:S(2)}) collective-permute-start(f32[256,128]{1,0:T(8,128)S(1)} %get-tuple-element.123), channel_id=1, source_target_pairs={{0,2},{1,3},{2,0},{3,1},{4,6},{5,7},{6,4},{7,5},{8,10},{9,11},{10,... | collective-permute-start | bytes 393224 | tf_op jit(solution)/shard_map/ppermute | solution.py:489
  116.5 0.6 shard_map.93
  117.3 2.1 %collective-permute-done.15.refs_2_ = f32[128,128]{1,0:T(8,128)S(1)} collective-permute-done((f32[128,128]{1,0:T(8,128)S(1)}, f32[128,128]{1,0:T(8,128)S(1)}, u32[]{:S(2)}, u32[]{:S(2)}) %collective-permute-start.15) | collective-permute-done | bytes 65568 | tf_op jit(solution)/shard_map/ppermute | solution.py:489
  120.0 0.7 collective-permute-done.16.refs_1_
  121.7 0.8 shard_map.95
  122.9 1.1 shard_map.96
  (36 shorter events, 4.7 us)
Async XLA Ops:
  64.8 3.2 %collective-permute-start = (f32[512,512]{1,0:T(8,128)}, f32[512,512]{1,0:T(8,128)S(1)}, u32[]{:S(2)}, u32[]{:S(2)}) collective-permute-start(f32[512,512]{1,0:T(8,128)} %get-tuple-element.73), channel_id=1, source_target_pairs={{0,1},{1,0},{2,3},{3,2},{4,5},{5,4},{6,7},{7,6},{8,9},{9,8},{10,11... | collective-permute-start | bytes 3145736 | tf_op jit(solution)/shard_map/ppermute | solution.py:483
  65.3 16.3 %collective-permute-start.3 = (f32[144,512]{1,0:T(8,128)}, f32[144,512]{1,0:T(8,128)S(1)}, u32[]{:S(2)}, u32[]{:S(2)}) collective-permute-start(f32[144,512]{1,0:T(8,128)} %get-tuple-element.76), channel_id=1, source_target_pairs={{0,2},{1,3},{2,0},{3,1},{4,6},{5,7},{6,4},{7,5},{8,10},{9,11},{10,... | collective-permute-start | bytes 884744 | tf_op jit(solution)/shard_map/ppermute | solution.py:489
  67.9 13.7 %collective-permute-start.2 = (f32[128,512]{1,0:T(8,128)}, f32[128,512]{1,0:T(8,128)S(1)}, u32[]{:S(2)}, u32[]{:S(2)}) collective-permute-start(f32[128,512]{1,0:T(8,128)} %get-tuple-element.75), channel_id=1, source_target_pairs={{0,2},{1,3},{2,0},{3,1},{4,6},{5,7},{6,4},{7,5},{8,10},{9,11},{10,... | collective-permute-start | bytes 786440 | tf_op jit(solution)/shard_map/ppermute | solution.py:489
  68.0 23.9 %collective-permute-start.1 = (f32[240,512]{1,0:T(8,128)}, f32[240,512]{1,0:T(8,128)S(1)}, u32[]{:S(2)}, u32[]{:S(2)}) collective-permute-start(f32[240,512]{1,0:T(8,128)} %get-tuple-element.74), channel_id=1, source_target_pairs={{0,2},{1,3},{2,0},{3,1},{4,6},{5,7},{6,4},{7,5},{8,10},{9,11},{10,... | collective-permute-start | bytes 1474568 | tf_op jit(solution)/shard_map/ppermute | solution.py:489
  70.7 2.2 %copy-start = (f32[2048,512]{1,0:T(8,128)S(1)}, f32[2048,512]{1,0:T(8,128)}, u32[]{:S(2)}) copy-start(f32[2048,512]{1,0:T(8,128)} %proj_ref.1) | copy-start | bytes 12582916
  72.8 1.2 copy-start.1
  74.1 0.9 copy-start.3
  78.9 10.1 %copy-start.4 = (f32[4,384]{1,0:T(4,128)S(1)}, f32[4,384]{1,0:T(4,128)}, u32[]{:S(2)}) copy-start(f32[4,384]{1,0:T(4,128)} %refs_6_.3) | copy-start | bytes 18436
  78.9 10.1 %copy-start.5 = (s32[512]{0:T(512)S(1)}, s32[512]{0:T(512)}, u32[]{:S(2)}) copy-start(s32[512]{0:T(512)} %param.13) | copy-start | bytes 6148
  78.9 13.0 %copy-start.2 = (f32[512,512]{1,0:T(8,128)S(1)}, f32[512,512]{1,0:T(8,128)}, u32[]{:S(2)}) copy-start(f32[512,512]{1,0:T(8,128)} %weight_ref.1) | copy-start | bytes 3145732
  81.6 2.0 %collective-permute-start.5 = (f32[144,512]{1,0:T(8,128)S(1)}, f32[144,512]{1,0:T(8,128)S(1)}, u32[]{:S(2)}, u32[]{:S(2)}) collective-permute-start(f32[144,512]{1,0:T(8,128)S(1)} %collective-permute-done.3.refs_2_), channel_id=1, source_target_pairs={{0,1},{1,0},{2,3},{3,2},{4,5},{5,4},{6,7},{7,6},{8,9},{9,8},{10,11... | collective-permute-start | bytes 884744 | tf_op jit(solution)/shard_map/ppermute | solution.py:483
  81.6 2.0 %collective-permute-start.4 = (f32[128,512]{1,0:T(8,128)S(1)}, f32[128,512]{1,0:T(8,128)S(1)}, u32[]{:S(2)}, u32[]{:S(2)}) collective-permute-start(f32[128,512]{1,0:T(8,128)S(1)} %collective-permute-done.2.refs_0_), channel_id=1, source_target_pairs={{0,1},{1,0},{2,3},{3,2},{4,5},{5,4},{6,7},{7,6},{8,9},{9,8},{10,11... | collective-permute-start | bytes 786440 | tf_op jit(solution)/shard_map/ppermute | solution.py:483
  85.0 6.8 %collective-permute-start.6 = (f32[16,384]{1,0:T(8,128)S(1)}, f32[16,384]{1,0:T(8,128)S(1)}, u32[]{:S(2)}, u32[]{:S(2)}) collective-permute-start(f32[16,384]{1,0:T(8,128)S(1)} %get-tuple-element.88), channel_id=1, source_target_pairs={{0,4},{4,8},{8,12},{12,16},{16,20},{20,24},{24,28},{1,5},{5,9},{9,... | collective-permute-start | bytes 73736 | tf_op jit(solution)/shard_map/ppermute | solution.py:549
  91.8 1.9 %collective-permute-start.7 = (f32[240,512]{1,0:T(8,128)S(1)}, f32[240,512]{1,0:T(8,128)S(1)}, u32[]{:S(2)}, u32[]{:S(2)}) collective-permute-start(f32[240,512]{1,0:T(8,128)S(1)} %collective-permute-done.1.refs_0_), channel_id=1, source_target_pairs={{0,1},{1,0},{2,3},{3,2},{4,5},{5,4},{6,7},{7,6},{8,9},{9,8},{10,11... | collective-permute-start | bytes 1474568 | tf_op jit(solution)/shard_map/ppermute | solution.py:483
  97.0 7.8 %collective-permute-start.8 = (f32[2,128,128]{2,1,0:T(8,128)S(1)}, f32[2,128,128]{2,1,0:T(8,128)S(1)}, u32[]{:S(2)}, u32[]{:S(2)}) collective-permute-start(f32[2,128,128]{2,1,0:T(8,128)S(1)} %get-tuple-element.92.own_ref), channel_id=1, source_target_pairs={{0,4},{4,0},{8,12},{12,8},{16,20},{20,16},{24,28},{28,24},{1,5},{5... | collective-permute-start | bytes 393224 | tf_op jit(solution)/shard_map/ppermute | solution.py:588
  98.7 7.3 %collective-permute-start.10 = (f32[2,128,128]{2,1,0:T(8,128)S(1)}, f32[2,128,128]{2,1,0:T(8,128)S(1)}, u32[]{:S(2)}, u32[]{:S(2)}) collective-permute-start(f32[2,128,128]{2,1,0:T(8,128)S(1)} %get-tuple-element.92.own_ref), channel_id=1, source_target_pairs={{0,12},{4,8},{8,4},{12,0},{16,28},{20,24},{24,20},{28,16},{1,13},{... | collective-permute-start | bytes 393224 | tf_op jit(solution)/shard_map/ppermute | solution.py:588
  100.3 6.4 %collective-permute-start.9 = (f32[2,128,128]{2,1,0:T(8,128)S(1)}, f32[2,128,128]{2,1,0:T(8,128)S(1)}, u32[]{:S(2)}, u32[]{:S(2)}) collective-permute-start(f32[2,128,128]{2,1,0:T(8,128)S(1)} %get-tuple-element.92.own_ref), channel_id=1, source_target_pairs={{0,8},{4,12},{8,0},{12,4},{16,24},{20,28},{24,16},{28,20},{1,9},{5... | collective-permute-start | bytes 393224 | tf_op jit(solution)/shard_map/ppermute | solution.py:588
  103.0 9.4 %copy-start.6 = (f32[128]{0:T(128)S(1)}, f32[128]{0:T(128)}, u32[]{:S(2)}) copy-start(f32[128]{0:T(128)} %param.14) | copy-start | bytes 1540
  107.2 5.2 %collective-permute-start.11 = (f32[128,128]{1,0:T(8,128)S(1)}, f32[128,128]{1,0:T(8,128)S(1)}, u32[]{:S(2)}, u32[]{:S(2)}) collective-permute-start(f32[128,128]{1,0:T(8,128)S(1)} %get-tuple-element.120), channel_id=1, source_target_pairs={{0,16},{4,20},{8,24},{12,28},{16,0},{20,4},{24,8},{28,12},{1,17},{... | collective-permute-start | bytes 196616 | tf_op jit(solution)/shard_map/ppermute | solution.py:607
  112.7 2.2 %collective-permute-start.12 = (f32[512,128]{1,0:T(8,128)S(1)}, f32[512,128]{1,0:T(8,128)S(1)}, u32[]{:S(2)}, u32[]{:S(2)}) collective-permute-start(f32[512,128]{1,0:T(8,128)S(1)} %get-tuple-element.122.own_ref), channel_id=1, source_target_pairs={{0,1},{1,0},{2,3},{3,2},{4,5},{5,4},{6,7},{7,6},{8,9},{9,8},{10,11... | collective-permute-start | bytes 786440 | tf_op jit(solution)/shard_map/ppermute | solution.py:483
  112.8 4.6 %collective-permute-start.14 = (f32[128,128]{1,0:T(8,128)S(1)}, f32[128,128]{1,0:T(8,128)S(1)}, u32[]{:S(2)}, u32[]{:S(2)}) collective-permute-start(f32[128,128]{1,0:T(8,128)S(1)} %get-tuple-element.124), channel_id=1, source_target_pairs={{0,2},{1,3},{2,0},{3,1},{4,6},{5,7},{6,4},{7,5},{8,10},{9,11},{10,... | collective-permute-start | bytes 196616 | tf_op jit(solution)/shard_map/ppermute | solution.py:489
  114.5 4.9 %collective-permute-start.15 = (f32[128,128]{1,0:T(8,128)S(1)}, f32[128,128]{1,0:T(8,128)S(1)}, u32[]{:S(2)}, u32[]{:S(2)}) collective-permute-start(f32[128,128]{1,0:T(8,128)S(1)} %get-tuple-element.125), channel_id=1, source_target_pairs={{0,2},{1,3},{2,0},{3,1},{4,6},{5,7},{6,4},{7,5},{8,10},{9,11},{10,... | collective-permute-start | bytes 196616 | tf_op jit(solution)/shard_map/ppermute | solution.py:489
  114.9 6.6 %collective-permute-start.13 = (f32[256,128]{1,0:T(8,128)S(1)}, f32[256,128]{1,0:T(8,128)S(1)}, u32[]{:S(2)}, u32[]{:S(2)}) collective-permute-start(f32[256,128]{1,0:T(8,128)S(1)} %get-tuple-element.123), channel_id=1, source_target_pairs={{0,2},{1,3},{2,0},{3,1},{4,6},{5,7},{6,4},{7,5},{8,10},{9,11},{10,... | collective-permute-start | bytes 393224 | tf_op jit(solution)/shard_map/ppermute | solution.py:489
  119.5 1.3 %collective-permute-start.16 = (f32[128,128]{1,0:T(8,128)S(1)}, f32[128,128]{1,0:T(8,128)S(1)}, u32[]{:S(2)}, u32[]{:S(2)}) collective-permute-start(f32[128,128]{1,0:T(8,128)S(1)} %collective-permute-done.14.refs_0_), channel_id=1, source_target_pairs={{0,1},{1,0},{2,3},{3,2},{4,5},{5,4},{6,7},{7,6},{8,9},{9,8},{10,11... | collective-permute-start | bytes 196616 | tf_op jit(solution)/shard_map/ppermute | solution.py:483
  119.5 1.4 %collective-permute-start.17 = (f32[128,128]{1,0:T(8,128)S(1)}, f32[128,128]{1,0:T(8,128)S(1)}, u32[]{:S(2)}, u32[]{:S(2)}) collective-permute-start(f32[128,128]{1,0:T(8,128)S(1)} %collective-permute-done.15.refs_2_), channel_id=1, source_target_pairs={{0,1},{1,0},{2,3},{3,2},{4,5},{5,4},{6,7},{7,6},{8,9},{9,8},{10,11... | collective-permute-start | bytes 196616 | tf_op jit(solution)/shard_map/ppermute | solution.py:483
  121.5 1.3 %collective-permute-start.18 = (f32[256,128]{1,0:T(8,128)S(1)}, f32[256,128]{1,0:T(8,128)S(1)}, u32[]{:S(2)}, u32[]{:S(2)}) collective-permute-start(f32[256,128]{1,0:T(8,128)S(1)} %collective-permute-done.13.refs_0_), channel_id=1, source_target_pairs={{0,1},{1,0},{2,3},{3,2},{4,5},{5,4},{6,7},{7,6},{8,9},{9,8},{10,11... | collective-permute-start | bytes 393224 | tf_op jit(solution)/shard_map/ppermute | solution.py:483

commit v17 on v14

--- a/solution.py
+++ b/solution.py
@@ -166,7 +166,7 @@
     row = lax.broadcasted_iota(jnp.int32, (CHUNK, CHUNK), 0)
     col = lax.broadcasted_iota(jnp.int32, (CHUNK, CHUNK), 1)
     lower = row >= col
-    tri = jnp.where(lower, 1.0, 0.0).astype(F32)
+    tri = jnp.where(lower, 1.0, 0.0).astype(BF16)
     eye = jnp.where(row == col, 1.0, 0.0).astype(F32)
     keys, values, betas, grids, gammas, tails = [], [], [], [], [], []
     for part in range(chunks):
@@ -182,15 +182,22 @@
         spot = first_chunk + part
         docs = jnp.broadcast_to(doc_ref[spot : spot + 1, :].astype(F32), (CHUNK, CHUNK))
         docs = jnp.transpose(docs)
-        steps = jnp.where(col == 1, -rate * plus, jnp.where(col == 0, docs, 0.0))
-        sums = jnp.dot(tri, steps, precision=lax.Precision.HIGHEST, preferred_element_type=F32)
+        smooth = -rate * plus[:, 1:2]
+        high = smooth.astype(BF16).astype(F32)
+        middle = (smooth - high).astype(BF16).astype(F32)
+        rest = smooth - high - middle
+        steps = jnp.where(col == 0, docs, jnp.where(col == 1, high, jnp.where(col == 2, middle, rest)))
+        steps = jnp.where(col < 4, steps, 0.0).astype(BF16)
+        sums = jnp.dot(tri, steps, preferred_element_type=F32)
         across = jnp.transpose(sums)
-        smooth, count = sums[:, 1:2], sums[:, 0:1]
+        across = jnp.concatenate([across[0:1, :], across[1:2, :] + (across[2:3, :] + across[3:4, :])], axis=0)
+        count = sums[:, 0:1]
+        smooth = sums[:, 1:2] + (sums[:, 2:3] + sums[:, 3:4])
         span = (smooth - across[1:2, :]) - 20.0 * (count - across[0:1, :])
         grids.append(jnp.exp(jnp.where(lower, span, -1e30)))
         gammas.append(jnp.exp(smooth - 20.0 * count))
-        last = sums[CHUNK - 1 : CHUNK, :]
-        tails.append(jnp.exp((last[:, 1:2] - smooth) - 20.0 * (last[:, 0:1] - count)))
+        end = slice(CHUNK - 1, CHUNK)
+        tails.append(jnp.exp((smooth[end] - smooth) - 20.0 * (count[end] - count)))
         key_ref[rows, :] = keys[part]
         grid_ref[rows, :] = grids[part]
         gamma_ref[rows, :] = jnp.broadcast_to(gammas[part], (CHUNK, width))

time: 60.4 us -> 60.4 us (level)
  no operation moved by 1% of the time
where the time goes in v17:
time: 60.4 us; the launch traced here: 60 us
  starting transfers between devices  20.5 us (34%)
  Pallas kernels  18.9 us (31%)
  waiting for transfers between devices  12.1 us (20%)
  local copies, waits for them, and re-layouts  7.44 us (12%)
  between operations  1.02 us (2%)
    pallas_call x14, Pallas kernels, vmem_call(): pl.pallas_call(kernel, out_shape=outs, in_specs=[free if spot in any_in e...  18.9 us
    ppermute x6, starting transfers between devices, to_chips(): lax.ppermute(value, 'head', [(source, (source + 2 * step) % count) for so...  8.47 us
    unnamed x14, local copies, waits for them, and re-layouts  4.34 us
    ppermute x1, starting transfers between devices, shards(): lax.ppermute(rim, 'ctx', [(source, source + 1) for source in range(blocks...  3.99 us
    ppermute x3, waiting for transfers between devices, shards(): lax.ppermute(pair, 'ctx', [(source, source ^ mask << bit) for source in r...  3.75 us
    ppermute x6, waiting for transfers between devices, to_chips(): lax.ppermute(value, 'head', [(source, (source + 2 * step) % count) for so...  3.58 us
    ppermute x3, starting transfers between devices, shards(): lax.ppermute(pair, 'ctx', [(source, source ^ mask << bit) for source in r...  3.55 us
    ppermute x1, starting transfers between devices, shards(): lax.ppermute(pair if carry else pair[1], 'ctx', [(source, source ^ reach)...  2.79 us
  transfers between devices with their start and end apart: 19, of which 14 were waited for; matrix products, arithmetic and copies ran while one was open for 5% of the time, Pallas kernels for 23%

profile of v17, /device:TPU:0, one launch (start us, length us, event | category | flops | bytes accessed | tf_op | source)
XLA Modules:
  0.0 60.0 jit_solution(13440270260095781228)
XLA Ops:
  0.5 1.0 %slice.11 = f32[144,512]{1,0:T(8,128)S(1)} slice(f32[512,512]{1,0:T(8,128)} %own_ref.1), slice={[368:512], [0:512]} | slice | bytes 589824 | tf_op jit(solution)/shard_map/slice | solution.py:512
  1.4 2.6 %collective-permute-start.3 = (f32[144,512]{1,0:T(8,128)S(1)}, f32[144,512]{1,0:T(8,128)S(1)}, u32[]{:S(2)}, u32[]{:S(2)}) collective-permute-start(f32[144,512]{1,0:T(8,128)S(1)} %slice.11), channel_id=1, source_target_pairs={{0,2},{1,3},{2,0},{3,1},{4,6},{5,7},{6,4},{7,5},{8,10},{9,11},{10,... | collective-permute-start | bytes 884744 | tf_op jit(solution)/shard_map/ppermute | solution.py:483
  4.0 1.0 %slice.10 = f32[128,512]{1,0:T(8,128)S(1)} slice(f32[512,512]{1,0:T(8,128)} %own_ref.1), slice={[240:368], [0:512]} | slice | bytes 524288 | tf_op jit(solution)/shard_map/slice | solution.py:512
  5.2 1.1 %slice.9 = f32[240,512]{1,0:T(8,128)S(1)} slice(f32[512,512]{1,0:T(8,128)} %own_ref.1), slice={[0:240], [0:512]} | slice | bytes 983040 | tf_op jit(solution)/shard_map/slice | solution.py:515
  6.2 2.1 %collective-permute-start.1 = (f32[240,512]{1,0:T(8,128)S(1)}, f32[240,512]{1,0:T(8,128)S(1)}, u32[]{:S(2)}, u32[]{:S(2)}) collective-permute-start(f32[240,512]{1,0:T(8,128)S(1)} %slice.9), channel_id=1, source_target_pairs={{0,2},{1,3},{2,0},{3,1},{4,6},{5,7},{6,4},{7,5},{8,10},{9,11},{10,... | collective-permute-start | bytes 1474568 | tf_op jit(solution)/shard_map/ppermute | solution.py:483
  8.3 1.2 %copy-done = f32[512,512]{1,0:T(8,128)S(1)} copy-done((f32[512,512]{1,0:T(8,128)S(1)}, f32[512,512]{1,0:T(8,128)}, u32[]{:S(2)}) %copy-start) | copy-done | bytes 1048600
  9.5 2.2 %copy-done.1 = f32[2048,512]{1,0:T(8,128)S(1)} copy-done((f32[2048,512]{1,0:T(8,128)S(1)}, f32[2048,512]{1,0:T(8,128)}, u32[]{:S(2)}) %copy-start.1) | copy-done | bytes 4194328
  11.7 0.9 %copy-done.3 = f32[2048,9]{0,1:T(8,128)S(1)} copy-done((f32[2048,9]{0,1:T(8,128)S(1)}, f32[2048,9]{0,1:T(8,128)}, u32[]{:S(2)}) %copy-start.3) | copy-done | bytes 73752
  12.6 4.0 %shard_map.82 = (f32[512,384]{1,0:T(8,128)S(1)}, f32[512,256]{1,0:T(8,128)S(1)}, bf16[1024,768]{1,0:T(8,128)(2,1)S(1)}, bf16[1024,512]{1,0:T(8,128)(2,1)S(1)}, s32[3,128]{1,0:T(4,128)S(1)}) custom-call(s32[7]{0:T(128)S(1)} %stack.31.index_ref, f32[512,512]{1,0:T(8,128)S(1)} %copy-done, f32[512,512]{1,0:T(8,128)S(1)} %collective-permute-done.beside_ref, ...), custom_call_target="tpu_custom_call" | custom-call | flops 3000000000 | bytes 1048576 | tf_op jit(solution)/shard_map/pallas_call | solution.py:458
  16.6 0.9 %collective-permute-done.2.refs_0_ = f32[128,512]{1,0:T(8,128)S(1)} collective-permute-done((f32[128,512]{1,0:T(8,128)S(1)}, f32[128,512]{1,0:T(8,128)S(1)}, u32[]{:S(2)}, u32[]{:S(2)}) %collective-permute-start.2) | collective-permute-done | bytes 262176 | tf_op jit(solution)/shard_map/ppermute | solution.py:483
  18.7 0.8 %collective-permute-done.4.refs_1_ = f32[128,512]{1,0:T(8,128)S(1)} collective-permute-done((f32[128,512]{1,0:T(8,128)S(1)}, f32[128,512]{1,0:T(8,128)S(1)}, u32[]{:S(2)}, u32[]{:S(2)}) %collective-permute-start.4) | collective-permute-done | bytes 262176 | tf_op jit(solution)/shard_map/ppermute | solution.py:477
  19.5 1.5 %shard_map.83 = (f32[272,384]{1,0:T(8,128)S(1)}, f32[272,256]{1,0:T(8,128)S(1)}, f32[16,384]{1,0:T(8,128)S(1)}) custom-call(f32[128,512]{1,0:T(8,128)S(1)} %collective-permute-done.2.refs_0_, f32[128,512]{1,0:T(8,128)S(1)} %collective-permute-done.4.refs_1_, f32[144,512]{1,0:T(8,128)S(1)} %collective-permute-done.3.refs_2_, ...), custom_call_target="tpu_custom_call" | custom-call | flops 500000000 | bytes 1048576 | tf_op jit(solution)/shard_map/pallas_call | solution.py:458
  21.0 4.0 %collective-permute-start.6 = (f32[16,384]{1,0:T(8,128)S(1)}, f32[16,384]{1,0:T(8,128)S(1)}, u32[]{:S(2)}, u32[]{:S(2)}) collective-permute-start(f32[16,384]{1,0:T(8,128)S(1)} %get-tuple-element.76), channel_id=1, source_target_pairs={{0,4},{4,8},{8,12},{12,16},{16,20},{20,24},{24,28},{1,5},{5,9},{9,... | collective-permute-start | bytes 73736 | tf_op jit(solution)/shard_map/ppermute | solution.py:536
  25.0 2.7 %shard_map.84 = (f32[256,128]{1,0:T(8,128)S(1)}, f32[256,128]{1,0:T(8,128)S(1)}, f32[256,128]{1,0:T(8,128)S(1)}, f32[256,128]{1,0:T(8,128)S(1)}, f32[256,128]{1,...) custom-call(f32[272,384]{1,0:T(8,128)S(1)} %get-tuple-element.74.raw_ref.refs_4_,, ...), custom_call_target="tpu_custom_call" | custom-call | flops 500000000 | bytes 1048576 | tf_op jit(solution)/shard_map/pallas_call | solution.py:458
  27.9 0.7 %shard_map.88.weight_ref.refs_4_.refs_1_ = bf16[512,1024]{1,0:T(8,128)(2,1)S(1)} custom-call(s32[7]{0:T(128)S(1)} %stack.31.index_ref, f32[512,512]{1,0:T(8,128)S(1)} %copy-done.2), custom_call_target="tpu_custom_call" | custom-call | flops 1000000000 | bytes 1048576 | tf_op jit(solution)/shard_map/pallas_call | solution.py:458
  29.0 0.7 %collective-permute-done.7.refs_0_.refs_1_ = f32[240,512]{1,0:T(8,128)S(1)} collective-permute-done((f32[240,512]{1,0:T(8,128)S(1)}, f32[240,512]{1,0:T(8,128)S(1)}, u32[]{:S(2)}, u32[]{:S(2)}) %collective-permute-start.7) | collective-permute-done | bytes 491552 | tf_op jit(solution)/shard_map/ppermute | solution.py:477
  29.7 3.2 %shard_map.86 = (f32[256,128]{1,0:T(8,128)S(1)}, f32[256,128]{1,0:T(8,128)S(1)}, f32[256,128]{1,0:T(8,128)S(1)}, f32[256,128]{1,0:T(8,128)S(1)}, f32[256,128]{1,...) custom-call(f32[240,512]{1,0:T(8,128)S(1)} %collective-permute-done.7.refs_0_.ref, ...), custom_call_target="tpu_custom_call" | custom-call | flops 5000000000 | bytes 1048576 | tf_op jit(solution)/shard_map/pallas_call | solution.py:458
  32.9 1.8 %collective-permute-start.8 = (f32[2,128,128]{2,1,0:T(8,128)S(1)}, f32[2,128,128]{2,1,0:T(8,128)S(1)}, u32[]{:S(2)}, u32[]{:S(2)}) collective-permute-start(f32[2,128,128]{2,1,0:T(8,128)S(1)} %get-tuple-element.80.own_ref), channel_id=1, source_target_pairs={{0,4},{4,0},{8,12},{12,8},{16,20},{20,16},{24,28},{28,24},{1,5},{5... | collective-permute-start | bytes 393224 | tf_op jit(solution)/shard_map/ppermute | solution.py:575
  34.7 1.6 %collective-permute-start.10 = (f32[2,128,128]{2,1,0:T(8,128)S(1)}, f32[2,128,128]{2,1,0:T(8,128)S(1)}, u32[]{:S(2)}, u32[]{:S(2)}) collective-permute-start(f32[2,128,128]{2,1,0:T(8,128)S(1)} %get-tuple-element.80.own_ref), channel_id=1, source_target_pairs={{0,12},{4,8},{8,4},{12,0},{16,28},{20,24},{24,20},{28,16},{1,13},{... | collective-permute-start | bytes 393224 | tf_op jit(solution)/shard_map/ppermute | solution.py:575
  36.5 2.4 %shard_map.87 = (f32[512,128]{1,0:T(8,128)S(1)}, f32[512,128]{1,0:T(8,128)S(1)}, f32[512,128]{1,0:T(8,128)S(1)}) custom-call(f32[240,512]{1,0:T(8,128)S(1)} %collective-permute-done.1.refs_0_, f32[240,512]{1,0:T(8,128)S(1)} %collective-permute-done.7.refs_0_.refs_1_, f32[512,256]{1,0:T(8,128)S(1)} %get-tuple-element.71.refs_5_.refs_2_, ...), custom_call_target="tpu_custom_call" | custom-call | flops 5000000000 | bytes 1048576 | tf_op jit(solution)/shard_map/pallas_call | solution.py:458
  38.9 1.8 %collective-permute-done.8.one_ref = f32[2,128,128]{2,1,0:T(8,128)S(1)} collective-permute-done((f32[2,128,128]{2,1,0:T(8,128)S(1)}, f32[2,128,128]{2,1,0:T(8,128)S(1)}, u32[]{:S(2)}, u32[]{:S(2)}) %collective-permute-start.8) | collective-permute-done | bytes 131104 | tf_op jit(solution)/shard_map/ppermute | solution.py:575
  40.7 1.3 %collective-permute-done.10.three_ref = f32[2,128,128]{2,1,0:T(8,128)S(1)} collective-permute-done((f32[2,128,128]{2,1,0:T(8,128)S(1)}, f32[2,128,128]{2,1,0:T(8,128)S(1)}, u32[]{:S(2)}, u32[]{:S(2)}) %collective-permute-start.10) | collective-permute-done | bytes 131104 | tf_op jit(solution)/shard_map/ppermute | solution.py:575
  42.0 0.7 %collective-permute-done.9.two_ref = f32[2,128,128]{2,1,0:T(8,128)S(1)} collective-permute-done((f32[2,128,128]{2,1,0:T(8,128)S(1)}, f32[2,128,128]{2,1,0:T(8,128)S(1)}, u32[]{:S(2)}, u32[]{:S(2)}) %collective-permute-start.9) | collective-permute-done | bytes 131104 | tf_op jit(solution)/shard_map/ppermute | solution.py:575
  43.1 2.8 %collective-permute-start.11 = (f32[128,128]{1,0:T(8,128)S(1)}, f32[128,128]{1,0:T(8,128)S(1)}, u32[]{:S(2)}, u32[]{:S(2)}) collective-permute-start(f32[128,128]{1,0:T(8,128)S(1)} %get-tuple-element.108), channel_id=1, source_target_pairs={{0,16},{4,20},{8,24},{12,28},{16,0},{20,4},{24,8},{28,12},{1,17},{... | collective-permute-start | bytes 196616 | tf_op jit(solution)/shard_map/ppermute | solution.py:594
  46.3 2.0 %collective-permute-done.11.refs_1_ = f32[128,128]{1,0:T(8,128)S(1)} collective-permute-done((f32[128,128]{1,0:T(8,128)S(1)}, f32[128,128]{1,0:T(8,128)S(1)}, u32[]{:S(2)}, u32[]{:S(2)}) %collective-permute-start.11) | collective-permute-done | bytes 65568 | tf_op jit(solution)/shard_map/ppermute | solution.py:594
  48.7 1.7 %collective-permute-start.14 = (f32[128,128]{1,0:T(8,128)S(1)}, f32[128,128]{1,0:T(8,128)S(1)}, u32[]{:S(2)}, u32[]{:S(2)}) collective-permute-start(f32[128,128]{1,0:T(8,128)S(1)} %get-tuple-element.112), channel_id=1, source_target_pairs={{0,2},{1,3},{2,0},{3,1},{4,6},{5,7},{6,4},{7,5},{8,10},{9,11},{10,... | collective-permute-start | bytes 196616 | tf_op jit(solution)/shard_map/ppermute | solution.py:483
  50.8 1.7 %collective-permute-start.13 = (f32[256,128]{1,0:T(8,128)S(1)}, f32[256,128]{1,0:T(8,128)S(1)}, u32[]{:S(2)}, u32[]{:S(2)}) collective-permute-start(f32[256,128]{1,0:T(8,128)S(1)} %get-tuple-element.111), channel_id=1, source_target_pairs={{0,2},{1,3},{2,0},{3,1},{4,6},{5,7},{6,4},{7,5},{8,10},{9,11},{10,... | collective-permute-start | bytes 393224 | tf_op jit(solution)/shard_map/ppermute | solution.py:483
  52.5 0.6 shard_map.92
  53.3 2.1 %collective-permute-done.15.refs_2_ = f32[128,128]{1,0:T(8,128)S(1)} collective-permute-done((f32[128,128]{1,0:T(8,128)S(1)}, f32[128,128]{1,0:T(8,128)S(1)}, u32[]{:S(2)}, u32[]{:S(2)}) %collective-permute-start.15) | collective-permute-done | bytes 65568 | tf_op jit(solution)/shard_map/ppermute | solution.py:483
  55.9 0.7 %collective-permute-done.16.refs_1_ = f32[128,128]{1,0:T(8,128)S(1)} collective-permute-done((f32[128,128]{1,0:T(8,128)S(1)}, f32[128,128]{1,0:T(8,128)S(1)}, u32[]{:S(2)}, u32[]{:S(2)}) %collective-permute-start.16) | collective-permute-done | bytes 65568 | tf_op jit(solution)/shard_map/ppermute | solution.py:477
  57.6 0.8 %shard_map.94 = (f32[512,512]{1,0:T(8,128)}, f32[256,512]{1,0:T(8,128)S(1)}) custom-call(f32[256,128]{1,0:T(8,128)S(1)} %collective-permute-done.13.refs_0_, bf16[512,1024]{1,0:T(8,128)(2,1)S(1)} %shard_map.88.weight_ref.refs_4_.refs_1_, f32[256,512]{1,0:T(8,128)S(1)} %shard_map.93.refs_2_, f32[256,512]{1,0:T(8,128)S(1)} %get-tuple-element.122.refs_3_), custom_call_target="tpu_custom_call" | custom-call | flops 1000000000 | bytes 1048576 | tf_op jit(solution)/shard_map/pallas_call | solution.py:458
  58.8 1.1 %shard_map.95 = f32[512,512]{1,0:T(8,128)} custom-call(f32[256,128]{1,0:T(8,128)S(1)} %collective-permute-done.18.refs_0_, bf16[512,1024]{1,0:T(8,128)(2,1)S(1)} %shard_map.88.weight_ref.refs_4_.refs_1_, f32[256,512]{1,0:T(8,128)S(1)} %get-tuple-element.123.refs_2_, f32[512,512]{1,0:T(8,128)} %get-tuple-element.124.refs_3_), custom_call_target="tpu_custom_call", output_to_operand_aliasing={{}: (3, {})} | custom-call | flops 1000000000 | bytes 1048576 | tf_op jit(solution)/shard_map/pallas_call | solution.py:458
  (38 shorter events, 5.7 us)
Async XLA Ops:
  0.0 5.2 %collective-permute-start = (f32[512,512]{1,0:T(8,128)}, f32[512,512]{1,0:T(8,128)S(1)}, u32[]{:S(2)}, u32[]{:S(2)}) collective-permute-start(f32[512,512]{1,0:T(8,128)} %own_ref.1), channel_id=1, source_target_pairs={{0,1},{1,0},{2,3},{3,2},{4,5},{5,4},{6,7},{7,6},{8,9},{9,8},{10,11... | collective-permute-start | bytes 3145736 | tf_op jit(solution)/shard_map/ppermute | solution.py:477
  1.4 16.1 %collective-permute-start.3 = (f32[144,512]{1,0:T(8,128)S(1)}, f32[144,512]{1,0:T(8,128)S(1)}, u32[]{:S(2)}, u32[]{:S(2)}) collective-permute-start(f32[144,512]{1,0:T(8,128)S(1)} %slice.11), channel_id=1, source_target_pairs={{0,2},{1,3},{2,0},{3,1},{4,6},{5,7},{6,4},{7,5},{8,10},{9,11},{10,... | collective-permute-start | bytes 884744 | tf_op jit(solution)/shard_map/ppermute | solution.py:483
  5.0 12.5 %collective-permute-start.2 = (f32[128,512]{1,0:T(8,128)S(1)}, f32[128,512]{1,0:T(8,128)S(1)}, u32[]{:S(2)}, u32[]{:S(2)}) collective-permute-start(f32[128,512]{1,0:T(8,128)S(1)} %slice.10), channel_id=1, source_target_pairs={{0,2},{1,3},{2,0},{3,1},{4,6},{5,7},{6,4},{7,5},{8,10},{9,11},{10,... | collective-permute-start | bytes 786440 | tf_op jit(solution)/shard_map/ppermute | solution.py:483
  6.2 21.6 %collective-permute-start.1 = (f32[240,512]{1,0:T(8,128)S(1)}, f32[240,512]{1,0:T(8,128)S(1)}, u32[]{:S(2)}, u32[]{:S(2)}) collective-permute-start(f32[240,512]{1,0:T(8,128)S(1)} %slice.9), channel_id=1, source_target_pairs={{0,2},{1,3},{2,0},{3,1},{4,6},{5,7},{6,4},{7,5},{8,10},{9,11},{10,... | collective-permute-start | bytes 1474568 | tf_op jit(solution)/shard_map/ppermute | solution.py:483
  8.3 1.2 %copy-start = (f32[512,512]{1,0:T(8,128)S(1)}, f32[512,512]{1,0:T(8,128)}, u32[]{:S(2)}) copy-start(f32[512,512]{1,0:T(8,128)} %own_ref.1) | copy-start | bytes 3145732
  9.5 2.2 %copy-start.1 = (f32[2048,512]{1,0:T(8,128)S(1)}, f32[2048,512]{1,0:T(8,128)}, u32[]{:S(2)}) copy-start(f32[2048,512]{1,0:T(8,128)} %proj_ref.1) | copy-start | bytes 12582916
  11.7 0.9 %copy-start.3 = (f32[2048,9]{0,1:T(8,128)S(1)}, f32[2048,9]{0,1:T(8,128)}, u32[]{:S(2)}) copy-start(f32[2048,9]{0,1:T(8,128)} %param.10) | copy-start | bytes 221188
  16.6 8.4 %copy-start.4 = (f32[4,384]{1,0:T(4,128)S(1)}, f32[4,384]{1,0:T(4,128)}, u32[]{:S(2)}) copy-start(f32[4,384]{1,0:T(4,128)} %refs_6_.3) | copy-start | bytes 18436
  16.6 8.4 %copy-start.5 = (s32[512]{0:T(512)S(1)}, s32[512]{0:T(512)}, u32[]{:S(2)}) copy-start(s32[512]{0:T(512)} %param.13) | copy-start | bytes 6148
  16.6 11.2 %copy-start.2 = (f32[512,512]{1,0:T(8,128)S(1)}, f32[512,512]{1,0:T(8,128)}, u32[]{:S(2)}) copy-start(f32[512,512]{1,0:T(8,128)} %weight_ref.1) | copy-start | bytes 3145732
  17.5 2.0 %collective-permute-start.5 = (f32[144,512]{1,0:T(8,128)S(1)}, f32[144,512]{1,0:T(8,128)S(1)}, u32[]{:S(2)}, u32[]{:S(2)}) collective-permute-start(f32[144,512]{1,0:T(8,128)S(1)} %collective-permute-done.3.refs_2_), channel_id=1, source_target_pairs={{0,1},{1,0},{2,3},{3,2},{4,5},{5,4},{6,7},{7,6},{8,9},{9,8},{10,11... | collective-permute-start | bytes 884744 | tf_op jit(solution)/shard_map/ppermute | solution.py:477
  17.5 2.0 %collective-permute-start.4 = (f32[128,512]{1,0:T(8,128)S(1)}, f32[128,512]{1,0:T(8,128)S(1)}, u32[]{:S(2)}, u32[]{:S(2)}) collective-permute-start(f32[128,512]{1,0:T(8,128)S(1)} %collective-permute-done.2.refs_0_), channel_id=1, source_target_pairs={{0,1},{1,0},{2,3},{3,2},{4,5},{5,4},{6,7},{7,6},{8,9},{9,8},{10,11... | collective-permute-start | bytes 786440 | tf_op jit(solution)/shard_map/ppermute | solution.py:477
  21.0 6.7 %collective-permute-start.6 = (f32[16,384]{1,0:T(8,128)S(1)}, f32[16,384]{1,0:T(8,128)S(1)}, u32[]{:S(2)}, u32[]{:S(2)}) collective-permute-start(f32[16,384]{1,0:T(8,128)S(1)} %get-tuple-element.76), channel_id=1, source_target_pairs={{0,4},{4,8},{8,12},{12,16},{16,20},{20,24},{24,28},{1,5},{5,9},{9,... | collective-permute-start | bytes 73736 | tf_op jit(solution)/shard_map/ppermute | solution.py:536
  27.9 1.9 %collective-permute-start.7 = (f32[240,512]{1,0:T(8,128)S(1)}, f32[240,512]{1,0:T(8,128)S(1)}, u32[]{:S(2)}, u32[]{:S(2)}) collective-permute-start(f32[240,512]{1,0:T(8,128)S(1)} %collective-permute-done.1.refs_0_), channel_id=1, source_target_pairs={{0,1},{1,0},{2,3},{3,2},{4,5},{5,4},{6,7},{7,6},{8,9},{9,8},{10,11... | collective-permute-start | bytes 1474568 | tf_op jit(solution)/shard_map/ppermute | solution.py:477
  32.9 7.8 %collective-permute-start.8 = (f32[2,128,128]{2,1,0:T(8,128)S(1)}, f32[2,128,128]{2,1,0:T(8,128)S(1)}, u32[]{:S(2)}, u32[]{:S(2)}) collective-permute-start(f32[2,128,128]{2,1,0:T(8,128)S(1)} %get-tuple-element.80.own_ref), channel_id=1, source_target_pairs={{0,4},{4,0},{8,12},{12,8},{16,20},{20,16},{24,28},{28,24},{1,5},{5... | collective-permute-start | bytes 393224 | tf_op jit(solution)/shard_map/ppermute | solution.py:575
  34.7 7.3 %collective-permute-start.10 = (f32[2,128,128]{2,1,0:T(8,128)S(1)}, f32[2,128,128]{2,1,0:T(8,128)S(1)}, u32[]{:S(2)}, u32[]{:S(2)}) collective-permute-start(f32[2,128,128]{2,1,0:T(8,128)S(1)} %get-tuple-element.80.own_ref), channel_id=1, source_target_pairs={{0,12},{4,8},{8,4},{12,0},{16,28},{20,24},{24,20},{28,16},{1,13},{... | collective-permute-start | bytes 393224 | tf_op jit(solution)/shard_map/ppermute | solution.py:575
  36.2 6.4 %collective-permute-start.9 = (f32[2,128,128]{2,1,0:T(8,128)S(1)}, f32[2,128,128]{2,1,0:T(8,128)S(1)}, u32[]{:S(2)}, u32[]{:S(2)}) collective-permute-start(f32[2,128,128]{2,1,0:T(8,128)S(1)} %get-tuple-element.80.own_ref), channel_id=1, source_target_pairs={{0,8},{4,12},{8,0},{12,4},{16,24},{20,28},{24,16},{28,20},{1,9},{5... | collective-permute-start | bytes 393224 | tf_op jit(solution)/shard_map/ppermute | solution.py:575
  38.9 9.5 %copy-start.6 = (f32[128]{0:T(128)S(1)}, f32[128]{0:T(128)}, u32[]{:S(2)}) copy-start(f32[128]{0:T(128)} %param.14) | copy-start | bytes 1540
  43.1 5.2 %collective-permute-start.11 = (f32[128,128]{1,0:T(8,128)S(1)}, f32[128,128]{1,0:T(8,128)S(1)}, u32[]{:S(2)}, u32[]{:S(2)}) collective-permute-start(f32[128,128]{1,0:T(8,128)S(1)} %get-tuple-element.108), channel_id=1, source_target_pairs={{0,16},{4,20},{8,24},{12,28},{16,0},{20,4},{24,8},{28,12},{1,17},{... | collective-permute-start | bytes 196616 | tf_op jit(solution)/shard_map/ppermute | solution.py:594
  48.7 2.2 %collective-permute-start.12 = (f32[512,128]{1,0:T(8,128)S(1)}, f32[512,128]{1,0:T(8,128)S(1)}, u32[]{:S(2)}, u32[]{:S(2)}) collective-permute-start(f32[512,128]{1,0:T(8,128)S(1)} %get-tuple-element.110.own_ref), channel_id=1, source_target_pairs={{0,1},{1,0},{2,3},{3,2},{4,5},{5,4},{6,7},{7,6},{8,9},{9,8},{10,11... | collective-permute-start | bytes 786440 | tf_op jit(solution)/shard_map/ppermute | solution.py:477
  48.7 4.6 %collective-permute-start.14 = (f32[128,128]{1,0:T(8,128)S(1)}, f32[128,128]{1,0:T(8,128)S(1)}, u32[]{:S(2)}, u32[]{:S(2)}) collective-permute-start(f32[128,128]{1,0:T(8,128)S(1)} %get-tuple-element.112), channel_id=1, source_target_pairs={{0,2},{1,3},{2,0},{3,1},{4,6},{5,7},{6,4},{7,5},{8,10},{9,11},{10,... | collective-permute-start | bytes 196616 | tf_op jit(solution)/shard_map/ppermute | solution.py:483
  50.5 4.9 %collective-permute-start.15 = (f32[128,128]{1,0:T(8,128)S(1)}, f32[128,128]{1,0:T(8,128)S(1)}, u32[]{:S(2)}, u32[]{:S(2)}) collective-permute-start(f32[128,128]{1,0:T(8,128)S(1)} %get-tuple-element.113), channel_id=1, source_target_pairs={{0,2},{1,3},{2,0},{3,1},{4,6},{5,7},{6,4},{7,5},{8,10},{9,11},{10,... | collective-permute-start | bytes 196616 | tf_op jit(solution)/shard_map/ppermute | solution.py:483
  50.8 6.6 %collective-permute-start.13 = (f32[256,128]{1,0:T(8,128)S(1)}, f32[256,128]{1,0:T(8,128)S(1)}, u32[]{:S(2)}, u32[]{:S(2)}) collective-permute-start(f32[256,128]{1,0:T(8,128)S(1)} %get-tuple-element.111), channel_id=1, source_target_pairs={{0,2},{1,3},{2,0},{3,1},{4,6},{5,7},{6,4},{7,5},{8,10},{9,11},{10,... | collective-permute-start | bytes 393224 | tf_op jit(solution)/shard_map/ppermute | solution.py:483
  55.4 1.3 %collective-permute-start.16 = (f32[128,128]{1,0:T(8,128)S(1)}, f32[128,128]{1,0:T(8,128)S(1)}, u32[]{:S(2)}, u32[]{:S(2)}) collective-permute-start(f32[128,128]{1,0:T(8,128)S(1)} %collective-permute-done.14.refs_0_), channel_id=1, source_target_pairs={{0,1},{1,0},{2,3},{3,2},{4,5},{5,4},{6,7},{7,6},{8,9},{9,8},{10,11... | collective-permute-start | bytes 196616 | tf_op jit(solution)/shard_map/ppermute | solution.py:477
  55.4 1.4 %collective-permute-start.17 = (f32[128,128]{1,0:T(8,128)S(1)}, f32[128,128]{1,0:T(8,128)S(1)}, u32[]{:S(2)}, u32[]{:S(2)}) collective-permute-start(f32[128,128]{1,0:T(8,128)S(1)} %collective-permute-done.15.refs_2_), channel_id=1, source_target_pairs={{0,1},{1,0},{2,3},{3,2},{4,5},{5,4},{6,7},{7,6},{8,9},{9,8},{10,11... | collective-permute-start | bytes 196616 | tf_op jit(solution)/shard_map/ppermute | solution.py:477
  57.5 1.3 %collective-permute-start.18 = (f32[256,128]{1,0:T(8,128)S(1)}, f32[256,128]{1,0:T(8,128)S(1)}, u32[]{:S(2)}, u32[]{:S(2)}) collective-permute-start(f32[256,128]{1,0:T(8,128)S(1)} %collective-permute-done.13.refs_0_), channel_id=1, source_target_pairs={{0,1},{1,0},{2,3},{3,2},{4,5},{5,4},{6,7},{7,6},{8,9},{9,8},{10,11... | collective-permute-start | bytes 393224 | tf_op jit(solution)/shard_map/ppermute | solution.py:477

commit v18 on v17

--- a/solution.py
+++ b/solution.py
@@ -58,7 +58,15 @@
             jnp.concatenate([jnp.where(off, part, jnp.zeros_like(part)) for part in parts], axis=1)
             for parts in lower_parts
         ]
-        onto = [parts_dot(left, right_parts(inverse)) for left, inverse in zip(offs, inverses)]
+        if step == 1:
+            pairs = [jnp.where((row >> 1) == (col >> 1), lower, 0.0) for lower in lowers]
+            entries = [jnp.sum(pair, axis=0, keepdims=True) for pair in pairs]
+            parts = [jnp.where(off, lower, 0.0) for lower in lowers]
+            onto = [
+                part - pltpu.roll(part, size - 1, 1) * entry for part, entry in zip(parts, entries)
+            ]
+        else:
+            onto = [parts_dot(left, right_parts(inverse)) for left, inverse in zip(offs, inverses)]
         rights = [right_parts(value) for value in onto]
         squares = [parts_dot(left_parts(value), right) for value, right in zip(onto, rights)]
         firsts = [

time: 60.4 us -> 60.3 us (level)
  no operation moved by 1% of the time
where the time goes in v18:
time: 60.3 us; the launch traced here: 59.9 us
  starting transfers between devices  20.5 us (34%)
  Pallas kernels  18.7 us (31%)
  waiting for transfers between devices  12.2 us (20%)
  local copies, waits for them, and re-layouts  7.44 us (12%)
  between operations  1.02 us (2%)
    pallas_call x14, Pallas kernels, vmem_call(): pl.pallas_call(kernel, out_shape=outs, in_specs=[free if spot in any_in e...  18.7 us
    ppermute x6, starting transfers between devices, to_chips(): lax.ppermute(value, 'head', [(source, (source + 2 * step) % count) for so...  8.47 us
    unnamed x14, local copies, waits for them, and re-layouts  4.34 us
    ppermute x1, starting transfers between devices, shards(): lax.ppermute(rim, 'ctx', [(source, source + 1) for source in range(blocks...  3.99 us
    ppermute x3, waiting for transfers between devices, shards(): lax.ppermute(pair, 'ctx', [(source, source ^ mask << bit) for source in r...  3.75 us
    ppermute x6, waiting for transfers between devices, to_chips(): lax.ppermute(value, 'head', [(source, (source + 2 * step) % count) for so...  3.68 us
    ppermute x3, starting transfers between devices, shards(): lax.ppermute(pair, 'ctx', [(source, source ^ mask << bit) for source in r...  3.55 us
    ppermute x1, starting transfers between devices, shards(): lax.ppermute(pair if carry else pair[1], 'ctx', [(source, source ^ reach)...  2.8 us
  transfers between devices with their start and end apart: 19, of which 14 were waited for; matrix products, arithmetic and copies ran while one was open for 5% of the time, Pallas kernels for 23%

profile of v18, /device:TPU:0, one launch (start us, length us, event | category | flops | bytes accessed | tf_op | source)
XLA Modules:
  0.0 59.9 jit_solution(13956909135970860432)
XLA Ops:
  0.5 1.0 %slice.11 = f32[144,512]{1,0:T(8,128)S(1)} slice(f32[512,512]{1,0:T(8,128)} %own_ref.1), slice={[368:512], [0:512]} | slice | bytes 589824 | tf_op jit(solution)/shard_map/slice | solution.py:520
  1.4 2.6 %collective-permute-start.3 = (f32[144,512]{1,0:T(8,128)S(1)}, f32[144,512]{1,0:T(8,128)S(1)}, u32[]{:S(2)}, u32[]{:S(2)}) collective-permute-start(f32[144,512]{1,0:T(8,128)S(1)} %slice.11), channel_id=1, source_target_pairs={{0,2},{1,3},{2,0},{3,1},{4,6},{5,7},{6,4},{7,5},{8,10},{9,11},{10,... | collective-permute-start | bytes 884744 | tf_op jit(solution)/shard_map/ppermute | solution.py:491
  4.0 1.0 %slice.10 = f32[128,512]{1,0:T(8,128)S(1)} slice(f32[512,512]{1,0:T(8,128)} %own_ref.1), slice={[240:368], [0:512]} | slice | bytes 524288 | tf_op jit(solution)/shard_map/slice | solution.py:520
  5.2 1.1 %slice.9 = f32[240,512]{1,0:T(8,128)S(1)} slice(f32[512,512]{1,0:T(8,128)} %own_ref.1), slice={[0:240], [0:512]} | slice | bytes 983040 | tf_op jit(solution)/shard_map/slice | solution.py:523
  6.2 2.1 %collective-permute-start.1 = (f32[240,512]{1,0:T(8,128)S(1)}, f32[240,512]{1,0:T(8,128)S(1)}, u32[]{:S(2)}, u32[]{:S(2)}) collective-permute-start(f32[240,512]{1,0:T(8,128)S(1)} %slice.9), channel_id=1, source_target_pairs={{0,2},{1,3},{2,0},{3,1},{4,6},{5,7},{6,4},{7,5},{8,10},{9,11},{10,... | collective-permute-start | bytes 1474568 | tf_op jit(solution)/shard_map/ppermute | solution.py:491
  8.3 1.2 %copy-done = f32[512,512]{1,0:T(8,128)S(1)} copy-done((f32[512,512]{1,0:T(8,128)S(1)}, f32[512,512]{1,0:T(8,128)}, u32[]{:S(2)}) %copy-start) | copy-done | bytes 1048600
  9.5 2.2 %copy-done.1 = f32[2048,512]{1,0:T(8,128)S(1)} copy-done((f32[2048,512]{1,0:T(8,128)S(1)}, f32[2048,512]{1,0:T(8,128)}, u32[]{:S(2)}) %copy-start.1) | copy-done | bytes 4194328
  11.7 0.9 %copy-done.3 = f32[2048,9]{0,1:T(8,128)S(1)} copy-done((f32[2048,9]{0,1:T(8,128)S(1)}, f32[2048,9]{0,1:T(8,128)}, u32[]{:S(2)}) %copy-start.3) | copy-done | bytes 73752
  12.6 4.0 %shard_map.82 = (f32[512,384]{1,0:T(8,128)S(1)}, f32[512,256]{1,0:T(8,128)S(1)}, bf16[1024,768]{1,0:T(8,128)(2,1)S(1)}, bf16[1024,512]{1,0:T(8,128)(2,1)S(1)}, s32[3,128]{1,0:T(4,128)S(1)}) custom-call(s32[7]{0:T(128)S(1)} %stack.31.index_ref, f32[512,512]{1,0:T(8,128)S(1)} %copy-done, f32[512,512]{1,0:T(8,128)S(1)} %collective-permute-done.beside_ref, ...), custom_call_target="tpu_custom_call" | custom-call | flops 3000000000 | bytes 1048576 | tf_op jit(solution)/shard_map/pallas_call | solution.py:466
  16.6 0.9 %collective-permute-done.2.refs_0_ = f32[128,512]{1,0:T(8,128)S(1)} collective-permute-done((f32[128,512]{1,0:T(8,128)S(1)}, f32[128,512]{1,0:T(8,128)S(1)}, u32[]{:S(2)}, u32[]{:S(2)}) %collective-permute-start.2) | collective-permute-done | bytes 262176 | tf_op jit(solution)/shard_map/ppermute | solution.py:491
  18.7 0.8 %collective-permute-done.4.refs_1_ = f32[128,512]{1,0:T(8,128)S(1)} collective-permute-done((f32[128,512]{1,0:T(8,128)S(1)}, f32[128,512]{1,0:T(8,128)S(1)}, u32[]{:S(2)}, u32[]{:S(2)}) %collective-permute-start.4) | collective-permute-done | bytes 262176 | tf_op jit(solution)/shard_map/ppermute | solution.py:485
  19.5 1.5 %shard_map.83 = (f32[272,384]{1,0:T(8,128)S(1)}, f32[272,256]{1,0:T(8,128)S(1)}, f32[16,384]{1,0:T(8,128)S(1)}) custom-call(f32[128,512]{1,0:T(8,128)S(1)} %collective-permute-done.2.refs_0_, f32[128,512]{1,0:T(8,128)S(1)} %collective-permute-done.4.refs_1_, f32[144,512]{1,0:T(8,128)S(1)} %collective-permute-done.3.refs_2_, ...), custom_call_target="tpu_custom_call" | custom-call | flops 500000000 | bytes 1048576 | tf_op jit(solution)/shard_map/pallas_call | solution.py:466
  21.0 4.0 %collective-permute-start.6 = (f32[16,384]{1,0:T(8,128)S(1)}, f32[16,384]{1,0:T(8,128)S(1)}, u32[]{:S(2)}, u32[]{:S(2)}) collective-permute-start(f32[16,384]{1,0:T(8,128)S(1)} %get-tuple-element.76), channel_id=1, source_target_pairs={{0,4},{4,8},{8,12},{12,16},{16,20},{20,24},{24,28},{1,5},{5,9},{9,... | collective-permute-start | bytes 73736 | tf_op jit(solution)/shard_map/ppermute | solution.py:544
  25.0 2.6 %shard_map.84 = (f32[256,128]{1,0:T(8,128)S(1)}, f32[256,128]{1,0:T(8,128)S(1)}, f32[256,128]{1,0:T(8,128)S(1)}, f32[256,128]{1,0:T(8,128)S(1)}, f32[256,128]{1,...) custom-call(f32[272,384]{1,0:T(8,128)S(1)} %get-tuple-element.74.raw_ref.refs_4_,, ...), custom_call_target="tpu_custom_call" | custom-call | flops 500000000 | bytes 1048576 | tf_op jit(solution)/shard_map/pallas_call | solution.py:466
  27.9 0.7 %shard_map.88.weight_ref.refs_4_.refs_1_ = bf16[512,1024]{1,0:T(8,128)(2,1)S(1)} custom-call(s32[7]{0:T(128)S(1)} %stack.31.index_ref, f32[512,512]{1,0:T(8,128)S(1)} %copy-done.2), custom_call_target="tpu_custom_call" | custom-call | flops 1000000000 | bytes 1048576 | tf_op jit(solution)/shard_map/pallas_call | solution.py:466
  29.0 0.7 %collective-permute-done.7.refs_0_.refs_1_ = f32[240,512]{1,0:T(8,128)S(1)} collective-permute-done((f32[240,512]{1,0:T(8,128)S(1)}, f32[240,512]{1,0:T(8,128)S(1)}, u32[]{:S(2)}, u32[]{:S(2)}) %collective-permute-start.7) | collective-permute-done | bytes 491552 | tf_op jit(solution)/shard_map/ppermute | solution.py:485
  29.7 3.1 %shard_map.86 = (f32[256,128]{1,0:T(8,128)S(1)}, f32[256,128]{1,0:T(8,128)S(1)}, f32[256,128]{1,0:T(8,128)S(1)}, f32[256,128]{1,0:T(8,128)S(1)}, f32[256,128]{1,...) custom-call(f32[240,512]{1,0:T(8,128)S(1)} %collective-permute-done.7.refs_0_.ref, ...), custom_call_target="tpu_custom_call" | custom-call | flops 5000000000 | bytes 1048576 | tf_op jit(solution)/shard_map/pallas_call | solution.py:466
  32.8 1.8 %collective-permute-start.8 = (f32[2,128,128]{2,1,0:T(8,128)S(1)}, f32[2,128,128]{2,1,0:T(8,128)S(1)}, u32[]{:S(2)}, u32[]{:S(2)}) collective-permute-start(f32[2,128,128]{2,1,0:T(8,128)S(1)} %get-tuple-element.80.own_ref), channel_id=1, source_target_pairs={{0,4},{4,0},{8,12},{12,8},{16,20},{20,16},{24,28},{28,24},{1,5},{5... | collective-permute-start | bytes 393224 | tf_op jit(solution)/shard_map/ppermute | solution.py:583
  34.6 1.5 %collective-permute-start.10 = (f32[2,128,128]{2,1,0:T(8,128)S(1)}, f32[2,128,128]{2,1,0:T(8,128)S(1)}, u32[]{:S(2)}, u32[]{:S(2)}) collective-permute-start(f32[2,128,128]{2,1,0:T(8,128)S(1)} %get-tuple-element.80.own_ref), channel_id=1, source_target_pairs={{0,12},{4,8},{8,4},{12,0},{16,28},{20,24},{24,20},{28,16},{1,13},{... | collective-permute-start | bytes 393224 | tf_op jit(solution)/shard_map/ppermute | solution.py:583
  36.4 2.4 %shard_map.87 = (f32[512,128]{1,0:T(8,128)S(1)}, f32[512,128]{1,0:T(8,128)S(1)}, f32[512,128]{1,0:T(8,128)S(1)}) custom-call(f32[240,512]{1,0:T(8,128)S(1)} %collective-permute-done.1.refs_0_, f32[240,512]{1,0:T(8,128)S(1)} %collective-permute-done.7.refs_0_.refs_1_, f32[512,256]{1,0:T(8,128)S(1)} %get-tuple-element.71.refs_5_.refs_2_, ...), custom_call_target="tpu_custom_call" | custom-call | flops 5000000000 | bytes 1048576 | tf_op jit(solution)/shard_map/pallas_call | solution.py:466
  38.8 1.8 %collective-permute-done.8.one_ref = f32[2,128,128]{2,1,0:T(8,128)S(1)} collective-permute-done((f32[2,128,128]{2,1,0:T(8,128)S(1)}, f32[2,128,128]{2,1,0:T(8,128)S(1)}, u32[]{:S(2)}, u32[]{:S(2)}) %collective-permute-start.8) | collective-permute-done | bytes 131104 | tf_op jit(solution)/shard_map/ppermute | solution.py:583
  40.6 1.3 %collective-permute-done.10.three_ref = f32[2,128,128]{2,1,0:T(8,128)S(1)} collective-permute-done((f32[2,128,128]{2,1,0:T(8,128)S(1)}, f32[2,128,128]{2,1,0:T(8,128)S(1)}, u32[]{:S(2)}, u32[]{:S(2)}) %collective-permute-start.10) | collective-permute-done | bytes 131104 | tf_op jit(solution)/shard_map/ppermute | solution.py:583
  41.9 0.7 %collective-permute-done.9.two_ref = f32[2,128,128]{2,1,0:T(8,128)S(1)} collective-permute-done((f32[2,128,128]{2,1,0:T(8,128)S(1)}, f32[2,128,128]{2,1,0:T(8,128)S(1)}, u32[]{:S(2)}, u32[]{:S(2)}) %collective-permute-start.9) | collective-permute-done | bytes 131104 | tf_op jit(solution)/shard_map/ppermute | solution.py:583
  43.0 2.8 %collective-permute-start.11 = (f32[128,128]{1,0:T(8,128)S(1)}, f32[128,128]{1,0:T(8,128)S(1)}, u32[]{:S(2)}, u32[]{:S(2)}) collective-permute-start(f32[128,128]{1,0:T(8,128)S(1)} %get-tuple-element.108), channel_id=1, source_target_pairs={{0,16},{4,20},{8,24},{12,28},{16,0},{20,4},{24,8},{28,12},{1,17},{... | collective-permute-start | bytes 196616 | tf_op jit(solution)/shard_map/ppermute | solution.py:602
  46.2 2.0 %collective-permute-done.11.refs_1_ = f32[128,128]{1,0:T(8,128)S(1)} collective-permute-done((f32[128,128]{1,0:T(8,128)S(1)}, f32[128,128]{1,0:T(8,128)S(1)}, u32[]{:S(2)}, u32[]{:S(2)}) %collective-permute-start.11) | collective-permute-done | bytes 65568 | tf_op jit(solution)/shard_map/ppermute | solution.py:602
  48.6 1.7 %collective-permute-start.14 = (f32[128,128]{1,0:T(8,128)S(1)}, f32[128,128]{1,0:T(8,128)S(1)}, u32[]{:S(2)}, u32[]{:S(2)}) collective-permute-start(f32[128,128]{1,0:T(8,128)S(1)} %get-tuple-element.112), channel_id=1, source_target_pairs={{0,2},{1,3},{2,0},{3,1},{4,6},{5,7},{6,4},{7,5},{8,10},{9,11},{10,... | collective-permute-start | bytes 196616 | tf_op jit(solution)/shard_map/ppermute | solution.py:491
  50.7 1.7 %collective-permute-start.13 = (f32[256,128]{1,0:T(8,128)S(1)}, f32[256,128]{1,0:T(8,128)S(1)}, u32[]{:S(2)}, u32[]{:S(2)}) collective-permute-start(f32[256,128]{1,0:T(8,128)S(1)} %get-tuple-element.111), channel_id=1, source_target_pairs={{0,2},{1,3},{2,0},{3,1},{4,6},{5,7},{6,4},{7,5},{8,10},{9,11},{10,... | collective-permute-start | bytes 393224 | tf_op jit(solution)/shard_map/ppermute | solution.py:491
  52.4 0.6 shard_map.92
  53.2 2.1 %collective-permute-done.15.refs_2_ = f32[128,128]{1,0:T(8,128)S(1)} collective-permute-done((f32[128,128]{1,0:T(8,128)S(1)}, f32[128,128]{1,0:T(8,128)S(1)}, u32[]{:S(2)}, u32[]{:S(2)}) %collective-permute-start.15) | collective-permute-done | bytes 65568 | tf_op jit(solution)/shard_map/ppermute | solution.py:491
  55.8 0.7 %collective-permute-done.16.refs_1_ = f32[128,128]{1,0:T(8,128)S(1)} collective-permute-done((f32[128,128]{1,0:T(8,128)S(1)}, f32[128,128]{1,0:T(8,128)S(1)}, u32[]{:S(2)}, u32[]{:S(2)}) %collective-permute-start.16) | collective-permute-done | bytes 65568 | tf_op jit(solution)/shard_map/ppermute | solution.py:485
  57.5 0.8 %shard_map.94 = (f32[512,512]{1,0:T(8,128)}, f32[256,512]{1,0:T(8,128)S(1)}) custom-call(f32[256,128]{1,0:T(8,128)S(1)} %collective-permute-done.13.refs_0_, bf16[512,1024]{1,0:T(8,128)(2,1)S(1)} %shard_map.88.weight_ref.refs_4_.refs_1_, f32[256,512]{1,0:T(8,128)S(1)} %shard_map.93.refs_2_, f32[256,512]{1,0:T(8,128)S(1)} %get-tuple-element.122.refs_3_), custom_call_target="tpu_custom_call" | custom-call | flops 1000000000 | bytes 1048576 | tf_op jit(solution)/shard_map/pallas_call | solution.py:466
  58.7 1.1 %shard_map.95 = f32[512,512]{1,0:T(8,128)} custom-call(f32[256,128]{1,0:T(8,128)S(1)} %collective-permute-done.18.refs_0_, bf16[512,1024]{1,0:T(8,128)(2,1)S(1)} %shard_map.88.weight_ref.refs_4_.refs_1_, f32[256,512]{1,0:T(8,128)S(1)} %get-tuple-element.123.refs_2_, f32[512,512]{1,0:T(8,128)} %get-tuple-element.124.refs_3_), custom_call_target="tpu_custom_call", output_to_operand_aliasing={{}: (3, {})} | custom-call | flops 1000000000 | bytes 1048576 | tf_op jit(solution)/shard_map/pallas_call | solution.py:466
  (38 shorter events, 5.8 us)
Async XLA Ops:
  0.0 5.2 %collective-permute-start = (f32[512,512]{1,0:T(8,128)}, f32[512,512]{1,0:T(8,128)S(1)}, u32[]{:S(2)}, u32[]{:S(2)}) collective-permute-start(f32[512,512]{1,0:T(8,128)} %own_ref.1), channel_id=1, source_target_pairs={{0,1},{1,0},{2,3},{3,2},{4,5},{5,4},{6,7},{7,6},{8,9},{9,8},{10,11... | collective-permute-start | bytes 3145736 | tf_op jit(solution)/shard_map/ppermute | solution.py:485
  1.4 16.1 %collective-permute-start.3 = (f32[144,512]{1,0:T(8,128)S(1)}, f32[144,512]{1,0:T(8,128)S(1)}, u32[]{:S(2)}, u32[]{:S(2)}) collective-permute-start(f32[144,512]{1,0:T(8,128)S(1)} %slice.11), channel_id=1, source_target_pairs={{0,2},{1,3},{2,0},{3,1},{4,6},{5,7},{6,4},{7,5},{8,10},{9,11},{10,... | collective-permute-start | bytes 884744 | tf_op jit(solution)/shard_map/ppermute | solution.py:491
  5.0 12.5 %collective-permute-start.2 = (f32[128,512]{1,0:T(8,128)S(1)}, f32[128,512]{1,0:T(8,128)S(1)}, u32[]{:S(2)}, u32[]{:S(2)}) collective-permute-start(f32[128,512]{1,0:T(8,128)S(1)} %slice.10), channel_id=1, source_target_pairs={{0,2},{1,3},{2,0},{3,1},{4,6},{5,7},{6,4},{7,5},{8,10},{9,11},{10,... | collective-permute-start | bytes 786440 | tf_op jit(solution)/shard_map/ppermute | solution.py:491
  6.2 21.6 %collective-permute-start.1 = (f32[240,512]{1,0:T(8,128)S(1)}, f32[240,512]{1,0:T(8,128)S(1)}, u32[]{:S(2)}, u32[]{:S(2)}) collective-permute-start(f32[240,512]{1,0:T(8,128)S(1)} %slice.9), channel_id=1, source_target_pairs={{0,2},{1,3},{2,0},{3,1},{4,6},{5,7},{6,4},{7,5},{8,10},{9,11},{10,... | collective-permute-start | bytes 1474568 | tf_op jit(solution)/shard_map/ppermute | solution.py:491
  8.3 1.2 %copy-start = (f32[512,512]{1,0:T(8,128)S(1)}, f32[512,512]{1,0:T(8,128)}, u32[]{:S(2)}) copy-start(f32[512,512]{1,0:T(8,128)} %own_ref.1) | copy-start | bytes 3145732
  9.5 2.2 %copy-start.1 = (f32[2048,512]{1,0:T(8,128)S(1)}, f32[2048,512]{1,0:T(8,128)}, u32[]{:S(2)}) copy-start(f32[2048,512]{1,0:T(8,128)} %proj_ref.1) | copy-start | bytes 12582916
  11.7 0.9 %copy-start.3 = (f32[2048,9]{0,1:T(8,128)S(1)}, f32[2048,9]{0,1:T(8,128)}, u32[]{:S(2)}) copy-start(f32[2048,9]{0,1:T(8,128)} %param.10) | copy-start | bytes 221188
  16.6 8.4 %copy-start.4 = (f32[4,384]{1,0:T(4,128)S(1)}, f32[4,384]{1,0:T(4,128)}, u32[]{:S(2)}) copy-start(f32[4,384]{1,0:T(4,128)} %refs_6_.3) | copy-start | bytes 18436
  16.6 8.4 %copy-start.5 = (s32[512]{0:T(512)S(1)}, s32[512]{0:T(512)}, u32[]{:S(2)}) copy-start(s32[512]{0:T(512)} %param.13) | copy-start | bytes 6148
  16.6 11.2 %copy-start.2 = (f32[512,512]{1,0:T(8,128)S(1)}, f32[512,512]{1,0:T(8,128)}, u32[]{:S(2)}) copy-start(f32[512,512]{1,0:T(8,128)} %weight_ref.1) | copy-start | bytes 3145732
  17.5 2.0 %collective-permute-start.5 = (f32[144,512]{1,0:T(8,128)S(1)}, f32[144,512]{1,0:T(8,128)S(1)}, u32[]{:S(2)}, u32[]{:S(2)}) collective-permute-start(f32[144,512]{1,0:T(8,128)S(1)} %collective-permute-done.3.refs_2_), channel_id=1, source_target_pairs={{0,1},{1,0},{2,3},{3,2},{4,5},{5,4},{6,7},{7,6},{8,9},{9,8},{10,11... | collective-permute-start | bytes 884744 | tf_op jit(solution)/shard_map/ppermute | solution.py:485
  17.5 2.0 %collective-permute-start.4 = (f32[128,512]{1,0:T(8,128)S(1)}, f32[128,512]{1,0:T(8,128)S(1)}, u32[]{:S(2)}, u32[]{:S(2)}) collective-permute-start(f32[128,512]{1,0:T(8,128)S(1)} %collective-permute-done.2.refs_0_), channel_id=1, source_target_pairs={{0,1},{1,0},{2,3},{3,2},{4,5},{5,4},{6,7},{7,6},{8,9},{9,8},{10,11... | collective-permute-start | bytes 786440 | tf_op jit(solution)/shard_map/ppermute | solution.py:485
  21.0 6.7 %collective-permute-start.6 = (f32[16,384]{1,0:T(8,128)S(1)}, f32[16,384]{1,0:T(8,128)S(1)}, u32[]{:S(2)}, u32[]{:S(2)}) collective-permute-start(f32[16,384]{1,0:T(8,128)S(1)} %get-tuple-element.76), channel_id=1, source_target_pairs={{0,4},{4,8},{8,12},{12,16},{16,20},{20,24},{24,28},{1,5},{5,9},{9,... | collective-permute-start | bytes 73736 | tf_op jit(solution)/shard_map/ppermute | solution.py:544
  27.9 1.9 %collective-permute-start.7 = (f32[240,512]{1,0:T(8,128)S(1)}, f32[240,512]{1,0:T(8,128)S(1)}, u32[]{:S(2)}, u32[]{:S(2)}) collective-permute-start(f32[240,512]{1,0:T(8,128)S(1)} %collective-permute-done.1.refs_0_), channel_id=1, source_target_pairs={{0,1},{1,0},{2,3},{3,2},{4,5},{5,4},{6,7},{7,6},{8,9},{9,8},{10,11... | collective-permute-start | bytes 1474568 | tf_op jit(solution)/shard_map/ppermute | solution.py:485
  32.8 7.8 %collective-permute-start.8 = (f32[2,128,128]{2,1,0:T(8,128)S(1)}, f32[2,128,128]{2,1,0:T(8,128)S(1)}, u32[]{:S(2)}, u32[]{:S(2)}) collective-permute-start(f32[2,128,128]{2,1,0:T(8,128)S(1)} %get-tuple-element.80.own_ref), channel_id=1, source_target_pairs={{0,4},{4,0},{8,12},{12,8},{16,20},{20,16},{24,28},{28,24},{1,5},{5... | collective-permute-start | bytes 393224 | tf_op jit(solution)/shard_map/ppermute | solution.py:583
  34.6 7.3 %collective-permute-start.10 = (f32[2,128,128]{2,1,0:T(8,128)S(1)}, f32[2,128,128]{2,1,0:T(8,128)S(1)}, u32[]{:S(2)}, u32[]{:S(2)}) collective-permute-start(f32[2,128,128]{2,1,0:T(8,128)S(1)} %get-tuple-element.80.own_ref), channel_id=1, source_target_pairs={{0,12},{4,8},{8,4},{12,0},{16,28},{20,24},{24,20},{28,16},{1,13},{... | collective-permute-start | bytes 393224 | tf_op jit(solution)/shard_map/ppermute | solution.py:583
  36.1 6.4 %collective-permute-start.9 = (f32[2,128,128]{2,1,0:T(8,128)S(1)}, f32[2,128,128]{2,1,0:T(8,128)S(1)}, u32[]{:S(2)}, u32[]{:S(2)}) collective-permute-start(f32[2,128,128]{2,1,0:T(8,128)S(1)} %get-tuple-element.80.own_ref), channel_id=1, source_target_pairs={{0,8},{4,12},{8,0},{12,4},{16,24},{20,28},{24,16},{28,20},{1,9},{5... | collective-permute-start | bytes 393224 | tf_op jit(solution)/shard_map/ppermute | solution.py:583
  38.8 9.5 %copy-start.6 = (f32[128]{0:T(128)S(1)}, f32[128]{0:T(128)}, u32[]{:S(2)}) copy-start(f32[128]{0:T(128)} %param.14) | copy-start | bytes 1540
  43.0 5.2 %collective-permute-start.11 = (f32[128,128]{1,0:T(8,128)S(1)}, f32[128,128]{1,0:T(8,128)S(1)}, u32[]{:S(2)}, u32[]{:S(2)}) collective-permute-start(f32[128,128]{1,0:T(8,128)S(1)} %get-tuple-element.108), channel_id=1, source_target_pairs={{0,16},{4,20},{8,24},{12,28},{16,0},{20,4},{24,8},{28,12},{1,17},{... | collective-permute-start | bytes 196616 | tf_op jit(solution)/shard_map/ppermute | solution.py:602
  48.6 2.2 %collective-permute-start.12 = (f32[512,128]{1,0:T(8,128)S(1)}, f32[512,128]{1,0:T(8,128)S(1)}, u32[]{:S(2)}, u32[]{:S(2)}) collective-permute-start(f32[512,128]{1,0:T(8,128)S(1)} %get-tuple-element.110.own_ref), channel_id=1, source_target_pairs={{0,1},{1,0},{2,3},{3,2},{4,5},{5,4},{6,7},{7,6},{8,9},{9,8},{10,11... | collective-permute-start | bytes 786440 | tf_op jit(solution)/shard_map/ppermute | solution.py:485
  48.6 4.6 %collective-permute-start.14 = (f32[128,128]{1,0:T(8,128)S(1)}, f32[128,128]{1,0:T(8,128)S(1)}, u32[]{:S(2)}, u32[]{:S(2)}) collective-permute-start(f32[128,128]{1,0:T(8,128)S(1)} %get-tuple-element.112), channel_id=1, source_target_pairs={{0,2},{1,3},{2,0},{3,1},{4,6},{5,7},{6,4},{7,5},{8,10},{9,11},{10,... | collective-permute-start | bytes 196616 | tf_op jit(solution)/shard_map/ppermute | solution.py:491
  50.4 4.9 %collective-permute-start.15 = (f32[128,128]{1,0:T(8,128)S(1)}, f32[128,128]{1,0:T(8,128)S(1)}, u32[]{:S(2)}, u32[]{:S(2)}) collective-permute-start(f32[128,128]{1,0:T(8,128)S(1)} %get-tuple-element.113), channel_id=1, source_target_pairs={{0,2},{1,3},{2,0},{3,1},{4,6},{5,7},{6,4},{7,5},{8,10},{9,11},{10,... | collective-permute-start | bytes 196616 | tf_op jit(solution)/shard_map/ppermute | solution.py:491
  50.7 6.6 %collective-permute-start.13 = (f32[256,128]{1,0:T(8,128)S(1)}, f32[256,128]{1,0:T(8,128)S(1)}, u32[]{:S(2)}, u32[]{:S(2)}) collective-permute-start(f32[256,128]{1,0:T(8,128)S(1)} %get-tuple-element.111), channel_id=1, source_target_pairs={{0,2},{1,3},{2,0},{3,1},{4,6},{5,7},{6,4},{7,5},{8,10},{9,11},{10,... | collective-permute-start | bytes 393224 | tf_op jit(solution)/shard_map/ppermute | solution.py:491
  55.3 1.3 %collective-permute-start.16 = (f32[128,128]{1,0:T(8,128)S(1)}, f32[128,128]{1,0:T(8,128)S(1)}, u32[]{:S(2)}, u32[]{:S(2)}) collective-permute-start(f32[128,128]{1,0:T(8,128)S(1)} %collective-permute-done.14.refs_0_), channel_id=1, source_target_pairs={{0,1},{1,0},{2,3},{3,2},{4,5},{5,4},{6,7},{7,6},{8,9},{9,8},{10,11... | collective-permute-start | bytes 196616 | tf_op jit(solution)/shard_map/ppermute | solution.py:485
  55.3 1.4 %collective-permute-start.17 = (f32[128,128]{1,0:T(8,128)S(1)}, f32[128,128]{1,0:T(8,128)S(1)}, u32[]{:S(2)}, u32[]{:S(2)}) collective-permute-start(f32[128,128]{1,0:T(8,128)S(1)} %collective-permute-done.15.refs_2_), channel_id=1, source_target_pairs={{0,1},{1,0},{2,3},{3,2},{4,5},{5,4},{6,7},{7,6},{8,9},{9,8},{10,11... | collective-permute-start | bytes 196616 | tf_op jit(solution)/shard_map/ppermute | solution.py:485
  57.4 1.3 %collective-permute-start.18 = (f32[256,128]{1,0:T(8,128)S(1)}, f32[256,128]{1,0:T(8,128)S(1)}, u32[]{:S(2)}, u32[]{:S(2)}) collective-permute-start(f32[256,128]{1,0:T(8,128)S(1)} %collective-permute-done.13.refs_0_), channel_id=1, source_target_pairs={{0,1},{1,0},{2,3},{3,2},{4,5},{5,4},{6,7},{7,6},{8,9},{9,8},{10,11... | collective-permute-start | bytes 393224 | tf_op jit(solution)/shard_map/ppermute | solution.py:485

commit v19 on v18

--- a/solution.py
+++ b/solution.py
@@ -69,10 +69,17 @@
             onto = [parts_dot(left, right_parts(inverse)) for left, inverse in zip(offs, inverses)]
         rights = [right_parts(value) for value in onto]
         squares = [parts_dot(left_parts(value), right) for value, right in zip(onto, rights)]
-        firsts = [
-            inverse - parts_dot(left_parts(inverse), right)
-            for inverse, right in zip(inverses, rights)
-        ]
+        if step == 1:
+            columns = [jnp.sum(pair, axis=1, keepdims=True) for pair in pairs]
+            firsts = [
+                inverse - value + column * pltpu.roll(value, 1, 0)
+                for inverse, value, column in zip(inverses, onto, columns)
+            ]
+        else:
+            firsts = [
+                inverse - parts_dot(left_parts(inverse), right)
+                for inverse, right in zip(inverses, rights)
+            ]
         inverses = [first + product(first, square) for first, square in zip(firsts, squares)]
         step += 2
     return inverses

time: 60.3 us -> 60.3 us (level)
  no operation moved by 1% of the time
where the time goes in v19:
time: 60.3 us; the launch traced here: 59.9 us
  starting transfers between devices  20.5 us (34%)
  Pallas kernels  18.7 us (31%)
  waiting for transfers between devices  12.2 us (20%)
  local copies, waits for them, and re-layouts  7.44 us (12%)
  between operations  1.02 us (2%)
    pallas_call x14, Pallas kernels, vmem_call(): pl.pallas_call(kernel, out_shape=outs, in_specs=[free if spot in any_in e...  18.7 us
    ppermute x6, starting transfers between devices, to_chips(): lax.ppermute(value, 'head', [(source, (source + 2 * step) % count) for so...  8.47 us
    unnamed x14, local copies, waits for them, and re-layouts  4.34 us
    ppermute x1, starting transfers between devices, shards(): lax.ppermute(rim, 'ctx', [(source, source + 1) for source in range(blocks...  3.99 us
    ppermute x3, waiting for transfers between devices, shards(): lax.ppermute(pair, 'ctx', [(source, source ^ mask << bit) for source in r...  3.75 us
    ppermute x6, waiting for transfers between devices, to_chips(): lax.ppermute(value, 'head', [(source, (source + 2 * step) % count) for so...  3.69 us
    ppermute x3, starting transfers between devices, shards(): lax.ppermute(pair, 'ctx', [(source, source ^ mask << bit) for source in r...  3.55 us
    ppermute x1, starting transfers between devices, shards(): lax.ppermute(pair if carry else pair[1], 'ctx', [(source, source ^ reach)...  2.79 us
  transfers between devices with their start and end apart: 19, of which 14 were waited for; matrix products, arithmetic and copies ran while one was open for 5% of the time, Pallas kernels for 23%

profile of v19, /device:TPU:0, one launch (start us, length us, event | category | flops | bytes accessed | tf_op | source)
XLA Modules:
  0.0 59.9 jit_solution(15331800303243373809)
XLA Ops:
  0.5 1.0 %slice.11 = f32[144,512]{1,0:T(8,128)S(1)} slice(f32[512,512]{1,0:T(8,128)} %own_ref.1), slice={[368:512], [0:512]} | slice | bytes 589824 | tf_op jit(solution)/shard_map/slice | solution.py:527
  1.4 2.6 %collective-permute-start.3 = (f32[144,512]{1,0:T(8,128)S(1)}, f32[144,512]{1,0:T(8,128)S(1)}, u32[]{:S(2)}, u32[]{:S(2)}) collective-permute-start(f32[144,512]{1,0:T(8,128)S(1)} %slice.11), channel_id=1, source_target_pairs={{0,2},{1,3},{2,0},{3,1},{4,6},{5,7},{6,4},{7,5},{8,10},{9,11},{10,... | collective-permute-start | bytes 884744 | tf_op jit(solution)/shard_map/ppermute | solution.py:498
  4.0 1.0 %slice.10 = f32[128,512]{1,0:T(8,128)S(1)} slice(f32[512,512]{1,0:T(8,128)} %own_ref.1), slice={[240:368], [0:512]} | slice | bytes 524288 | tf_op jit(solution)/shard_map/slice | solution.py:527
  5.2 1.1 %slice.9 = f32[240,512]{1,0:T(8,128)S(1)} slice(f32[512,512]{1,0:T(8,128)} %own_ref.1), slice={[0:240], [0:512]} | slice | bytes 983040 | tf_op jit(solution)/shard_map/slice | solution.py:530
  6.2 2.1 %collective-permute-start.1 = (f32[240,512]{1,0:T(8,128)S(1)}, f32[240,512]{1,0:T(8,128)S(1)}, u32[]{:S(2)}, u32[]{:S(2)}) collective-permute-start(f32[240,512]{1,0:T(8,128)S(1)} %slice.9), channel_id=1, source_target_pairs={{0,2},{1,3},{2,0},{3,1},{4,6},{5,7},{6,4},{7,5},{8,10},{9,11},{10,... | collective-permute-start | bytes 1474568 | tf_op jit(solution)/shard_map/ppermute | solution.py:498
  8.3 1.2 %copy-done = f32[512,512]{1,0:T(8,128)S(1)} copy-done((f32[512,512]{1,0:T(8,128)S(1)}, f32[512,512]{1,0:T(8,128)}, u32[]{:S(2)}) %copy-start) | copy-done | bytes 1048600
  9.5 2.2 %copy-done.1 = f32[2048,512]{1,0:T(8,128)S(1)} copy-done((f32[2048,512]{1,0:T(8,128)S(1)}, f32[2048,512]{1,0:T(8,128)}, u32[]{:S(2)}) %copy-start.1) | copy-done | bytes 4194328
  11.7 0.9 %copy-done.3 = f32[2048,9]{0,1:T(8,128)S(1)} copy-done((f32[2048,9]{0,1:T(8,128)S(1)}, f32[2048,9]{0,1:T(8,128)}, u32[]{:S(2)}) %copy-start.3) | copy-done | bytes 73752
  12.6 4.0 %shard_map.82 = (f32[512,384]{1,0:T(8,128)S(1)}, f32[512,256]{1,0:T(8,128)S(1)}, bf16[1024,768]{1,0:T(8,128)(2,1)S(1)}, bf16[1024,512]{1,0:T(8,128)(2,1)S(1)}, s32[3,128]{1,0:T(4,128)S(1)}) custom-call(s32[7]{0:T(128)S(1)} %stack.31.index_ref, f32[512,512]{1,0:T(8,128)S(1)} %copy-done, f32[512,512]{1,0:T(8,128)S(1)} %collective-permute-done.beside_ref, ...), custom_call_target="tpu_custom_call" | custom-call | flops 3000000000 | bytes 1048576 | tf_op jit(solution)/shard_map/pallas_call | solution.py:473
  16.6 0.9 %collective-permute-done.2.refs_0_ = f32[128,512]{1,0:T(8,128)S(1)} collective-permute-done((f32[128,512]{1,0:T(8,128)S(1)}, f32[128,512]{1,0:T(8,128)S(1)}, u32[]{:S(2)}, u32[]{:S(2)}) %collective-permute-start.2) | collective-permute-done | bytes 262176 | tf_op jit(solution)/shard_map/ppermute | solution.py:498
  18.7 0.8 %collective-permute-done.4.refs_1_ = f32[128,512]{1,0:T(8,128)S(1)} collective-permute-done((f32[128,512]{1,0:T(8,128)S(1)}, f32[128,512]{1,0:T(8,128)S(1)}, u32[]{:S(2)}, u32[]{:S(2)}) %collective-permute-start.4) | collective-permute-done | bytes 262176 | tf_op jit(solution)/shard_map/ppermute | solution.py:492
  19.5 1.5 %shard_map.83 = (f32[272,384]{1,0:T(8,128)S(1)}, f32[272,256]{1,0:T(8,128)S(1)}, f32[16,384]{1,0:T(8,128)S(1)}) custom-call(f32[128,512]{1,0:T(8,128)S(1)} %collective-permute-done.2.refs_0_, f32[128,512]{1,0:T(8,128)S(1)} %collective-permute-done.4.refs_1_, f32[144,512]{1,0:T(8,128)S(1)} %collective-permute-done.3.refs_2_, ...), custom_call_target="tpu_custom_call" | custom-call | flops 500000000 | bytes 1048576 | tf_op jit(solution)/shard_map/pallas_call | solution.py:473
  21.0 4.0 %collective-permute-start.6 = (f32[16,384]{1,0:T(8,128)S(1)}, f32[16,384]{1,0:T(8,128)S(1)}, u32[]{:S(2)}, u32[]{:S(2)}) collective-permute-start(f32[16,384]{1,0:T(8,128)S(1)} %get-tuple-element.76), channel_id=1, source_target_pairs={{0,4},{4,8},{8,12},{12,16},{16,20},{20,24},{24,28},{1,5},{5,9},{9,... | collective-permute-start | bytes 73736 | tf_op jit(solution)/shard_map/ppermute | solution.py:551
  25.0 2.6 %shard_map.84 = (f32[256,128]{1,0:T(8,128)S(1)}, f32[256,128]{1,0:T(8,128)S(1)}, f32[256,128]{1,0:T(8,128)S(1)}, f32[256,128]{1,0:T(8,128)S(1)}, f32[256,128]{1,...) custom-call(f32[272,384]{1,0:T(8,128)S(1)} %get-tuple-element.74.raw_ref.refs_4_,, ...), custom_call_target="tpu_custom_call" | custom-call | flops 500000000 | bytes 1048576 | tf_op jit(solution)/shard_map/pallas_call | solution.py:473
  27.9 0.7 %shard_map.88.weight_ref.refs_4_.refs_1_ = bf16[512,1024]{1,0:T(8,128)(2,1)S(1)} custom-call(s32[7]{0:T(128)S(1)} %stack.31.index_ref, f32[512,512]{1,0:T(8,128)S(1)} %copy-done.2), custom_call_target="tpu_custom_call" | custom-call | flops 1000000000 | bytes 1048576 | tf_op jit(solution)/shard_map/pallas_call | solution.py:473
  29.0 0.7 %collective-permute-done.7.refs_0_.refs_1_ = f32[240,512]{1,0:T(8,128)S(1)} collective-permute-done((f32[240,512]{1,0:T(8,128)S(1)}, f32[240,512]{1,0:T(8,128)S(1)}, u32[]{:S(2)}, u32[]{:S(2)}) %collective-permute-start.7) | collective-permute-done | bytes 491552 | tf_op jit(solution)/shard_map/ppermute | solution.py:492
  29.7 3.1 %shard_map.86 = (f32[256,128]{1,0:T(8,128)S(1)}, f32[256,128]{1,0:T(8,128)S(1)}, f32[256,128]{1,0:T(8,128)S(1)}, f32[256,128]{1,0:T(8,128)S(1)}, f32[256,128]{1,...) custom-call(f32[240,512]{1,0:T(8,128)S(1)} %collective-permute-done.7.refs_0_.ref, ...), custom_call_target="tpu_custom_call" | custom-call | flops 5000000000 | bytes 1048576 | tf_op jit(solution)/shard_map/pallas_call | solution.py:473
  32.8 1.8 %collective-permute-start.8 = (f32[2,128,128]{2,1,0:T(8,128)S(1)}, f32[2,128,128]{2,1,0:T(8,128)S(1)}, u32[]{:S(2)}, u32[]{:S(2)}) collective-permute-start(f32[2,128,128]{2,1,0:T(8,128)S(1)} %get-tuple-element.80.own_ref), channel_id=1, source_target_pairs={{0,4},{4,0},{8,12},{12,8},{16,20},{20,16},{24,28},{28,24},{1,5},{5... | collective-permute-start | bytes 393224 | tf_op jit(solution)/shard_map/ppermute | solution.py:590
  34.6 1.5 %collective-permute-start.10 = (f32[2,128,128]{2,1,0:T(8,128)S(1)}, f32[2,128,128]{2,1,0:T(8,128)S(1)}, u32[]{:S(2)}, u32[]{:S(2)}) collective-permute-start(f32[2,128,128]{2,1,0:T(8,128)S(1)} %get-tuple-element.80.own_ref), channel_id=1, source_target_pairs={{0,12},{4,8},{8,4},{12,0},{16,28},{20,24},{24,20},{28,16},{1,13},{... | collective-permute-start | bytes 393224 | tf_op jit(solution)/shard_map/ppermute | solution.py:590
  36.3 2.4 %shard_map.87 = (f32[512,128]{1,0:T(8,128)S(1)}, f32[512,128]{1,0:T(8,128)S(1)}, f32[512,128]{1,0:T(8,128)S(1)}) custom-call(f32[240,512]{1,0:T(8,128)S(1)} %collective-permute-done.1.refs_0_, f32[240,512]{1,0:T(8,128)S(1)} %collective-permute-done.7.refs_0_.refs_1_, f32[512,256]{1,0:T(8,128)S(1)} %get-tuple-element.71.refs_5_.refs_2_, ...), custom_call_target="tpu_custom_call" | custom-call | flops 5000000000 | bytes 1048576 | tf_op jit(solution)/shard_map/pallas_call | solution.py:473
  38.8 1.8 %collective-permute-done.8.one_ref = f32[2,128,128]{2,1,0:T(8,128)S(1)} collective-permute-done((f32[2,128,128]{2,1,0:T(8,128)S(1)}, f32[2,128,128]{2,1,0:T(8,128)S(1)}, u32[]{:S(2)}, u32[]{:S(2)}) %collective-permute-start.8) | collective-permute-done | bytes 131104 | tf_op jit(solution)/shard_map/ppermute | solution.py:590
  40.6 1.3 %collective-permute-done.10.three_ref = f32[2,128,128]{2,1,0:T(8,128)S(1)} collective-permute-done((f32[2,128,128]{2,1,0:T(8,128)S(1)}, f32[2,128,128]{2,1,0:T(8,128)S(1)}, u32[]{:S(2)}, u32[]{:S(2)}) %collective-permute-start.10) | collective-permute-done | bytes 131104 | tf_op jit(solution)/shard_map/ppermute | solution.py:590
  41.9 0.7 %collective-permute-done.9.two_ref = f32[2,128,128]{2,1,0:T(8,128)S(1)} collective-permute-done((f32[2,128,128]{2,1,0:T(8,128)S(1)}, f32[2,128,128]{2,1,0:T(8,128)S(1)}, u32[]{:S(2)}, u32[]{:S(2)}) %collective-permute-start.9) | collective-permute-done | bytes 131104 | tf_op jit(solution)/shard_map/ppermute | solution.py:590
  43.0 2.8 %collective-permute-start.11 = (f32[128,128]{1,0:T(8,128)S(1)}, f32[128,128]{1,0:T(8,128)S(1)}, u32[]{:S(2)}, u32[]{:S(2)}) collective-permute-start(f32[128,128]{1,0:T(8,128)S(1)} %get-tuple-element.108), channel_id=1, source_target_pairs={{0,16},{4,20},{8,24},{12,28},{16,0},{20,4},{24,8},{28,12},{1,17},{... | collective-permute-start | bytes 196616 | tf_op jit(solution)/shard_map/ppermute | solution.py:609
  46.2 2.0 %collective-permute-done.11.refs_1_ = f32[128,128]{1,0:T(8,128)S(1)} collective-permute-done((f32[128,128]{1,0:T(8,128)S(1)}, f32[128,128]{1,0:T(8,128)S(1)}, u32[]{:S(2)}, u32[]{:S(2)}) %collective-permute-start.11) | collective-permute-done | bytes 65568 | tf_op jit(solution)/shard_map/ppermute | solution.py:609
  48.6 1.7 %collective-permute-start.14 = (f32[128,128]{1,0:T(8,128)S(1)}, f32[128,128]{1,0:T(8,128)S(1)}, u32[]{:S(2)}, u32[]{:S(2)}) collective-permute-start(f32[128,128]{1,0:T(8,128)S(1)} %get-tuple-element.112), channel_id=1, source_target_pairs={{0,2},{1,3},{2,0},{3,1},{4,6},{5,7},{6,4},{7,5},{8,10},{9,11},{10,... | collective-permute-start | bytes 196616 | tf_op jit(solution)/shard_map/ppermute | solution.py:498
  50.7 1.7 %collective-permute-start.13 = (f32[256,128]{1,0:T(8,128)S(1)}, f32[256,128]{1,0:T(8,128)S(1)}, u32[]{:S(2)}, u32[]{:S(2)}) collective-permute-start(f32[256,128]{1,0:T(8,128)S(1)} %get-tuple-element.111), channel_id=1, source_target_pairs={{0,2},{1,3},{2,0},{3,1},{4,6},{5,7},{6,4},{7,5},{8,10},{9,11},{10,... | collective-permute-start | bytes 393224 | tf_op jit(solution)/shard_map/ppermute | solution.py:498
  52.4 0.6 shard_map.92
  53.2 2.1 %collective-permute-done.15.refs_2_ = f32[128,128]{1,0:T(8,128)S(1)} collective-permute-done((f32[128,128]{1,0:T(8,128)S(1)}, f32[128,128]{1,0:T(8,128)S(1)}, u32[]{:S(2)}, u32[]{:S(2)}) %collective-permute-start.15) | collective-permute-done | bytes 65568 | tf_op jit(solution)/shard_map/ppermute | solution.py:498
  55.8 0.7 %collective-permute-done.16.refs_1_ = f32[128,128]{1,0:T(8,128)S(1)} collective-permute-done((f32[128,128]{1,0:T(8,128)S(1)}, f32[128,128]{1,0:T(8,128)S(1)}, u32[]{:S(2)}, u32[]{:S(2)}) %collective-permute-start.16) | collective-permute-done | bytes 65568 | tf_op jit(solution)/shard_map/ppermute | solution.py:492
  57.5 0.8 %shard_map.94 = (f32[512,512]{1,0:T(8,128)}, f32[256,512]{1,0:T(8,128)S(1)}) custom-call(f32[256,128]{1,0:T(8,128)S(1)} %collective-permute-done.13.refs_0_, bf16[512,1024]{1,0:T(8,128)(2,1)S(1)} %shard_map.88.weight_ref.refs_4_.refs_1_, f32[256,512]{1,0:T(8,128)S(1)} %shard_map.93.refs_2_, f32[256,512]{1,0:T(8,128)S(1)} %get-tuple-element.122.refs_3_), custom_call_target="tpu_custom_call" | custom-call | flops 1000000000 | bytes 1048576 | tf_op jit(solution)/shard_map/pallas_call | solution.py:473
  58.7 1.1 %shard_map.95 = f32[512,512]{1,0:T(8,128)} custom-call(f32[256,128]{1,0:T(8,128)S(1)} %collective-permute-done.18.refs_0_, bf16[512,1024]{1,0:T(8,128)(2,1)S(1)} %shard_map.88.weight_ref.refs_4_.refs_1_, f32[256,512]{1,0:T(8,128)S(1)} %get-tuple-element.123.refs_2_, f32[512,512]{1,0:T(8,128)} %get-tuple-element.124.refs_3_), custom_call_target="tpu_custom_call", output_to_operand_aliasing={{}: (3, {})} | custom-call | flops 1000000000 | bytes 1048576 | tf_op jit(solution)/shard_map/pallas_call | solution.py:473
  (38 shorter events, 5.8 us)
Async XLA Ops:
  0.0 5.2 %collective-permute-start = (f32[512,512]{1,0:T(8,128)}, f32[512,512]{1,0:T(8,128)S(1)}, u32[]{:S(2)}, u32[]{:S(2)}) collective-permute-start(f32[512,512]{1,0:T(8,128)} %own_ref.1), channel_id=1, source_target_pairs={{0,1},{1,0},{2,3},{3,2},{4,5},{5,4},{6,7},{7,6},{8,9},{9,8},{10,11... | collective-permute-start | bytes 3145736 | tf_op jit(solution)/shard_map/ppermute | solution.py:492
  1.4 16.1 %collective-permute-start.3 = (f32[144,512]{1,0:T(8,128)S(1)}, f32[144,512]{1,0:T(8,128)S(1)}, u32[]{:S(2)}, u32[]{:S(2)}) collective-permute-start(f32[144,512]{1,0:T(8,128)S(1)} %slice.11), channel_id=1, source_target_pairs={{0,2},{1,3},{2,0},{3,1},{4,6},{5,7},{6,4},{7,5},{8,10},{9,11},{10,... | collective-permute-start | bytes 884744 | tf_op jit(solution)/shard_map/ppermute | solution.py:498
  5.0 12.5 %collective-permute-start.2 = (f32[128,512]{1,0:T(8,128)S(1)}, f32[128,512]{1,0:T(8,128)S(1)}, u32[]{:S(2)}, u32[]{:S(2)}) collective-permute-start(f32[128,512]{1,0:T(8,128)S(1)} %slice.10), channel_id=1, source_target_pairs={{0,2},{1,3},{2,0},{3,1},{4,6},{5,7},{6,4},{7,5},{8,10},{9,11},{10,... | collective-permute-start | bytes 786440 | tf_op jit(solution)/shard_map/ppermute | solution.py:498
  6.2 21.6 %collective-permute-start.1 = (f32[240,512]{1,0:T(8,128)S(1)}, f32[240,512]{1,0:T(8,128)S(1)}, u32[]{:S(2)}, u32[]{:S(2)}) collective-permute-start(f32[240,512]{1,0:T(8,128)S(1)} %slice.9), channel_id=1, source_target_pairs={{0,2},{1,3},{2,0},{3,1},{4,6},{5,7},{6,4},{7,5},{8,10},{9,11},{10,... | collective-permute-start | bytes 1474568 | tf_op jit(solution)/shard_map/ppermute | solution.py:498
  8.3 1.2 %copy-start = (f32[512,512]{1,0:T(8,128)S(1)}, f32[512,512]{1,0:T(8,128)}, u32[]{:S(2)}) copy-start(f32[512,512]{1,0:T(8,128)} %own_ref.1) | copy-start | bytes 3145732
  9.5 2.2 %copy-start.1 = (f32[2048,512]{1,0:T(8,128)S(1)}, f32[2048,512]{1,0:T(8,128)}, u32[]{:S(2)}) copy-start(f32[2048,512]{1,0:T(8,128)} %proj_ref.1) | copy-start | bytes 12582916
  11.7 0.9 %copy-start.3 = (f32[2048,9]{0,1:T(8,128)S(1)}, f32[2048,9]{0,1:T(8,128)}, u32[]{:S(2)}) copy-start(f32[2048,9]{0,1:T(8,128)} %param.10) | copy-start | bytes 221188
  16.6 8.4 %copy-start.4 = (f32[4,384]{1,0:T(4,128)S(1)}, f32[4,384]{1,0:T(4,128)}, u32[]{:S(2)}) copy-start(f32[4,384]{1,0:T(4,128)} %refs_6_.3) | copy-start | bytes 18436
  16.6 8.4 %copy-start.5 = (s32[512]{0:T(512)S(1)}, s32[512]{0:T(512)}, u32[]{:S(2)}) copy-start(s32[512]{0:T(512)} %param.13) | copy-start | bytes 6148
  16.6 11.2 %copy-start.2 = (f32[512,512]{1,0:T(8,128)S(1)}, f32[512,512]{1,0:T(8,128)}, u32[]{:S(2)}) copy-start(f32[512,512]{1,0:T(8,128)} %weight_ref.1) | copy-start | bytes 3145732
  17.5 2.0 %collective-permute-start.5 = (f32[144,512]{1,0:T(8,128)S(1)}, f32[144,512]{1,0:T(8,128)S(1)}, u32[]{:S(2)}, u32[]{:S(2)}) collective-permute-start(f32[144,512]{1,0:T(8,128)S(1)} %collective-permute-done.3.refs_2_), channel_id=1, source_target_pairs={{0,1},{1,0},{2,3},{3,2},{4,5},{5,4},{6,7},{7,6},{8,9},{9,8},{10,11... | collective-permute-start | bytes 884744 | tf_op jit(solution)/shard_map/ppermute | solution.py:492
  17.5 2.0 %collective-permute-start.4 = (f32[128,512]{1,0:T(8,128)S(1)}, f32[128,512]{1,0:T(8,128)S(1)}, u32[]{:S(2)}, u32[]{:S(2)}) collective-permute-start(f32[128,512]{1,0:T(8,128)S(1)} %collective-permute-done.2.refs_0_), channel_id=1, source_target_pairs={{0,1},{1,0},{2,3},{3,2},{4,5},{5,4},{6,7},{7,6},{8,9},{9,8},{10,11... | collective-permute-start | bytes 786440 | tf_op jit(solution)/shard_map/ppermute | solution.py:492
  21.0 6.7 %collective-permute-start.6 = (f32[16,384]{1,0:T(8,128)S(1)}, f32[16,384]{1,0:T(8,128)S(1)}, u32[]{:S(2)}, u32[]{:S(2)}) collective-permute-start(f32[16,384]{1,0:T(8,128)S(1)} %get-tuple-element.76), channel_id=1, source_target_pairs={{0,4},{4,8},{8,12},{12,16},{16,20},{20,24},{24,28},{1,5},{5,9},{9,... | collective-permute-start | bytes 73736 | tf_op jit(solution)/shard_map/ppermute | solution.py:551
  27.9 1.9 %collective-permute-start.7 = (f32[240,512]{1,0:T(8,128)S(1)}, f32[240,512]{1,0:T(8,128)S(1)}, u32[]{:S(2)}, u32[]{:S(2)}) collective-permute-start(f32[240,512]{1,0:T(8,128)S(1)} %collective-permute-done.1.refs_0_), channel_id=1, source_target_pairs={{0,1},{1,0},{2,3},{3,2},{4,5},{5,4},{6,7},{7,6},{8,9},{9,8},{10,11... | collective-permute-start | bytes 1474568 | tf_op jit(solution)/shard_map/ppermute | solution.py:492
  32.8 7.8 %collective-permute-start.8 = (f32[2,128,128]{2,1,0:T(8,128)S(1)}, f32[2,128,128]{2,1,0:T(8,128)S(1)}, u32[]{:S(2)}, u32[]{:S(2)}) collective-permute-start(f32[2,128,128]{2,1,0:T(8,128)S(1)} %get-tuple-element.80.own_ref), channel_id=1, source_target_pairs={{0,4},{4,0},{8,12},{12,8},{16,20},{20,16},{24,28},{28,24},{1,5},{5... | collective-permute-start | bytes 393224 | tf_op jit(solution)/shard_map/ppermute | solution.py:590
  34.6 7.3 %collective-permute-start.10 = (f32[2,128,128]{2,1,0:T(8,128)S(1)}, f32[2,128,128]{2,1,0:T(8,128)S(1)}, u32[]{:S(2)}, u32[]{:S(2)}) collective-permute-start(f32[2,128,128]{2,1,0:T(8,128)S(1)} %get-tuple-element.80.own_ref), channel_id=1, source_target_pairs={{0,12},{4,8},{8,4},{12,0},{16,28},{20,24},{24,20},{28,16},{1,13},{... | collective-permute-start | bytes 393224 | tf_op jit(solution)/shard_map/ppermute | solution.py:590
  36.1 6.4 %collective-permute-start.9 = (f32[2,128,128]{2,1,0:T(8,128)S(1)}, f32[2,128,128]{2,1,0:T(8,128)S(1)}, u32[]{:S(2)}, u32[]{:S(2)}) collective-permute-start(f32[2,128,128]{2,1,0:T(8,128)S(1)} %get-tuple-element.80.own_ref), channel_id=1, source_target_pairs={{0,8},{4,12},{8,0},{12,4},{16,24},{20,28},{24,16},{28,20},{1,9},{5... | collective-permute-start | bytes 393224 | tf_op jit(solution)/shard_map/ppermute | solution.py:590
  38.8 9.5 %copy-start.6 = (f32[128]{0:T(128)S(1)}, f32[128]{0:T(128)}, u32[]{:S(2)}) copy-start(f32[128]{0:T(128)} %param.14) | copy-start | bytes 1540
  43.0 5.2 %collective-permute-start.11 = (f32[128,128]{1,0:T(8,128)S(1)}, f32[128,128]{1,0:T(8,128)S(1)}, u32[]{:S(2)}, u32[]{:S(2)}) collective-permute-start(f32[128,128]{1,0:T(8,128)S(1)} %get-tuple-element.108), channel_id=1, source_target_pairs={{0,16},{4,20},{8,24},{12,28},{16,0},{20,4},{24,8},{28,12},{1,17},{... | collective-permute-start | bytes 196616 | tf_op jit(solution)/shard_map/ppermute | solution.py:609
  48.5 2.2 %collective-permute-start.12 = (f32[512,128]{1,0:T(8,128)S(1)}, f32[512,128]{1,0:T(8,128)S(1)}, u32[]{:S(2)}, u32[]{:S(2)}) collective-permute-start(f32[512,128]{1,0:T(8,128)S(1)} %get-tuple-element.110.own_ref), channel_id=1, source_target_pairs={{0,1},{1,0},{2,3},{3,2},{4,5},{5,4},{6,7},{7,6},{8,9},{9,8},{10,11... | collective-permute-start | bytes 786440 | tf_op jit(solution)/shard_map/ppermute | solution.py:492
  48.6 4.6 %collective-permute-start.14 = (f32[128,128]{1,0:T(8,128)S(1)}, f32[128,128]{1,0:T(8,128)S(1)}, u32[]{:S(2)}, u32[]{:S(2)}) collective-permute-start(f32[128,128]{1,0:T(8,128)S(1)} %get-tuple-element.112), channel_id=1, source_target_pairs={{0,2},{1,3},{2,0},{3,1},{4,6},{5,7},{6,4},{7,5},{8,10},{9,11},{10,... | collective-permute-start | bytes 196616 | tf_op jit(solution)/shard_map/ppermute | solution.py:498
  50.3 4.9 %collective-permute-start.15 = (f32[128,128]{1,0:T(8,128)S(1)}, f32[128,128]{1,0:T(8,128)S(1)}, u32[]{:S(2)}, u32[]{:S(2)}) collective-permute-start(f32[128,128]{1,0:T(8,128)S(1)} %get-tuple-element.113), channel_id=1, source_target_pairs={{0,2},{1,3},{2,0},{3,1},{4,6},{5,7},{6,4},{7,5},{8,10},{9,11},{10,... | collective-permute-start | bytes 196616 | tf_op jit(solution)/shard_map/ppermute | solution.py:498
  50.7 6.6 %collective-permute-start.13 = (f32[256,128]{1,0:T(8,128)S(1)}, f32[256,128]{1,0:T(8,128)S(1)}, u32[]{:S(2)}, u32[]{:S(2)}) collective-permute-start(f32[256,128]{1,0:T(8,128)S(1)} %get-tuple-element.111), channel_id=1, source_target_pairs={{0,2},{1,3},{2,0},{3,1},{4,6},{5,7},{6,4},{7,5},{8,10},{9,11},{10,... | collective-permute-start | bytes 393224 | tf_op jit(solution)/shard_map/ppermute | solution.py:498
  55.3 1.3 %collective-permute-start.16 = (f32[128,128]{1,0:T(8,128)S(1)}, f32[128,128]{1,0:T(8,128)S(1)}, u32[]{:S(2)}, u32[]{:S(2)}) collective-permute-start(f32[128,128]{1,0:T(8,128)S(1)} %collective-permute-done.14.refs_0_), channel_id=1, source_target_pairs={{0,1},{1,0},{2,3},{3,2},{4,5},{5,4},{6,7},{7,6},{8,9},{9,8},{10,11... | collective-permute-start | bytes 196616 | tf_op jit(solution)/shard_map/ppermute | solution.py:492
  55.3 1.4 %collective-permute-start.17 = (f32[128,128]{1,0:T(8,128)S(1)}, f32[128,128]{1,0:T(8,128)S(1)}, u32[]{:S(2)}, u32[]{:S(2)}) collective-permute-start(f32[128,128]{1,0:T(8,128)S(1)} %collective-permute-done.15.refs_2_), channel_id=1, source_target_pairs={{0,1},{1,0},{2,3},{3,2},{4,5},{5,4},{6,7},{7,6},{8,9},{9,8},{10,11... | collective-permute-start | bytes 196616 | tf_op jit(solution)/shard_map/ppermute | solution.py:492
  57.4 1.3 %collective-permute-start.18 = (f32[256,128]{1,0:T(8,128)S(1)}, f32[256,128]{1,0:T(8,128)S(1)}, u32[]{:S(2)}, u32[]{:S(2)}) collective-permute-start(f32[256,128]{1,0:T(8,128)S(1)} %collective-permute-done.13.refs_0_), channel_id=1, source_target_pairs={{0,1},{1,0},{2,3},{3,2},{4,5},{5,4},{6,7},{7,6},{8,9},{9,8},{10,11... | collective-permute-start | bytes 393224 | tf_op jit(solution)/shard_map/ppermute | solution.py:492
